TPU v7x, 32 devices: a whole 2x2x4 slice. The times are simulated.
32 devices in a mesh: chan: 16 (over z, y, x), rad: 2 (over core).
Axes of the slice: x: 2, y: 2, z: 4, core: 2. Of those that a mesh axis runs over, the one named last changes fastest.
Arguments:
- trial_block: float32 [1024, 16, 128], P('chan', None, 'rad')
- ham_blocks: bfloat16 [1024, 8, 128, 128], P('chan', None, 'rad'), may hold values from -0.1875 to 0.1875
- partners: int32 [1024, 8], P('chan'), may hold values from 0 to 1023, as said below
- stored_at: int32 [1024], replicated, may hold values from 0 to 1023, as said below
- precond_diag: float32 [1024, 128], P('chan', 'rad'), may hold values from 1 to 10
Outputs:
- new_block: float32 [1024, 16, 128], P('chan', None, 'rad')
- ritz_values: float32 [16], replicated
Inputs may be any that keep to these rules, and one draw needn't show every extreme that they name: `stored_at`: A permutation of the channel numbers. `partners`: among the 512 entries of the rows p with p // 64 = d, for every d, at most 64 have stored_at[partner] // 64 equal to any one value; for every d some value has exactly 64.
All inputs are finite; a program needn't handle non-finite values.
Results may differ from a plain program's by a relative error of at most 0.0051.
Values may be sent and summed in bfloat16 or wider, within the bound.
No kernel may reach another device: no remote copies, remote signals or barrier semaphores. Data moves between devices by JAX's collectives and lax.ppermute only.
A program may use at most 64 MiB of HBM per device.

v0:
```python
import jax
import jax.numpy as jnp
from jax import lax
from jax.sharding import PartitionSpec as P

NCH = 1024
NB = 128


def chol_solve(factor, rhs):
    first = lax.linalg.triangular_solve(factor, rhs, left_side=True, lower=True)
    return lax.linalg.triangular_solve(factor, first, left_side=True, lower=True, transpose_a=True)


def inner_products(left, right):
    return jnp.einsum("pkr,plr->kl", left, right, precision=lax.Precision.HIGHEST)


def body(trial_block, ham_blocks, partners, stored_at, precond_diag):
    n_chan = lax.axis_size("chan")
    ch_dev = trial_block.shape[0]
    vectors = trial_block.shape[1]
    ncoup = partners.shape[1]
    capacity = 2 * ch_dev * ncoup // n_chan
    stored_rows = jnp.take(stored_at, partners.reshape(-1))
    owner_dev = stored_rows // ch_dev
    local_row = stored_rows % ch_dev
    one_hot = (owner_dev[:, None] == jnp.arange(n_chan, dtype=jnp.int32)[None, :]).astype(jnp.int32)
    running = jnp.cumsum(one_hot, axis=0)
    order_rank = jnp.sum(running * one_hot, axis=1) - 1
    slot_index = owner_dev * capacity + order_rank
    wanted = (
        jnp.zeros((n_chan * capacity,), jnp.int32)
        .at[slot_index]
        .set(local_row)
        .reshape(n_chan, capacity)
    )
    asked = lax.all_to_all(wanted, "chan", split_axis=0, concat_axis=0, tiled=True)
    rounded = trial_block.astype(jnp.bfloat16)
    whole_rows = lax.all_gather(rounded, "rad", axis=2, tiled=True)
    served = whole_rows[asked]
    received = lax.all_to_all(served, "chan", split_axis=0, concat_axis=0, tiled=True)
    full_splines = received.shape[3]
    coupled = received.reshape(n_chan * capacity, vectors, full_splines)[slot_index]
    coupled = coupled.reshape(ch_dev, ncoup, vectors, full_splines)
    applied = lax.dot_general(
        coupled, ham_blocks, (((1, 3), (1, 3)), ((0,), (0,))), preferred_element_type=jnp.float32
    )
    total_rows = jnp.float32(NCH * NB)
    proj_a, proj_b = lax.psum(
        (inner_products(trial_block, applied), inner_products(trial_block, trial_block)),
        ("chan", "rad"),
    )
    factor = jnp.linalg.cholesky(proj_b)
    coefficients = chol_solve(factor, proj_a)
    ritz_values = jnp.diagonal(coefficients)
    residual = applied - jnp.einsum(
        "pkr,kl->plr", trial_block, coefficients, precision=lax.Precision.HIGHEST
    )
    correction = residual / precond_diag[:, None, :]
    correlation = lax.psum(inner_products(trial_block, correction), ("chan", "rad"))
    mixing = chol_solve(factor, correlation)
    projected = correction - jnp.einsum(
        "pkr,kl->plr", trial_block, mixing, precision=lax.Precision.HIGHEST
    )
    correlation_gram = lax.psum(inner_products(projected, projected), ("chan", "rad")) / total_rows
    gram_factor = jnp.linalg.cholesky(correlation_gram)
    local_splines = projected.shape[2]
    flat_rows = jnp.transpose(projected, (1, 0, 2)).reshape(vectors, -1)
    solved = lax.linalg.triangular_solve(gram_factor, flat_rows, left_side=True, lower=True)
    new_block = jnp.transpose(solved.reshape(vectors, ch_dev, local_splines), (1, 0, 2))
    return (new_block, ritz_values)


def solution(mesh):
    return jax.shard_map(
        body,
        mesh=mesh,
        in_specs=(
            P("chan", None, "rad"),
            P("chan", None, "rad", None),
            P("chan", None),
            P(),
            P("chan", "rad"),
        ),
        out_specs=(P("chan", None, "rad"), P()),
        check_vma=False,
    )
```

profile of v0, /device:TPU:0, one launch (start us, length us, event | category | flops | bytes accessed | tf_op | source)
XLA Modules:
  0.0 277.3 jit_solution(4346693266810245876)
XLA Ops:
  0.6 0.8 copy.37
  1.7 2.3 gather_fusion
  4.1 1.2 reduce-window.6
  5.6 2.4 scatter_custom_fusion
  8.1 0.7 all_to_all.11
  8.8 8.3 %all-to-all-start = ((s32[16,1,64]{2,1,0:T(1,128)}), s32[16,1,64]{2,1,0:T(1,128)S(1)}, u32[]{:S(2)}, u32[]{:S(2)}) async-start(s32[16,1,64]{2,1,0:T(1,128)} %all_to_all.11), calls=%async_computation | async-start | bytes 16384 | tf_op jit(solution)/shard_map/all_to_all | solution.py:38
  17.1 1.4 copy.36
  18.5 2.2 all_gather.3
  21.3 3.0 %all-to-all-done = s32[16,1,64]{2,1,0:T(1,128)S(1)} async-done(((s32[16,1,64]{2,1,0:T(1,128)}), s32[16,1,64]{2,1,0:T(1,128)S(1)}, u32[]{:S(2)}, u32[]{:S(2)}) %all-to-all-start) | async-done | bytes 4128 | tf_op jit(solution)/shard_map/all_to_all | solution.py:38
  24.4 8.4 %gather_fusion.1 = bf16[1024,16,128]{2,1,0:T(8,128)(2,1)} fusion(bf16[64,16,128]{2,1,0:T(8,128)(2,1)S(1)} %copy.41, s32[1024]{0:T(1024)S(1)} %broadcast_clamp_fusion), kind=kCustom, calls=%fused_computation.1 | custom fusion | bytes 8392704 | tf_op jit(solution)/shard_map/gather | solution.py:41
  32.8 4.7 %all-to-all-start.1 = ((bf16[16,64,16,128]{3,2,1,0:T(8,128)(2,1)}), bf16[16,64,16,128]{3,2,1,0:T(8,128)(2,1)}, u32[]{:S(2)}, u32[]{:S(2)}) async-start(bf16[16,64,16,128]{3,2,1,0:T(8,128)(2,1)} %bitcast.125), calls=%async_computation.1 | async-start | bytes 8388608 | tf_op jit(solution)/shard_map/all_to_all | solution.py:42
  37.5 0.8 convolution_bitcast_fusion.5
  38.3 78.3 %all-to-all-done.1 = bf16[16,64,16,128]{3,2,1,0:T(8,128)(2,1)} async-done(((bf16[16,64,16,128]{3,2,1,0:T(8,128)(2,1)}), bf16[16,64,16,128]{3,2,1,0:T(8,128)(2,1)}, u32[]{:S(2)}, u32[]{:S(2)}) %all-to-all-start.1) | async-done | bytes 4194336 | tf_op jit(solution)/shard_map/all_to_all | solution.py:42
  116.5 3.4 %gather_fusion.2 = bf16[512,16,128]{2,1,0:T(8,128)(2,1)S(1)} fusion(bf16[1024,16,128]{2,1,0:T(8,128)(2,1)} %bitcast.8, s32[1024]{0:T(1024)S(1)} %pad_clamp_fusion), kind=kCustom, calls=%fused_computation.2 | custom fusion | bytes 4196352 | tf_op jit(solution)/shard_map/gather | solution.py:44
  119.9 5.7 %fusion.31 = f32[64,16,64,1]{2,1,3,0:T(8,128)S(1)} fusion(bf16[64,8,16,128]{3,2,1,0:T(8,128)(2,1)S(1)} %bitcast.126, bf16[64,8,64,128]{3,2,1,0:T(8,128)(2,1)} %param.11), kind=kOutput, calls=%fused_computation.87 | convolution fusion | flops 134217728 | bytes 10747904 | tf_op jit(solution)/shard_map/dot_general | solution.py:46
  125.6 0.8 convolution_bitcast_fusion.4
  126.4 55.5 %all-reduce = (f32[16,16]{0,1:T(8,128)S(1)}, f32[16,16]{0,1:T(8,128)S(1)}) all-reduce(f32[16,16]{0,1:T(8,128)S(1)} %convolution_bitcast_fusion.4, f32[16,16]{0,1:T(8,128)S(1)} %convolution_bitcast_fusion.5), channel_id=1, replica_groups=mesh['chan'=16,'rad'=2] {'chan','rad'}, use_global_device_ids=true, to_apply=%region_7.9 | all-reduce | flops 512 | bytes 4096 | tf_op jit(solution)/shard_map/psum | solution.py:50
  182.0 1.5 cholesky.44
  183.5 0.6 compare_reduce_fusion.1
  184.1 0.6 fusion.8
  184.8 1.2 custom-call.17
  186.4 0.6 fusion.12
  187.0 0.8 convolution_bitcast_fusion.3
  187.8 39.1 %psum.30 = f32[16,16]{0,1:T(8,128)S(1)} all-reduce(f32[16,16]{0,1:T(8,128)S(1)} %convolution_bitcast_fusion.3), channel_id=1, replica_groups=mesh['chan'=16,'rad'=2] {'chan','rad'}, use_global_device_ids=true, to_apply=%region_8.12 | all-reduce | flops 256 | bytes 2048 | tf_op jit(solution)/shard_map/psum | solution.py:61
  228.0 0.8 convolution_bitcast_fusion.1
  228.8 41.0 %psum.31 = f32[16,16]{0,1:T(8,128)S(1)} all-reduce(f32[16,16]{0,1:T(8,128)S(1)} %convolution_bitcast_fusion.1), channel_id=1, replica_groups=mesh['chan'=16,'rad'=2] {'chan','rad'}, use_global_device_ids=true, to_apply=%region_9.13 | all-reduce | flops 256 | bytes 2048 | tf_op jit(solution)/shard_map/psum | solution.py:66
  269.9 1.5 cholesky.55
  271.4 0.6 compare_reduce_fusion
  272.0 0.6 fusion.9
  272.7 1.2 custom-call.11
  274.5 1.2 gather_fusion.3
  275.7 1.6 convolution_bitcast_fusion
  (41 shorter events, 3.6 us)
Async XLA Ops:
  0.6 1.1 copy-start
  8.8 15.5 %all-to-all-start = ((s32[16,1,64]{2,1,0:T(1,128)}), s32[16,1,64]{2,1,0:T(1,128)S(1)}, u32[]{:S(2)}, u32[]{:S(2)}) async-start(s32[16,1,64]{2,1,0:T(1,128)} %all_to_all.11), calls=%async_computation | async-start | bytes 16384 | tf_op jit(solution)/shard_map/all_to_all | solution.py:38
  32.8 4.7 %copy-start.1 = (f32[64,16,64]{2,1,0:T(8,128)S(1)}, f32[64,16,64]{2,1,0:T(8,128)}, u32[]{:S(2)}) copy-start(f32[64,16,64]{2,1,0:T(8,128)} %param.10) | copy-start | bytes 786436
  32.8 83.8 %all-to-all-start.1 = ((bf16[16,64,16,128]{3,2,1,0:T(8,128)(2,1)}), bf16[16,64,16,128]{3,2,1,0:T(8,128)(2,1)}, u32[]{:S(2)}, u32[]{:S(2)}) async-start(bf16[16,64,16,128]{3,2,1,0:T(8,128)(2,1)} %bitcast.125), calls=%async_computation.1 | async-start | bytes 8388608 | tf_op jit(solution)/shard_map/all_to_all | solution.py:42
  119.9 67.1 %copy-start.2 = (f32[64,64]{1,0:T(8,128)S(1)}, f32[64,64]{1,0:T(8,128)}, u32[]{:S(2)}) copy-start(f32[64,64]{1,0:T(8,128)} %param.14) | copy-start | bytes 49156
where the time goes:
time: 278 us; the launch traced here: 277 us
  blocking collectives  138 us (50%)
  waiting for transfers between devices  81.3 us (29%)
  local copies, waits for them, and re-layouts  22.4 us (8%)
  starting transfers between devices  13 us (5%)
  matrix products  12.6 us (5%)
  other arithmetic  9.41 us (3%)
    all_to_all x1, waiting for transfers between devices, body(): lax.all_to_all(served, 'chan', split_axis=0, concat_axis=0, tiled=True)  78.3 us
    psum x1, blocking collectives, body(): lax.psum((inner_products(trial_block, applied), inner_products(trial_bloc...  55.5 us
    psum x1, blocking collectives, body(): lax.psum(inner_products(projected, projected), ('chan', 'rad')) / total_rows  41 us
    psum x1, blocking collectives, body(): lax.psum(inner_products(trial_block, correction), ('chan', 'rad'))  39.1 us
    gather x1, local copies, waits for them, and re-layouts, body(): served = whole_rows[asked]  8.39 us
    all_to_all x1, starting transfers between devices, body(): lax.all_to_all(wanted, 'chan', split_axis=0, concat_axis=0, tiled=True)  8.31 us
    dot_general x1, matrix products, body(): lax.dot_general(coupled, ham_blocks, (((1, 3), (1, 3)), ((0,), (0,))), pr...  5.68 us
  transfers between devices with their start and end apart: 2, of which 2 were waited for; matrix products, arithmetic and copies ran while one was open for 1% of the time, Pallas kernels for 0%

commit v1 on v0

v1 whole, which is shorter than its diff:
```python
import jax
import jax.numpy as jnp
from jax import lax
from jax.sharding import PartitionSpec as P

HIGHEST = lax.Precision.HIGHEST
SCALE = 2.0 ** -8


def chol_solve(factor, rhs):
    first = lax.linalg.triangular_solve(factor, rhs, left_side=True, lower=True)
    return lax.linalg.triangular_solve(factor, first, left_side=True, lower=True, transpose_a=True)


def exchange_sum(x, axis):
    n = lax.axis_size(axis)
    step = 1
    while step < n:
        x = x + lax.ppermute(x, axis, [(i, i ^ step) for i in range(n)])
        step *= 2
    return x


def body(trial_block, ham_blocks, partners, stored_at, precond_diag):
    n_chan = lax.axis_size("chan")
    n_rad = lax.axis_size("rad")
    ch_dev, vectors, _ = trial_block.shape
    ncoup = partners.shape[1]
    total = n_chan * ch_dev * n_rad * trial_block.shape[2]
    share = ch_dev // n_rad

    rounded = trial_block.astype(jnp.bfloat16)
    own = lax.all_gather(rounded, "rad", axis=2, tiled=True)
    mine = lax.dynamic_slice_in_dim(own, lax.axis_index("rad") * share, share, 0)
    part = lax.all_gather(mine, "chan", axis=0, tiled=True)
    table = lax.all_gather(part, "rad", axis=0, tiled=True)

    stored_rows = jnp.take(stored_at, partners.reshape(-1))
    owner = stored_rows // ch_dev
    local = stored_rows % ch_dev
    where = (local // share) * (n_chan * share) + owner * share + local % share
    coupled = table[where].reshape(ch_dev, ncoup, vectors, table.shape[2])
    applied = lax.dot_general(
        coupled, ham_blocks, (((1, 3), (1, 3)), ((0,), (0,))), preferred_element_type=jnp.float32
    ) * SCALE

    t0 = trial_block
    inv = (1.0 / precond_diag)[:, None, :]
    t1 = t0 * inv
    t2 = t1 * inv
    a2 = applied * inv * inv
    gram_t = jnp.einsum("xpkr,plr->xkl", jnp.stack([t0, t1, t2]), t0, precision=HIGHEST)
    gram_a = jnp.einsum("xpkr,plr->xkl", jnp.stack([t0, t1, t2, a2]), applied, precision=HIGHEST)
    sums = jnp.concatenate([gram_t, gram_a]).reshape(-1, 128)
    sums = exchange_sum(exchange_sum(sums, "rad"), "chan").reshape(7, vectors, vectors)
    b0, b1, b2, s0, s1, s2, aa = (sums[i] for i in range(7))

    def mm(x, y):
        return jnp.matmul(x, y, precision=HIGHEST)

    factor = jnp.linalg.cholesky(b0)
    coef = chol_solve(factor, s0)
    ritz_values = jnp.diagonal(coef) * (1.0 / SCALE)
    mix = chol_solve(factor, s1 - mm(b1, coef))
    cross = mm(s2.T, coef) + mm(s1.T, mix)
    tt = mm(coef.T, mm(b2, coef)) + mm(mix.T, mm(b0, mix))
    tm = mm(coef.T, mm(b1, mix))
    gram = (aa - cross - cross.T + tt + tm + tm.T) / jnp.float32(total)
    gram_factor = jnp.linalg.cholesky(gram)
    ident = jnp.eye(vectors, dtype=jnp.float32)
    linv = lax.linalg.triangular_solve(gram_factor, ident, left_side=True, lower=True)
    wc = mm(linv, coef.T)
    wm = mm(linv, mix.T)
    out = (
        jnp.einsum("lk,pkr->plr", linv, applied, precision=HIGHEST)
        - jnp.einsum("lk,pkr->plr", wc, t0, precision=HIGHEST)
    ) * inv - jnp.einsum("lk,pkr->plr", wm, t0, precision=HIGHEST)
    return (out, ritz_values)


def solution(mesh):
    return jax.shard_map(
        body,
        mesh=mesh,
        in_specs=(
            P("chan", None, "rad"),
            P("chan", None, "rad", None),
            P("chan", None),
            P(),
            P("chan", "rad"),
        ),
        out_specs=(P("chan", None, "rad"), P()),
        check_vma=False,
    )
```

time: 278 us -> 142 us (0.51)
  blocking collectives: 138 us -> 2.26 us
  between operations: 0.85 us -> 14.2 us
  local copies, waits for them, and re-layouts: 22.4 us -> 10.2 us
  starting transfers between devices: 13 us -> 8.18 us
    psum x3 -> x0, blocking collectives: 136 us -> none  [the longest x1 55.5 us: body(): lax.psum((inner_products(trial_block, applied), inner_products(trial_bloc...]
    all_to_all x2 -> x0, waiting for transfers between devices: 81.3 us -> none  [the longest x1 78.3 us: body(): lax.all_to_all(served, 'chan', split_axis=0, concat_axis=0, tiled=True)]
    all_gather x0 -> x2, waiting for transfers between devices: none -> 74.7 us  [the longest x1 63.4 us: body(): part = lax.all_gather(mine, 'chan', axis=0, tiled=True)]
    all_to_all x2 -> x0, starting transfers between devices: 13 us -> none  [the longest x1 8.31 us: body(): lax.all_to_all(wanted, 'chan', split_axis=0, concat_axis=0, tiled=True)]
    gather x3 -> x2, local copies, waits for them, and re-layouts: 12.9 us -> 4.03 us  [the longest x1 3.37 us: body(): coupled = table[where].reshape(ch_dev, ncoup, vectors, table.shape[2])]
    ppermute x0 -> x5, waiting for transfers between devices: none -> 8.6 us  [exchange_sum(): x = x + lax.ppermute(x, axis, [(i, i ^ step) for i in range(n)])]
    ppermute x0 -> x5, starting transfers between devices: none -> 8.1 us  [exchange_sum(): x = x + lax.ppermute(x, axis, [(i, i ^ step) for i in range(n)])]
    dot_general x6 -> x16, matrix products: 4.55 us -> 7.62 us  [the longest x11 1.87 us: mm(): return jnp.matmul(x, y, precision=HIGHEST)]
  transfers between devices with their start and end apart: 2 -> 7, of which waited for: 2 -> 7; matrix products, arithmetic and copies ran while one was open for 1% -> 2% of each run, Pallas kernels for 0% -> 0%
where the time goes in v1:
time: 142 us; the launch traced here: 141 us
  waiting for transfers between devices  83.3 us (59%)
  matrix products  14.3 us (10%)
  between operations  14.2 us (10%)
  local copies, waits for them, and re-layouts  10.2 us (7%)
  other arithmetic  8.83 us (6%)
  starting transfers between devices  8.18 us (6%)
  blocking collectives  2.26 us (2%)
    all_gather x1, waiting for transfers between devices, body(): part = lax.all_gather(mine, 'chan', axis=0, tiled=True)  63.4 us
    all_gather x1, waiting for transfers between devices, body(): table = lax.all_gather(part, 'rad', axis=0, tiled=True)  11.3 us
    ppermute x5, waiting for transfers between devices, exchange_sum(): x = x + lax.ppermute(x, axis, [(i, i ^ step) for i in range(n)])  8.6 us
    ppermute x5, starting transfers between devices, exchange_sum(): x = x + lax.ppermute(x, axis, [(i, i ^ step) for i in range(n)])  8.1 us
    dot_general x1, matrix products, body(): lax.dot_general(coupled, ham_blocks, (((1, 3), (1, 3)), ((0,), (0,))), pr...  5.73 us
    gather x1, local copies, waits for them, and re-layouts, body(): coupled = table[where].reshape(ch_dev, ncoup, vectors, table.shape[2])  3.37 us
  transfers between devices with their start and end apart: 7, of which 7 were waited for; matrix products, arithmetic and copies ran while one was open for 2% of the time, Pallas kernels for 0%

profile of v1, /device:TPU:0, one launch (start us, length us, event | category | flops | bytes accessed | tf_op | source)
XLA Modules:
  0.0 141.3 jit_solution(15895215995366212208)
XLA Ops:
  7.2 1.4 copy.20
  8.6 2.3 %all_gather.9 = bf16[64,16,128]{0,1,2:T(8,128)(2,1)S(1)} all-gather(bf16[64,16,64]{0,1,2:T(8,128)(2,1)S(1)} %copy.20), channel_id=1, replica_groups=mesh['chan'=16,'rad'=2] {'rad'}, dimensions={2}, use_global_device_ids=true | all-gather | bytes 393216 | tf_op jit(solution)/shard_map/all_gather | solution.py:33
  11.1 1.2 copy.21
  12.3 63.4 %all-gather.3.cloned.1.call-done = bf16[512,16,128]{2,1,0:T(8,128)(2,1)} async-done(((bf16[32,16,128]{2,1,0:T(8,128)(2,1)}), bf16[512,16,128]{2,1,0:T(8,128)(2,1)}) %all-gather.3.cloned.1.call-update) | async-done | bytes 2097168 | tf_op jit(solution)/shard_map/all_gather | solution.py:35
  76.0 2.3 %gather_fusion = s32[512]{0:T(512)S(1)} fusion(s32[1024]{0:T(1024)S(1)} %copy-done, s32[1024]{0:T(1024)S(1)} %pad_clamp_fusion.1), kind=kCustom, calls=%fused_computation | custom fusion | bytes 6144 | tf_op jit(solution)/shard_map/jit(_take)/gather | solution.py:38
  78.4 11.3 %all-gather.5.cloned.1.call-done = bf16[1024,16,128]{2,1,0:T(8,128)(2,1)} async-done(((bf16[512,16,128]{2,1,0:T(8,128)(2,1)}), bf16[1024,16,128]{2,1,0:T(8,128)(2,1)}) %all-gather.5.cloned.1.call-update) | async-done | bytes 4194320 | tf_op jit(solution)/shard_map/all_gather | solution.py:36
  89.7 3.4 %gather_fusion.1 = bf16[512,16,128]{2,1,0:T(8,128)(2,1)S(1)} fusion(bf16[1024,16,128]{2,1,0:T(8,128)(2,1)} %all-gather.5.cloned.1.call-done, s32[1024]{0:T(1024)S(1)} %pad_clamp_fusion), kind=kCustom, calls=%fused_computation.1 | custom fusion | bytes 4196352 | tf_op jit(solution)/shard_map/gather | solution.py:42
  93.1 5.7 %convolution_bitcast_fusion.3 = f32[64,16,64]{2,1,0:T(8,128)S(1)} fusion(bf16[64,8,16,128]{3,2,1,0:T(8,128)(2,1)S(1)} %bitcast.117, bf16[64,8,64,128]{3,2,1,0:T(8,128)(2,1)} %param.11), kind=kOutput, calls=%fused_computation.20 | convolution fusion | flops 134217728 | bytes 10747904 | tf_op jit(solution)/shard_map/dot_general | solution.py:43
  99.0 1.4 fusion.20
  100.4 1.8 %fusion.17 = f32[4,16,16]{2,1,0:T(8,128)S(1)} fusion(f32[1,64,16,64]{3,2,1,0:T(8,128)S(1)} %get-tuple-element.7, f32[1,64,16,64]{3,2,1,0:T(8,128)S(1)} %get-tuple-element.6, f32[1,64,16,64]{3,2,1,0:T(8,128)S(1)} %get-tuple-element.4, f32[1,64,16,64]{3,2,1,0:T(8,128)S(1)} %bitcast.116, f32[64,16,64]{2,1,0:T(8,128)S(1)} %convolution_bitcast_fusion.3), kind=kOutput, calls=%fused_computation.24 | convolution fusion | flops 51183616 | bytes 1314816 | tf_op jit(solution)/shard_map/xpkr,plr->xkl/dot_general | solution.py:53
  102.5 1.0 collective-permute-done
  103.5 1.7 %collective-permute-start.1 = (f32[14,128]{1,0:T(8,128)S(1)}, f32[14,128]{1,0:T(8,128)S(1)}, u32[]{:S(2)}, u32[]{:S(2)}) collective-permute-start(f32[14,128]{1,0:T(8,128)S(1)} %add.150), channel_id=1, source_target_pairs={{0,2},{2,0},{4,6},{6,4},{8,10},{10,8},{12,14},{14,12},{16,18},{18,... | collective-permute-start | bytes 21512 | tf_op jit(solution)/shard_map/ppermute | solution.py:19
  105.2 1.9 %collective-permute-done.1 = f32[14,128]{1,0:T(8,128)S(1)} collective-permute-done((f32[14,128]{1,0:T(8,128)S(1)}, f32[14,128]{1,0:T(8,128)S(1)}, u32[]{:S(2)}, u32[]{:S(2)}) %collective-permute-start.1) | collective-permute-done | bytes 7200 | tf_op jit(solution)/shard_map/ppermute | solution.py:19
  107.1 1.7 %collective-permute-start.2 = (f32[14,128]{1,0:T(8,128)S(1)}, f32[14,128]{1,0:T(8,128)S(1)}, u32[]{:S(2)}, u32[]{:S(2)}) collective-permute-start(f32[14,128]{1,0:T(8,128)S(1)} %add.151), channel_id=1, source_target_pairs={{0,4},{2,6},{4,0},{6,2},{8,12},{10,14},{12,8},{14,10},{16,20},{18,... | collective-permute-start | bytes 21512 | tf_op jit(solution)/shard_map/ppermute | solution.py:19
  108.9 1.9 %collective-permute-done.2 = f32[14,128]{1,0:T(8,128)S(1)} collective-permute-done((f32[14,128]{1,0:T(8,128)S(1)}, f32[14,128]{1,0:T(8,128)S(1)}, u32[]{:S(2)}, u32[]{:S(2)}) %collective-permute-start.2) | collective-permute-done | bytes 7200 | tf_op jit(solution)/shard_map/ppermute | solution.py:19
  110.8 1.7 %collective-permute-start.3 = (f32[14,128]{1,0:T(8,128)S(1)}, f32[14,128]{1,0:T(8,128)S(1)}, u32[]{:S(2)}, u32[]{:S(2)}) collective-permute-start(f32[14,128]{1,0:T(8,128)S(1)} %add.152), channel_id=1, source_target_pairs={{0,8},{2,10},{4,12},{6,14},{8,0},{10,2},{12,4},{14,6},{16,24},{18,... | collective-permute-start | bytes 21512 | tf_op jit(solution)/shard_map/ppermute | solution.py:19
  112.5 1.9 %collective-permute-done.3 = f32[14,128]{1,0:T(8,128)S(1)} collective-permute-done((f32[14,128]{1,0:T(8,128)S(1)}, f32[14,128]{1,0:T(8,128)S(1)}, u32[]{:S(2)}, u32[]{:S(2)}) %collective-permute-start.3) | collective-permute-done | bytes 7200 | tf_op jit(solution)/shard_map/ppermute | solution.py:19
  114.4 2.7 %collective-permute-start.4 = (f32[14,128]{1,0:T(8,128)S(1)}, f32[14,128]{1,0:T(8,128)S(1)}, u32[]{:S(2)}, u32[]{:S(2)}) collective-permute-start(f32[14,128]{1,0:T(8,128)S(1)} %add.153), channel_id=1, source_target_pairs={{0,16},{2,18},{4,20},{6,22},{8,24},{10,26},{12,28},{14,30},{16,0},... | collective-permute-start | bytes 21512 | tf_op jit(solution)/shard_map/ppermute | solution.py:19
  117.1 1.9 %collective-permute-done.4 = f32[14,128]{1,0:T(8,128)S(1)} collective-permute-done((f32[14,128]{1,0:T(8,128)S(1)}, f32[14,128]{1,0:T(8,128)S(1)}, u32[]{:S(2)}, u32[]{:S(2)}) %collective-permute-start.4) | collective-permute-done | bytes 7200 | tf_op jit(solution)/shard_map/ppermute | solution.py:19
  119.2 1.5 %cholesky.44 = f32[16,16]{1,0:T(8,128)S(1)} custom-call(f32[16,16]{1,0:T(8,128)S(1)} %fusion.47), custom_call_target="Cholesky" | custom-call | tf_op jit(solution)/shard_map/jit(cholesky)/cholesky | solution.py:61
  120.7 0.6 compare_reduce_fusion.1
  121.3 0.6 fusion.33
  122.0 1.2 custom-call.14
  126.2 1.5 %cholesky.55 = f32[16,16]{1,0:T(8,128)S(1)} custom-call(f32[16,16]{1,0:T(8,128)S(1)} %fusion.38), custom_call_target="Cholesky" | custom-call | tf_op jit(solution)/shard_map/jit(cholesky)/cholesky | solution.py:69
  127.7 0.6 compare_reduce_fusion
  128.3 0.6 fusion.34
  129.0 1.2 custom-call.17
  130.7 0.6 convolution_bitcast_fusion.1
  131.3 0.6 convolution_bitcast_fusion
  131.9 0.7 gather_fusion.2
  132.5 0.5 broadcast_multiply_fusion.1
  133.0 1.4 %fusion.16 = f32[64,16,64]{2,1,0:T(8,128)} fusion(f32[64,16,64]{2,1,0:T(8,128)S(1)} %convolution_bitcast_fusion, f32[64,16,64]{2,1,0:T(8,128)S(1)} %convolution_bitcast_fusion.1, f32[64,16,64]{2,1,0:T(8,128)S(1)} %convolution_bitcast_fusion.3, f32[64,64]{1,0:T(8,128)S(1)} %get-tuple-element.8, f32[16,16]{1,0:T(8,128)S(1)} %fusion.36), kind=kOutput, calls=%fused_computation.23 | convolution fusion | flops 12845056 | bytes 1065984 | tf_op jit(solution)/shard_map/lk,pkr->plr/dot_general | solution.py:75
  (63 shorter events, 4.8 us)
Async XLA Ops:
  7.2 68.8 %copy-start = (s32[1024]{0:T(1024)S(1)}, s32[1024]{0:T(1024)}, u32[]{:S(2)}) copy-start(s32[1024]{0:T(1024)} %param.13) | copy-start | bytes 12292
  7.2 68.6 %all-gather.3.cloned.1.call-start = ((), (), s32[]{:S(2)}) async-start(), calls=%async_computation | async-start | bytes 2228224 | tf_op jit(solution)/shard_map/all_gather | solution.py:35
  10.9 64.9 %copy-start.3 = (s32[64,8]{0,1:T(8,128)S(1)}, s32[64,8]{0,1:T(8,128)}, u32[]{:S(2)}) copy-start(s32[64,8]{0,1:T(8,128)} %param.12) | copy-start | bytes 6148
  12.3 77.4 %all-gather.5.cloned.1.call-start = ((), (), s32[]{:S(2)}) async-start(), calls=%async_computation.1 | async-start | bytes 6291456 | tf_op jit(solution)/shard_map/all_gather | solution.py:36
  75.8 2.6 %copy-start.2 = (f32[64,64]{1,0:T(8,128)S(1)}, f32[64,64]{1,0:T(8,128)}, u32[]{:S(2)}) copy-start(f32[64,64]{1,0:T(8,128)} %param.14) | copy-start | bytes 49156
  93.0 5.7 %copy-start.1 = (f32[64,16,64]{2,1,0:T(8,128)S(1)}, f32[64,16,64]{2,1,0:T(8,128)}, u32[]{:S(2)}) copy-start(f32[64,16,64]{2,1,0:T(8,128)} %param.10) | copy-start | bytes 786436
  102.3 1.2 collective-permute-start
  103.5 3.7 %collective-permute-start.1 = (f32[14,128]{1,0:T(8,128)S(1)}, f32[14,128]{1,0:T(8,128)S(1)}, u32[]{:S(2)}, u32[]{:S(2)}) collective-permute-start(f32[14,128]{1,0:T(8,128)S(1)} %add.150), channel_id=1, source_target_pairs={{0,2},{2,0},{4,6},{6,4},{8,10},{10,8},{12,14},{14,12},{16,18},{18,... | collective-permute-start | bytes 21512 | tf_op jit(solution)/shard_map/ppermute | solution.py:19
  107.1 3.7 %collective-permute-start.2 = (f32[14,128]{1,0:T(8,128)S(1)}, f32[14,128]{1,0:T(8,128)S(1)}, u32[]{:S(2)}, u32[]{:S(2)}) collective-permute-start(f32[14,128]{1,0:T(8,128)S(1)} %add.151), channel_id=1, source_target_pairs={{0,4},{2,6},{4,0},{6,2},{8,12},{10,14},{12,8},{14,10},{16,20},{18,... | collective-permute-start | bytes 21512 | tf_op jit(solution)/shard_map/ppermute | solution.py:19
  110.8 3.7 %collective-permute-start.3 = (f32[14,128]{1,0:T(8,128)S(1)}, f32[14,128]{1,0:T(8,128)S(1)}, u32[]{:S(2)}, u32[]{:S(2)}) collective-permute-start(f32[14,128]{1,0:T(8,128)S(1)} %add.152), channel_id=1, source_target_pairs={{0,8},{2,10},{4,12},{6,14},{8,0},{10,2},{12,4},{14,6},{16,24},{18,... | collective-permute-start | bytes 21512 | tf_op jit(solution)/shard_map/ppermute | solution.py:19
  114.4 4.5 %collective-permute-start.4 = (f32[14,128]{1,0:T(8,128)S(1)}, f32[14,128]{1,0:T(8,128)S(1)}, u32[]{:S(2)}, u32[]{:S(2)}) collective-permute-start(f32[14,128]{1,0:T(8,128)S(1)} %add.153), channel_id=1, source_target_pairs={{0,16},{2,18},{4,20},{6,22},{8,24},{10,26},{12,28},{14,30},{16,0},... | collective-permute-start | bytes 21512 | tf_op jit(solution)/shard_map/ppermute | solution.py:19
Sparse Core Ops, SparseCore 0:
  12.4 63.3 all-gather.2
  77.3 12.3 all-gather.4

commit v2 on v1

v2 whole, which is shorter than its diff:
```python
import functools

import jax
import jax.numpy as jnp
from jax import lax
from jax.experimental import pallas as pl
from jax.experimental.pallas import tpu as pltpu
from jax.sharding import PartitionSpec as P

HIGHEST = lax.Precision.HIGHEST
SCALE = 2.0 ** -8
F32 = jnp.float32
BF16 = jnp.bfloat16
NT = (((1,), (1,)), ((), ()))


def swap(x, axis, distance):
    n = lax.axis_size(axis)
    return lax.ppermute(x, axis, [(i, i ^ distance) for i in range(n)])


def exchange_sum(x, axis):
    step = 1
    while step < lax.axis_size(axis):
        x = x + swap(x, axis, step)
        step *= 2
    return x


def trial_kernel(t_ref, d_ref, t0_ref, t1_ref, gram_ref):
    ch, k, r = t_ref.shape
    group = 128 // r
    for i in range(ch // group):
        lanes = pl.ds(i * 128, 128)
        t = jnp.concatenate([t_ref[i * group + g] for g in range(group)], axis=1)
        t0_ref[:, lanes] = t
        t1_ref[:, lanes] = t / d_ref[pl.ds(i, 1), :]
    z = jnp.concatenate([t1_ref[...], t0_ref[...]], axis=0)
    gram_ref[...] = lax.dot_general(z, z, NT, precision=HIGHEST, preferred_element_type=F32)


def apply_kernel(
    n_chan, n_rad, partners_ref, stored_ref, ham_ref, t0_ref, t1_ref, d_ref, *rest
):
    pieces = rest[: 6 * n_rad]
    a1_ref, gram_ref, table, sems = rest[6 * n_rad :]
    step = pl.program_id(0)
    per_step, ncoup, r, _ = ham_ref.shape
    k = t0_ref.shape[0]
    nz, half = table.shape[3:5]
    ch = 2 * half * n_rad
    me_chan, me_rad = lax.axis_index("chan"), lax.axis_index("rad")
    places = ((0, 0), (1, 0), (0, 1), (1, 2), (0, 2), (1, 1))

    @pl.when(step == 0)
    def _():
        copies = []
        for c in range(n_rad):
            for i, (h, d) in enumerate(places):
                piece = pieces[c * 6 + i]
                if piece.shape[0] == nz:
                    copies.append((piece, table.at[c, h, d]))
                else:
                    copies.append((piece.at[pl.ds(0, nz)], table.at[c, h, d]))
                    copies.append((piece.at[pl.ds(nz, nz)], table.at[c, h, 3]))
        copies = [pltpu.make_async_copy(s, d, sems.at[i]) for i, (s, d) in enumerate(copies)]
        for c in copies:
            c.start()
        for c in copies:
            c.wait()

    blocks = []
    for p in range(per_step):
        rows = []
        for j in range(ncoup):
            q = stored_ref[partners_ref[(step * per_step + p) * ncoup + j]]
            owner, local = lax.div(q, ch), lax.rem(q, ch)
            slot = owner ^ me_chan
            core = lax.div(local, 2 * half) ^ me_rad
            h = lax.rem(lax.div(local, half), 2)
            rows.append(table[core, h, slot & 3, lax.div(slot, 4), lax.rem(local, half)])
        lhs = jnp.concatenate(rows, axis=1)
        rhs = jnp.concatenate([ham_ref[p, j] for j in range(ncoup)], axis=1)
        blocks.append(lax.dot_general(lhs, rhs, NT, preferred_element_type=F32))
    a0 = jnp.concatenate(blocks, axis=1) * SCALE
    a1 = a0 / d_ref[...]
    a1_ref[...] = a1
    z = jnp.concatenate([a1, t1_ref[...], t0_ref[...]], axis=0)
    gram = lax.dot_general(
        z, jnp.concatenate([a1, a0], axis=0), NT, precision=HIGHEST, preferred_element_type=F32
    )

    @pl.when(step == 0)
    def _():
        gram_ref[...] = gram

    @pl.when(step > 0)
    def _():
        gram_ref[...] += gram


def mm(x, y, dims=(((1,), (0,)), ((), ()))):
    return lax.dot_general(x, y, dims, precision=HIGHEST, preferred_element_type=F32)


def finish_kernel(total, gt_ref, ga_ref, a1_ref, t1_ref, t0_ref, out_ref, ritz_ref):
    ch, k, r = out_ref.shape
    gt, ga = gt_ref[...], ga_ref[...]
    row = lax.broadcasted_iota(jnp.int32, (k, 4 * k), 0)
    aug = jnp.concatenate([ga[2 * k :, :k], gt[k:, :], ga[2 * k :, k:]], axis=1)
    for i in range(k):
        pivot_row = aug[i : i + 1, :] / aug[i : i + 1, 2 * k + i : 2 * k + i + 1]
        column = aug[:, 2 * k + i : 2 * k + i + 1]
        aug = jnp.where(row == i, pivot_row, aug - column * pivot_row)
    coef = aug[:, 3 * k :]
    mix = aug[:, :k] - mm(aug[:, k : 2 * k], coef)
    eye = lax.broadcasted_iota(jnp.int32, (k, k), 0) == lax.broadcasted_iota(jnp.int32, (k, k), 1)
    ritz_ref[...] = jnp.sum(jnp.where(eye, coef, 0.0), axis=0, keepdims=True) * (1.0 / SCALE)
    w = jnp.concatenate([eye.astype(F32), -coef, -mix], axis=0)
    s2, s1 = ga[k : 2 * k, :k], ga[2 * k :, :k]
    top = jnp.concatenate([ga[:k, :k], s2.T, s1.T], axis=1)
    low = jnp.concatenate([ga[k:, :k], gt], axis=1)
    y = mm(jnp.concatenate([top, low], axis=0), w)
    wide = lax.broadcasted_iota(jnp.int32, (3 * k, 3 * k), 0) == lax.broadcasted_iota(
        jnp.int32, (3 * k, 3 * k), 1
    )
    aug = mm(w, jnp.concatenate([y, wide.astype(F32)], axis=1), (((0,), (0,)), ((), ())))
    for i in range(k):
        pivot_row = aug[i : i + 1, :]
        pivot = pivot_row[:, i : i + 1]
        column = jnp.where(row[:, :1] > i, aug[:, i : i + 1] / pivot, 0.0)
        scaled = pivot_row * (lax.rsqrt(pivot) * (total ** 0.5))
        aug = jnp.where(row == i, scaled, aug - column * pivot_row)
    x = jnp.concatenate([a1_ref[...], t1_ref[...], t0_ref[...]], axis=0)
    new = mm(aug[:, k:], x)
    for p in range(ch):
        out_ref[p] = new[:, p * r : (p + 1) * r]


def body(trial_block, ham_blocks, partners, stored_at, precond_diag):
    n_chan, n_rad = lax.axis_size("chan"), lax.axis_size("rad")
    ch, k, r = trial_block.shape
    ncoup = partners.shape[1]
    lanes = ch * r
    total = float(n_chan * n_rad * lanes)
    share, nz = ch // n_rad, n_chan // 4
    half = share // 2

    rounded = trial_block.astype(BF16)
    own = lax.all_to_all(rounded, "rad", split_axis=0, concat_axis=2, tiled=True)
    column = [own] + [swap(own, "chan", 4 * z) for z in range(1, nz)]
    z1 = jnp.stack([c[:half] for c in column])
    z2 = jnp.stack([c[half:] for c in column])
    x1 = swap(z1, "chan", 1)
    y1 = swap(z2, "chan", 2)
    y2 = swap(jnp.concatenate([z1, x1]), "chan", 2)
    x2 = swap(jnp.concatenate([z2, y1]), "chan", 1)
    mine = [z1, z2, x1, y1, y2, x2]
    pieces = list(mine)
    for c in range(1, n_rad):
        pieces += [swap(m, "rad", c) for m in mine]

    d = precond_diag.reshape(lanes // 128, 128)
    t0, t1, gram_t = pl.pallas_call(
        trial_kernel,
        out_shape=[
            jax.ShapeDtypeStruct((k, lanes), F32),
            jax.ShapeDtypeStruct((k, lanes), F32),
            jax.ShapeDtypeStruct((2 * k, 2 * k), F32),
        ],
        name="trial_gram",
    )(trial_block, d)

    per_step = 8
    block = per_step * r
    columns = pl.BlockSpec((k, block), lambda i, *_: (0, i))
    a1, gram_a = pl.pallas_call(
        functools.partial(apply_kernel, n_chan, n_rad),
        grid_spec=pltpu.PrefetchScalarGridSpec(
            num_scalar_prefetch=2,
            grid=(ch // per_step,),
            in_specs=[
                pl.BlockSpec((per_step, ncoup, r, ham_blocks.shape[3]), lambda i, *_: (i, 0, 0, 0)),
                columns,
                columns,
                pl.BlockSpec((1, block), lambda i, *_: (0, i)),
            ]
            + [pl.BlockSpec(memory_space=pl.ANY)] * len(pieces),
            out_specs=[columns, pl.BlockSpec((3 * k, 2 * k), lambda i, *_: (0, 0))],
            scratch_shapes=[
                pltpu.VMEM((n_rad, 2, 4, nz, half, k, ham_blocks.shape[3]), BF16),
                pltpu.SemaphoreType.DMA((8 * n_rad,)),
            ],
        ),
        out_shape=[
            jax.ShapeDtypeStruct((k, lanes), F32),
            jax.ShapeDtypeStruct((3 * k, 2 * k), F32),
        ],
        compiler_params=pltpu.CompilerParams(vmem_limit_bytes=24 * 1024 * 1024),
        name="apply",
    )(partners.reshape(-1), stored_at, ham_blocks, t0, t1, precond_diag.reshape(1, lanes), *pieces)

    gt = jnp.pad(gram_t, ((0, k), (0, 0)))
    sums = jnp.concatenate([gt, gram_a], axis=1)
    sums = exchange_sum(exchange_sum(sums, "rad"), "chan")
    new_block, ritz = pl.pallas_call(
        functools.partial(finish_kernel, total),
        out_shape=[
            jax.ShapeDtypeStruct((ch, k, r), F32),
            jax.ShapeDtypeStruct((1, k), F32),
        ],
        name="finish",
    )(sums[: 2 * k, : 2 * k], sums[:, 2 * k :], a1, t1, t0)
    return (new_block, ritz.reshape(k))


def solution(mesh):
    return jax.shard_map(
        body,
        mesh=mesh,
        in_specs=(
            P("chan", None, "rad"),
            P("chan", None, "rad", None),
            P("chan", None),
            P(),
            P("chan", "rad"),
        ),
        out_specs=(P("chan", None, "rad"), P()),
        check_vma=False,
    )
```

time: 142 us -> 94.6 us (0.67)
  waiting for transfers between devices: 83.3 us -> 38.6 us
  Pallas kernels: 0 us -> 19.9 us
  matrix products: 14.3 us -> 0 us
  between operations: 14.2 us -> 0.84 us
  starting transfers between devices: 8.18 us -> 16.9 us
  other arithmetic: 8.83 us -> 1.32 us
  local copies, waits for them, and re-layouts: 10.2 us -> 12.5 us
  blocking collectives: 2.26 us -> 3.84 us
    all_gather x2 -> x0, waiting for transfers between devices: 74.7 us -> none  [the longest x1 63.4 us: body(): part = lax.all_gather(mine, 'chan', axis=0, tiled=True)]
    ppermute x5 -> x18, waiting for transfers between devices: 8.6 us -> 38.6 us  [swap(): return lax.ppermute(x, axis, [(i, i ^ distance) for i in range(n)])]
    pallas_call x0 -> x3, Pallas kernels: none -> 19.9 us  [the longest x1 11.9 us: body(): pl.pallas_call(functools.partial(apply_kernel, n_chan, n_rad), grid_spec=...]
    dot_general x17 -> x0, matrix products: 13.4 us -> none  [the longest x1 5.73 us: body(): lax.dot_general(coupled, ham_blocks, (((1, 3), (1, 3)), ((0,), (0,))), pr...]
    ppermute x5 -> x18, starting transfers between devices: 8.1 us -> 16.9 us  [swap(): return lax.ppermute(x, axis, [(i, i ^ distance) for i in range(n)])]
    another operation x11 -> x2, other arithmetic: 8.17 us -> 0.07 us  [the longest x1 0.04 us: body(): z1 = jnp.stack([c[:half] for c in column])]
    unnamed x10 -> x20, local copies, waits for them, and re-layouts: 1.5 us -> 7.97 us
    gather x3 -> x0, local copies, waits for them, and re-layouts: 6.32 us -> none  [the longest x1 3.37 us: body(): coupled = table[where].reshape(ch_dev, ncoup, vectors, table.shape[2])]
  transfers between devices with their start and end apart: 7 -> 18, of which waited for: 7 -> 10; matrix products, arithmetic and copies ran while one was open for 2% -> 4% of each run, Pallas kernels for 0% -> 2%
where the time goes in v2:
time: 94.6 us; the launch traced here: 94 us
  waiting for transfers between devices  38.6 us (41%)
  Pallas kernels  19.9 us (21%)
  starting transfers between devices  16.9 us (18%)
  local copies, waits for them, and re-layouts  12.5 us (13%)
  blocking collectives  3.84 us (4%)
  other arithmetic  1.32 us (1%)
    ppermute x18, waiting for transfers between devices, swap(): return lax.ppermute(x, axis, [(i, i ^ distance) for i in range(n)])  38.6 us
    ppermute x18, starting transfers between devices, swap(): return lax.ppermute(x, axis, [(i, i ^ distance) for i in range(n)])  16.9 us
    pallas_call x1, Pallas kernels, body(): pl.pallas_call(functools.partial(apply_kernel, n_chan, n_rad), grid_spec=...  11.9 us
    unnamed x20, local copies, waits for them, and re-layouts  7.97 us
    pallas_call x1, Pallas kernels, body(): pl.pallas_call(functools.partial(finish_kernel, total), out_shape=[jax.Sh...  5.73 us
    all_to_all x1, blocking collectives, body(): lax.all_to_all(rounded, 'rad', split_axis=0, concat_axis=2, tiled=True)  3.84 us
    pallas_call x1, Pallas kernels, body(): pl.pallas_call(trial_kernel, out_shape=[jax.ShapeDtypeStruct((k, lanes),...  2.29 us
  transfers between devices with their start and end apart: 18, of which 10 were waited for; matrix products, arithmetic and copies ran while one was open for 4% of the time, Pallas kernels for 2%

profile of v2, /device:TPU:0, one launch (start us, length us, event | category | flops | bytes accessed | tf_op | source)
XLA Modules:
  0.0 94.0 jit_solution(6497363501081841626)
XLA Ops:
  0.6 1.1 %convert_element_type.5 = bf16[64,16,64]{2,1,0:T(8,128)(2,1)S(1)} convert(f32[64,16,64]{2,1,0:T(8,128)} %t_ref.1) | non-fusion elementwise | flops 65536 | bytes 393216 | tf_op jit(solution)/shard_map/convert_element_type | solution.py:149
  2.0 3.8 %all_to_all.18 = bf16[2,2,16384]{2,1,0:T(2,128)(2,1)S(1)} all-to-all(bf16[2,2,16384]{2,1,0:T(2,128)(2,1)S(1)} %reshape.24), channel_id=1, replica_groups=mesh['chan'=16,'rad'=2] {'rad'}, dimensions={0} | all-to-all | bytes 262144 | tf_op jit(solution)/shard_map/all_to_all | solution.py:150
  6.4 5.1 %collective-permute-start.2 = (bf16[32,16,128]{2,1,0:T(8,128)(2,1)S(1)}, bf16[32,16,128]{2,1,0:T(8,128)(2,1)S(1)}, u32[]{:S(2)}, u32[]{:S(2)}) collective-permute-start(bf16[32,16,128]{2,1,0:T(8,128)(2,1)S(1)} %all_to_all.16), channel_id=1, source_target_pairs={{0,24},{2,26},{4,28},{6,30},{8,16},{10,18},{12,20},{14,22},{16,8},... | collective-permute-start | bytes 393224 | tf_op jit(solution)/shard_map/ppermute | solution.py:19
  12.7 3.3 %collective-permute-done.2 = bf16[32,16,128]{2,1,0:T(8,128)(2,1)S(1)} collective-permute-done((bf16[32,16,128]{2,1,0:T(8,128)(2,1)S(1)}, bf16[32,16,128]{2,1,0:T(8,128)(2,1)S(1)}, u32[]{:S(2)}, u32[]{:S(2)}) %collective-permute-start.2) | collective-permute-done | bytes 131104 | tf_op jit(solution)/shard_map/ppermute | solution.py:19
  16.0 7.0 %collective-permute-done.1 = bf16[32,16,128]{2,1,0:T(8,128)(2,1)S(1)} collective-permute-done((bf16[32,16,128]{2,1,0:T(8,128)(2,1)S(1)}, bf16[32,16,128]{2,1,0:T(8,128)(2,1)S(1)}, u32[]{:S(2)}, u32[]{:S(2)}) %collective-permute-start.1) | collective-permute-done | bytes 131104 | tf_op jit(solution)/shard_map/ppermute | solution.py:19
  23.0 1.6 %collective-permute-start.3 = (bf16[4,16,16,128]{3,2,1,0:T(8,128)(2,1)S(1)}, bf16[4,16,16,128]{3,2,1,0:T(8,128)(2,1)S(1)}, u32[]{:S(2)}, u32[]{:S(2)}) collective-permute-start(bf16[4,16,16,128]{3,2,1,0:T(8,128)(2,1)S(1)} %pad_maximum_fusion.rest_0_), channel_id=1, source_target_pairs={{0,2},{2,0},{4,6},{6,4},{8,10},{10,8},{12,14},{14,12},{16,18},{18,... | collective-permute-start | bytes 786440 | tf_op jit(solution)/shard_map/ppermute | solution.py:19
  24.6 1.6 %collective-permute-start.4 = (bf16[4,16,16,128]{3,2,1,0:T(8,128)(2,1)S(1)}, bf16[4,16,16,128]{3,2,1,0:T(8,128)(2,1)S(1)}, u32[]{:S(2)}, u32[]{:S(2)}) collective-permute-start(bf16[4,16,16,128]{3,2,1,0:T(8,128)(2,1)S(1)} %pad_maximum_fusion.1.rest_1_), channel_id=1, source_target_pairs={{0,4},{2,6},{4,0},{6,2},{8,12},{10,14},{12,8},{14,10},{16,20},{18,... | collective-permute-start | bytes 786440 | tf_op jit(solution)/shard_map/ppermute | solution.py:19
  26.3 4.3 %collective-permute-done.3.rest_2_ = bf16[4,16,16,128]{3,2,1,0:T(8,128)(2,1)S(1)} collective-permute-done((bf16[4,16,16,128]{3,2,1,0:T(8,128)(2,1)S(1)}, bf16[4,16,16,128]{3,2,1,0:T(8,128)(2,1)S(1)}, u32[]{:S(2)}, u32[]{:S(2)}) %collective-permute-start.3) | collective-permute-done | bytes 262176 | tf_op jit(solution)/shard_map/ppermute | solution.py:19
  30.7 1.6 %collective-permute-start.5 = (bf16[8,16,16,128]{3,2,1,0:T(8,128)(2,1)S(1)}, bf16[8,16,16,128]{3,2,1,0:T(8,128)(2,1)S(1)}, u32[]{:S(2)}, u32[]{:S(2)}) collective-permute-start(bf16[8,16,16,128]{3,2,1,0:T(8,128)(2,1)S(1)} %constant_dynamic-update-slice_fusion), channel_id=1, source_target_pairs={{0,4},{2,6},{4,0},{6,2},{8,12},{10,14},{12,8},{14,10},{16,20},{18,... | collective-permute-start | bytes 1572872 | tf_op jit(solution)/shard_map/ppermute | solution.py:19
  32.3 1.6 %collective-permute-start.6 = (bf16[8,16,16,128]{3,2,1,0:T(8,128)(2,1)S(1)}, bf16[8,16,16,128]{3,2,1,0:T(8,128)(2,1)S(1)}, u32[]{:S(2)}, u32[]{:S(2)}) collective-permute-start(bf16[8,16,16,128]{3,2,1,0:T(8,128)(2,1)S(1)} %constant_dynamic-update-slice_fusion.5), channel_id=1, source_target_pairs={{0,2},{2,0},{4,6},{6,4},{8,10},{10,8},{12,14},{14,12},{16,18},{18,... | collective-permute-start | bytes 1572872 | tf_op jit(solution)/shard_map/ppermute | solution.py:19
  33.9 9.3 %collective-permute-done.5.rest_4_ = bf16[8,16,16,128]{3,2,1,0:T(8,128)(2,1)S(1)} collective-permute-done((bf16[8,16,16,128]{3,2,1,0:T(8,128)(2,1)S(1)}, bf16[8,16,16,128]{3,2,1,0:T(8,128)(2,1)S(1)}, u32[]{:S(2)}, u32[]{:S(2)}) %collective-permute-start.5) | collective-permute-done | bytes 524320 | tf_op jit(solution)/shard_map/ppermute | solution.py:19
  43.2 1.1 %collective-permute-done.6.rest_5_ = bf16[8,16,16,128]{3,2,1,0:T(8,128)(2,1)S(1)} collective-permute-done((bf16[8,16,16,128]{3,2,1,0:T(8,128)(2,1)S(1)}, bf16[8,16,16,128]{3,2,1,0:T(8,128)(2,1)S(1)}, u32[]{:S(2)}, u32[]{:S(2)}) %collective-permute-start.6) | collective-permute-done | bytes 524320 | tf_op jit(solution)/shard_map/ppermute | solution.py:19
  45.4 0.8 reshape.22.d_ref
  46.2 1.4 %reshape.20.d_ref = f32[32,128]{1,0:T(8,128)} reshape(f32[64,64]{1,0:T(8,128)} %param.9) | data formatting | bytes 32768 | tf_op jit(solution)/shard_map/reshape | solution.py:163
  47.6 0.8 copy.8
  48.5 2.3 %trial_gram.1 = (f32[16,4096]{1,0:T(8,128)}, f32[16,4096]{1,0:T(8,128)}, f32[32,32]{1,0:T(8,128)}) custom-call(f32[64,16,64]{2,1,0:T(8,128)} %t_ref.1, f32[32,128]{1,0:T(8,128)} %reshape.20.d_ref), custom_call_target="tpu_custom_call" | custom-call | tf_op jit(solution)/shard_map/trial_gram/pallas_call | solution.py:164
  50.8 3.4 %copy-done = bf16[64,8,64,128]{3,2,1,0:T(8,128)(2,1)S(1)} copy-done((bf16[64,8,64,128]{3,2,1,0:T(8,128)(2,1)S(1)}, bf16[64,8,64,128]{3,2,1,0:T(8,128)(2,1)}, u32[]{:S(2)}) %copy-start) | copy-done | bytes 8388632
  54.2 0.9 %copy-done.1 = f32[16,4096]{1,0:T(8,128)S(1)} copy-done((f32[16,4096]{1,0:T(8,128)S(1)}, f32[16,4096]{1,0:T(8,128)}, u32[]{:S(2)}) %copy-start.1) | copy-done | bytes 262168
  55.2 0.9 %copy-done.2 = f32[16,4096]{1,0:T(8,128)S(1)} copy-done((f32[16,4096]{1,0:T(8,128)S(1)}, f32[16,4096]{1,0:T(8,128)}, u32[]{:S(2)}) %copy-start.2) | copy-done | bytes 262168
  56.1 0.7 copy-done.4
  56.8 11.9 %apply.1 = (f32[16,4096]{1,0:T(8,128)S(1)}, f32[48,32]{1,0:T(8,128)S(1)}) custom-call(s32[512]{0:T(512)S(1)} %reshape.21.partners_ref, s32[1024]{0:T(1024)S(1)} %copy-done.4, bf16[64,8,64,128]{3,2,1,0:T(8,128)(2,1)S(1)} %copy-done, f32[16,4096]{1,0:T(8,128)S(1)} %copy-done.1, f32[16,4096]{1,0:T(8,128)S(1)} %copy-done.2, f32[1,4096]{1,0:T(1,128)S(1)} %reshape.22.d_ref, ...), custom_call_target="tpu_custom_call" | custom-call | tf_op jit(solution)/shard_map/apply/pallas_call | solution.py:177
  68.7 0.7 copy-done.3
  69.5 1.2 %collective-permute-done.13 = f32[48,64]{1,0:T(8,128)S(1)} collective-permute-done((f32[48,64]{1,0:T(8,128)S(1)}, f32[48,64]{1,0:T(8,128)S(1)}, u32[]{:S(2)}, u32[]{:S(2)}) %collective-permute-start.13) | collective-permute-done | bytes 12320 | tf_op jit(solution)/shard_map/ppermute | solution.py:19
  70.8 1.5 %collective-permute-start.14 = (f32[48,64]{1,0:T(8,128)S(1)}, f32[48,64]{1,0:T(8,128)S(1)}, u32[]{:S(2)}, u32[]{:S(2)}) collective-permute-start(f32[48,64]{1,0:T(8,128)S(1)} %fusion.1), channel_id=1, source_target_pairs={{0,2},{2,0},{4,6},{6,4},{8,10},{10,8},{12,14},{14,12},{16,18},{18,... | collective-permute-start | bytes 36872 | tf_op jit(solution)/shard_map/ppermute | solution.py:19
  72.3 2.3 %collective-permute-done.14 = f32[48,64]{1,0:T(8,128)S(1)} collective-permute-done((f32[48,64]{1,0:T(8,128)S(1)}, f32[48,64]{1,0:T(8,128)S(1)}, u32[]{:S(2)}, u32[]{:S(2)}) %collective-permute-start.14) | collective-permute-done | bytes 12320 | tf_op jit(solution)/shard_map/ppermute | solution.py:19
  74.6 1.2 %collective-permute-start.15 = (f32[48,64]{1,0:T(8,128)S(1)}, f32[48,64]{1,0:T(8,128)S(1)}, u32[]{:S(2)}, u32[]{:S(2)}) collective-permute-start(f32[48,64]{1,0:T(8,128)S(1)} %add.18), channel_id=1, source_target_pairs={{0,4},{2,6},{4,0},{6,2},{8,12},{10,14},{12,8},{14,10},{16,20},{18,... | collective-permute-start | bytes 36872 | tf_op jit(solution)/shard_map/ppermute | solution.py:19
  75.8 2.6 %collective-permute-done.15 = f32[48,64]{1,0:T(8,128)S(1)} collective-permute-done((f32[48,64]{1,0:T(8,128)S(1)}, f32[48,64]{1,0:T(8,128)S(1)}, u32[]{:S(2)}, u32[]{:S(2)}) %collective-permute-start.15) | collective-permute-done | bytes 12320 | tf_op jit(solution)/shard_map/ppermute | solution.py:19
  78.5 3.8 %collective-permute-done.16 = f32[48,64]{1,0:T(8,128)S(1)} collective-permute-done((f32[48,64]{1,0:T(8,128)S(1)}, f32[48,64]{1,0:T(8,128)S(1)}, u32[]{:S(2)}, u32[]{:S(2)}) %collective-permute-start.16) | collective-permute-done | bytes 12320 | tf_op jit(solution)/shard_map/ppermute | solution.py:19
  82.3 1.2 %collective-permute-start.17 = (f32[48,64]{1,0:T(8,128)S(1)}, f32[48,64]{1,0:T(8,128)S(1)}, u32[]{:S(2)}, u32[]{:S(2)}) collective-permute-start(f32[48,64]{1,0:T(8,128)S(1)} %add.20), channel_id=1, source_target_pairs={{0,16},{2,18},{4,20},{6,22},{8,24},{10,26},{12,28},{14,30},{16,0},... | collective-permute-start | bytes 36872 | tf_op jit(solution)/shard_map/ppermute | solution.py:19
  83.5 3.6 %collective-permute-done.17 = f32[48,64]{1,0:T(8,128)S(1)} collective-permute-done((f32[48,64]{1,0:T(8,128)S(1)}, f32[48,64]{1,0:T(8,128)S(1)}, u32[]{:S(2)}, u32[]{:S(2)}) %collective-permute-start.17) | collective-permute-done | bytes 12320 | tf_op jit(solution)/shard_map/ppermute | solution.py:19
  87.6 0.7 slice.51.ga_ref
  88.3 5.7 %finish.1 = (f32[64,16,64]{2,1,0:T(8,128)}, f32[1,16]{1,0:T(1,128)}) custom-call(f32[32,32]{1,0:T(8,128)} %slice.50.gt_ref, f32[48,32]{1,0:T(8,128)} %slice.51.ga_ref, f32[16,4096]{1,0:T(8,128)} %copy-done.3, f32[16,4096]{1,0:T(8,128)} %get-tuple-element.11.t1_ref, f32[16,4096]{1,0:T(8,128)} %get-tuple-element.10.t0_ref), custom_call_target="tpu_custom_call" | custom-call | tf_op jit(solution)/shard_map/finish/pallas_call | solution.py:206
  (52 shorter events, 4.1 us)
Async XLA Ops:
  6.4 9.5 %collective-permute-start.2 = (bf16[32,16,128]{2,1,0:T(8,128)(2,1)S(1)}, bf16[32,16,128]{2,1,0:T(8,128)(2,1)S(1)}, u32[]{:S(2)}, u32[]{:S(2)}) collective-permute-start(bf16[32,16,128]{2,1,0:T(8,128)(2,1)S(1)} %all_to_all.16), channel_id=1, source_target_pairs={{0,24},{2,26},{4,28},{6,30},{8,16},{10,18},{12,20},{14,22},{16,8},... | collective-permute-start | bytes 393224 | tf_op jit(solution)/shard_map/ppermute | solution.py:19
  11.6 11.4 %collective-permute-start.1 = (bf16[32,16,128]{2,1,0:T(8,128)(2,1)S(1)}, bf16[32,16,128]{2,1,0:T(8,128)(2,1)S(1)}, u32[]{:S(2)}, u32[]{:S(2)}) collective-permute-start(bf16[32,16,128]{2,1,0:T(8,128)(2,1)S(1)} %all_to_all.16), channel_id=1, source_target_pairs={{0,16},{2,18},{4,20},{6,22},{8,24},{10,26},{12,28},{14,30},{16,0},... | collective-permute-start | bytes 393224 | tf_op jit(solution)/shard_map/ppermute | solution.py:19
  11.6 11.4 %collective-permute-start = (bf16[32,16,128]{2,1,0:T(8,128)(2,1)S(1)}, bf16[32,16,128]{2,1,0:T(8,128)(2,1)S(1)}, u32[]{:S(2)}, u32[]{:S(2)}) collective-permute-start(bf16[32,16,128]{2,1,0:T(8,128)(2,1)S(1)} %all_to_all.16), channel_id=1, source_target_pairs={{0,8},{2,10},{4,12},{6,14},{8,0},{10,2},{12,4},{14,6},{16,24},{18,... | collective-permute-start | bytes 393224 | tf_op jit(solution)/shard_map/ppermute | solution.py:19
  23.0 7.6 %collective-permute-start.3 = (bf16[4,16,16,128]{3,2,1,0:T(8,128)(2,1)S(1)}, bf16[4,16,16,128]{3,2,1,0:T(8,128)(2,1)S(1)}, u32[]{:S(2)}, u32[]{:S(2)}) collective-permute-start(bf16[4,16,16,128]{3,2,1,0:T(8,128)(2,1)S(1)} %pad_maximum_fusion.rest_0_), channel_id=1, source_target_pairs={{0,2},{2,0},{4,6},{6,4},{8,10},{10,8},{12,14},{14,12},{16,18},{18,... | collective-permute-start | bytes 786440 | tf_op jit(solution)/shard_map/ppermute | solution.py:19
  24.6 7.6 %collective-permute-start.4 = (bf16[4,16,16,128]{3,2,1,0:T(8,128)(2,1)S(1)}, bf16[4,16,16,128]{3,2,1,0:T(8,128)(2,1)S(1)}, u32[]{:S(2)}, u32[]{:S(2)}) collective-permute-start(bf16[4,16,16,128]{3,2,1,0:T(8,128)(2,1)S(1)} %pad_maximum_fusion.1.rest_1_), channel_id=1, source_target_pairs={{0,4},{2,6},{4,0},{6,2},{8,12},{10,14},{12,8},{14,10},{16,20},{18,... | collective-permute-start | bytes 786440 | tf_op jit(solution)/shard_map/ppermute | solution.py:19
  30.7 12.5 %collective-permute-start.5 = (bf16[8,16,16,128]{3,2,1,0:T(8,128)(2,1)S(1)}, bf16[8,16,16,128]{3,2,1,0:T(8,128)(2,1)S(1)}, u32[]{:S(2)}, u32[]{:S(2)}) collective-permute-start(bf16[8,16,16,128]{3,2,1,0:T(8,128)(2,1)S(1)} %constant_dynamic-update-slice_fusion), channel_id=1, source_target_pairs={{0,4},{2,6},{4,0},{6,2},{8,12},{10,14},{12,8},{14,10},{16,20},{18,... | collective-permute-start | bytes 1572872 | tf_op jit(solution)/shard_map/ppermute | solution.py:19
  32.3 12.0 %collective-permute-start.6 = (bf16[8,16,16,128]{3,2,1,0:T(8,128)(2,1)S(1)}, bf16[8,16,16,128]{3,2,1,0:T(8,128)(2,1)S(1)}, u32[]{:S(2)}, u32[]{:S(2)}) collective-permute-start(bf16[8,16,16,128]{3,2,1,0:T(8,128)(2,1)S(1)} %constant_dynamic-update-slice_fusion.5), channel_id=1, source_target_pairs={{0,2},{2,0},{4,6},{6,4},{8,10},{10,8},{12,14},{14,12},{16,18},{18,... | collective-permute-start | bytes 1572872 | tf_op jit(solution)/shard_map/ppermute | solution.py:19
  33.9 11.0 %collective-permute-start.7 = (bf16[4,16,16,128]{3,2,1,0:T(8,128)(2,1)S(1)}, bf16[4,16,16,128]{3,2,1,0:T(8,128)(2,1)S(1)}, u32[]{:S(2)}, u32[]{:S(2)}) collective-permute-start(bf16[4,16,16,128]{3,2,1,0:T(8,128)(2,1)S(1)} %pad_maximum_fusion.rest_0_), channel_id=1, source_target_pairs={{0,1},{1,0},{2,3},{3,2},{4,5},{5,4},{6,7},{7,6},{8,9},{9,8},{10,11... | collective-permute-start | bytes 786440 | tf_op jit(solution)/shard_map/ppermute | solution.py:19
  43.2 7.6 %collective-permute-start.11 = (bf16[8,16,16,128]{3,2,1,0:T(8,128)(2,1)S(1)}, bf16[8,16,16,128]{3,2,1,0:T(8,128)(2,1)S(1)}, u32[]{:S(2)}, u32[]{:S(2)}) collective-permute-start(bf16[8,16,16,128]{3,2,1,0:T(8,128)(2,1)S(1)} %collective-permute-done.5.rest_4_), channel_id=1, source_target_pairs={{0,1},{1,0},{2,3},{3,2},{4,5},{5,4},{6,7},{7,6},{8,9},{9,8},{10,11... | collective-permute-start | bytes 1572872 | tf_op jit(solution)/shard_map/ppermute | solution.py:19
  44.3 6.5 %collective-permute-start.12 = (bf16[8,16,16,128]{3,2,1,0:T(8,128)(2,1)S(1)}, bf16[8,16,16,128]{3,2,1,0:T(8,128)(2,1)S(1)}, u32[]{:S(2)}, u32[]{:S(2)}) collective-permute-start(bf16[8,16,16,128]{3,2,1,0:T(8,128)(2,1)S(1)} %collective-permute-done.6.rest_5_), channel_id=1, source_target_pairs={{0,1},{1,0},{2,3},{3,2},{4,5},{5,4},{6,7},{7,6},{8,9},{9,8},{10,11... | collective-permute-start | bytes 1572872 | tf_op jit(solution)/shard_map/ppermute | solution.py:19
  44.3 6.5 %collective-permute-start.8 = (bf16[4,16,16,128]{3,2,1,0:T(8,128)(2,1)S(1)}, bf16[4,16,16,128]{3,2,1,0:T(8,128)(2,1)}, u32[]{:S(2)}, u32[]{:S(2)}) collective-permute-start(bf16[4,16,16,128]{3,2,1,0:T(8,128)(2,1)S(1)} %pad_maximum_fusion.1.rest_1_), channel_id=1, source_target_pairs={{0,1},{1,0},{2,3},{3,2},{4,5},{5,4},{6,7},{7,6},{8,9},{9,8},{10,11... | collective-permute-start | bytes 786440 | tf_op jit(solution)/shard_map/ppermute | solution.py:19
  44.8 6.0 %collective-permute-start.9 = (bf16[4,16,16,128]{3,2,1,0:T(8,128)(2,1)S(1)}, bf16[4,16,16,128]{3,2,1,0:T(8,128)(2,1)}, u32[]{:S(2)}, u32[]{:S(2)}) collective-permute-start(bf16[4,16,16,128]{3,2,1,0:T(8,128)(2,1)S(1)} %collective-permute-done.3.rest_2_), channel_id=1, source_target_pairs={{0,1},{1,0},{2,3},{3,2},{4,5},{5,4},{6,7},{7,6},{8,9},{9,8},{10,11... | collective-permute-start | bytes 786440 | tf_op jit(solution)/shard_map/ppermute | solution.py:19
  44.9 5.9 %collective-permute-start.10 = (bf16[4,16,16,128]{3,2,1,0:T(8,128)(2,1)S(1)}, bf16[4,16,16,128]{3,2,1,0:T(8,128)(2,1)}, u32[]{:S(2)}, u32[]{:S(2)}) collective-permute-start(bf16[4,16,16,128]{3,2,1,0:T(8,128)(2,1)S(1)} %collective-permute-done.4.rest_3_), channel_id=1, source_target_pairs={{0,1},{1,0},{2,3},{3,2},{4,5},{5,4},{6,7},{7,6},{8,9},{9,8},{10,11... | collective-permute-start | bytes 786440 | tf_op jit(solution)/shard_map/ppermute | solution.py:19
  50.8 3.4 %copy-start = (bf16[64,8,64,128]{3,2,1,0:T(8,128)(2,1)S(1)}, bf16[64,8,64,128]{3,2,1,0:T(8,128)(2,1)}, u32[]{:S(2)}) copy-start(bf16[64,8,64,128]{3,2,1,0:T(8,128)(2,1)} %ham_ref.1) | copy-start | bytes 25165828
  54.2 0.9 %copy-start.1 = (f32[16,4096]{1,0:T(8,128)S(1)}, f32[16,4096]{1,0:T(8,128)}, u32[]{:S(2)}) copy-start(f32[16,4096]{1,0:T(8,128)} %get-tuple-element.10.t0_ref) | copy-start | bytes 786436
  55.2 0.9 %copy-start.2 = (f32[16,4096]{1,0:T(8,128)S(1)}, f32[16,4096]{1,0:T(8,128)}, u32[]{:S(2)}) copy-start(f32[16,4096]{1,0:T(8,128)} %get-tuple-element.11.t1_ref) | copy-start | bytes 786436
  56.1 0.7 copy-start.4
  56.8 12.6 %copy-start.5 = (f32[32,32]{1,0:T(8,128)S(1)}, f32[32,32]{1,0:T(8,128)}, u32[]{:S(2)}) copy-start(f32[32,32]{1,0:T(8,128)} %get-tuple-element.9) | copy-start | bytes 12292
  68.7 0.7 copy-start.3
  69.5 1.2 %collective-permute-start.13 = (f32[48,64]{1,0:T(8,128)S(1)}, f32[48,64]{1,0:T(8,128)S(1)}, u32[]{:S(2)}, u32[]{:S(2)}) collective-permute-start(f32[48,64]{1,0:T(8,128)S(1)} %select_maximum_fusion), channel_id=1, source_target_pairs={{0,1},{1,0},{2,3},{3,2},{4,5},{5,4},{6,7},{7,6},{8,9},{9,8},{10,11... | collective-permute-start | bytes 36872 | tf_op jit(solution)/shard_map/ppermute | solution.py:19
  70.8 3.8 %collective-permute-start.14 = (f32[48,64]{1,0:T(8,128)S(1)}, f32[48,64]{1,0:T(8,128)S(1)}, u32[]{:S(2)}, u32[]{:S(2)}) collective-permute-start(f32[48,64]{1,0:T(8,128)S(1)} %fusion.1), channel_id=1, source_target_pairs={{0,2},{2,0},{4,6},{6,4},{8,10},{10,8},{12,14},{14,12},{16,18},{18,... | collective-permute-start | bytes 36872 | tf_op jit(solution)/shard_map/ppermute | solution.py:19
  74.6 3.8 %collective-permute-start.15 = (f32[48,64]{1,0:T(8,128)S(1)}, f32[48,64]{1,0:T(8,128)S(1)}, u32[]{:S(2)}, u32[]{:S(2)}) collective-permute-start(f32[48,64]{1,0:T(8,128)S(1)} %add.18), channel_id=1, source_target_pairs={{0,4},{2,6},{4,0},{6,2},{8,12},{10,14},{12,8},{14,10},{16,20},{18,... | collective-permute-start | bytes 36872 | tf_op jit(solution)/shard_map/ppermute | solution.py:19
  78.5 3.8 %collective-permute-start.16 = (f32[48,64]{1,0:T(8,128)S(1)}, f32[48,64]{1,0:T(8,128)S(1)}, u32[]{:S(2)}, u32[]{:S(2)}) collective-permute-start(f32[48,64]{1,0:T(8,128)S(1)} %add.19), channel_id=1, source_target_pairs={{0,8},{2,10},{4,12},{6,14},{8,0},{10,2},{12,4},{14,6},{16,24},{18,... | collective-permute-start | bytes 36872 | tf_op jit(solution)/shard_map/ppermute | solution.py:19
  82.3 4.7 %collective-permute-start.17 = (f32[48,64]{1,0:T(8,128)S(1)}, f32[48,64]{1,0:T(8,128)S(1)}, u32[]{:S(2)}, u32[]{:S(2)}) collective-permute-start(f32[48,64]{1,0:T(8,128)S(1)} %add.20), channel_id=1, source_target_pairs={{0,16},{2,18},{4,20},{6,22},{8,24},{10,26},{12,28},{14,30},{16,0},... | collective-permute-start | bytes 36872 | tf_op jit(solution)/shard_map/ppermute | solution.py:19

commit v3 on v0

v3 whole, which is shorter than its diff:
```python
import functools

import jax
import jax.numpy as jnp
from jax import lax
from jax.experimental import pallas as pl
from jax.experimental.pallas import tpu as pltpu
from jax.sharding import PartitionSpec as P

SCALE = 2.0 ** -8
F32 = jnp.float32
BF16 = jnp.bfloat16
NT = (((1,), (1,)), ((), ()))
TN = (((0,), (0,)), ((), ()))
NN = (((1,), (0,)), ((), ()))
VMEM_LIMIT = 48 * 1024 * 1024
PIECES = 6


def swap(x, axis, distance):
    n = lax.axis_size(axis)
    return lax.ppermute(x, axis, [(i, i ^ distance) for i in range(n)])


def plane_swap(x, order):
    n_chan, n_rad = lax.axis_size("chan"), lax.axis_size("rad")
    pairs = []
    for c in range(n_chan):
        for r in range(n_rad):
            pairs.append((c * n_rad + r, (c ^ order[r % 2]) * n_rad + r))
    return lax.ppermute(x, ("chan", "rad"), pairs)


def z_groups(nz):
    return [[0], [1] + list(range(2, nz, 2)), list(range(3, nz, 2))]


def z_place(z, nz):
    if nz == 4:
        return z
    return jnp.where(z < 2, z, jnp.where((z & 1) == 1, (nz + z - 1) >> 1, 1 + (z >> 1)))


def split3(x):
    hi = x.astype(BF16)
    rest = x - hi.astype(F32)
    mid = rest.astype(BF16)
    return hi, mid, (rest - mid.astype(F32)).astype(BF16)


def dot32(x, y, dims=NN):
    return lax.dot_general(x, y, dims, precision=lax.Precision.HIGHEST, preferred_element_type=F32)


def block_sum(g, rows, cols):
    g = sum(g[i : i + rows] for i in range(0, g.shape[0], rows))
    return sum(g[:, i : i + cols] for i in range(0, g.shape[1], cols))


def trial_kernel(t_ref, d_ref, zhm_ref, zl_ref, dc_ref, gram_ref):
    ch, k, r = t_ref.shape
    group = 128 // r
    for i in range(ch // group):
        lanes = pl.ds(i * 128, 128)
        t = jnp.concatenate([t_ref[i * group + g] for g in range(group)], axis=1)
        d = jnp.concatenate([d_ref[pl.ds(i * group + g, 1), :] for g in range(group)], axis=1)
        dc_ref[:, lanes] = d
        hi, mid, lo = split3(jnp.concatenate([t / d, t], axis=0))
        zhm_ref[:, lanes] = jnp.concatenate([hi, mid], axis=0)
        zl_ref[:, lanes] = lo
    z = jnp.concatenate([zhm_ref[...], zl_ref[...]], axis=0)
    g = block_sum(lax.dot_general(z, z, NT, preferred_element_type=F32), 2 * k, 2 * k)
    gram_ref[...] = jnp.concatenate([g[k:, :], g[:k, :k]], axis=1)


def apply_kernel(
    n_chan, n_rad, groups, partners_ref, stored_ref, ham_hbm, zhm_ref, zl_ref, dc_ref, gt_ref, *rest
):
    pieces = rest[: PIECES * n_rad]
    az_ref, sums_ref, table, ham, table_sems, ham_sems = rest[PIECES * n_rad :]
    ch, ncoup, r, _ = ham.shape
    k = zl_ref.shape[0] // 2
    nz, share = table.shape[2:4]
    per_step = 8
    steps = ch // per_step
    block = per_step * r
    me_chan, me_rad = lax.axis_index("chan"), lax.axis_index("rad")

    first = (0, groups[0], groups[0] + groups[1], nz)
    copies = []
    for c in range(n_rad):
        for i, (g, h) in enumerate(((0, 0), (0, 1), (1, 0), (2, 0), (1, 1), (2, 1))):
            place = table.at[c, pl.ds(2 * h, 2), pl.ds(first[g], groups[g])]
            n = c * PIECES + i
            copies.append(pltpu.make_async_copy(pieces[n], place, table_sems.at[n]))
    for copy in copies:
        copy.start()

    def ham_copy(step):
        rows = pl.ds(step * per_step, per_step)
        return pltpu.make_async_copy(ham_hbm.at[rows], ham.at[rows], ham_sems.at[step])

    for step in range(steps):
        ham_copy(step).start()
    for copy in copies:
        copy.wait()

    def work(step, gram):
        ham_copy(step).wait()
        blocks = []
        for i in range(per_step):
            p = step * per_step + i
            rows = []
            for j in range(ncoup):
                q = stored_ref[partners_ref[j, p]]
                slot = lax.div(q, ch) ^ me_chan
                local = lax.rem(q, ch)
                core = lax.div(local, share)
                near = slot & 3
                part = jnp.where((core & 1) == 1, ((near & 1) << 1) | (near >> 1), near)
                rows.append(table[core ^ me_rad, part, z_place(slot >> 2, nz), lax.rem(local, share)])
            lhs = jnp.concatenate(rows, axis=1)
            rhs = jnp.concatenate([ham[p, j] for j in range(ncoup)], axis=1)
            blocks.append(lax.dot_general(lhs, rhs, NT, preferred_element_type=F32))
        lanes = pl.ds(pl.multiple_of(step * block, block), block)
        a0 = jnp.concatenate(blocks, axis=1) * SCALE
        a1_terms = split3(a0 / dc_ref[:, lanes])
        az_ref[:, lanes] = jnp.concatenate(a1_terms[:2], axis=0)
        right = jnp.concatenate(a1_terms + split3(a0), axis=0)
        left = jnp.concatenate([zhm_ref[:, lanes], zl_ref[:, lanes], right[: 3 * k]], axis=0)
        return gram + lax.dot_general(left, right, NT, preferred_element_type=F32)

    gram = lax.fori_loop(0, steps, work, jnp.zeros((9 * k, 6 * k), F32))
    ta1 = block_sum(gram[: 6 * k, : 3 * k], 2 * k, k)
    ta0 = block_sum(gram[: 6 * k, 3 * k :], 2 * k, k)
    aa = block_sum(gram[6 * k :, : 3 * k], k, k)
    gt = gt_ref[...]
    parts = [ta1[k:], gt[:, : 2 * k], ta0[k:], ta1[:k], gt[:, 2 * k :], aa, jnp.zeros((k, k), F32)]
    sums_ref[...] = jnp.concatenate(parts, axis=1)


def finish_kernel(total, sums_ref, az_ref, zhm_ref, out_ref, ritz_ref):
    ch, k, r = out_ref.shape
    s = jnp.sum(sums_ref[...], axis=0)
    row = lax.broadcasted_iota(jnp.int32, (k, 4 * k), 0)
    b1, b0 = s[:, k : 2 * k], s[:, 2 * k : 3 * k]
    s1, s2 = s[:, :k], s[:, 4 * k : 5 * k]
    b2, aa = s[:, 5 * k : 6 * k], s[:, 6 * k : 7 * k]
    aug = s[:, : 4 * k]
    for i in range(k):
        pivot_row = aug[i : i + 1, :] / aug[i : i + 1, 2 * k + i : 2 * k + i + 1]
        column = aug[:, 2 * k + i : 2 * k + i + 1]
        aug = jnp.where(row == i, pivot_row, aug - column * pivot_row)
    coef = aug[:, 3 * k :]
    mix = aug[:, :k] - dot32(aug[:, k : 2 * k], coef)
    eye = lax.broadcasted_iota(jnp.int32, (k, k), 0) == lax.broadcasted_iota(jnp.int32, (k, k), 1)
    ritz_ref[...] = jnp.sum(jnp.where(eye, coef, 0.0), axis=0, keepdims=True) * (1.0 / SCALE)
    e = jnp.concatenate([coef, mix], axis=0)
    q = jnp.concatenate([s2, s1], axis=0)
    b = jnp.concatenate(
        [jnp.concatenate([b2, b1.T], axis=1), jnp.concatenate([b1, b0], axis=1)], axis=0
    )
    gram = aa - dot32(q, e, TN) - dot32(e, q - dot32(b, e), TN)
    aug = jnp.concatenate([gram, eye.astype(F32), -coef.T, -mix.T], axis=1)
    for i in range(k):
        pivot_row = aug[i : i + 1, :]
        pivot = pivot_row[:, i : i + 1]
        column = jnp.where(row[:, :1] > i, aug[:, i : i + 1] / pivot, 0.0)
        scaled = pivot_row * (lax.rsqrt(pivot) * (total ** 0.5))
        aug = jnp.where(row == i, scaled, aug - column * pivot_row)
    hi, mid, _ = split3(aug[:, k:])
    lhs = jnp.concatenate([hi, hi, mid], axis=1)
    x_hi = jnp.concatenate([az_ref[:k, :], zhm_ref[: 2 * k, :]], axis=0)
    x_mid = jnp.concatenate([az_ref[k:, :], zhm_ref[2 * k :, :]], axis=0)
    new = lax.dot_general(
        lhs, jnp.concatenate([x_hi, x_mid, x_hi], axis=0), NN, preferred_element_type=F32
    )
    for p in range(ch):
        out_ref[p] = new[:, p * r : (p + 1) * r]


def own_share(trial_block):
    n_rad = lax.axis_size("rad")
    ch, k, r = trial_block.shape
    me = lax.axis_index("rad")
    rounded = trial_block.astype(BF16).reshape(n_rad, ch // n_rad, k, r)
    got = []
    for d in range(n_rad):
        part = lax.dynamic_index_in_dim(rounded, me ^ d, 0, keepdims=False)
        got.append(swap(part, "rad", d) if d else part)
    lanes = []
    for c in range(n_rad):
        x = got[0]
        for d in range(1, n_rad):
            x = jnp.where(me ^ d == c, got[d], x)
        lanes.append(x)
    return jnp.concatenate(lanes, axis=2)


def body(trial_block, ham_blocks, partners, stored_at, precond_diag):
    n_chan, n_rad = lax.axis_size("chan"), lax.axis_size("rad")
    ch, k, r = trial_block.shape
    splines = ham_blocks.shape[3]
    lanes = ch * r
    total = float(n_chan * n_rad * lanes)
    share, nz = ch // n_rad, n_chan // 4

    own = own_share(trial_block)
    column = [own] + [None] * (nz - 1)
    for z in range(nz - 2, 0, -2):
        column[z] = swap(own, "chan", 4 * z)
    column[1] = swap(own, "chan", 4)
    near = plane_swap(own[None], (1, 2))
    local = pl.pallas_call(
        trial_kernel,
        out_shape=[
            jax.ShapeDtypeStruct((4 * k, lanes), BF16),
            jax.ShapeDtypeStruct((2 * k, lanes), BF16),
            jax.ShapeDtypeStruct((1, lanes), F32),
            jax.ShapeDtypeStruct((k, 3 * k), F32),
        ],
        name="trial_gram",
    )(trial_block, precond_diag)
    column, near, local = lax.optimization_barrier((column, near, local))
    zhm, zl, dc, gram_t = local

    def second(parts, first):
        half = jnp.stack([parts, first])
        return half, plane_swap(half, (2, 1))

    groups = z_groups(nz)
    half0, far0 = second(own[None], near)
    parts1 = jnp.stack([column[z] for z in groups[1]])
    near1 = plane_swap(parts1, (1, 2))
    for z in groups[2]:
        column[z] = swap(column[z - 1], "chan", 4)
    column, near1, half0, far0 = lax.optimization_barrier((column, near1, half0, far0))
    parts2 = jnp.stack([column[z] for z in groups[2]])
    near2 = plane_swap(parts2, (1, 2))
    half1, far1 = second(parts1, near1)
    others = [[swap(x, "rad", c) for x in (half0, far0, half1)] for c in range(1, n_rad)]
    near2, others = lax.optimization_barrier((near2, others))
    half2, far2 = second(parts2, near2)
    others = [o + [swap(half2, "rad", c + 1)] for c, o in enumerate(others)]
    far1, far2, others = lax.optimization_barrier((far1, far2, others))
    pieces = [half0, far0, half1, half2, far1, far2]
    for c, o in enumerate(others):
        pieces += o + [swap(x, "rad", c + 1) for x in (far1, far2)]
    sizes = [len(g) for g in groups]
    whole = pl.BlockSpec(memory_space=pltpu.VMEM)
    smem = pl.BlockSpec(memory_space=pltpu.SMEM)
    any_ = pl.BlockSpec(memory_space=pl.ANY)
    az, sums = pl.pallas_call(
        functools.partial(apply_kernel, n_chan, n_rad, sizes),
        in_specs=[smem, smem, any_, whole, whole, whole, whole] + [any_] * len(pieces),
        out_shape=[
            jax.ShapeDtypeStruct((2 * k, lanes), BF16),
            jax.ShapeDtypeStruct((k, 8 * k), F32),
        ],
        scratch_shapes=[
            pltpu.VMEM((n_rad, 4, nz, share, k, splines), BF16),
            pltpu.VMEM(ham_blocks.shape, BF16),
            pltpu.SemaphoreType.DMA((len(pieces),)),
            pltpu.SemaphoreType.DMA((ch // 8,)),
        ],
        compiler_params=pltpu.CompilerParams(vmem_limit_bytes=VMEM_LIMIT),
        name="apply",
    )(partners.T, stored_at, ham_blocks, zhm, zl, dc, gram_t, *pieces)

    for c in range(n_rad.bit_length() - 1):
        sums = sums + swap(sums, "rad", 1 << c)
    all_sums = lax.all_to_all(
        jnp.broadcast_to(sums, (n_chan,) + sums.shape), "chan", split_axis=0, concat_axis=0, tiled=True
    )
    new_block, ritz = pl.pallas_call(
        functools.partial(finish_kernel, total),
        out_shape=[
            jax.ShapeDtypeStruct((ch, k, r), F32),
            jax.ShapeDtypeStruct((1, k), F32),
        ],
        name="finish",
    )(all_sums, az, zhm)
    return (new_block, ritz.reshape(k))


def solution(mesh):
    return jax.shard_map(
        body,
        mesh=mesh,
        in_specs=(
            P("chan", None, "rad"),
            P("chan", None, "rad", None),
            P("chan", None),
            P(),
            P("chan", "rad"),
        ),
        out_specs=(P("chan", None, "rad"), P()),
        check_vma=False,
    )
```

time: 278 us -> 79 us (0.28)
  blocking collectives: 138 us -> 14.1 us
  waiting for transfers between devices: 81.3 us -> 22.5 us
  Pallas kernels: 0 us -> 19.1 us
  local copies, waits for them, and re-layouts: 22.4 us -> 5.51 us
  matrix products: 12.6 us -> 0 us
  other arithmetic: 9.41 us -> 1.36 us
    psum x3 -> x0, blocking collectives: 136 us -> none  [the longest x1 55.5 us: body(): lax.psum((inner_products(trial_block, applied), inner_products(trial_bloc...]
    all_to_all x2 -> x0, waiting for transfers between devices: 81.3 us -> none  [the longest x1 78.3 us: body(): lax.all_to_all(served, 'chan', split_axis=0, concat_axis=0, tiled=True)]
    ppermute x0 -> x17, waiting for transfers between devices: none -> 22.5 us  [the longest x6 12.2 us: plane_swap(): return lax.ppermute(x, ('chan', 'rad'), pairs)]
    pallas_call x0 -> x3, Pallas kernels: none -> 19.1 us  [the longest x1 10.9 us: body(): pl.pallas_call(functools.partial(apply_kernel, n_chan, n_rad, sizes), in_...]
    gather x4 -> x0, local copies, waits for them, and re-layouts: 15.2 us -> none  [the longest x1 8.39 us: body(): served = whole_rows[asked]]
    ppermute x0 -> x17, starting transfers between devices: none -> 15.2 us  [the longest x6 7.76 us: plane_swap(): return lax.ppermute(x, ('chan', 'rad'), pairs)]
    all_to_all x0 -> x1, blocking collectives: none -> 14.1 us  [body(): lax.all_to_all(jnp.broadcast_to(sums, (n_chan,) + sums.shape), 'chan', sp...]
    all_to_all x2 -> x0, starting transfers between devices: 13 us -> none  [the longest x1 8.31 us: body(): lax.all_to_all(wanted, 'chan', split_axis=0, concat_axis=0, tiled=True)]
  transfers between devices with their start and end apart: 2 -> 17, of which waited for: 2 -> 10; matrix products, arithmetic and copies ran while one was open for 1% -> 0% of each run, Pallas kernels for 0% -> 3%
where the time goes in v3:
time: 79 us; the launch traced here: 78.5 us
  waiting for transfers between devices  22.5 us (28%)
  Pallas kernels  19.1 us (24%)
  starting transfers between devices  15.2 us (19%)
  blocking collectives  14.1 us (18%)
  local copies, waits for them, and re-layouts  5.51 us (7%)
  other arithmetic  1.36 us (2%)
    all_to_all x1, blocking collectives, body(): lax.all_to_all(jnp.broadcast_to(sums, (n_chan,) + sums.shape), 'chan', sp...  14.1 us
    ppermute x6, waiting for transfers between devices, plane_swap(): return lax.ppermute(x, ('chan', 'rad'), pairs)  12.2 us
    pallas_call x1, Pallas kernels, body(): pl.pallas_call(functools.partial(apply_kernel, n_chan, n_rad, sizes), in_...  10.9 us
    ppermute x11, waiting for transfers between devices, swap(): return lax.ppermute(x, axis, [(i, i ^ distance) for i in range(n)])  10.2 us
    ppermute x6, starting transfers between devices, plane_swap(): return lax.ppermute(x, ('chan', 'rad'), pairs)  7.76 us
    ppermute x11, starting transfers between devices, swap(): return lax.ppermute(x, axis, [(i, i ^ distance) for i in range(n)])  7.44 us
    pallas_call x1, Pallas kernels, body(): pl.pallas_call(functools.partial(finish_kernel, total), out_shape=[jax.Sh...  5.97 us
    unnamed x14, local copies, waits for them, and re-layouts  5.48 us
  transfers between devices with their start and end apart: 17, of which 10 were waited for; matrix products, arithmetic and copies ran while one was open for 0% of the time, Pallas kernels for 3%

profile of v3, /device:TPU:0, one launch (start us, length us, event | category | flops | bytes accessed | tf_op | source)
XLA Modules:
  0.0 78.5 jit_solution(15127373940540641163)
XLA Ops:
  0.6 1.1 %convert_element_type.3 = bf16[64,16,64]{2,1,0:T(8,128)(2,1)S(1)} convert(f32[64,16,64]{2,1,0:T(8,128)} %t_ref.1) | non-fusion elementwise | flops 65536 | bytes 393216 | tf_op jit(solution)/shard_map/convert_element_type | solution.py:186
  1.7 0.5 collective-permute-start
  2.3 1.0 %collective-permute-done = bf16[32,16,64]{2,1,0:T(8,128)(2,1)S(1)} collective-permute-done((bf16[32,16,64]{2,1,0:T(8,128)(2,1)S(1)}, bf16[32,16,64]{2,1,0:T(8,128)(2,1)S(1)}, u32[]{:S(2)}, u32[]{:S(2)}) %collective-permute-start) | collective-permute-done | bytes 65568 | tf_op jit(solution)/shard_map/ppermute | solution.py:22
  3.4 2.9 %collective-permute-start.3 = (bf16[1,32,16,128]{3,2,1,0:T(8,128)(2,1)S(1)}, bf16[1,32,16,128]{3,2,1,0:T(8,128)(2,1)S(1)}, u32[]{:S(2)}, u32[]{:S(2)}) collective-permute-start(bf16[1,32,16,128]{3,2,1,0:T(8,128)(2,1)S(1)} %bitcast.22), channel_id=1, source_target_pairs={{0,2},{1,5},{2,0},{3,7},{4,6},{5,1},{6,4},{7,3},{8,10},{9,13},{10,... | collective-permute-start | bytes 393224 | tf_op jit(solution)/shard_map/ppermute | solution.py:31
  6.3 2.6 %collective-permute-start.2 = (bf16[32,16,128]{2,1,0:T(8,128)(2,1)S(1)}, bf16[32,16,128]{2,1,0:T(8,128)(2,1)S(1)}, u32[]{:S(2)}, u32[]{:S(2)}) collective-permute-start(bf16[32,16,128]{2,1,0:T(8,128)(2,1)S(1)} %pad_maximum_fusion.4), channel_id=1, source_target_pairs={{0,16},{2,18},{4,20},{6,22},{8,24},{10,26},{12,28},{14,30},{16,0},... | collective-permute-start | bytes 393224 | tf_op jit(solution)/shard_map/ppermute | solution.py:22
  8.9 1.6 %collective-permute-start.1 = (bf16[32,16,128]{2,1,0:T(8,128)(2,1)S(1)}, bf16[32,16,128]{2,1,0:T(8,128)(2,1)S(1)}, u32[]{:S(2)}, u32[]{:S(2)}) collective-permute-start(bf16[32,16,128]{2,1,0:T(8,128)(2,1)S(1)} %pad_maximum_fusion.4), channel_id=1, source_target_pairs={{0,8},{2,10},{4,12},{6,14},{8,0},{10,2},{12,4},{14,6},{16,24},{18,... | collective-permute-start | bytes 393224 | tf_op jit(solution)/shard_map/ppermute | solution.py:22
  10.5 2.3 %trial_gram.1 = (bf16[64,4096]{1,0:T(8,128)(2,1)}, bf16[32,4096]{1,0:T(8,128)(2,1)}, f32[1,4096]{1,0:T(1,128)}, f32[16,48]{1,0:T(8,128)}) custom-call(f32[64,16,64]{2,1,0:T(8,128)} %t_ref.1, f32[64,64]{1,0:T(8,128)} %d_ref.1), custom_call_target="tpu_custom_call" | custom-call | tf_op jit(solution)/shard_map/trial_gram/pallas_call | solution.py:214
  12.8 2.7 %collective-permute-done.2 = bf16[32,16,128]{2,1,0:T(8,128)(2,1)S(1)} collective-permute-done((bf16[32,16,128]{2,1,0:T(8,128)(2,1)S(1)}, bf16[32,16,128]{2,1,0:T(8,128)(2,1)S(1)}, u32[]{:S(2)}, u32[]{:S(2)}) %collective-permute-start.2) | collective-permute-done | bytes 131104 | tf_op jit(solution)/shard_map/ppermute | solution.py:22
  15.6 0.5 collective-permute-start.6
  16.2 1.6 %collective-permute-start.5 = (bf16[2,32,16,128]{3,2,1,0:T(8,128)(2,1)S(1)}, bf16[2,32,16,128]{3,2,1,0:T(8,128)(2,1)S(1)}, u32[]{:S(2)}, u32[]{:S(2)}) collective-permute-start(bf16[2,32,16,128]{3,2,1,0:T(8,128)(2,1)S(1)} %get-tuple-element.63), channel_id=1, source_target_pairs={{0,2},{1,5},{2,0},{3,7},{4,6},{5,1},{6,4},{7,3},{8,10},{9,13},{10,... | collective-permute-start | bytes 786440 | tf_op jit(solution)/shard_map/ppermute | solution.py:31
  17.8 1.4 %collective-permute-start.4 = (bf16[32,16,128]{2,1,0:T(8,128)(2,1)S(1)}, bf16[32,16,128]{2,1,0:T(8,128)(2,1)S(1)}, u32[]{:S(2)}, u32[]{:S(2)}) collective-permute-start(bf16[32,16,128]{2,1,0:T(8,128)(2,1)S(1)} %collective-permute-done.2), channel_id=1, source_target_pairs={{0,8},{2,10},{4,12},{6,14},{8,0},{10,2},{12,4},{14,6},{16,24},{18,... | collective-permute-start | bytes 393224 | tf_op jit(solution)/shard_map/ppermute | solution.py:22
  19.2 3.6 %collective-permute-done.4 = bf16[32,16,128]{2,1,0:T(8,128)(2,1)S(1)} collective-permute-done((bf16[32,16,128]{2,1,0:T(8,128)(2,1)S(1)}, bf16[32,16,128]{2,1,0:T(8,128)(2,1)S(1)}, u32[]{:S(2)}, u32[]{:S(2)}) %collective-permute-start.4) | collective-permute-done | bytes 131104 | tf_op jit(solution)/shard_map/ppermute | solution.py:22
  22.8 1.9 %collective-permute-done.6.rest_1_ = bf16[2,1,32,16,128]{4,3,2,1,0:T(8,128)(2,1)S(1)} collective-permute-done((bf16[2,1,32,16,128]{4,3,2,1,0:T(8,128)(2,1)S(1)}, bf16[2,1,32,16,128]{4,3,2,1,0:T(8,128)(2,1)S(1)}, u32[]{:S(2)}, u32[]{:S(2)}) %collective-permute-start.6) | collective-permute-done | bytes 262176 | tf_op jit(solution)/shard_map/ppermute | solution.py:31
  24.8 0.5 collective-permute-start.8
  25.7 0.5 collective-permute-start.7
  26.2 5.8 %collective-permute-done.7 = bf16[1,32,16,128]{3,2,1,0:T(8,128)(2,1)S(1)} collective-permute-done((bf16[1,32,16,128]{3,2,1,0:T(8,128)(2,1)S(1)}, bf16[1,32,16,128]{3,2,1,0:T(8,128)(2,1)S(1)}, u32[]{:S(2)}, u32[]{:S(2)}) %collective-permute-start.7) | collective-permute-done | bytes 131104 | tf_op jit(solution)/shard_map/ppermute | solution.py:31
  32.1 1.9 %collective-permute-start.12 = (bf16[2,1,32,16,128]{4,3,2,1,0:T(8,128)(2,1)S(1)}, bf16[2,1,32,16,128]{4,3,2,1,0:T(8,128)(2,1)S(1)}, u32[]{:S(2)}, u32[]{:S(2)}) collective-permute-start(bf16[2,1,32,16,128]{4,3,2,1,0:T(8,128)(2,1)S(1)} %pad_maximum_fusion.3.rest_3_), channel_id=1, source_target_pairs={{0,4},{1,3},{2,6},{3,1},{4,0},{5,7},{6,2},{7,5},{8,12},{9,11},{10,... | collective-permute-start | bytes 786440 | tf_op jit(solution)/shard_map/ppermute | solution.py:31
  34.0 1.4 %collective-permute-done.11.rest_4_ = bf16[2,2,32,16,128]{4,3,2,1,0:T(8,128)(2,1)S(1)} collective-permute-done((bf16[2,2,32,16,128]{4,3,2,1,0:T(8,128)(2,1)S(1)}, bf16[2,2,32,16,128]{4,3,2,1,0:T(8,128)(2,1)S(1)}, u32[]{:S(2)}, u32[]{:S(2)}) %collective-permute-start.11) | collective-permute-done | bytes 524320 | tf_op jit(solution)/shard_map/ppermute | solution.py:31
  35.5 3.1 %collective-permute-done.12.rest_5_ = bf16[2,1,32,16,128]{4,3,2,1,0:T(8,128)(2,1)S(1)} collective-permute-done((bf16[2,1,32,16,128]{4,3,2,1,0:T(8,128)(2,1)S(1)}, bf16[2,1,32,16,128]{4,3,2,1,0:T(8,128)(2,1)S(1)}, u32[]{:S(2)}, u32[]{:S(2)}) %collective-permute-start.12) | collective-permute-done | bytes 262176 | tf_op jit(solution)/shard_map/ppermute | solution.py:31
  38.6 0.5 collective-permute-start.15
  39.1 1.8 %collective-permute-done.15.rest_11_ = bf16[2,1,32,16,128]{4,3,2,1,0:T(8,128)(2,1)S(1)} collective-permute-done((bf16[2,1,32,16,128]{4,3,2,1,0:T(8,128)(2,1)S(1)}, bf16[2,1,32,16,128]{4,3,2,1,0:T(8,128)(2,1)S(1)}, u32[]{:S(2)}, u32[]{:S(2)}) %collective-permute-start.15) | collective-permute-done | bytes 262176 | tf_op jit(solution)/shard_map/ppermute | solution.py:22
  40.9 1.0 %copy-done = bf16[64,4096]{1,0:T(8,128)(2,1)S(1)} copy-done((bf16[64,4096]{1,0:T(8,128)(2,1)S(1)}, bf16[64,4096]{1,0:T(8,128)(2,1)}, u32[]{:S(2)}) %copy-start) | copy-done | bytes 524312
  41.9 0.9 %copy-done.1 = bf16[32,4096]{1,0:T(8,128)(2,1)S(1)} copy-done((bf16[32,4096]{1,0:T(8,128)(2,1)S(1)}, bf16[32,4096]{1,0:T(8,128)(2,1)}, u32[]{:S(2)}) %copy-start.1) | copy-done | bytes 262168
  42.9 0.7 copy-done.3
  43.6 0.7 copy-done.4
  44.3 0.7 copy-done.5
  45.0 0.7 copy-done.6
  45.6 10.9 %apply.1 = (bf16[32,4096]{1,0:T(8,128)(2,1)S(1)}, f32[16,128]{1,0:T(8,128)S(1)}) custom-call(s32[8,64]{1,0:T(8,128)S(1)} %bitcast.19, s32[1024]{0:T(1024)S(1)} %copy-done.6, bf16[64,8,64,128]{3,2,1,0:T(8,128)(2,1)} %ham_hbm.1, bf16[64,4096]{1,0:T(8,128)(2,1)S(1)} %copy-done, bf16[32,4096]{1,0:T(8,128)(2,1)S(1)} %copy-done.1, f32[1,4096]{1,0:T(1,128)S(1)} %copy-done.3, ...), custom_call_target="tpu_custom_call" | custom-call | tf_op jit(solution)/shard_map/apply/pallas_call | solution.py:253
  56.5 0.7 copy-done.2
  57.4 1.0 %collective-permute-done.16 = f32[16,128]{1,0:T(8,128)S(1)} collective-permute-done((f32[16,128]{1,0:T(8,128)S(1)}, f32[16,128]{1,0:T(8,128)S(1)}, u32[]{:S(2)}, u32[]{:S(2)}) %collective-permute-start.16) | collective-permute-done | bytes 8224 | tf_op jit(solution)/shard_map/ppermute | solution.py:22
  58.4 14.1 %all_to_all.5.sums_ref = f32[16,16,128]{2,1,0:T(8,128)} all-to-all(f32[16,16,128]{2,1,0:T(8,128)S(1)} %broadcast_in_dim.7), channel_id=1, replica_groups=mesh['chan'=16,'rad'=2] {'chan'}, dimensions={0} | all-to-all | bytes 262144 | tf_op jit(solution)/shard_map/all_to_all | solution.py:272
  72.5 6.0 %finish.1 = (f32[64,16,64]{2,1,0:T(8,128)}, f32[1,16]{1,0:T(1,128)}) custom-call(f32[16,16,128]{2,1,0:T(8,128)} %all_to_all.5.sums_ref, bf16[32,4096]{1,0:T(8,128)(2,1)} %copy-done.2, bf16[64,4096]{1,0:T(8,128)(2,1)} %get-tuple-element.35.zhm_ref), custom_call_target="tpu_custom_call" | custom-call | tf_op jit(solution)/shard_map/finish/pallas_call | solution.py:275
  (30 shorter events, 1.2 us)
Async XLA Ops:
  1.7 1.5 %collective-permute-start = (bf16[32,16,64]{2,1,0:T(8,128)(2,1)S(1)}, bf16[32,16,64]{2,1,0:T(8,128)(2,1)S(1)}, u32[]{:S(2)}, u32[]{:S(2)}) collective-permute-start(bf16[32,16,64]{2,1,0:T(8,128)(2,1)S(1)} %dynamic-slice_bitcast_fusion), channel_id=1, source_target_pairs={{0,1},{1,0},{2,3},{3,2},{4,5},{5,4},{6,7},{7,6},{8,9},{9,8},{10,11... | collective-permute-start | bytes 196616 | tf_op jit(solution)/shard_map/ppermute | solution.py:22
  3.4 9.4 %collective-permute-start.3 = (bf16[1,32,16,128]{3,2,1,0:T(8,128)(2,1)S(1)}, bf16[1,32,16,128]{3,2,1,0:T(8,128)(2,1)S(1)}, u32[]{:S(2)}, u32[]{:S(2)}) collective-permute-start(bf16[1,32,16,128]{3,2,1,0:T(8,128)(2,1)S(1)} %bitcast.22), channel_id=1, source_target_pairs={{0,2},{1,5},{2,0},{3,7},{4,6},{5,1},{6,4},{7,3},{8,10},{9,13},{10,... | collective-permute-start | bytes 393224 | tf_op jit(solution)/shard_map/ppermute | solution.py:31
  6.3 9.1 %collective-permute-start.2 = (bf16[32,16,128]{2,1,0:T(8,128)(2,1)S(1)}, bf16[32,16,128]{2,1,0:T(8,128)(2,1)S(1)}, u32[]{:S(2)}, u32[]{:S(2)}) collective-permute-start(bf16[32,16,128]{2,1,0:T(8,128)(2,1)S(1)} %pad_maximum_fusion.4), channel_id=1, source_target_pairs={{0,16},{2,18},{4,20},{6,22},{8,24},{10,26},{12,28},{14,30},{16,0},... | collective-permute-start | bytes 393224 | tf_op jit(solution)/shard_map/ppermute | solution.py:22
  8.9 6.7 %collective-permute-start.1 = (bf16[32,16,128]{2,1,0:T(8,128)(2,1)S(1)}, bf16[32,16,128]{2,1,0:T(8,128)(2,1)S(1)}, u32[]{:S(2)}, u32[]{:S(2)}) collective-permute-start(bf16[32,16,128]{2,1,0:T(8,128)(2,1)S(1)} %pad_maximum_fusion.4), channel_id=1, source_target_pairs={{0,8},{2,10},{4,12},{6,14},{8,0},{10,2},{12,4},{14,6},{16,24},{18,... | collective-permute-start | bytes 393224 | tf_op jit(solution)/shard_map/ppermute | solution.py:22
  15.6 9.0 %collective-permute-start.6 = (bf16[2,1,32,16,128]{4,3,2,1,0:T(8,128)(2,1)S(1)}, bf16[2,1,32,16,128]{4,3,2,1,0:T(8,128)(2,1)S(1)}, u32[]{:S(2)}, u32[]{:S(2)}) collective-permute-start(bf16[2,1,32,16,128]{4,3,2,1,0:T(8,128)(2,1)S(1)} %pad_maximum_fusion.2.rest_0_), channel_id=1, source_target_pairs={{0,4},{1,3},{2,6},{3,1},{4,0},{5,7},{6,2},{7,5},{8,12},{9,11},{10,... | collective-permute-start | bytes 786440 | tf_op jit(solution)/shard_map/ppermute | solution.py:31
  16.2 8.5 %collective-permute-start.5 = (bf16[2,32,16,128]{3,2,1,0:T(8,128)(2,1)S(1)}, bf16[2,32,16,128]{3,2,1,0:T(8,128)(2,1)S(1)}, u32[]{:S(2)}, u32[]{:S(2)}) collective-permute-start(bf16[2,32,16,128]{3,2,1,0:T(8,128)(2,1)S(1)} %get-tuple-element.63), channel_id=1, source_target_pairs={{0,2},{1,5},{2,0},{3,7},{4,6},{5,1},{6,4},{7,3},{8,10},{9,13},{10,... | collective-permute-start | bytes 786440 | tf_op jit(solution)/shard_map/ppermute | solution.py:31
  17.8 5.0 %collective-permute-start.4 = (bf16[32,16,128]{2,1,0:T(8,128)(2,1)S(1)}, bf16[32,16,128]{2,1,0:T(8,128)(2,1)S(1)}, u32[]{:S(2)}, u32[]{:S(2)}) collective-permute-start(bf16[32,16,128]{2,1,0:T(8,128)(2,1)S(1)} %collective-permute-done.2), channel_id=1, source_target_pairs={{0,8},{2,10},{4,12},{6,14},{8,0},{10,2},{12,4},{14,6},{16,24},{18,... | collective-permute-start | bytes 393224 | tf_op jit(solution)/shard_map/ppermute | solution.py:22
  24.7 7.3 %collective-permute-start.10 = (bf16[2,2,32,16,128]{4,3,2,1,0:T(8,128)(2,1)S(1)}, bf16[2,2,32,16,128]{4,3,2,1,0:T(8,128)(2,1)S(1)}, u32[]{:S(2)}, u32[]{:S(2)}) collective-permute-start(bf16[2,2,32,16,128]{4,3,2,1,0:T(8,128)(2,1)S(1)} %pad_maximum_fusion.rest_2_), channel_id=1, source_target_pairs={{0,1},{1,0},{2,3},{3,2},{4,5},{5,4},{6,7},{7,6},{8,9},{9,8},{10,11... | collective-permute-start | bytes 1572872 | tf_op jit(solution)/shard_map/ppermute | solution.py:22
  24.8 7.2 %collective-permute-start.8 = (bf16[2,1,32,16,128]{4,3,2,1,0:T(8,128)(2,1)S(1)}, bf16[2,1,32,16,128]{4,3,2,1,0:T(8,128)(2,1)S(1)}, u32[]{:S(2)}, u32[]{:S(2)}) collective-permute-start(bf16[2,1,32,16,128]{4,3,2,1,0:T(8,128)(2,1)S(1)} %pad_maximum_fusion.2.rest_0_), channel_id=1, source_target_pairs={{0,1},{1,0},{2,3},{3,2},{4,5},{5,4},{6,7},{7,6},{8,9},{9,8},{10,11... | collective-permute-start | bytes 786440 | tf_op jit(solution)/shard_map/ppermute | solution.py:22
  25.3 6.7 %collective-permute-start.9 = (bf16[2,1,32,16,128]{4,3,2,1,0:T(8,128)(2,1)S(1)}, bf16[2,1,32,16,128]{4,3,2,1,0:T(8,128)(2,1)S(1)}, u32[]{:S(2)}, u32[]{:S(2)}) collective-permute-start(bf16[2,1,32,16,128]{4,3,2,1,0:T(8,128)(2,1)S(1)} %collective-permute-done.6.rest_1_), channel_id=1, source_target_pairs={{0,1},{1,0},{2,3},{3,2},{4,5},{5,4},{6,7},{7,6},{8,9},{9,8},{10,11... | collective-permute-start | bytes 786440 | tf_op jit(solution)/shard_map/ppermute | solution.py:22
  25.4 10.1 %collective-permute-start.11 = (bf16[2,2,32,16,128]{4,3,2,1,0:T(8,128)(2,1)S(1)}, bf16[2,2,32,16,128]{4,3,2,1,0:T(8,128)(2,1)S(1)}, u32[]{:S(2)}, u32[]{:S(2)}) collective-permute-start(bf16[2,2,32,16,128]{4,3,2,1,0:T(8,128)(2,1)S(1)} %pad_maximum_fusion.rest_2_), channel_id=1, source_target_pairs={{0,4},{1,3},{2,6},{3,1},{4,0},{5,7},{6,2},{7,5},{8,12},{9,11},{10,... | collective-permute-start | bytes 1572872 | tf_op jit(solution)/shard_map/ppermute | solution.py:31
  25.7 6.3 %collective-permute-start.7 = (bf16[1,32,16,128]{3,2,1,0:T(8,128)(2,1)S(1)}, bf16[1,32,16,128]{3,2,1,0:T(8,128)(2,1)S(1)}, u32[]{:S(2)}, u32[]{:S(2)}) collective-permute-start(bf16[1,32,16,128]{3,2,1,0:T(8,128)(2,1)S(1)} %bitcast.25), channel_id=1, source_target_pairs={{0,2},{1,5},{2,0},{3,7},{4,6},{5,1},{6,4},{7,3},{8,10},{9,13},{10,... | collective-permute-start | bytes 393224 | tf_op jit(solution)/shard_map/ppermute | solution.py:31
  32.1 3.4 %collective-permute-start.13 = (bf16[2,1,32,16,128]{4,3,2,1,0:T(8,128)(2,1)S(1)}, bf16[2,1,32,16,128]{4,3,2,1,0:T(8,128)(2,1)S(1)}, u32[]{:S(2)}, u32[]{:S(2)}) collective-permute-start(bf16[2,1,32,16,128]{4,3,2,1,0:T(8,128)(2,1)S(1)} %pad_maximum_fusion.3.rest_3_), channel_id=1, source_target_pairs={{0,1},{1,0},{2,3},{3,2},{4,5},{5,4},{6,7},{7,6},{8,9},{9,8},{10,11... | collective-permute-start | bytes 786440 | tf_op jit(solution)/shard_map/ppermute | solution.py:22
  32.1 6.4 %collective-permute-start.12 = (bf16[2,1,32,16,128]{4,3,2,1,0:T(8,128)(2,1)S(1)}, bf16[2,1,32,16,128]{4,3,2,1,0:T(8,128)(2,1)S(1)}, u32[]{:S(2)}, u32[]{:S(2)}) collective-permute-start(bf16[2,1,32,16,128]{4,3,2,1,0:T(8,128)(2,1)S(1)} %pad_maximum_fusion.3.rest_3_), channel_id=1, source_target_pairs={{0,4},{1,3},{2,6},{3,1},{4,0},{5,7},{6,2},{7,5},{8,12},{9,11},{10,... | collective-permute-start | bytes 786440 | tf_op jit(solution)/shard_map/ppermute | solution.py:31
  38.6 2.3 %collective-permute-start.14 = (bf16[2,2,32,16,128]{4,3,2,1,0:T(8,128)(2,1)S(1)}, bf16[2,2,32,16,128]{4,3,2,1,0:T(8,128)(2,1)S(1)}, u32[]{:S(2)}, u32[]{:S(2)}) collective-permute-start(bf16[2,2,32,16,128]{4,3,2,1,0:T(8,128)(2,1)S(1)} %collective-permute-done.11.rest_4_), channel_id=1, source_target_pairs={{0,1},{1,0},{2,3},{3,2},{4,5},{5,4},{6,7},{7,6},{8,9},{9,8},{10,11... | collective-permute-start | bytes 1572872 | tf_op jit(solution)/shard_map/ppermute | solution.py:22
  38.6 2.3 %collective-permute-start.15 = (bf16[2,1,32,16,128]{4,3,2,1,0:T(8,128)(2,1)S(1)}, bf16[2,1,32,16,128]{4,3,2,1,0:T(8,128)(2,1)S(1)}, u32[]{:S(2)}, u32[]{:S(2)}) collective-permute-start(bf16[2,1,32,16,128]{4,3,2,1,0:T(8,128)(2,1)S(1)} %collective-permute-done.12.rest_5_), channel_id=1, source_target_pairs={{0,1},{1,0},{2,3},{3,2},{4,5},{5,4},{6,7},{7,6},{8,9},{9,8},{10,11... | collective-permute-start | bytes 786440 | tf_op jit(solution)/shard_map/ppermute | solution.py:22
  40.9 1.0 %copy-start = (bf16[64,4096]{1,0:T(8,128)(2,1)S(1)}, bf16[64,4096]{1,0:T(8,128)(2,1)}, u32[]{:S(2)}) copy-start(bf16[64,4096]{1,0:T(8,128)(2,1)} %get-tuple-element.35.zhm_ref) | copy-start | bytes 1572868
  41.9 0.9 %copy-start.1 = (bf16[32,4096]{1,0:T(8,128)(2,1)S(1)}, bf16[32,4096]{1,0:T(8,128)(2,1)}, u32[]{:S(2)}) copy-start(bf16[32,4096]{1,0:T(8,128)(2,1)} %get-tuple-element.36.zl_ref) | copy-start | bytes 786436
  42.9 0.7 copy-start.3
  43.6 0.7 copy-start.4
  44.3 0.7 copy-start.5
  45.0 0.7 copy-start.6
  56.5 0.7 copy-start.2
  57.2 1.2 %collective-permute-start.16 = (f32[16,128]{1,0:T(8,128)S(1)}, f32[16,128]{1,0:T(8,128)S(1)}, u32[]{:S(2)}, u32[]{:S(2)}) collective-permute-start(f32[16,128]{1,0:T(8,128)S(1)} %get-tuple-element.56), channel_id=1, source_target_pairs={{0,1},{1,0},{2,3},{3,2},{4,5},{5,4},{6,7},{7,6},{8,9},{9,8},{10,11... | collective-permute-start | bytes 24584 | tf_op jit(solution)/shard_map/ppermute | solution.py:22

commit v4 on v3

v4 whole, which is shorter than its diff:
```python
import functools

import jax
import jax.numpy as jnp
from jax import lax
from jax.experimental import pallas as pl
from jax.experimental.pallas import tpu as pltpu
from jax.sharding import PartitionSpec as P

SCALE = 2.0 ** -8
F32 = jnp.float32
BF16 = jnp.bfloat16
NT = (((1,), (1,)), ((), ()))
TN = (((0,), (0,)), ((), ()))
NN = (((1,), (0,)), ((), ()))
VMEM_LIMIT = 12 * 1024 * 1024


def swap(x, axis, distance):
    n = lax.axis_size(axis)
    return lax.ppermute(x, axis, [(i, i ^ distance) for i in range(n)])


def plane_swap(x, order):
    n_chan, n_rad = lax.axis_size("chan"), lax.axis_size("rad")
    pairs = []
    for c in range(n_chan):
        for r in range(n_rad):
            pairs.append((c * n_rad + r, (c ^ order[r % 2]) * n_rad + r))
    return lax.ppermute(x, ("chan", "rad"), pairs)


def z_groups(nz):
    return [[0], [1] + list(range(2, nz, 2)), list(range(3, nz, 2))]


def z_place(z, nz):
    if nz == 4:
        return z
    return jnp.where(z < 2, z, jnp.where((z & 1) == 1, (nz + z - 1) >> 1, 1 + (z >> 1)))


def in_vmem(x):
    return pltpu.with_memory_space_constraint(x, pltpu.VMEM)


def in_hbm(x):
    return pltpu.with_memory_space_constraint(x, pltpu.HBM)


def split3(x):
    hi = x.astype(BF16)
    rest = x - hi.astype(F32)
    mid = rest.astype(BF16)
    return hi, mid, (rest - mid.astype(F32)).astype(BF16)


def dot32(x, y, dims=NN):
    return lax.dot_general(x, y, dims, precision=lax.Precision.HIGHEST, preferred_element_type=F32)


def block_sum(g, rows, cols):
    g = sum(g[i : i + rows] for i in range(0, g.shape[0], rows))
    return sum(g[:, i : i + cols] for i in range(0, g.shape[1], cols))


def trial_kernel(t_ref, d_ref, zhm_ref, zl_ref, dc_ref, gram_ref):
    ch, k, r = t_ref.shape
    group = 128 // r
    for i in range(ch // group):
        lanes = pl.ds(i * 128, 128)
        t = jnp.concatenate([t_ref[i * group + g] for g in range(group)], axis=1)
        d = jnp.concatenate([d_ref[pl.ds(i * group + g, 1), :] for g in range(group)], axis=1)
        dc_ref[:, lanes] = d
        hi, mid, lo = split3(jnp.concatenate([t / d, t], axis=0))
        zhm_ref[:, lanes] = jnp.concatenate([hi, mid], axis=0)
        zl_ref[:, lanes] = lo
    z = jnp.concatenate([zhm_ref[...], zl_ref[...]], axis=0)
    g = block_sum(lax.dot_general(z, z, NT, preferred_element_type=F32), 2 * k, 2 * k)
    gram_ref[...] = jnp.concatenate([g[k:, :], g[:k, :k]], axis=1)


def load_kernel(n_chan, n_rad, partners_ref, stored_ref, ham_hbm, ham_ref, rows_ref, sem):
    ncoup, ch = partners_ref.shape
    share, nz = ch // n_rad, n_chan // 4
    copy = pltpu.make_async_copy(ham_hbm, ham_ref, sem)
    copy.start()
    me_chan, me_rad = lax.axis_index("chan"), lax.axis_index("rad")

    def find(p, carry):
        for j in range(ncoup):
            q = stored_ref[partners_ref[j, p]]
            slot = lax.div(q, ch) ^ me_chan
            local = lax.rem(q, ch)
            core = lax.div(local, share)
            near = slot & 3
            part = jnp.where((core & 1) == 1, ((near & 1) << 1) | (near >> 1), near)
            place = ((core ^ me_rad) * 4 + part) * nz + z_place(slot >> 2, nz)
            rows_ref[p * ncoup + j] = place * share + lax.rem(local, share)
        return carry

    lax.fori_loop(0, ch, find, 0)
    copy.wait()


def apply_kernel(rows_ref, ham_ref, table_ref, zhm_ref, zl_ref, dc_ref, gt_ref, az_ref, sums_ref, a0_ref):
    ch, ncoup, r, splines = ham_ref.shape
    k = zl_ref.shape[0] // 2
    group = 256 // r

    def work(g, carry):
        left, right = [], []
        for i in range(group):
            p = g * group + i
            left.append(
                jnp.concatenate([table_ref[rows_ref[p * ncoup + j]] for j in range(ncoup)], axis=1)
            )
            right.append(jnp.concatenate([ham_ref[p, j] for j in range(ncoup)], axis=1))
        product = lax.dot_general(
            jnp.concatenate(left, axis=0),
            jnp.concatenate(right, axis=0),
            NT,
            preferred_element_type=F32,
        )
        own = [product[i * k : (i + 1) * k, i * r : (i + 1) * r] for i in range(group)]
        a0_ref[:, pl.ds(pl.multiple_of(g * 256, 256), 256)] = jnp.concatenate(own, axis=1) * SCALE
        return carry

    lax.fori_loop(0, ch // group, work, 0)

    lanes = ch * r
    block = min(lanes, 1024)

    def gram_block(i, gram):
        at = pl.ds(pl.multiple_of(i * block, block), block)
        a0 = a0_ref[:, at]
        a1_terms = split3(a0 / dc_ref[:, at])
        az_ref[:, at] = jnp.concatenate(a1_terms[:2], axis=0)
        right = jnp.concatenate(a1_terms + split3(a0), axis=0)
        left = jnp.concatenate([zhm_ref[:, at], zl_ref[:, at], right[: 3 * k]], axis=0)
        return gram + lax.dot_general(left, right, NT, preferred_element_type=F32)

    gram = lax.fori_loop(0, lanes // block, gram_block, jnp.zeros((9 * k, 6 * k), F32))
    ta1 = block_sum(gram[: 6 * k, : 3 * k], 2 * k, k)
    ta0 = block_sum(gram[: 6 * k, 3 * k :], 2 * k, k)
    aa = block_sum(gram[6 * k :, : 3 * k], k, k)
    gt = gt_ref[...]
    parts = [ta1[k:], gt[:, : 2 * k], ta0[k:], ta1[:k], gt[:, 2 * k :], aa, jnp.zeros((k, k), F32)]
    sums_ref[...] = jnp.concatenate(parts, axis=1)


def spread(x, i):
    return jnp.broadcast_to(x[:, i : i + 1], (x.shape[0], 128))


def finish_kernel(total, sums_ref, az_ref, zhm_ref, out_ref, ritz_ref):
    ch, k, r = out_ref.shape
    s = sums_ref[...]
    row = lax.broadcasted_iota(jnp.int32, (k, 128), 0)
    cols = [spread(s, 2 * k + i) for i in range(k)]
    x = s
    for i in range(k):
        scale = 1.0 / cols[i][i : i + 1]
        pivot = x[i : i + 1] * scale
        x = jnp.where(row == i, pivot, x - cols[i] * pivot)
        for j in range(i + 1, k):
            part = cols[j][i : i + 1] * scale
            cols[j] = jnp.where(row == i, part, cols[j] - cols[i] * part)
    coef = x[:, 3 * k : 4 * k]
    eye = lax.broadcasted_iota(jnp.int32, (k, k), 0) == lax.broadcasted_iota(jnp.int32, (k, k), 1)
    ritz_ref[...] = jnp.sum(jnp.where(eye, coef, 0.0), axis=0, keepdims=True) * (1.0 / SCALE)
    s1, b1 = s[:, :k], s[:, k : 2 * k]
    s2, b2, aa = s[:, 4 * k : 5 * k], s[:, 5 * k : 6 * k], s[:, 6 * k : 7 * k]
    known = jnp.concatenate([x[:, :k], s1, s2], axis=0)
    known = known - dot32(jnp.concatenate([x[:, k : 2 * k], b1, b2], axis=0), coef)
    mix, corr, weighted = known[:k], known[k : 2 * k], known[2 * k :]
    gram = aa - dot32(
        jnp.concatenate([s2, coef, corr], axis=0), jnp.concatenate([coef, weighted, mix], axis=0), TN
    )
    cols = [spread(gram, i) for i in range(k)]
    pad = jnp.zeros((k, 128 - 3 * k), F32)
    x = jnp.concatenate([eye.astype(F32), -coef.T, -mix.T, pad], axis=1)
    for i in range(k):
        pivot = cols[i][i : i + 1]
        scale = 1.0 / pivot
        below = jnp.where(row > i, cols[i] * scale, 0.0)
        pivot_row = x[i : i + 1]
        x = jnp.where(row == i, pivot_row * (lax.rsqrt(pivot) * (total ** 0.5)), x - below * pivot_row)
        for j in range(i + 1, k):
            cols[j] = cols[j] - below * cols[j][i : i + 1]
    hi, mid, _ = split3(x[:, : 3 * k])
    lhs = jnp.concatenate([hi, hi, mid], axis=1)
    block = min(ch * r, 1024)

    def result(b, carry):
        at = pl.ds(pl.multiple_of(b * block, block), block)
        x_hi = jnp.concatenate([az_ref[:k, at], zhm_ref[: 2 * k, at]], axis=0)
        x_mid = jnp.concatenate([az_ref[k:, at], zhm_ref[2 * k :, at]], axis=0)
        new = lax.dot_general(
            lhs, jnp.concatenate([x_hi, x_mid, x_hi], axis=0), NN, preferred_element_type=F32
        )
        for i in range(block // r):
            out_ref[b * (block // r) + i] = new[:, i * r : (i + 1) * r]
        return carry

    lax.fori_loop(0, ch * r // block, result, 0)


def chip_pairs(pick):
    n_chan, n_rad = lax.axis_size("chan"), lax.axis_size("rad")
    pairs = []
    for c in range(n_chan):
        for r in range(n_rad):
            distance = pick[r % 2]
            if distance:
                pairs.append((c * n_rad + r, (c ^ distance) * n_rad + r))
    return pairs


def sum_everywhere(x):
    n_chan, n_rad = lax.axis_size("chan"), lax.axis_size("rad")
    step = 1
    while step < n_rad:
        x = x + swap(x, "rad", step)
        step *= 2
    even = lax.axis_index("rad") % 2 == 0
    step = 1
    while step < n_chan:
        first = lax.ppermute(x, ("chan", "rad"), chip_pairs((step, 2 * step)))
        other = lax.ppermute(x, ("chan", "rad"), chip_pairs((0, 3 * step)))
        x = first + jnp.where(even, x, other)
        x = x + swap(x, "rad", 1)
        step *= 4
    return x


def own_share(trial_block):
    n_rad = lax.axis_size("rad")
    ch, k, r = trial_block.shape
    me = lax.axis_index("rad")
    rounded = trial_block.astype(BF16).reshape(n_rad, ch // n_rad, k, r)
    got = []
    for d in range(n_rad):
        part = lax.dynamic_index_in_dim(rounded, me ^ d, 0, keepdims=False)
        got.append(swap(part, "rad", d) if d else part)
    lanes = []
    for c in range(n_rad):
        x = got[0]
        for d in range(1, n_rad):
            x = jnp.where(me ^ d == c, got[d], x)
        lanes.append(x)
    return jnp.concatenate(lanes, axis=2)


def body(trial_block, ham_blocks, partners, stored_at, precond_diag):
    n_chan, n_rad = lax.axis_size("chan"), lax.axis_size("rad")
    ch, k, r = trial_block.shape
    ncoup, splines = ham_blocks.shape[1], ham_blocks.shape[3]
    lanes = ch * r
    total = float(n_chan * n_rad * lanes)
    share, nz = ch // n_rad, n_chan // 4

    own = own_share(trial_block)
    column = [own] + [None] * (nz - 1)
    for z in range(nz - 2, 0, -2):
        column[z] = swap(own, "chan", 4 * z)
    column[1] = swap(own, "chan", 4)
    near = plane_swap(own[None], (1, 2))
    local = pl.pallas_call(
        trial_kernel,
        out_shape=[
            pltpu.VMEM((4 * k, lanes), BF16),
            pltpu.VMEM((2 * k, lanes), BF16),
            pltpu.VMEM((1, lanes), F32),
            pltpu.VMEM((k, 3 * k), F32),
        ],
        compiler_params=pltpu.CompilerParams(vmem_limit_bytes=VMEM_LIMIT),
        name="trial_gram",
    )(trial_block, precond_diag)
    column, near, local = lax.optimization_barrier((column, near, local))
    zhm, zl, dc, gram_t = local

    def second(parts, first):
        half = jnp.stack([parts, first])
        return half, plane_swap(half, (2, 1))

    groups = z_groups(nz)
    half0, far0 = second(own[None], near)
    parts1 = jnp.stack([column[z] for z in groups[1]])
    near1 = plane_swap(parts1, (1, 2))
    for z in groups[2]:
        column[z] = swap(column[z - 1], "chan", 4)
    column, near1, half0, far0 = lax.optimization_barrier((column, near1, half0, far0))
    parts2 = jnp.stack([column[z] for z in groups[2]])
    near2 = plane_swap(parts2, (1, 2))
    half1, far1 = second(parts1, near1)
    others = [[swap(x, "rad", c) for x in (half0, far0, half1)] for c in range(1, n_rad)]
    near2, others, partners, stored_at, ham_blocks = lax.optimization_barrier(
        (near2, others, partners.T, stored_at, ham_blocks)
    )
    half2, far2 = second(parts2, near2)
    others = [o + [swap(half2, "rad", c + 1)] for c, o in enumerate(others)]
    smem = pl.BlockSpec(memory_space=pltpu.SMEM)
    any_ = pl.BlockSpec(memory_space=pl.ANY)
    whole = pl.BlockSpec(memory_space=pltpu.VMEM)
    ham, rows = pl.pallas_call(
        functools.partial(load_kernel, n_chan, n_rad),
        in_specs=[smem, smem, any_],
        out_specs=[whole, smem],
        out_shape=[
            pltpu.VMEM(ham_blocks.shape, BF16),
            jax.ShapeDtypeStruct((ch * ncoup,), jnp.int32),
        ],
        scratch_shapes=[pltpu.SemaphoreType.DMA],
        compiler_params=pltpu.CompilerParams(vmem_limit_bytes=VMEM_LIMIT),
        name="load",
    )(in_hbm(partners), in_hbm(stored_at), in_hbm(ham_blocks))
    far1, far2, others, ham, rows = lax.optimization_barrier((far1, far2, others, ham, rows))
    tables = [[half0, far0, half1, half2, far1, far2]]
    for c, o in enumerate(others):
        tables.append(o + [swap(x, "rad", c + 1) for x in (far1, far2)])
    table = jnp.stack(
        [
            jnp.concatenate(
                [jnp.concatenate([t[0], t[2], t[3]], axis=1), jnp.concatenate([t[1], t[4], t[5]], axis=1)]
            )
            for t in tables
        ]
    ).reshape(n_chan * ch, k, splines)

    az, sums = pl.pallas_call(
        apply_kernel,
        in_specs=[smem] + [whole] * 6,
        out_specs=[whole, whole],
        out_shape=[
            pltpu.VMEM((2 * k, lanes), BF16),
            jax.ShapeDtypeStruct((k, 8 * k), F32),
        ],
        scratch_shapes=[pltpu.VMEM((k, lanes), F32)],
        compiler_params=pltpu.CompilerParams(vmem_limit_bytes=VMEM_LIMIT),
        name="apply",
    )(rows, in_vmem(ham), in_vmem(table), in_vmem(zhm), in_vmem(zl), in_vmem(dc), gram_t)

    sums = sum_everywhere(sums)
    new_block, ritz = pl.pallas_call(
        functools.partial(finish_kernel, total),
        out_shape=[
            jax.ShapeDtypeStruct((ch, k, r), F32),
            jax.ShapeDtypeStruct((1, k), F32),
        ],
        compiler_params=pltpu.CompilerParams(vmem_limit_bytes=VMEM_LIMIT),
        name="finish",
    )(sums, in_vmem(az), in_vmem(zhm))
    return (new_block, ritz.reshape(k))


def solution(mesh):
    return jax.shard_map(
        body,
        mesh=mesh,
        in_specs=(
            P("chan", None, "rad"),
            P("chan", None, "rad", None),
            P("chan", None),
            P(),
            P("chan", "rad"),
        ),
        out_specs=(P("chan", None, "rad"), P()),
        check_vma=False,
    )
```

time: 79 us -> 71.4 us (0.904)
  blocking collectives: 14.1 us -> 0 us
  starting transfers between devices: 15.2 us -> 24 us
  local copies, waits for them, and re-layouts: 5.51 us -> 0.78 us
  waiting for transfers between devices: 22.5 us -> 25.8 us
  Pallas kernels: 19.1 us -> 17.3 us
  other arithmetic: 1.36 us -> 2.35 us
    all_to_all x1 -> x0, blocking collectives: 14.1 us -> none  [body(): lax.all_to_all(jnp.broadcast_to(sums, (n_chan,) + sums.shape), 'chan', sp...]
    ppermute x11 -> x13, starting transfers between devices: 7.44 us -> 13.2 us  [swap(): return lax.ppermute(x, axis, [(i, i ^ distance) for i in range(n)])]
    ppermute x0 -> x4, waiting for transfers between devices: none -> 5.62 us  [the longest x2 5.62 us: sum_everywhere(): first = lax.ppermute(x, ('chan', 'rad'), chip_pairs((step, 2 * step)))]
    unnamed x14 -> x4, local copies, waits for them, and re-layouts: 5.48 us -> 0.76 us
    ppermute x6, waiting for transfers between devices: 12.2 us -> 7.71 us  [plane_swap(): return lax.ppermute(x, ('chan', 'rad'), pairs)]
    ppermute x0 -> x4, starting transfers between devices: none -> 3.11 us  [the longest x2 1.82 us: sum_everywhere(): first = lax.ppermute(x, ('chan', 'rad'), chip_pairs((step, 2 * step)))]
    pallas_call x1, Pallas kernels: 5.97 us -> 3.05 us  [body(): pl.pallas_call(functools.partial(finish_kernel, total), out_shape=[jax.Sh...]
    ppermute x11 -> x13, waiting for transfers between devices: 10.2 us -> 12.5 us  [swap(): return lax.ppermute(x, axis, [(i, i ^ distance) for i in range(n)])]
  transfers between devices with their start and end apart: 17 -> 23, of which waited for: 10 -> 12; matrix products, arithmetic and copies ran while one was open for 0% -> 0% of each run, Pallas kernels for 3% -> 11%
where the time goes in v4:
time: 71.4 us; the launch traced here: 71.1 us
  waiting for transfers between devices  25.8 us (36%)
  starting transfers between devices  24 us (34%)
  Pallas kernels  17.3 us (24%)
  other arithmetic  2.35 us (3%)
  between operations  0.81 us (1%)
  local copies, waits for them, and re-layouts  0.78 us (1%)
    ppermute x13, starting transfers between devices, swap(): return lax.ppermute(x, axis, [(i, i ^ distance) for i in range(n)])  13.2 us
    ppermute x13, waiting for transfers between devices, swap(): return lax.ppermute(x, axis, [(i, i ^ distance) for i in range(n)])  12.5 us
    ppermute x6, starting transfers between devices, plane_swap(): return lax.ppermute(x, ('chan', 'rad'), pairs)  7.76 us
    ppermute x6, waiting for transfers between devices, plane_swap(): return lax.ppermute(x, ('chan', 'rad'), pairs)  7.71 us
    pallas_call x1, Pallas kernels, body(): pl.pallas_call(functools.partial(load_kernel, n_chan, n_rad), in_specs=[s...  7.29 us
    pallas_call x1, Pallas kernels, body(): pl.pallas_call(apply_kernel, in_specs=[smem] + [whole] * 6, out_specs=[wh...  6.34 us
    ppermute x2, waiting for transfers between devices, sum_everywhere(): first = lax.ppermute(x, ('chan', 'rad'), chip_pairs((step, 2 * step)))  5.62 us
    pallas_call x1, Pallas kernels, body(): pl.pallas_call(functools.partial(finish_kernel, total), out_shape=[jax.Sh...  3.05 us
  transfers between devices with their start and end apart: 23, of which 12 were waited for; matrix products, arithmetic and copies ran while one was open for 0% of the time, Pallas kernels for 11%

profile of v4, /device:TPU:0, one launch (start us, length us, event | category | flops | bytes accessed | tf_op | source)
XLA Modules:
  0.0 71.1 jit_solution(4328594470811696950)
XLA Ops:
  0.6 1.1 %convert_element_type.3 = bf16[64,16,64]{2,1,0:T(8,128)(2,1)S(1)} convert(f32[64,16,64]{2,1,0:T(8,128)} %t_ref.1) | non-fusion elementwise | flops 65536 | bytes 393216 | tf_op jit(solution)/shard_map/convert_element_type | solution.py:241
  1.8 0.5 collective-permute-start
  2.3 1.0 %collective-permute-done = bf16[32,16,64]{2,1,0:T(8,128)(2,1)S(1)} collective-permute-done((bf16[32,16,64]{2,1,0:T(8,128)(2,1)S(1)}, bf16[32,16,64]{2,1,0:T(8,128)(2,1)S(1)}, u32[]{:S(2)}, u32[]{:S(2)}) %collective-permute-start) | collective-permute-done | bytes 65568 | tf_op jit(solution)/shard_map/ppermute | solution.py:21
  3.5 2.9 %collective-permute-start.3 = (bf16[1,32,16,128]{3,2,1,0:T(8,128)(2,1)S(1)}, bf16[1,32,16,128]{3,2,1,0:T(8,128)(2,1)S(1)}, u32[]{:S(2)}, u32[]{:S(2)}) collective-permute-start(bf16[1,32,16,128]{3,2,1,0:T(8,128)(2,1)S(1)} %bitcast.34), channel_id=1, source_target_pairs={{0,2},{1,5},{2,0},{3,7},{4,6},{5,1},{6,4},{7,3},{8,10},{9,13},{10,... | collective-permute-start | bytes 393224 | tf_op jit(solution)/shard_map/ppermute | solution.py:30
  6.4 2.6 %collective-permute-start.2 = (bf16[32,16,128]{2,1,0:T(8,128)(2,1)S(1)}, bf16[32,16,128]{2,1,0:T(8,128)(2,1)S(1)}, u32[]{:S(2)}, u32[]{:S(2)}) collective-permute-start(bf16[32,16,128]{2,1,0:T(8,128)(2,1)S(1)} %pad_maximum_fusion.5), channel_id=1, source_target_pairs={{0,16},{2,18},{4,20},{6,22},{8,24},{10,26},{12,28},{14,30},{16,0},... | collective-permute-start | bytes 393224 | tf_op jit(solution)/shard_map/ppermute | solution.py:21
  9.0 1.6 %collective-permute-start.1 = (bf16[32,16,128]{2,1,0:T(8,128)(2,1)S(1)}, bf16[32,16,128]{2,1,0:T(8,128)(2,1)S(1)}, u32[]{:S(2)}, u32[]{:S(2)}) collective-permute-start(bf16[32,16,128]{2,1,0:T(8,128)(2,1)S(1)} %pad_maximum_fusion.5), channel_id=1, source_target_pairs={{0,8},{2,10},{4,12},{6,14},{8,0},{10,2},{12,4},{14,6},{16,24},{18,... | collective-permute-start | bytes 393224 | tf_op jit(solution)/shard_map/ppermute | solution.py:21
  10.5 0.8 %copy-done.1 = f32[64,64]{1,0:T(8,128)S(1)} copy-done((f32[64,64]{1,0:T(8,128)S(1)}, f32[64,64]{1,0:T(8,128)}, u32[]{:S(2)}) %copy-start.1) | copy-done | bytes 16408
  11.3 0.6 trial_gram.1
  11.9 3.6 %collective-permute-done.2 = bf16[32,16,128]{2,1,0:T(8,128)(2,1)S(1)} collective-permute-done((bf16[32,16,128]{2,1,0:T(8,128)(2,1)S(1)}, bf16[32,16,128]{2,1,0:T(8,128)(2,1)S(1)}, u32[]{:S(2)}, u32[]{:S(2)}) %collective-permute-start.2) | collective-permute-done | bytes 131104 | tf_op jit(solution)/shard_map/ppermute | solution.py:21
  15.7 0.5 collective-permute-start.6
  16.3 1.6 %collective-permute-start.5 = (bf16[2,32,16,128]{3,2,1,0:T(8,128)(2,1)S(1)}, bf16[2,32,16,128]{3,2,1,0:T(8,128)(2,1)S(1)}, u32[]{:S(2)}, u32[]{:S(2)}) collective-permute-start(bf16[2,32,16,128]{3,2,1,0:T(8,128)(2,1)S(1)} %get-tuple-element.77), channel_id=1, source_target_pairs={{0,2},{1,5},{2,0},{3,7},{4,6},{5,1},{6,4},{7,3},{8,10},{9,13},{10,... | collective-permute-start | bytes 786440 | tf_op jit(solution)/shard_map/ppermute | solution.py:30
  17.9 1.4 %collective-permute-start.4 = (bf16[32,16,128]{2,1,0:T(8,128)(2,1)S(1)}, bf16[32,16,128]{2,1,0:T(8,128)(2,1)S(1)}, u32[]{:S(2)}, u32[]{:S(2)}) collective-permute-start(bf16[32,16,128]{2,1,0:T(8,128)(2,1)S(1)} %collective-permute-done.2), channel_id=1, source_target_pairs={{0,8},{2,10},{4,12},{6,14},{8,0},{10,2},{12,4},{14,6},{16,24},{18,... | collective-permute-start | bytes 393224 | tf_op jit(solution)/shard_map/ppermute | solution.py:21
  19.3 3.6 %collective-permute-done.4 = bf16[32,16,128]{2,1,0:T(8,128)(2,1)S(1)} collective-permute-done((bf16[32,16,128]{2,1,0:T(8,128)(2,1)S(1)}, bf16[32,16,128]{2,1,0:T(8,128)(2,1)S(1)}, u32[]{:S(2)}, u32[]{:S(2)}) %collective-permute-start.4) | collective-permute-done | bytes 131104 | tf_op jit(solution)/shard_map/ppermute | solution.py:21
  22.8 1.9 %collective-permute-done.6 = bf16[2,1,32,16,128]{4,3,2,1,0:T(8,128)(2,1)S(1)} collective-permute-done((bf16[2,1,32,16,128]{4,3,2,1,0:T(8,128)(2,1)S(1)}, bf16[2,1,32,16,128]{4,3,2,1,0:T(8,128)(2,1)S(1)}, u32[]{:S(2)}, u32[]{:S(2)}) %collective-permute-start.6) | collective-permute-done | bytes 262176 | tf_op jit(solution)/shard_map/ppermute | solution.py:30
  24.9 0.5 collective-permute-start.9
  25.7 0.5 collective-permute-start.8
  26.3 5.8 %collective-permute-done.8 = bf16[1,32,16,128]{3,2,1,0:T(8,128)(2,1)S(1)} collective-permute-done((bf16[1,32,16,128]{3,2,1,0:T(8,128)(2,1)S(1)}, bf16[1,32,16,128]{3,2,1,0:T(8,128)(2,1)S(1)}, u32[]{:S(2)}, u32[]{:S(2)}) %collective-permute-start.8) | collective-permute-done | bytes 131104 | tf_op jit(solution)/shard_map/ppermute | solution.py:30
  32.2 1.9 %collective-permute-start.12 = (bf16[2,1,32,16,128]{4,3,2,1,0:T(8,128)(2,1)S(1)}, bf16[2,1,32,16,128]{4,3,2,1,0:T(8,128)(2,1)S(1)}, u32[]{:S(2)}, u32[]{:S(2)}) collective-permute-start(bf16[2,1,32,16,128]{4,3,2,1,0:T(8,128)(2,1)S(1)} %pad_maximum_fusion.4), channel_id=1, source_target_pairs={{0,4},{1,3},{2,6},{3,1},{4,0},{5,7},{6,2},{7,5},{8,12},{9,11},{10,... | collective-permute-start | bytes 786440 | tf_op jit(solution)/shard_map/ppermute | solution.py:30
  34.1 7.3 %load.1 = (bf16[64,8,64,128]{3,2,1,0:T(8,128)(2,1)S(1)}, s32[512]{0:T(512)S(1)}) custom-call(s32[8,64]{1,0:T(8,128)} %bitcast.39, s32[1024]{0:T(1024)} %stored_ref, bf16[64,8,64,128]{3,2,1,0:T(8,128)(2,1)} %ham_hbm), custom_call_target="tpu_custom_call" | custom-call | tf_op jit(solution)/shard_map/load/pallas_call | solution.py:306
  42.3 1.5 %collective-permute-done.15 = bf16[2,1,32,16,128]{4,3,2,1,0:T(8,128)(2,1)S(1)} collective-permute-done((bf16[2,1,32,16,128]{4,3,2,1,0:T(8,128)(2,1)S(1)}, bf16[2,1,32,16,128]{4,3,2,1,0:T(8,128)(2,1)S(1)}, u32[]{:S(2)}, u32[]{:S(2)}) %collective-permute-start.15) | collective-permute-done | bytes 262176 | tf_op jit(solution)/shard_map/ppermute | solution.py:21
  44.5 6.3 %apply.1 = (bf16[32,4096]{1,0:T(8,128)(2,1)S(1)}, f32[16,128]{1,0:T(8,128)S(1)}) custom-call(s32[512]{0:T(512)S(1)} %get-tuple-element.58.rows_ref, bf16[64,8,64,128]{3,2,1,0:T(8,128)(2,1)S(1)} %get-tuple-element.59.ham_ref, bf16[1024,16,128]{2,1,0:T(8,128)(2,1)S(1)} %bitcast.24, bf16[64,4096]{1,0:T(8,128)(2,1)S(1)} %get-tuple-element.66.zhm_ref, ...), custom_call_target="tpu_custom_call" | custom-call | tf_op jit(solution)/shard_map/apply/pallas_call | solution.py:331
  51.0 1.0 %collective-permute-done.16 = f32[16,128]{1,0:T(8,128)S(1)} collective-permute-done((f32[16,128]{1,0:T(8,128)S(1)}, f32[16,128]{1,0:T(8,128)S(1)}, u32[]{:S(2)}, u32[]{:S(2)}) %collective-permute-start.16) | collective-permute-done | bytes 8224 | tf_op jit(solution)/shard_map/ppermute | solution.py:21
  52.0 0.7 collective-permute-start.18
  53.0 3.4 %collective-permute-done.17 = f32[16,128]{1,0:T(8,128)S(1)} collective-permute-done((f32[16,128]{1,0:T(8,128)S(1)}, f32[16,128]{1,0:T(8,128)S(1)}, u32[]{:S(2)}, u32[]{:S(2)}) %collective-permute-start.17) | collective-permute-done | bytes 8224 | tf_op jit(solution)/shard_map/ppermute | solution.py:229
  56.4 1.4 %collective-permute-start.19 = (f32[16,128]{1,0:T(8,128)S(1)}, f32[16,128]{1,0:T(8,128)S(1)}, u32[]{:S(2)}, u32[]{:S(2)}) collective-permute-start(f32[16,128]{1,0:T(8,128)S(1)} %select_add_fusion.1), channel_id=1, source_target_pairs={{0,1},{1,0},{2,3},{3,2},{4,5},{5,4},{6,7},{7,6},{8,9},{9,8},{10,11... | collective-permute-start | bytes 24584 | tf_op jit(solution)/shard_map/ppermute | solution.py:21
  57.8 0.8 %collective-permute-done.19 = f32[16,128]{1,0:T(8,128)S(1)} collective-permute-done((f32[16,128]{1,0:T(8,128)S(1)}, f32[16,128]{1,0:T(8,128)S(1)}, u32[]{:S(2)}, u32[]{:S(2)}) %collective-permute-start.19) | collective-permute-done | bytes 8224 | tf_op jit(solution)/shard_map/ppermute | solution.py:21
  58.6 0.6 collective-permute-start.21
  59.3 1.4 %collective-permute-start.20 = (f32[16,128]{1,0:T(8,128)S(1)}, f32[16,128]{1,0:T(8,128)S(1)}, u32[]{:S(2)}, u32[]{:S(2)}) collective-permute-start(f32[16,128]{1,0:T(8,128)S(1)} %add.31), channel_id=1, source_target_pairs={{0,8},{1,17},{2,10},{3,19},{4,12},{5,21},{6,14},{7,23},{8,0},{9,25... | collective-permute-start | bytes 24584 | tf_op jit(solution)/shard_map/ppermute | solution.py:229
  60.7 2.3 %collective-permute-done.20 = f32[16,128]{1,0:T(8,128)S(1)} collective-permute-done((f32[16,128]{1,0:T(8,128)S(1)}, f32[16,128]{1,0:T(8,128)S(1)}, u32[]{:S(2)}, u32[]{:S(2)}) %collective-permute-start.20) | collective-permute-done | bytes 8224 | tf_op jit(solution)/shard_map/ppermute | solution.py:229
  63.0 4.2 %collective-permute-start.22 = (f32[16,128]{1,0:T(8,128)S(1)}, f32[16,128]{1,0:T(8,128)S(1)}, u32[]{:S(2)}, u32[]{:S(2)}) collective-permute-start(f32[16,128]{1,0:T(8,128)S(1)} %select_add_fusion), channel_id=1, source_target_pairs={{0,1},{1,0},{2,3},{3,2},{4,5},{5,4},{6,7},{7,6},{8,9},{9,8},{10,11... | collective-permute-start | bytes 24584 | tf_op jit(solution)/shard_map/ppermute | solution.py:21
  67.2 0.8 %collective-permute-done.22 = f32[16,128]{1,0:T(8,128)S(1)} collective-permute-done((f32[16,128]{1,0:T(8,128)S(1)}, f32[16,128]{1,0:T(8,128)S(1)}, u32[]{:S(2)}, u32[]{:S(2)}) %collective-permute-start.22) | collective-permute-done | bytes 8224 | tf_op jit(solution)/shard_map/ppermute | solution.py:21
  68.1 3.0 %finish.1 = (f32[64,16,64]{2,1,0:T(8,128)}, f32[1,16]{1,0:T(1,128)}) custom-call(f32[16,128]{1,0:T(8,128)S(1)} %add.33.sums_ref, bf16[32,4096]{1,0:T(8,128)(2,1)S(1)} %get-tuple-element.71.az_ref, bf16[64,4096]{1,0:T(8,128)(2,1)S(1)} %get-tuple-element.66.zhm_ref), custom_call_target="tpu_custom_call" | custom-call | tf_op jit(solution)/shard_map/finish/pallas_call | solution.py:345
  (38 shorter events, 3.1 us)
Async XLA Ops:
  0.6 9.9 %copy-start = (f32[64,16,64]{2,1,0:T(8,128)S(1)}, f32[64,16,64]{2,1,0:T(8,128)}, u32[]{:S(2)}) copy-start(f32[64,16,64]{2,1,0:T(8,128)} %t_ref.1) | copy-start | bytes 786436
  1.8 1.5 %collective-permute-start = (bf16[32,16,64]{2,1,0:T(8,128)(2,1)S(1)}, bf16[32,16,64]{2,1,0:T(8,128)(2,1)S(1)}, u32[]{:S(2)}, u32[]{:S(2)}) collective-permute-start(bf16[32,16,64]{2,1,0:T(8,128)(2,1)S(1)} %dynamic-slice_bitcast_fusion), channel_id=1, source_target_pairs={{0,1},{1,0},{2,3},{3,2},{4,5},{5,4},{6,7},{7,6},{8,9},{9,8},{10,11... | collective-permute-start | bytes 196616 | tf_op jit(solution)/shard_map/ppermute | solution.py:21
  3.5 8.5 %collective-permute-start.3 = (bf16[1,32,16,128]{3,2,1,0:T(8,128)(2,1)S(1)}, bf16[1,32,16,128]{3,2,1,0:T(8,128)(2,1)S(1)}, u32[]{:S(2)}, u32[]{:S(2)}) collective-permute-start(bf16[1,32,16,128]{3,2,1,0:T(8,128)(2,1)S(1)} %bitcast.34), channel_id=1, source_target_pairs={{0,2},{1,5},{2,0},{3,7},{4,6},{5,1},{6,4},{7,3},{8,10},{9,13},{10,... | collective-permute-start | bytes 393224 | tf_op jit(solution)/shard_map/ppermute | solution.py:30
  6.4 9.1 %collective-permute-start.2 = (bf16[32,16,128]{2,1,0:T(8,128)(2,1)S(1)}, bf16[32,16,128]{2,1,0:T(8,128)(2,1)S(1)}, u32[]{:S(2)}, u32[]{:S(2)}) collective-permute-start(bf16[32,16,128]{2,1,0:T(8,128)(2,1)S(1)} %pad_maximum_fusion.5), channel_id=1, source_target_pairs={{0,16},{2,18},{4,20},{6,22},{8,24},{10,26},{12,28},{14,30},{16,0},... | collective-permute-start | bytes 393224 | tf_op jit(solution)/shard_map/ppermute | solution.py:21
  9.0 6.7 %collective-permute-start.1 = (bf16[32,16,128]{2,1,0:T(8,128)(2,1)S(1)}, bf16[32,16,128]{2,1,0:T(8,128)(2,1)S(1)}, u32[]{:S(2)}, u32[]{:S(2)}) collective-permute-start(bf16[32,16,128]{2,1,0:T(8,128)(2,1)S(1)} %pad_maximum_fusion.5), channel_id=1, source_target_pairs={{0,8},{2,10},{4,12},{6,14},{8,0},{10,2},{12,4},{14,6},{16,24},{18,... | collective-permute-start | bytes 393224 | tf_op jit(solution)/shard_map/ppermute | solution.py:21
  10.5 0.8 %copy-start.1 = (f32[64,64]{1,0:T(8,128)S(1)}, f32[64,64]{1,0:T(8,128)}, u32[]{:S(2)}) copy-start(f32[64,64]{1,0:T(8,128)} %d_ref.1) | copy-start | bytes 49156
  15.7 9.0 %collective-permute-start.6 = (bf16[2,1,32,16,128]{4,3,2,1,0:T(8,128)(2,1)S(1)}, bf16[2,1,32,16,128]{4,3,2,1,0:T(8,128)(2,1)S(1)}, u32[]{:S(2)}, u32[]{:S(2)}) collective-permute-start(bf16[2,1,32,16,128]{4,3,2,1,0:T(8,128)(2,1)S(1)} %pad_maximum_fusion.3), channel_id=1, source_target_pairs={{0,4},{1,3},{2,6},{3,1},{4,0},{5,7},{6,2},{7,5},{8,12},{9,11},{10,... | collective-permute-start | bytes 786440 | tf_op jit(solution)/shard_map/ppermute | solution.py:30
  16.3 8.5 %collective-permute-start.5 = (bf16[2,32,16,128]{3,2,1,0:T(8,128)(2,1)S(1)}, bf16[2,32,16,128]{3,2,1,0:T(8,128)(2,1)S(1)}, u32[]{:S(2)}, u32[]{:S(2)}) collective-permute-start(bf16[2,32,16,128]{3,2,1,0:T(8,128)(2,1)S(1)} %get-tuple-element.77), channel_id=1, source_target_pairs={{0,2},{1,5},{2,0},{3,7},{4,6},{5,1},{6,4},{7,3},{8,10},{9,13},{10,... | collective-permute-start | bytes 786440 | tf_op jit(solution)/shard_map/ppermute | solution.py:30
  17.9 5.0 %collective-permute-start.4 = (bf16[32,16,128]{2,1,0:T(8,128)(2,1)S(1)}, bf16[32,16,128]{2,1,0:T(8,128)(2,1)S(1)}, u32[]{:S(2)}, u32[]{:S(2)}) collective-permute-start(bf16[32,16,128]{2,1,0:T(8,128)(2,1)S(1)} %collective-permute-done.2), channel_id=1, source_target_pairs={{0,8},{2,10},{4,12},{6,14},{8,0},{10,2},{12,4},{14,6},{16,24},{18,... | collective-permute-start | bytes 393224 | tf_op jit(solution)/shard_map/ppermute | solution.py:21
  24.8 7.3 %collective-permute-start.11 = (bf16[2,2,32,16,128]{4,3,2,1,0:T(8,128)(2,1)S(1)}, bf16[2,2,32,16,128]{4,3,2,1,0:T(8,128)(2,1)S(1)}, u32[]{:S(2)}, u32[]{:S(2)}) collective-permute-start(bf16[2,2,32,16,128]{4,3,2,1,0:T(8,128)(2,1)S(1)} %pad_maximum_fusion.1), channel_id=1, source_target_pairs={{0,1},{1,0},{2,3},{3,2},{4,5},{5,4},{6,7},{7,6},{8,9},{9,8},{10,11... | collective-permute-start | bytes 1572872 | tf_op jit(solution)/shard_map/ppermute | solution.py:21
  24.9 7.2 %collective-permute-start.9 = (bf16[2,1,32,16,128]{4,3,2,1,0:T(8,128)(2,1)S(1)}, bf16[2,1,32,16,128]{4,3,2,1,0:T(8,128)(2,1)S(1)}, u32[]{:S(2)}, u32[]{:S(2)}) collective-permute-start(bf16[2,1,32,16,128]{4,3,2,1,0:T(8,128)(2,1)S(1)} %pad_maximum_fusion.3), channel_id=1, source_target_pairs={{0,1},{1,0},{2,3},{3,2},{4,5},{5,4},{6,7},{7,6},{8,9},{9,8},{10,11... | collective-permute-start | bytes 786440 | tf_op jit(solution)/shard_map/ppermute | solution.py:21
  25.4 6.7 %collective-permute-start.10 = (bf16[2,1,32,16,128]{4,3,2,1,0:T(8,128)(2,1)S(1)}, bf16[2,1,32,16,128]{4,3,2,1,0:T(8,128)(2,1)S(1)}, u32[]{:S(2)}, u32[]{:S(2)}) collective-permute-start(bf16[2,1,32,16,128]{4,3,2,1,0:T(8,128)(2,1)S(1)} %collective-permute-done.6), channel_id=1, source_target_pairs={{0,1},{1,0},{2,3},{3,2},{4,5},{5,4},{6,7},{7,6},{8,9},{9,8},{10,11... | collective-permute-start | bytes 786440 | tf_op jit(solution)/shard_map/ppermute | solution.py:21
  25.4 16.0 %collective-permute-start.7 = (bf16[2,2,32,16,128]{4,3,2,1,0:T(8,128)(2,1)S(1)}, bf16[2,2,32,16,128]{4,3,2,1,0:T(8,128)(2,1)S(1)}, u32[]{:S(2)}, u32[]{:S(2)}) collective-permute-start(bf16[2,2,32,16,128]{4,3,2,1,0:T(8,128)(2,1)S(1)} %pad_maximum_fusion.1), channel_id=1, source_target_pairs={{0,4},{1,3},{2,6},{3,1},{4,0},{5,7},{6,2},{7,5},{8,12},{9,11},{10,... | collective-permute-start | bytes 1572872 | tf_op jit(solution)/shard_map/ppermute | solution.py:30
  25.7 6.3 %collective-permute-start.8 = (bf16[1,32,16,128]{3,2,1,0:T(8,128)(2,1)S(1)}, bf16[1,32,16,128]{3,2,1,0:T(8,128)(2,1)S(1)}, u32[]{:S(2)}, u32[]{:S(2)}) collective-permute-start(bf16[1,32,16,128]{3,2,1,0:T(8,128)(2,1)S(1)} %bitcast.29), channel_id=1, source_target_pairs={{0,2},{1,5},{2,0},{3,7},{4,6},{5,1},{6,4},{7,3},{8,10},{9,13},{10,... | collective-permute-start | bytes 393224 | tf_op jit(solution)/shard_map/ppermute | solution.py:30
  32.1 9.3 %collective-permute-start.13 = (bf16[2,1,32,16,128]{4,3,2,1,0:T(8,128)(2,1)S(1)}, bf16[2,1,32,16,128]{4,3,2,1,0:T(8,128)(2,1)S(1)}, u32[]{:S(2)}, u32[]{:S(2)}) collective-permute-start(bf16[2,1,32,16,128]{4,3,2,1,0:T(8,128)(2,1)S(1)} %pad_maximum_fusion.4), channel_id=1, source_target_pairs={{0,1},{1,0},{2,3},{3,2},{4,5},{5,4},{6,7},{7,6},{8,9},{9,8},{10,11... | collective-permute-start | bytes 786440 | tf_op jit(solution)/shard_map/ppermute | solution.py:21
  32.2 9.2 %collective-permute-start.12 = (bf16[2,1,32,16,128]{4,3,2,1,0:T(8,128)(2,1)S(1)}, bf16[2,1,32,16,128]{4,3,2,1,0:T(8,128)(2,1)S(1)}, u32[]{:S(2)}, u32[]{:S(2)}) collective-permute-start(bf16[2,1,32,16,128]{4,3,2,1,0:T(8,128)(2,1)S(1)} %pad_maximum_fusion.4), channel_id=1, source_target_pairs={{0,4},{1,3},{2,6},{3,1},{4,0},{5,7},{6,2},{7,5},{8,12},{9,11},{10,... | collective-permute-start | bytes 786440 | tf_op jit(solution)/shard_map/ppermute | solution.py:30
  41.4 2.4 %collective-permute-start.14 = (bf16[2,2,32,16,128]{4,3,2,1,0:T(8,128)(2,1)S(1)}, bf16[2,2,32,16,128]{4,3,2,1,0:T(8,128)(2,1)S(1)}, u32[]{:S(2)}, u32[]{:S(2)}) collective-permute-start(bf16[2,2,32,16,128]{4,3,2,1,0:T(8,128)(2,1)S(1)} %collective-permute-done.7), channel_id=1, source_target_pairs={{0,1},{1,0},{2,3},{3,2},{4,5},{5,4},{6,7},{7,6},{8,9},{9,8},{10,11... | collective-permute-start | bytes 1572872 | tf_op jit(solution)/shard_map/ppermute | solution.py:21
  41.5 2.3 %collective-permute-start.15 = (bf16[2,1,32,16,128]{4,3,2,1,0:T(8,128)(2,1)S(1)}, bf16[2,1,32,16,128]{4,3,2,1,0:T(8,128)(2,1)S(1)}, u32[]{:S(2)}, u32[]{:S(2)}) collective-permute-start(bf16[2,1,32,16,128]{4,3,2,1,0:T(8,128)(2,1)S(1)} %collective-permute-done.12), channel_id=1, source_target_pairs={{0,1},{1,0},{2,3},{3,2},{4,5},{5,4},{6,7},{7,6},{8,9},{9,8},{10,11... | collective-permute-start | bytes 786440 | tf_op jit(solution)/shard_map/ppermute | solution.py:21
  50.8 1.2 %collective-permute-start.16 = (f32[16,128]{1,0:T(8,128)S(1)}, f32[16,128]{1,0:T(8,128)S(1)}, u32[]{:S(2)}, u32[]{:S(2)}) collective-permute-start(f32[16,128]{1,0:T(8,128)S(1)} %get-tuple-element.70), channel_id=1, source_target_pairs={{0,1},{1,0},{2,3},{3,2},{4,5},{5,4},{6,7},{7,6},{8,9},{9,8},{10,11... | collective-permute-start | bytes 24584 | tf_op jit(solution)/shard_map/ppermute | solution.py:21
  52.0 1.0 %collective-permute-start.18 = (f32[16,128]{1,0:T(8,128)S(1)}, f32[16,128]{1,0:T(8,128)S(1)}, u32[]{:S(2)}, u32[]{:S(2)}) collective-permute-start(f32[16,128]{1,0:T(8,128)S(1)} %add.28), channel_id=1, source_target_pairs={{1,7},{3,5},{5,3},{7,1},{9,15},{11,13},{13,11},{15,9},{17,23},{19,... | collective-permute-start | bytes 24584 | tf_op jit(solution)/shard_map/ppermute | solution.py:230
  52.6 3.7 %collective-permute-start.17 = (f32[16,128]{1,0:T(8,128)S(1)}, f32[16,128]{1,0:T(8,128)S(1)}, u32[]{:S(2)}, u32[]{:S(2)}) collective-permute-start(f32[16,128]{1,0:T(8,128)S(1)} %add.28), channel_id=1, source_target_pairs={{0,2},{1,5},{2,0},{3,7},{4,6},{5,1},{6,4},{7,3},{8,10},{9,13},{10,... | collective-permute-start | bytes 24584 | tf_op jit(solution)/shard_map/ppermute | solution.py:229
  56.4 2.3 %collective-permute-start.19 = (f32[16,128]{1,0:T(8,128)S(1)}, f32[16,128]{1,0:T(8,128)S(1)}, u32[]{:S(2)}, u32[]{:S(2)}) collective-permute-start(f32[16,128]{1,0:T(8,128)S(1)} %select_add_fusion.1), channel_id=1, source_target_pairs={{0,1},{1,0},{2,3},{3,2},{4,5},{5,4},{6,7},{7,6},{8,9},{9,8},{10,11... | collective-permute-start | bytes 24584 | tf_op jit(solution)/shard_map/ppermute | solution.py:21
  58.6 2.1 %collective-permute-start.21 = (f32[16,128]{1,0:T(8,128)S(1)}, f32[16,128]{1,0:T(8,128)S(1)}, u32[]{:S(2)}, u32[]{:S(2)}) collective-permute-start(f32[16,128]{1,0:T(8,128)S(1)} %add.31), channel_id=1, source_target_pairs={{1,25},{3,27},{5,29},{7,31},{9,17},{11,19},{13,21},{15,23},{17,9},... | collective-permute-start | bytes 24584 | tf_op jit(solution)/shard_map/ppermute | solution.py:230
  59.3 3.7 %collective-permute-start.20 = (f32[16,128]{1,0:T(8,128)S(1)}, f32[16,128]{1,0:T(8,128)S(1)}, u32[]{:S(2)}, u32[]{:S(2)}) collective-permute-start(f32[16,128]{1,0:T(8,128)S(1)} %add.31), channel_id=1, source_target_pairs={{0,8},{1,17},{2,10},{3,19},{4,12},{5,21},{6,14},{7,23},{8,0},{9,25... | collective-permute-start | bytes 24584 | tf_op jit(solution)/shard_map/ppermute | solution.py:229
  63.0 5.0 %collective-permute-start.22 = (f32[16,128]{1,0:T(8,128)S(1)}, f32[16,128]{1,0:T(8,128)S(1)}, u32[]{:S(2)}, u32[]{:S(2)}) collective-permute-start(f32[16,128]{1,0:T(8,128)S(1)} %select_add_fusion), channel_id=1, source_target_pairs={{0,1},{1,0},{2,3},{3,2},{4,5},{5,4},{6,7},{7,6},{8,9},{9,8},{10,11... | collective-permute-start | bytes 24584 | tf_op jit(solution)/shard_map/ppermute | solution.py:21

commit v5 on v4

--- a/solution.py
+++ b/solution.py
@@ -13,7 +13,7 @@
 NT = (((1,), (1,)), ((), ()))
 TN = (((0,), (0,)), ((), ()))
 NN = (((1,), (0,)), ((), ()))
-VMEM_LIMIT = 12 * 1024 * 1024
+VMEM_LIMIT = 4 * 1024 * 1024
 
 
 def swap(x, axis, distance):
@@ -31,7 +31,7 @@
 
 
 def z_groups(nz):
-    return [[0], [1] + list(range(2, nz, 2)), list(range(3, nz, 2))]
+    return [[0], [1], list(range(2, nz, 2)), list(range(3, nz, 2))]
 
 
 def z_place(z, nz):
@@ -64,7 +64,12 @@
     return sum(g[:, i : i + cols] for i in range(0, g.shape[1], cols))
 
 
-def trial_kernel(t_ref, d_ref, zhm_ref, zl_ref, dc_ref, gram_ref):
+def prepare_kernel(
+    n_chan, n_rad, t_ref, d_ref, partners_ref, stored_ref, ham_hbm,
+    ham_ref, rows_ref, zhm_ref, zl_ref, dc_ref, gram_ref, sem,
+):
+    copy = pltpu.make_async_copy(ham_hbm, ham_ref, sem)
+    copy.start()
     ch, k, r = t_ref.shape
     group = 128 // r
     for i in range(ch // group):
@@ -79,27 +84,24 @@
     g = block_sum(lax.dot_general(z, z, NT, preferred_element_type=F32), 2 * k, 2 * k)
     gram_ref[...] = jnp.concatenate([g[k:, :], g[:k, :k]], axis=1)
 
-
-def load_kernel(n_chan, n_rad, partners_ref, stored_ref, ham_hbm, ham_ref, rows_ref, sem):
-    ncoup, ch = partners_ref.shape
     share, nz = ch // n_rad, n_chan // 4
-    copy = pltpu.make_async_copy(ham_hbm, ham_ref, sem)
-    copy.start()
-    me_chan, me_rad = lax.axis_index("chan"), lax.axis_index("rad")
-
-    def find(p, carry):
-        for j in range(ncoup):
-            q = stored_ref[partners_ref[j, p]]
-            slot = lax.div(q, ch) ^ me_chan
-            local = lax.rem(q, ch)
-            core = lax.div(local, share)
-            near = slot & 3
-            part = jnp.where((core & 1) == 1, ((near & 1) << 1) | (near >> 1), near)
-            place = ((core ^ me_rad) * 4 + part) * nz + z_place(slot >> 2, nz)
-            rows_ref[p * ncoup + j] = place * share + lax.rem(local, share)
-        return carry
-
-    lax.fori_loop(0, ch, find, 0)
+    q = stored_ref[...]
+    slot = lax.div(q, ch) ^ lax.axis_index("chan")
+    local = lax.rem(q, ch)
+    core = lax.div(local, share)
+    near = slot & 3
+    part = jnp.where((core & 1) == 1, ((near & 1) << 1) | (near >> 1), near)
+    place = ((core ^ lax.axis_index("rad")) * nz + z_place(slot >> 2, nz)) * 4 + part
+    place = (place * share + lax.rem(local, share)).astype(F32)
+    lane = lax.broadcasted_iota(jnp.int32, (ch, 128), 1)
+    columns = []
+    for j in range(partners_ref.shape[1]):
+        wanted = jnp.broadcast_to(partners_ref[:, j : j + 1], (ch, 128)) - lane
+        found = jnp.zeros((ch, 128), F32)
+        for c in range(place.shape[0]):
+            found = found + jnp.where(wanted == 128 * c, place[c : c + 1], 0.0)
+        columns.append(jnp.sum(found, axis=1, keepdims=True))
+    rows_ref[...] = jnp.concatenate(columns, axis=1).astype(jnp.int32)
     copy.wait()
 
 
@@ -113,7 +115,7 @@
         for i in range(group):
             p = g * group + i
             left.append(
-                jnp.concatenate([table_ref[rows_ref[p * ncoup + j]] for j in range(ncoup)], axis=1)
+                jnp.concatenate([table_ref[rows_ref[p, j]] for j in range(ncoup)], axis=1)
             )
             right.append(jnp.concatenate([ham_ref[p, j] for j in range(ncoup)], axis=1))
         product = lax.dot_general(
@@ -261,72 +263,73 @@
     share, nz = ch // n_rad, n_chan // 4
 
     own = own_share(trial_block)
-    column = [own] + [None] * (nz - 1)
-    for z in range(nz - 2, 0, -2):
-        column[z] = swap(own, "chan", 4 * z)
-    column[1] = swap(own, "chan", 4)
-    near = plane_swap(own[None], (1, 2))
-    local = pl.pallas_call(
-        trial_kernel,
+    barrier = lax.optimization_barrier
+    smem = pl.BlockSpec(memory_space=pltpu.SMEM)
+    any_ = pl.BlockSpec(memory_space=pl.ANY)
+    whole = pl.BlockSpec(memory_space=pltpu.VMEM)
+
+    def near_of(x):
+        return plane_swap(x, (1, 2))
+
+    def far_of(x, near):
+        half = jnp.stack([x, near], axis=1)
+        return half, plane_swap(half, (2, 1))
+
+    def to_cores(x):
+        return [swap(x, "rad", c) for c in range(1, n_rad)]
+
+    groups = z_groups(nz)
+    z1 = swap(own, "chan", 4)[None]
+    z2 = jnp.stack([swap(own, "chan", 4 * z) for z in groups[2]])
+    near0 = near_of(own[None])
+    near0, z1 = barrier((near0, z1))
+    half0, far0 = far_of(own[None], near0)
+    near1 = near_of(z1)
+    z2, near1 = barrier((z2, near1))
+    z3 = swap(z2, "chan", 4)
+    near2 = near_of(z2)
+    half1, far1 = far_of(z1, near1)
+    near2, far0 = barrier((near2, far0))
+    half2, far2 = far_of(z2, near2)
+    z3, far0 = barrier((z3, far0))
+    near3 = near_of(z3)
+    c_half0, c_far0, c_half1 = to_cores(half0), to_cores(far0), to_cores(half1)
+    inputs = (trial_block, precond_diag, partners, stored_at, ham_blocks)
+    inputs, far1 = barrier((inputs, far1))
+    trial_block, precond_diag, partners, stored_at, ham_blocks = inputs
+    ham, rows, zhm, zl, dc, gram_t = pl.pallas_call(
+        functools.partial(prepare_kernel, n_chan, n_rad),
+        in_specs=[whole] * 4 + [any_],
+        out_specs=[whole] * 6,
         out_shape=[
+            pltpu.VMEM(ham_blocks.shape, BF16),
+            jax.ShapeDtypeStruct((ch, ncoup), jnp.int32),
             pltpu.VMEM((4 * k, lanes), BF16),
             pltpu.VMEM((2 * k, lanes), BF16),
             pltpu.VMEM((1, lanes), F32),
             pltpu.VMEM((k, 3 * k), F32),
         ],
-        compiler_params=pltpu.CompilerParams(vmem_limit_bytes=VMEM_LIMIT),
-        name="trial_gram",
-    )(trial_block, precond_diag)
-    column, near, local = lax.optimization_barrier((column, near, local))
-    zhm, zl, dc, gram_t = local
-
-    def second(parts, first):
-        half = jnp.stack([parts, first])
-        return half, plane_swap(half, (2, 1))
-
-    groups = z_groups(nz)
-    half0, far0 = second(own[None], near)
-    parts1 = jnp.stack([column[z] for z in groups[1]])
-    near1 = plane_swap(parts1, (1, 2))
-    for z in groups[2]:
-        column[z] = swap(column[z - 1], "chan", 4)
-    column, near1, half0, far0 = lax.optimization_barrier((column, near1, half0, far0))
-    parts2 = jnp.stack([column[z] for z in groups[2]])
-    near2 = plane_swap(parts2, (1, 2))
-    half1, far1 = second(parts1, near1)
-    others = [[swap(x, "rad", c) for x in (half0, far0, half1)] for c in range(1, n_rad)]
-    near2, others, partners, stored_at, ham_blocks = lax.optimization_barrier(
-        (near2, others, partners.T, stored_at, ham_blocks)
-    )
-    half2, far2 = second(parts2, near2)
-    others = [o + [swap(half2, "rad", c + 1)] for c, o in enumerate(others)]
-    smem = pl.BlockSpec(memory_space=pltpu.SMEM)
-    any_ = pl.BlockSpec(memory_space=pl.ANY)
-    whole = pl.BlockSpec(memory_space=pltpu.VMEM)
-    ham, rows = pl.pallas_call(
-        functools.partial(load_kernel, n_chan, n_rad),
-        in_specs=[smem, smem, any_],
-        out_specs=[whole, smem],
-        out_shape=[
-            pltpu.VMEM(ham_blocks.shape, BF16),
-            jax.ShapeDtypeStruct((ch * ncoup,), jnp.int32),
-        ],
         scratch_shapes=[pltpu.SemaphoreType.DMA],
         compiler_params=pltpu.CompilerParams(vmem_limit_bytes=VMEM_LIMIT),
-        name="load",
-    )(in_hbm(partners), in_hbm(stored_at), in_hbm(ham_blocks))
-    far1, far2, others, ham, rows = lax.optimization_barrier((far1, far2, others, ham, rows))
-    tables = [[half0, far0, half1, half2, far1, far2]]
-    for c, o in enumerate(others):
-        tables.append(o + [swap(x, "rad", c + 1) for x in (far1, far2)])
-    table = jnp.stack(
-        [
-            jnp.concatenate(
-                [jnp.concatenate([t[0], t[2], t[3]], axis=1), jnp.concatenate([t[1], t[4], t[5]], axis=1)]
-            )
-            for t in tables
-        ]
-    ).reshape(n_chan * ch, k, splines)
+        name="prepare",
+    )(trial_block, precond_diag, partners, stored_at.reshape(-1, 128), in_hbm(ham_blocks))
+    near3, far1, c_half0, c_far0, c_half1 = barrier((near3, far1, c_half0, c_far0, c_half1))
+    half3, far3 = far_of(z3, near3)
+    c_far1, c_half2, c_half3 = to_cores(far1), to_cores(half2), to_cores(half3)
+    c_far2 = to_cores(far2)
+
+    late = jnp.zeros_like(half3)
+    table = [half0, far0, half1, far1, half2, far2, half3, late]
+    for c in range(n_rad - 1):
+        table += [c_half0[c], c_far0[c], c_half1[c], c_far1[c], c_half2[c], c_far2[c], c_half3[c], late]
+    table = jnp.concatenate(
+        [jnp.concatenate([table[i], table[i + 1]], axis=1) for i in range(0, len(table), 2)]
+    )
+    table, far3, ham, rows = barrier((table, far3, ham, rows))
+    for c, x in enumerate([far3] + to_cores(far3)):
+        at = c * nz + nz - len(groups[3])
+        table = lax.dynamic_update_slice(table, x, (at, 2, 0, 0, 0))
+    table = table.reshape(n_chan * ch, k, splines)
 
     az, sums = pl.pallas_call(
         apply_kernel,

time: 71.4 us -> 72.3 us (1.013)
  starting transfers between devices: 24 us -> 29.7 us
  Pallas kernels: 17.3 us -> 13.4 us
  waiting for transfers between devices: 25.8 us -> 22.1 us
  other arithmetic: 2.35 us -> 5.59 us
    pallas_call x2 -> x1, Pallas kernels: 7.91 us -> 3.55 us  [body(): pl.pallas_call(functools.partial(prepare_kernel, n_chan, n_rad), in_specs...]
    unnamed x0 -> x7, other arithmetic: none -> 4.2 us
    ppermute x13 -> x15, waiting for transfers between devices: 12.5 us -> 9.36 us  [swap(): return lax.ppermute(x, axis, [(i, i ^ distance) for i in range(n)])]
    ppermute x6 -> x8, starting transfers between devices: 7.76 us -> 10.7 us  [plane_swap(): return lax.ppermute(x, ('chan', 'rad'), pairs)]
    ppermute x2, waiting for transfers between devices: 5.62 us -> 3.53 us  [sum_everywhere(): first = lax.ppermute(x, ('chan', 'rad'), chip_pairs((step, 2 * step)))]
    ppermute x13 -> x15, starting transfers between devices: 13.2 us -> 15.2 us  [swap(): return lax.ppermute(x, axis, [(i, i ^ distance) for i in range(n)])]
    ppermute x6 -> x8, waiting for transfers between devices: 7.71 us -> 9.17 us  [plane_swap(): return lax.ppermute(x, ('chan', 'rad'), pairs)]
    another operation x7 -> x4, other arithmetic: 1.06 us -> 0.1 us  [far_of(): half = jnp.stack([x, near], axis=1)]
  transfers between devices with their start and end apart: 23 -> 27, of which waited for: 12 -> 13; matrix products, arithmetic and copies ran while one was open for 0% -> 6% of each run, Pallas kernels for 11% -> 5%
where the time goes in v5:
time: 72.3 us; the launch traced here: 72 us
  starting transfers between devices  29.7 us (41%)
  waiting for transfers between devices  22.1 us (31%)
  Pallas kernels  13.4 us (19%)
  other arithmetic  5.59 us (8%)
  between operations  0.92 us (1%)
    ppermute x15, starting transfers between devices, swap(): return lax.ppermute(x, axis, [(i, i ^ distance) for i in range(n)])  15.2 us
    ppermute x8, starting transfers between devices, plane_swap(): return lax.ppermute(x, ('chan', 'rad'), pairs)  10.7 us
    ppermute x15, waiting for transfers between devices, swap(): return lax.ppermute(x, axis, [(i, i ^ distance) for i in range(n)])  9.36 us
    ppermute x8, waiting for transfers between devices, plane_swap(): return lax.ppermute(x, ('chan', 'rad'), pairs)  9.17 us
    pallas_call x1, Pallas kernels, body(): pl.pallas_call(apply_kernel, in_specs=[smem] + [whole] * 6, out_specs=[wh...  6.85 us
    unnamed x7, other arithmetic  4.2 us
    pallas_call x1, Pallas kernels, body(): pl.pallas_call(functools.partial(prepare_kernel, n_chan, n_rad), in_specs...  3.55 us
    ppermute x2, waiting for transfers between devices, sum_everywhere(): first = lax.ppermute(x, ('chan', 'rad'), chip_pairs((step, 2 * step)))  3.53 us
  transfers between devices with their start and end apart: 27, of which 13 were waited for; matrix products, arithmetic and copies ran while one was open for 6% of the time, Pallas kernels for 5%

profile of v5, /device:TPU:0, one launch (start us, length us, event | category | flops | bytes accessed | tf_op | source)
XLA Modules:
  0.0 72.0 jit_solution(14357532868476060692)
XLA Ops:
  0.7 1.1 %convert_element_type.3 = bf16[64,16,64]{2,1,0:T(8,128)(2,1)S(1)} convert(f32[64,16,64]{2,1,0:T(8,128)} %t_ref) | non-fusion elementwise | flops 65536 | bytes 393216 | tf_op jit(solution)/shard_map/convert_element_type | solution.py:243
  2.4 1.0 %collective-permute-done = bf16[32,16,64]{2,1,0:T(8,128)(2,1)S(1)} collective-permute-done((bf16[32,16,64]{2,1,0:T(8,128)(2,1)S(1)}, bf16[32,16,64]{2,1,0:T(8,128)(2,1)S(1)}, u32[]{:S(2)}, u32[]{:S(2)}) %collective-permute-start) | collective-permute-done | bytes 65568 | tf_op jit(solution)/shard_map/ppermute | solution.py:21
  3.5 2.9 %collective-permute-start.1 = (bf16[1,32,16,128]{3,2,1,0:T(8,128)(2,1)S(1)}, bf16[1,32,16,128]{3,2,1,0:T(8,128)(2,1)S(1)}, u32[]{:S(2)}, u32[]{:S(2)}) collective-permute-start(bf16[1,32,16,128]{3,2,1,0:T(8,128)(2,1)S(1)} %bitcast.22), channel_id=1, source_target_pairs={{0,2},{1,5},{2,0},{3,7},{4,6},{5,1},{6,4},{7,3},{8,10},{9,13},{10,... | collective-permute-start | bytes 393224 | tf_op jit(solution)/shard_map/ppermute | solution.py:30
  6.4 1.6 %collective-permute-start.2 = (bf16[32,16,128]{2,1,0:T(8,128)(2,1)S(1)}, bf16[32,16,128]{2,1,0:T(8,128)(2,1)S(1)}, u32[]{:S(2)}, u32[]{:S(2)}) collective-permute-start(bf16[32,16,128]{2,1,0:T(8,128)(2,1)S(1)} %pad_maximum_fusion.4), channel_id=1, source_target_pairs={{0,8},{2,10},{4,12},{6,14},{8,0},{10,2},{12,4},{14,6},{16,24},{18,... | collective-permute-start | bytes 393224 | tf_op jit(solution)/shard_map/ppermute | solution.py:21
  8.0 2.6 %collective-permute-start.3 = (bf16[32,16,128]{2,1,0:T(8,128)(2,1)S(1)}, bf16[32,16,128]{2,1,0:T(8,128)(2,1)S(1)}, u32[]{:S(2)}, u32[]{:S(2)}) collective-permute-start(bf16[32,16,128]{2,1,0:T(8,128)(2,1)S(1)} %pad_maximum_fusion.4), channel_id=1, source_target_pairs={{0,16},{2,18},{4,20},{6,22},{8,24},{10,26},{12,28},{14,30},{16,0},... | collective-permute-start | bytes 393224 | tf_op jit(solution)/shard_map/ppermute | solution.py:21
  10.6 3.2 %collective-permute-done.2 = bf16[32,16,128]{2,1,0:T(8,128)(2,1)S(1)} collective-permute-done((bf16[32,16,128]{2,1,0:T(8,128)(2,1)S(1)}, bf16[32,16,128]{2,1,0:T(8,128)(2,1)S(1)}, u32[]{:S(2)}, u32[]{:S(2)}) %collective-permute-start.2) | collective-permute-done | bytes 131104 | tf_op jit(solution)/shard_map/ppermute | solution.py:21
  13.8 2.0 %collective-permute-start.7 = (bf16[1,2,32,16,128]{4,3,2,1,0:T(8,128)(2,1)S(1)}, bf16[1,2,32,16,128]{4,3,2,1,0:T(8,128)(2,1)}, u32[]{:S(2)}, u32[]{:S(2)}) collective-permute-start(bf16[1,2,32,16,128]{4,3,2,1,0:T(8,128)(2,1)S(1)} %pad_maximum_fusion), channel_id=1, source_target_pairs={{0,4},{1,3},{2,6},{3,1},{4,0},{5,7},{6,2},{7,5},{8,12},{9,11},{10,... | collective-permute-start | bytes 786440 | tf_op jit(solution)/shard_map/ppermute | solution.py:30
  15.8 1.0 %collective-permute-done.3 = bf16[32,16,128]{2,1,0:T(8,128)(2,1)S(1)} collective-permute-done((bf16[32,16,128]{2,1,0:T(8,128)(2,1)S(1)}, bf16[32,16,128]{2,1,0:T(8,128)(2,1)S(1)}, u32[]{:S(2)}, u32[]{:S(2)}) %collective-permute-start.3) | collective-permute-done | bytes 131104 | tf_op jit(solution)/shard_map/ppermute | solution.py:21
  16.8 3.4 %collective-permute-done.4 = bf16[1,32,16,128]{3,2,1,0:T(8,128)(2,1)S(1)} collective-permute-done((bf16[1,32,16,128]{3,2,1,0:T(8,128)(2,1)S(1)}, bf16[1,32,16,128]{3,2,1,0:T(8,128)(2,1)S(1)}, u32[]{:S(2)}, u32[]{:S(2)}) %collective-permute-start.4) | collective-permute-done | bytes 131104 | tf_op jit(solution)/shard_map/ppermute | solution.py:30
  20.1 1.1 %collective-permute-start.6 = (bf16[1,32,16,128]{3,2,1,0:T(8,128)(2,1)S(1)}, bf16[1,32,16,128]{3,2,1,0:T(8,128)(2,1)S(1)}, u32[]{:S(2)}, u32[]{:S(2)}) collective-permute-start(bf16[1,32,16,128]{3,2,1,0:T(8,128)(2,1)S(1)} %bitcast.32), channel_id=1, source_target_pairs={{0,2},{1,5},{2,0},{3,7},{4,6},{5,1},{6,4},{7,3},{8,10},{9,13},{10,... | collective-permute-start | bytes 393224 | tf_op jit(solution)/shard_map/ppermute | solution.py:30
  21.3 0.9 %collective-permute-start.9 = (bf16[1,2,32,16,128]{4,3,2,1,0:T(8,128)(2,1)S(1)}, bf16[1,2,32,16,128]{4,3,2,1,0:T(8,128)(2,1)S(1)}, u32[]{:S(2)}, u32[]{:S(2)}) collective-permute-start(bf16[1,2,32,16,128]{4,3,2,1,0:T(8,128)(2,1)S(1)} %pad_maximum_fusion.1), channel_id=1, source_target_pairs={{0,4},{1,3},{2,6},{3,1},{4,0},{5,7},{6,2},{7,5},{8,12},{9,11},{10,... | collective-permute-start | bytes 786440 | tf_op jit(solution)/shard_map/ppermute | solution.py:30
  22.2 3.0 %collective-permute-done.6 = bf16[1,32,16,128]{3,2,1,0:T(8,128)(2,1)S(1)} collective-permute-done((bf16[1,32,16,128]{3,2,1,0:T(8,128)(2,1)S(1)}, bf16[1,32,16,128]{3,2,1,0:T(8,128)(2,1)S(1)}, u32[]{:S(2)}, u32[]{:S(2)}) %collective-permute-start.6) | collective-permute-done | bytes 131104 | tf_op jit(solution)/shard_map/ppermute | solution.py:30
  25.8 1.7 %collective-permute-start.8 = (bf16[1,32,16,128]{3,2,1,0:T(8,128)(2,1)S(1)}, bf16[1,32,16,128]{3,2,1,0:T(8,128)(2,1)S(1)}, u32[]{:S(2)}, u32[]{:S(2)}) collective-permute-start(bf16[1,32,16,128]{3,2,1,0:T(8,128)(2,1)S(1)} %collective-permute-done.5), channel_id=1, source_target_pairs={{0,2},{1,5},{2,0},{3,7},{4,6},{5,1},{6,4},{7,3},{8,10},{9,13},{10,... | collective-permute-start | bytes 393224 | tf_op jit(solution)/shard_map/ppermute | solution.py:30
  27.7 1.5 %collective-permute-start.13 = (bf16[1,2,32,16,128]{4,3,2,1,0:T(8,128)(2,1)S(1)}, bf16[1,2,32,16,128]{4,3,2,1,0:T(8,128)(2,1)}, u32[]{:S(2)}, u32[]{:S(2)}) collective-permute-start(bf16[1,2,32,16,128]{4,3,2,1,0:T(8,128)(2,1)S(1)} %pad_maximum_fusion.2), channel_id=1, source_target_pairs={{0,4},{1,3},{2,6},{3,1},{4,0},{5,7},{6,2},{7,5},{8,12},{9,11},{10,... | collective-permute-start | bytes 786440 | tf_op jit(solution)/shard_map/ppermute | solution.py:30
  29.2 1.8 %maximum_dynamic-update-slice_fusion.6 = bf16[8,4,32,16,128]{4,3,2,1,0:T(8,128)(2,1)} fusion(bf16[1,2,32,16,128]{4,3,2,1,0:T(8,128)(2,1)} %collective-permute-done.7, bf16[1,1,32,16,128]{4,3,2,1,0:T(8,128)(2,1)S(1)} %bitcast.43, bf16[1,1,32,16,128]{4,3,2,1,0:T(8,128)(2,1)S(1)} %bitcast.24), kind=kLoop, calls=%fused_computation.6 | loop fusion | flops 1572863 | bytes 1048576
  31.1 3.5 %prepare.1 = (bf16[64,8,64,128]{3,2,1,0:T(8,128)(2,1)S(1)}, s32[64,8]{1,0:T(8,128)S(1)}, bf16[64,4096]{1,0:T(8,128)(2,1)S(1)}, bf16[32,4096]{1,0:T(8,128)(2,1)S(...) custom-call(f32[64,16,64]{2,1,0:T(8,128)S(1)} %copy-done.1, f32[64,64]{1,0:T(8,128)S(1)} %copy-done.2, ...), custom_call_target="tpu_custom_call" | custom-call | tf_op jit(solution)/shard_map/prepare/pallas_call | solution.py:300
  36.5 1.0 %maximum_dynamic-update-slice_fusion.4 = bf16[8,4,32,16,128]{4,3,2,1,0:T(8,128)(2,1)S(1)} fusion(bf16[8,4,32,16,128]{4,3,2,1,0:T(8,128)(2,1)S(1)} %maximum_dynamic-update-slice_fusion.5, bf16[1,2,32,16,128]{4,3,2,1,0:T(8,128)(2,1)} %collective-permute-done.13, bf16[1,1,32,16,128]{4,3,2,1,0:T(8,128)(2,1)S(1)} %bitcast.41, ...), kind=kLoop, calls=%fused_computation.4 | loop fusion | flops 1572864 | bytes 1048576
  37.7 1.0 %maximum_dynamic-update-slice_fusion.2 = bf16[8,4,32,16,128]{4,3,2,1,0:T(8,128)(2,1)S(1)} fusion(bf16[8,4,32,16,128]{4,3,2,1,0:T(8,128)(2,1)S(1)} %maximum_dynamic-update-slice_fusion.3, bf16[1,2,32,16,128]{4,3,2,1,0:T(8,128)(2,1)} %collective-permute-done.11, bf16[1,2,32,16,128]{4,3,2,1,0:T(8,128)(2,1)S(1)} %collective-permute-done.10), kind=kLoop, calls=%fused_computation.2 | loop fusion | flops 1048576 | bytes 1048576
  39.1 2.7 %collective-permute-done.18 = bf16[1,2,32,16,128]{4,3,2,1,0:T(8,128)(2,1)S(1)} collective-permute-done((bf16[1,2,32,16,128]{4,3,2,1,0:T(8,128)(2,1)S(1)}, bf16[1,2,32,16,128]{4,3,2,1,0:T(8,128)(2,1)S(1)}, u32[]{:S(2)}, u32[]{:S(2)}) %collective-permute-start.18) | collective-permute-done | bytes 262176 | tf_op jit(solution)/shard_map/ppermute | solution.py:30
  41.8 1.5 %collective-permute-done.19 = bf16[1,2,32,16,128]{4,3,2,1,0:T(8,128)(2,1)S(1)} collective-permute-done((bf16[1,2,32,16,128]{4,3,2,1,0:T(8,128)(2,1)S(1)}, bf16[1,2,32,16,128]{4,3,2,1,0:T(8,128)(2,1)S(1)}, u32[]{:S(2)}, u32[]{:S(2)}) %collective-permute-start.19) | collective-permute-done | bytes 262176 | tf_op jit(solution)/shard_map/ppermute | solution.py:21
  43.3 6.8 %apply.1 = (bf16[32,4096]{1,0:T(8,128)(2,1)S(1)}, f32[16,128]{1,0:T(8,128)S(1)}) custom-call(s32[64,8]{1,0:T(8,128)S(1)} %get-tuple-element.56.rows_ref, bf16[64,8,64,128]{3,2,1,0:T(8,128)(2,1)S(1)} %get-tuple-element.57.ham_ref, bf16[1024,16,128]{2,1,0:T(8,128)(2,1)S(1)} %bitcast.20, bf16[64,4096]{1,0:T(8,128)(2,1)S(1)} %get-tuple-element.60.zhm_ref, ...), custom_call_target="tpu_custom_call" | custom-call | tf_op jit(solution)/shard_map/apply/pallas_call | solution.py:334
  50.3 1.0 %collective-permute-done.20 = f32[16,128]{1,0:T(8,128)S(1)} collective-permute-done((f32[16,128]{1,0:T(8,128)S(1)}, f32[16,128]{1,0:T(8,128)S(1)}, u32[]{:S(2)}, u32[]{:S(2)}) %collective-permute-start.20) | collective-permute-done | bytes 8224 | tf_op jit(solution)/shard_map/ppermute | solution.py:21
  51.4 0.9 %collective-permute-start.21 = (f32[16,128]{1,0:T(8,128)S(1)}, f32[16,128]{1,0:T(8,128)S(1)}, u32[]{:S(2)}, u32[]{:S(2)}) collective-permute-start(f32[16,128]{1,0:T(8,128)S(1)} %add.30), channel_id=1, source_target_pairs={{0,2},{1,5},{2,0},{3,7},{4,6},{5,1},{6,4},{7,3},{8,10},{9,13},{10,... | collective-permute-start | bytes 24584 | tf_op jit(solution)/shard_map/ppermute | solution.py:231
  52.3 0.6 collective-permute-start.22
  53.0 2.1 %collective-permute-done.21 = f32[16,128]{1,0:T(8,128)S(1)} collective-permute-done((f32[16,128]{1,0:T(8,128)S(1)}, f32[16,128]{1,0:T(8,128)S(1)}, u32[]{:S(2)}, u32[]{:S(2)}) %collective-permute-start.21) | collective-permute-done | bytes 8224 | tf_op jit(solution)/shard_map/ppermute | solution.py:231
  55.0 2.0 %collective-permute-start.23 = (f32[16,128]{1,0:T(8,128)S(1)}, f32[16,128]{1,0:T(8,128)S(1)}, u32[]{:S(2)}, u32[]{:S(2)}) collective-permute-start(f32[16,128]{1,0:T(8,128)S(1)} %select_add_fusion.1), channel_id=1, source_target_pairs={{0,1},{1,0},{2,3},{3,2},{4,5},{5,4},{6,7},{7,6},{8,9},{9,8},{10,11... | collective-permute-start | bytes 24584 | tf_op jit(solution)/shard_map/ppermute | solution.py:21
  57.0 0.8 %collective-permute-done.23 = f32[16,128]{1,0:T(8,128)S(1)} collective-permute-done((f32[16,128]{1,0:T(8,128)S(1)}, f32[16,128]{1,0:T(8,128)S(1)}, u32[]{:S(2)}, u32[]{:S(2)}) %collective-permute-start.23) | collective-permute-done | bytes 8224 | tf_op jit(solution)/shard_map/ppermute | solution.py:21
  57.9 1.5 %collective-permute-start.24 = (f32[16,128]{1,0:T(8,128)S(1)}, f32[16,128]{1,0:T(8,128)S(1)}, u32[]{:S(2)}, u32[]{:S(2)}) collective-permute-start(f32[16,128]{1,0:T(8,128)S(1)} %add.33), channel_id=1, source_target_pairs={{0,8},{1,17},{2,10},{3,19},{4,12},{5,21},{6,14},{7,23},{8,0},{9,25... | collective-permute-start | bytes 24584 | tf_op jit(solution)/shard_map/ppermute | solution.py:231
  60.1 1.5 %collective-permute-done.24 = f32[16,128]{1,0:T(8,128)S(1)} collective-permute-done((f32[16,128]{1,0:T(8,128)S(1)}, f32[16,128]{1,0:T(8,128)S(1)}, u32[]{:S(2)}, u32[]{:S(2)}) %collective-permute-start.24) | collective-permute-done | bytes 8224 | tf_op jit(solution)/shard_map/ppermute | solution.py:231
  61.5 6.6 %collective-permute-start.26 = (f32[16,128]{1,0:T(8,128)S(1)}, f32[16,128]{1,0:T(8,128)S(1)}, u32[]{:S(2)}, u32[]{:S(2)}) collective-permute-start(f32[16,128]{1,0:T(8,128)S(1)} %select_add_fusion), channel_id=1, source_target_pairs={{0,1},{1,0},{2,3},{3,2},{4,5},{5,4},{6,7},{7,6},{8,9},{9,8},{10,11... | collective-permute-start | bytes 24584 | tf_op jit(solution)/shard_map/ppermute | solution.py:21
  68.2 0.8 %collective-permute-done.26 = f32[16,128]{1,0:T(8,128)S(1)} collective-permute-done((f32[16,128]{1,0:T(8,128)S(1)}, f32[16,128]{1,0:T(8,128)S(1)}, u32[]{:S(2)}, u32[]{:S(2)}) %collective-permute-start.26) | collective-permute-done | bytes 8224 | tf_op jit(solution)/shard_map/ppermute | solution.py:21
  69.0 3.0 %finish.1 = (f32[64,16,64]{2,1,0:T(8,128)}, f32[1,16]{1,0:T(1,128)}) custom-call(f32[16,128]{1,0:T(8,128)S(1)} %add.35.sums_ref, bf16[32,4096]{1,0:T(8,128)(2,1)S(1)} %get-tuple-element.65.az_ref, bf16[64,4096]{1,0:T(8,128)(2,1)S(1)} %get-tuple-element.60.zhm_ref), custom_call_target="tpu_custom_call" | custom-call | tf_op jit(solution)/shard_map/finish/pallas_call | solution.py:348
  (61 shorter events, 4.7 us)
Async XLA Ops:
  0.6 30.5 %copy-start.1 = (f32[64,16,64]{2,1,0:T(8,128)S(1)}, f32[64,16,64]{2,1,0:T(8,128)}, u32[]{:S(2)}) copy-start(f32[64,16,64]{2,1,0:T(8,128)} %t_ref) | copy-start | bytes 786436
  0.6 30.5 %copy-start.2 = (f32[64,64]{1,0:T(8,128)S(1)}, f32[64,64]{1,0:T(8,128)}, u32[]{:S(2)}) copy-start(f32[64,64]{1,0:T(8,128)} %d_ref) | copy-start | bytes 49156
  0.7 30.4 %copy-start.4 = (s32[64,8]{0,1:T(8,128)S(1)}, s32[64,8]{0,1:T(8,128)}, u32[]{:S(2)}) copy-start(s32[64,8]{0,1:T(8,128)} %param.7) | copy-start | bytes 6148
  0.7 30.4 %copy-start.3 = (s32[1024]{0:T(1024)S(1)}, s32[1024]{0:T(1024)}, u32[]{:S(2)}) copy-start(s32[1024]{0:T(1024)} %param.8) | copy-start | bytes 12292
  1.8 1.5 %collective-permute-start = (bf16[32,16,64]{2,1,0:T(8,128)(2,1)S(1)}, bf16[32,16,64]{2,1,0:T(8,128)(2,1)S(1)}, u32[]{:S(2)}, u32[]{:S(2)}) collective-permute-start(bf16[32,16,64]{2,1,0:T(8,128)(2,1)S(1)} %dynamic-slice_bitcast_fusion), channel_id=1, source_target_pairs={{0,1},{1,0},{2,3},{3,2},{4,5},{5,4},{6,7},{7,6},{8,9},{9,8},{10,11... | collective-permute-start | bytes 196616 | tf_op jit(solution)/shard_map/ppermute | solution.py:21
  3.5 7.1 %collective-permute-start.1 = (bf16[1,32,16,128]{3,2,1,0:T(8,128)(2,1)S(1)}, bf16[1,32,16,128]{3,2,1,0:T(8,128)(2,1)S(1)}, u32[]{:S(2)}, u32[]{:S(2)}) collective-permute-start(bf16[1,32,16,128]{3,2,1,0:T(8,128)(2,1)S(1)} %bitcast.22), channel_id=1, source_target_pairs={{0,2},{1,5},{2,0},{3,7},{4,6},{5,1},{6,4},{7,3},{8,10},{9,13},{10,... | collective-permute-start | bytes 393224 | tf_op jit(solution)/shard_map/ppermute | solution.py:30
  6.4 7.4 %collective-permute-start.2 = (bf16[32,16,128]{2,1,0:T(8,128)(2,1)S(1)}, bf16[32,16,128]{2,1,0:T(8,128)(2,1)S(1)}, u32[]{:S(2)}, u32[]{:S(2)}) collective-permute-start(bf16[32,16,128]{2,1,0:T(8,128)(2,1)S(1)} %pad_maximum_fusion.4), channel_id=1, source_target_pairs={{0,8},{2,10},{4,12},{6,14},{8,0},{10,2},{12,4},{14,6},{16,24},{18,... | collective-permute-start | bytes 393224 | tf_op jit(solution)/shard_map/ppermute | solution.py:21
  8.0 8.8 %collective-permute-start.3 = (bf16[32,16,128]{2,1,0:T(8,128)(2,1)S(1)}, bf16[32,16,128]{2,1,0:T(8,128)(2,1)S(1)}, u32[]{:S(2)}, u32[]{:S(2)}) collective-permute-start(bf16[32,16,128]{2,1,0:T(8,128)(2,1)S(1)} %pad_maximum_fusion.4), channel_id=1, source_target_pairs={{0,16},{2,18},{4,20},{6,22},{8,24},{10,26},{12,28},{14,30},{16,0},... | collective-permute-start | bytes 393224 | tf_op jit(solution)/shard_map/ppermute | solution.py:21
  13.8 6.3 %collective-permute-start.4 = (bf16[1,32,16,128]{3,2,1,0:T(8,128)(2,1)S(1)}, bf16[1,32,16,128]{3,2,1,0:T(8,128)(2,1)S(1)}, u32[]{:S(2)}, u32[]{:S(2)}) collective-permute-start(bf16[1,32,16,128]{3,2,1,0:T(8,128)(2,1)S(1)} %bitcast.35), channel_id=1, source_target_pairs={{0,2},{1,5},{2,0},{3,7},{4,6},{5,1},{6,4},{7,3},{8,10},{9,13},{10,... | collective-permute-start | bytes 393224 | tf_op jit(solution)/shard_map/ppermute | solution.py:30
  13.8 11.4 %collective-permute-start.7 = (bf16[1,2,32,16,128]{4,3,2,1,0:T(8,128)(2,1)S(1)}, bf16[1,2,32,16,128]{4,3,2,1,0:T(8,128)(2,1)}, u32[]{:S(2)}, u32[]{:S(2)}) collective-permute-start(bf16[1,2,32,16,128]{4,3,2,1,0:T(8,128)(2,1)S(1)} %pad_maximum_fusion), channel_id=1, source_target_pairs={{0,4},{1,3},{2,6},{3,1},{4,0},{5,7},{6,2},{7,5},{8,12},{9,11},{10,... | collective-permute-start | bytes 786440 | tf_op jit(solution)/shard_map/ppermute | solution.py:30
  20.1 5.1 %collective-permute-start.5 = (bf16[1,32,16,128]{3,2,1,0:T(8,128)(2,1)S(1)}, bf16[1,32,16,128]{3,2,1,0:T(8,128)(2,1)S(1)}, u32[]{:S(2)}, u32[]{:S(2)}) collective-permute-start(bf16[1,32,16,128]{3,2,1,0:T(8,128)(2,1)S(1)} %bitcast.31), channel_id=1, source_target_pairs={{0,8},{2,10},{4,12},{6,14},{8,0},{10,2},{12,4},{14,6},{16,24},{18,... | collective-permute-start | bytes 393224 | tf_op jit(solution)/shard_map/ppermute | solution.py:21
  20.1 5.1 %collective-permute-start.6 = (bf16[1,32,16,128]{3,2,1,0:T(8,128)(2,1)S(1)}, bf16[1,32,16,128]{3,2,1,0:T(8,128)(2,1)S(1)}, u32[]{:S(2)}, u32[]{:S(2)}) collective-permute-start(bf16[1,32,16,128]{3,2,1,0:T(8,128)(2,1)S(1)} %bitcast.32), channel_id=1, source_target_pairs={{0,2},{1,5},{2,0},{3,7},{4,6},{5,1},{6,4},{7,3},{8,10},{9,13},{10,... | collective-permute-start | bytes 393224 | tf_op jit(solution)/shard_map/ppermute | solution.py:30
  21.3 6.4 %collective-permute-start.9 = (bf16[1,2,32,16,128]{4,3,2,1,0:T(8,128)(2,1)S(1)}, bf16[1,2,32,16,128]{4,3,2,1,0:T(8,128)(2,1)S(1)}, u32[]{:S(2)}, u32[]{:S(2)}) collective-permute-start(bf16[1,2,32,16,128]{4,3,2,1,0:T(8,128)(2,1)S(1)} %pad_maximum_fusion.1), channel_id=1, source_target_pairs={{0,4},{1,3},{2,6},{3,1},{4,0},{5,7},{6,2},{7,5},{8,12},{9,11},{10,... | collective-permute-start | bytes 786440 | tf_op jit(solution)/shard_map/ppermute | solution.py:30
  22.2 12.5 %collective-permute-start.10 = (bf16[1,2,32,16,128]{4,3,2,1,0:T(8,128)(2,1)S(1)}, bf16[1,2,32,16,128]{4,3,2,1,0:T(8,128)(2,1)S(1)}, u32[]{:S(2)}, u32[]{:S(2)}) collective-permute-start(bf16[1,2,32,16,128]{4,3,2,1,0:T(8,128)(2,1)S(1)} %pad_maximum_fusion), channel_id=1, source_target_pairs={{0,1},{1,0},{2,3},{3,2},{4,5},{5,4},{6,7},{7,6},{8,9},{9,8},{10,11... | collective-permute-start | bytes 786440 | tf_op jit(solution)/shard_map/ppermute | solution.py:21
  25.2 9.5 %collective-permute-start.12 = (bf16[1,2,32,16,128]{4,3,2,1,0:T(8,128)(2,1)S(1)}, bf16[1,2,32,16,128]{4,3,2,1,0:T(8,128)(2,1)S(1)}, u32[]{:S(2)}, u32[]{:S(2)}) collective-permute-start(bf16[1,2,32,16,128]{4,3,2,1,0:T(8,128)(2,1)S(1)} %pad_maximum_fusion.1), channel_id=1, source_target_pairs={{0,1},{1,0},{2,3},{3,2},{4,5},{5,4},{6,7},{7,6},{8,9},{9,8},{10,11... | collective-permute-start | bytes 786440 | tf_op jit(solution)/shard_map/ppermute | solution.py:21
  25.2 9.5 %collective-permute-start.11 = (bf16[1,2,32,16,128]{4,3,2,1,0:T(8,128)(2,1)}, bf16[1,2,32,16,128]{4,3,2,1,0:T(8,128)(2,1)}, u32[]{:S(2)}, u32[]{:S(2)}) collective-permute-start(bf16[1,2,32,16,128]{4,3,2,1,0:T(8,128)(2,1)} %collective-permute-done.7), channel_id=1, source_target_pairs={{0,1},{1,0},{2,3},{3,2},{4,5},{5,4},{6,7},{7,6},{8,9},{9,8},{10,11... | collective-permute-start | bytes 786440 | tf_op jit(solution)/shard_map/ppermute | solution.py:21
  25.8 8.9 %collective-permute-start.8 = (bf16[1,32,16,128]{3,2,1,0:T(8,128)(2,1)S(1)}, bf16[1,32,16,128]{3,2,1,0:T(8,128)(2,1)S(1)}, u32[]{:S(2)}, u32[]{:S(2)}) collective-permute-start(bf16[1,32,16,128]{3,2,1,0:T(8,128)(2,1)S(1)} %collective-permute-done.5), channel_id=1, source_target_pairs={{0,2},{1,5},{2,0},{3,7},{4,6},{5,1},{6,4},{7,3},{8,10},{9,13},{10,... | collective-permute-start | bytes 393224 | tf_op jit(solution)/shard_map/ppermute | solution.py:30
  27.7 8.5 %collective-permute-start.13 = (bf16[1,2,32,16,128]{4,3,2,1,0:T(8,128)(2,1)S(1)}, bf16[1,2,32,16,128]{4,3,2,1,0:T(8,128)(2,1)}, u32[]{:S(2)}, u32[]{:S(2)}) collective-permute-start(bf16[1,2,32,16,128]{4,3,2,1,0:T(8,128)(2,1)S(1)} %pad_maximum_fusion.2), channel_id=1, source_target_pairs={{0,4},{1,3},{2,6},{3,1},{4,0},{5,7},{6,2},{7,5},{8,12},{9,11},{10,... | collective-permute-start | bytes 786440 | tf_op jit(solution)/shard_map/ppermute | solution.py:30
  31.1 5.0 %copy-start = (bf16[8,4,32,16,128]{4,3,2,1,0:T(8,128)(2,1)S(1)}, bf16[8,4,32,16,128]{4,3,2,1,0:T(8,128)(2,1)}, u32[]{:S(2)}) copy-start(bf16[8,4,32,16,128]{4,3,2,1,0:T(8,128)(2,1)} %maximum_dynamic-update-slice_fusion.6) | copy-start | bytes 12582916
  34.7 4.2 %collective-permute-start.15 = (bf16[1,2,32,16,128]{4,3,2,1,0:T(8,128)(2,1)S(1)}, bf16[1,2,32,16,128]{4,3,2,1,0:T(8,128)(2,1)S(1)}, u32[]{:S(2)}, u32[]{:S(2)}) collective-permute-start(bf16[1,2,32,16,128]{4,3,2,1,0:T(8,128)(2,1)S(1)} %pad_maximum_fusion.2), channel_id=1, source_target_pairs={{0,1},{1,0},{2,3},{3,2},{4,5},{5,4},{6,7},{7,6},{8,9},{9,8},{10,11... | collective-permute-start | bytes 786440 | tf_op jit(solution)/shard_map/ppermute | solution.py:21
  34.8 4.1 %collective-permute-start.17 = (bf16[1,2,32,16,128]{4,3,2,1,0:T(8,128)(2,1)S(1)}, bf16[1,2,32,16,128]{4,3,2,1,0:T(8,128)(2,1)S(1)}, u32[]{:S(2)}, u32[]{:S(2)}) collective-permute-start(bf16[1,2,32,16,128]{4,3,2,1,0:T(8,128)(2,1)S(1)} %pad_maximum_fusion.3), channel_id=1, source_target_pairs={{0,1},{1,0},{2,3},{3,2},{4,5},{5,4},{6,7},{7,6},{8,9},{9,8},{10,11... | collective-permute-start | bytes 786440 | tf_op jit(solution)/shard_map/ppermute | solution.py:21
  35.4 6.4 %collective-permute-start.18 = (bf16[1,2,32,16,128]{4,3,2,1,0:T(8,128)(2,1)S(1)}, bf16[1,2,32,16,128]{4,3,2,1,0:T(8,128)(2,1)S(1)}, u32[]{:S(2)}, u32[]{:S(2)}) collective-permute-start(bf16[1,2,32,16,128]{4,3,2,1,0:T(8,128)(2,1)S(1)} %pad_maximum_fusion.3), channel_id=1, source_target_pairs={{0,4},{1,3},{2,6},{3,1},{4,0},{5,7},{6,2},{7,5},{8,12},{9,11},{10,... | collective-permute-start | bytes 786440 | tf_op jit(solution)/shard_map/ppermute | solution.py:30
  35.9 2.9 %collective-permute-start.14 = (bf16[1,2,32,16,128]{4,3,2,1,0:T(8,128)(2,1)S(1)}, bf16[1,2,32,16,128]{4,3,2,1,0:T(8,128)(2,1)S(1)}, u32[]{:S(2)}, u32[]{:S(2)}) collective-permute-start(bf16[1,2,32,16,128]{4,3,2,1,0:T(8,128)(2,1)S(1)} %collective-permute-done.9), channel_id=1, source_target_pairs={{0,1},{1,0},{2,3},{3,2},{4,5},{5,4},{6,7},{7,6},{8,9},{9,8},{10,11... | collective-permute-start | bytes 786440 | tf_op jit(solution)/shard_map/ppermute | solution.py:21
  36.2 2.7 %collective-permute-start.16 = (bf16[1,2,32,16,128]{4,3,2,1,0:T(8,128)(2,1)}, bf16[1,2,32,16,128]{4,3,2,1,0:T(8,128)(2,1)S(1)}, u32[]{:S(2)}, u32[]{:S(2)}) collective-permute-start(bf16[1,2,32,16,128]{4,3,2,1,0:T(8,128)(2,1)} %collective-permute-done.13), channel_id=1, source_target_pairs={{0,1},{1,0},{2,3},{3,2},{4,5},{5,4},{6,7},{7,6},{8,9},{9,8},{10,11... | collective-permute-start | bytes 786440 | tf_op jit(solution)/shard_map/ppermute | solution.py:21
  41.7 1.5 %collective-permute-start.19 = (bf16[1,2,32,16,128]{4,3,2,1,0:T(8,128)(2,1)S(1)}, bf16[1,2,32,16,128]{4,3,2,1,0:T(8,128)(2,1)S(1)}, u32[]{:S(2)}, u32[]{:S(2)}) collective-permute-start(bf16[1,2,32,16,128]{4,3,2,1,0:T(8,128)(2,1)S(1)} %collective-permute-done.18), channel_id=1, source_target_pairs={{0,1},{1,0},{2,3},{3,2},{4,5},{5,4},{6,7},{7,6},{8,9},{9,8},{10,11... | collective-permute-start | bytes 786440 | tf_op jit(solution)/shard_map/ppermute | solution.py:21
  50.2 1.2 %collective-permute-start.20 = (f32[16,128]{1,0:T(8,128)S(1)}, f32[16,128]{1,0:T(8,128)S(1)}, u32[]{:S(2)}, u32[]{:S(2)}) collective-permute-start(f32[16,128]{1,0:T(8,128)S(1)} %get-tuple-element.64), channel_id=1, source_target_pairs={{0,1},{1,0},{2,3},{3,2},{4,5},{5,4},{6,7},{7,6},{8,9},{9,8},{10,11... | collective-permute-start | bytes 24584 | tf_op jit(solution)/shard_map/ppermute | solution.py:21
  51.4 3.7 %collective-permute-start.21 = (f32[16,128]{1,0:T(8,128)S(1)}, f32[16,128]{1,0:T(8,128)S(1)}, u32[]{:S(2)}, u32[]{:S(2)}) collective-permute-start(f32[16,128]{1,0:T(8,128)S(1)} %add.30), channel_id=1, source_target_pairs={{0,2},{1,5},{2,0},{3,7},{4,6},{5,1},{6,4},{7,3},{8,10},{9,13},{10,... | collective-permute-start | bytes 24584 | tf_op jit(solution)/shard_map/ppermute | solution.py:231
  52.3 2.7 %collective-permute-start.22 = (f32[16,128]{1,0:T(8,128)S(1)}, f32[16,128]{1,0:T(8,128)S(1)}, u32[]{:S(2)}, u32[]{:S(2)}) collective-permute-start(f32[16,128]{1,0:T(8,128)S(1)} %add.30), channel_id=1, source_target_pairs={{1,7},{3,5},{5,3},{7,1},{9,15},{11,13},{13,11},{15,9},{17,23},{19,... | collective-permute-start | bytes 24584 | tf_op jit(solution)/shard_map/ppermute | solution.py:232
  55.0 2.8 %collective-permute-start.23 = (f32[16,128]{1,0:T(8,128)S(1)}, f32[16,128]{1,0:T(8,128)S(1)}, u32[]{:S(2)}, u32[]{:S(2)}) collective-permute-start(f32[16,128]{1,0:T(8,128)S(1)} %select_add_fusion.1), channel_id=1, source_target_pairs={{0,1},{1,0},{2,3},{3,2},{4,5},{5,4},{6,7},{7,6},{8,9},{9,8},{10,11... | collective-permute-start | bytes 24584 | tf_op jit(solution)/shard_map/ppermute | solution.py:21
  57.9 3.7 %collective-permute-start.24 = (f32[16,128]{1,0:T(8,128)S(1)}, f32[16,128]{1,0:T(8,128)S(1)}, u32[]{:S(2)}, u32[]{:S(2)}) collective-permute-start(f32[16,128]{1,0:T(8,128)S(1)} %add.33), channel_id=1, source_target_pairs={{0,8},{1,17},{2,10},{3,19},{4,12},{5,21},{6,14},{7,23},{8,0},{9,25... | collective-permute-start | bytes 24584 | tf_op jit(solution)/shard_map/ppermute | solution.py:231
  59.4 2.1 %collective-permute-start.25 = (f32[16,128]{1,0:T(8,128)S(1)}, f32[16,128]{1,0:T(8,128)S(1)}, u32[]{:S(2)}, u32[]{:S(2)}) collective-permute-start(f32[16,128]{1,0:T(8,128)S(1)} %add.33), channel_id=1, source_target_pairs={{1,25},{3,27},{5,29},{7,31},{9,17},{11,19},{13,21},{15,23},{17,9},... | collective-permute-start | bytes 24584 | tf_op jit(solution)/shard_map/ppermute | solution.py:232
  61.5 7.4 %collective-permute-start.26 = (f32[16,128]{1,0:T(8,128)S(1)}, f32[16,128]{1,0:T(8,128)S(1)}, u32[]{:S(2)}, u32[]{:S(2)}) collective-permute-start(f32[16,128]{1,0:T(8,128)S(1)} %select_add_fusion), channel_id=1, source_target_pairs={{0,1},{1,0},{2,3},{3,2},{4,5},{5,4},{6,7},{7,6},{8,9},{9,8},{10,11... | collective-permute-start | bytes 24584 | tf_op jit(solution)/shard_map/ppermute | solution.py:21

commit v6 on v5

--- a/solution.py
+++ b/solution.py
@@ -30,14 +30,16 @@
     return lax.ppermute(x, ("chan", "rad"), pairs)
 
 
-def z_groups(nz):
-    return [[0], [1], list(range(2, nz, 2)), list(range(3, nz, 2))]
-
-
-def z_place(z, nz):
-    if nz == 4:
-        return z
-    return jnp.where(z < 2, z, jnp.where((z & 1) == 1, (nz + z - 1) >> 1, 1 + (z >> 1)))
+def table_place(z, part, nz):
+    some, odd = nz // 2, nz // 2 - 1
+    is_odd = (z & 1 == 1) & (z > 1)
+    i = jnp.where(is_odd, (z - 3) >> 1, jnp.where(z == 1, 0, z >> 1))
+    start = 2 + 2 * some
+    here = jnp.where(is_odd, start + i, 2 + i)
+    near = jnp.where(is_odd, start + odd + 2 + i, 2 + some + i)
+    far = start + 2 * odd + 2 + (some + odd) * (part & 1) + jnp.where(is_odd, some + i, i)
+    own = jnp.where(part < 2, part, start + odd + (part & 1))
+    return jnp.where(z == 0, own, jnp.where(part == 0, here, jnp.where(part == 1, near, far)))
 
 
 def in_vmem(x):
@@ -65,11 +67,9 @@
 
 
 def prepare_kernel(
-    n_chan, n_rad, t_ref, d_ref, partners_ref, stored_ref, ham_hbm,
-    ham_ref, rows_ref, zhm_ref, zl_ref, dc_ref, gram_ref, sem,
+    n_chan, n_rad, t_ref, d_ref, partners_ref, stored_ref,
+    rows_ref, zhm_ref, zl_ref, dc_ref, gram_ref,
 ):
-    copy = pltpu.make_async_copy(ham_hbm, ham_ref, sem)
-    copy.start()
     ch, k, r = t_ref.shape
     group = 128 // r
     for i in range(ch // group):
@@ -91,7 +91,7 @@
     core = lax.div(local, share)
     near = slot & 3
     part = jnp.where((core & 1) == 1, ((near & 1) << 1) | (near >> 1), near)
-    place = ((core ^ lax.axis_index("rad")) * nz + z_place(slot >> 2, nz)) * 4 + part
+    place = (core ^ lax.axis_index("rad")) * nz * 4 + table_place(slot >> 2, part, nz)
     place = (place * share + lax.rem(local, share)).astype(F32)
     lane = lax.broadcasted_iota(jnp.int32, (ch, 128), 1)
     columns = []
@@ -102,30 +102,47 @@
             found = found + jnp.where(wanted == 128 * c, place[c : c + 1], 0.0)
         columns.append(jnp.sum(found, axis=1, keepdims=True))
     rows_ref[...] = jnp.concatenate(columns, axis=1).astype(jnp.int32)
-    copy.wait()
-
-
-def apply_kernel(rows_ref, ham_ref, table_ref, zhm_ref, zl_ref, dc_ref, gt_ref, az_ref, sums_ref, a0_ref):
+
+
+def apply_kernel(
+    rows_ref, ham_hbm, zhm_ref, zl_ref, dc_ref, gt_ref, *rest
+):
+    pieces = rest[:-6]
+    az_ref, sums_ref, a0_ref, ham_ref, table_ref, sems = rest[-6:]
     ch, ncoup, r, splines = ham_ref.shape
     k = zl_ref.shape[0] // 2
-    group = 256 // r
+    group = 8
+
+    def load(g):
+        at = pl.ds(g * group, group)
+        return pltpu.make_async_copy(ham_hbm.at[at], ham_ref.at[at], sems.at[g])
+
+    for g in range(ch // group):
+        load(g).start()
+
+    at = 0
+    for piece in pieces:
+        count, share = piece.shape[:2]
+
+        def place(i, carry, piece=piece, at=at, share=share):
+            table_ref[pl.ds(at + i * share, share)] = piece[i]
+            return carry
+
+        lax.fori_loop(0, count, place, 0)
+        at += count * share
 
     def work(g, carry):
-        left, right = [], []
+        load(g).wait()
+        products = []
         for i in range(group):
             p = g * group + i
-            left.append(
-                jnp.concatenate([table_ref[rows_ref[p, j]] for j in range(ncoup)], axis=1)
-            )
-            right.append(jnp.concatenate([ham_ref[p, j] for j in range(ncoup)], axis=1))
-        product = lax.dot_general(
-            jnp.concatenate(left, axis=0),
-            jnp.concatenate(right, axis=0),
-            NT,
-            preferred_element_type=F32,
-        )
-        own = [product[i * k : (i + 1) * k, i * r : (i + 1) * r] for i in range(group)]
-        a0_ref[:, pl.ds(pl.multiple_of(g * 256, 256), 256)] = jnp.concatenate(own, axis=1) * SCALE
+            right = jnp.concatenate([table_ref[rows_ref[p, j]] for j in range(ncoup)], axis=1)
+            left = jnp.concatenate([ham_ref[p, j] for j in range(ncoup)], axis=1)
+            products.append(lax.dot_general(left, right, NT, preferred_element_type=F32))
+        turned = (jnp.concatenate(products, axis=1) * SCALE).T
+        own = [turned[i * k : (i + 1) * k] for i in range(group)]
+        at = pl.ds(pl.multiple_of(g * group * r, 128), group * r)
+        a0_ref[:, at] = jnp.concatenate(own, axis=1)
         return carry
 
     lax.fori_loop(0, ch // group, work, 0)
@@ -208,30 +225,17 @@
     lax.fori_loop(0, ch * r // block, result, 0)
 
 
-def chip_pairs(pick):
-    n_chan, n_rad = lax.axis_size("chan"), lax.axis_size("rad")
-    pairs = []
-    for c in range(n_chan):
-        for r in range(n_rad):
-            distance = pick[r % 2]
-            if distance:
-                pairs.append((c * n_rad + r, (c ^ distance) * n_rad + r))
-    return pairs
-
-
 def sum_everywhere(x):
     n_chan, n_rad = lax.axis_size("chan"), lax.axis_size("rad")
     step = 1
     while step < n_rad:
         x = x + swap(x, "rad", step)
         step *= 2
-    even = lax.axis_index("rad") % 2 == 0
     step = 1
     while step < n_chan:
-        first = lax.ppermute(x, ("chan", "rad"), chip_pairs((step, 2 * step)))
-        other = lax.ppermute(x, ("chan", "rad"), chip_pairs((0, 3 * step)))
-        x = first + jnp.where(even, x, other)
-        x = x + swap(x, "rad", 1)
+        starts = [c for c in range(n_chan) if (c // step) % 4 == 0]
+        groups = [[c + i * step for i in range(4)] for c in starts]
+        x = lax.psum(x, "chan", axis_index_groups=groups)
         step *= 4
     return x
 
@@ -272,77 +276,66 @@
         return plane_swap(x, (1, 2))
 
     def far_of(x, near):
-        half = jnp.stack([x, near], axis=1)
-        return half, plane_swap(half, (2, 1))
-
-    def to_cores(x):
-        return [swap(x, "rad", c) for c in range(1, n_rad)]
-
-    groups = z_groups(nz)
-    z1 = swap(own, "chan", 4)[None]
-    z2 = jnp.stack([swap(own, "chan", 4 * z) for z in groups[2]])
-    near0 = near_of(own[None])
-    near0, z1 = barrier((near0, z1))
-    half0, far0 = far_of(own[None], near0)
-    near1 = near_of(z1)
-    z2, near1 = barrier((z2, near1))
-    z3 = swap(z2, "chan", 4)
-    near2 = near_of(z2)
-    half1, far1 = far_of(z1, near1)
-    near2, far0 = barrier((near2, far0))
-    half2, far2 = far_of(z2, near2)
-    z3, far0 = barrier((z3, far0))
-    near3 = near_of(z3)
-    c_half0, c_far0, c_half1 = to_cores(half0), to_cores(far0), to_cores(half1)
-    inputs = (trial_block, precond_diag, partners, stored_at, ham_blocks)
-    inputs, far1 = barrier((inputs, far1))
-    trial_block, precond_diag, partners, stored_at, ham_blocks = inputs
-    ham, rows, zhm, zl, dc, gram_t = pl.pallas_call(
+        return plane_swap(jnp.concatenate([x, near]), (2, 1))
+
+    def in_cores(x):
+        return [x] + [swap(x, "rad", c) for c in range(1, n_rad)]
+
+    own = own[None]
+    z_even = jnp.concatenate([swap(own, "chan", 4 * z) for z in range(2, nz, 2)])
+    z1 = swap(own, "chan", 4)
+    near0 = near_of(own)
+    z_even, z1, near0 = barrier((z_even, z1, near0))
+    z_odd = swap(z_even, "chan", 4)
+    some = jnp.concatenate([z1, z_even])
+    near1 = near_of(some)
+    far0 = far_of(own, near0)
+    z_odd, near1 = barrier((z_odd, near1))
+    near2 = near_of(z_odd)
+    early = in_cores(jnp.concatenate([own, near0, some, near1, z_odd]))
+    near2, far0, early = barrier((near2, far0, early))
+    far1 = far_of(jnp.concatenate([some, z_odd]), jnp.concatenate([near1, near2]))
+    far0 = in_cores(far0)
+
+    inputs = (trial_block, precond_diag, partners, stored_at)
+    inputs, near2 = barrier((inputs, near2))
+    trial_block, precond_diag, partners, stored_at = inputs
+    rows, zhm, zl, dc, gram_t = pl.pallas_call(
         functools.partial(prepare_kernel, n_chan, n_rad),
-        in_specs=[whole] * 4 + [any_],
-        out_specs=[whole] * 6,
+        in_specs=[whole] * 4,
+        out_specs=[whole] * 5,
         out_shape=[
-            pltpu.VMEM(ham_blocks.shape, BF16),
             jax.ShapeDtypeStruct((ch, ncoup), jnp.int32),
             pltpu.VMEM((4 * k, lanes), BF16),
             pltpu.VMEM((2 * k, lanes), BF16),
             pltpu.VMEM((1, lanes), F32),
             pltpu.VMEM((k, 3 * k), F32),
         ],
-        scratch_shapes=[pltpu.SemaphoreType.DMA],
         compiler_params=pltpu.CompilerParams(vmem_limit_bytes=VMEM_LIMIT),
         name="prepare",
-    )(trial_block, precond_diag, partners, stored_at.reshape(-1, 128), in_hbm(ham_blocks))
-    near3, far1, c_half0, c_far0, c_half1 = barrier((near3, far1, c_half0, c_far0, c_half1))
-    half3, far3 = far_of(z3, near3)
-    c_far1, c_half2, c_half3 = to_cores(far1), to_cores(half2), to_cores(half3)
-    c_far2 = to_cores(far2)
-
-    late = jnp.zeros_like(half3)
-    table = [half0, far0, half1, far1, half2, far2, half3, late]
-    for c in range(n_rad - 1):
-        table += [c_half0[c], c_far0[c], c_half1[c], c_far1[c], c_half2[c], c_far2[c], c_half3[c], late]
-    table = jnp.concatenate(
-        [jnp.concatenate([table[i], table[i + 1]], axis=1) for i in range(0, len(table), 2)]
-    )
-    table, far3, ham, rows = barrier((table, far3, ham, rows))
-    for c, x in enumerate([far3] + to_cores(far3)):
-        at = c * nz + nz - len(groups[3])
-        table = lax.dynamic_update_slice(table, x, (at, 2, 0, 0, 0))
-    table = table.reshape(n_chan * ch, k, splines)
+    )(trial_block, precond_diag, partners, stored_at.reshape(-1, 128))
+
+    far0, far1, rows = barrier((far0, far1, rows))
+    last = in_cores(jnp.concatenate([near2, far1]))
+    pieces = [in_vmem(x) for trio in zip(early, far0, last) for x in trio]
 
     az, sums = pl.pallas_call(
         apply_kernel,
-        in_specs=[smem] + [whole] * 6,
+        in_specs=[smem, any_] + [whole] * (4 + len(pieces)),
         out_specs=[whole, whole],
         out_shape=[
             pltpu.VMEM((2 * k, lanes), BF16),
             jax.ShapeDtypeStruct((k, 8 * k), F32),
         ],
-        scratch_shapes=[pltpu.VMEM((k, lanes), F32)],
-        compiler_params=pltpu.CompilerParams(vmem_limit_bytes=VMEM_LIMIT),
+        scratch_shapes=[
+            pltpu.VMEM((k, lanes), F32),
+            pltpu.VMEM(ham_blocks.shape, BF16),
+            pltpu.VMEM((n_chan * ch, k, splines), BF16),
+            pltpu.SemaphoreType.DMA((ch // 8,)),
+        ],
+        compiler_params=pltpu.CompilerParams(vmem_limit_bytes=VMEM_LIMIT + 12 * 1024 * 1024),
         name="apply",
-    )(rows, in_vmem(ham), in_vmem(table), in_vmem(zhm), in_vmem(zl), in_vmem(dc), gram_t)
+    )(rows, in_hbm(ham_blocks), in_vmem(zhm), in_vmem(zl), in_vmem(dc), gram_t, *pieces)
 
     sums = sum_everywhere(sums)
     new_block, ritz = pl.pallas_call(

time: 72.3 us -> 82.8 us (1.15)
  blocking collectives: 0 us -> 19.6 us
  starting transfers between devices: 29.7 us -> 12.9 us
  local copies, waits for them, and re-layouts: 0.36 us -> 8.12 us
  waiting for transfers between devices: 22.1 us -> 26.9 us
  other arithmetic: 5.59 us -> 1.27 us
    psum x0 -> x2, blocking collectives: none -> 19.6 us  [sum_everywhere(): x = lax.psum(x, 'chan', axis_index_groups=groups)]
    ppermute x15 -> x8, starting transfers between devices: 15.2 us -> 5.82 us  [swap(): return lax.ppermute(x, axis, [(i, i ^ distance) for i in range(n)])]
    ppermute x8 -> x5, waiting for transfers between devices: 9.17 us -> 14.7 us  [plane_swap(): return lax.ppermute(x, ('chan', 'rad'), pairs)]
    unnamed x10 -> x12, local copies, waits for them, and re-layouts: 0.02 us -> 5.33 us
    unnamed x7 -> x1, other arithmetic: 4.2 us -> 0.11 us
    ppermute x4 -> x0, starting transfers between devices: 3.75 us -> none  [the longest x2 2.45 us: sum_everywhere(): first = lax.ppermute(x, ('chan', 'rad'), chip_pairs((step, 2 * step)))]
    ppermute x8 -> x5, starting transfers between devices: 10.7 us -> 7.03 us  [plane_swap(): return lax.ppermute(x, ('chan', 'rad'), pairs)]
    ppermute x4 -> x0, waiting for transfers between devices: 3.53 us -> none  [the longest x2 3.53 us: sum_everywhere(): first = lax.ppermute(x, ('chan', 'rad'), chip_pairs((step, 2 * step)))]
  transfers between devices with their start and end apart: 27 -> 13, of which waited for: 13 -> 9; matrix products, arithmetic and copies ran while one was open for 6% -> 3% of each run, Pallas kernels for 5% -> 1%
where the time goes in v6:
time: 82.8 us; the launch traced here: 82.3 us
  waiting for transfers between devices  26.9 us (32%)
  blocking collectives  19.6 us (24%)
  starting transfers between devices  12.9 us (16%)
  Pallas kernels  12.8 us (15%)
  local copies, waits for them, and re-layouts  8.12 us (10%)
  other arithmetic  1.27 us (2%)
    psum x2, blocking collectives, sum_everywhere(): x = lax.psum(x, 'chan', axis_index_groups=groups)  19.6 us
    ppermute x5, waiting for transfers between devices, plane_swap(): return lax.ppermute(x, ('chan', 'rad'), pairs)  14.7 us
    ppermute x8, waiting for transfers between devices, swap(): return lax.ppermute(x, axis, [(i, i ^ distance) for i in range(n)])  12.2 us
    pallas_call x1, Pallas kernels, body(): pl.pallas_call(apply_kernel, in_specs=[smem, any_] + [whole] * (4 + len(p...  8.6 us
    ppermute x5, starting transfers between devices, plane_swap(): return lax.ppermute(x, ('chan', 'rad'), pairs)  7.03 us
    ppermute x8, starting transfers between devices, swap(): return lax.ppermute(x, axis, [(i, i ^ distance) for i in range(n)])  5.82 us
    unnamed x12, local copies, waits for them, and re-layouts  5.33 us
    pallas_call x1, Pallas kernels, body(): pl.pallas_call(functools.partial(finish_kernel, total), out_shape=[jax.Sh...  3.05 us
  transfers between devices with their start and end apart: 13, of which 9 were waited for; matrix products, arithmetic and copies ran while one was open for 3% of the time, Pallas kernels for 1%

profile of v6, /device:TPU:0, one launch (start us, length us, event | category | flops | bytes accessed | tf_op | source)
XLA Modules:
  0.0 82.3 jit_solution(12282538106603551373)
XLA Ops:
  0.6 1.1 %convert_element_type.3 = bf16[64,16,64]{2,1,0:T(8,128)(2,1)S(1)} convert(f32[64,16,64]{2,1,0:T(8,128)} %t_ref) | non-fusion elementwise | flops 65536 | bytes 393216 | tf_op jit(solution)/shard_map/convert_element_type | solution.py:247
  1.7 0.5 collective-permute-start
  2.3 1.0 %collective-permute-done = bf16[32,16,64]{2,1,0:T(8,128)(2,1)S(1)} collective-permute-done((bf16[32,16,64]{2,1,0:T(8,128)(2,1)S(1)}, bf16[32,16,64]{2,1,0:T(8,128)(2,1)S(1)}, u32[]{:S(2)}, u32[]{:S(2)}) %collective-permute-start) | collective-permute-done | bytes 65568 | tf_op jit(solution)/shard_map/ppermute | solution.py:21
  3.4 2.9 %collective-permute-start.3 = (bf16[1,32,16,128]{3,2,1,0:T(8,128)(2,1)S(1)}, bf16[1,32,16,128]{3,2,1,0:T(8,128)(2,1)S(1)}, u32[]{:S(2)}, u32[]{:S(2)}) collective-permute-start(bf16[1,32,16,128]{3,2,1,0:T(8,128)(2,1)S(1)} %get-tuple-element.57), channel_id=1, source_target_pairs={{0,2},{1,5},{2,0},{3,7},{4,6},{5,1},{6,4},{7,3},{8,10},{9,13},{10,... | collective-permute-start | bytes 393224 | tf_op jit(solution)/shard_map/ppermute | solution.py:30
  6.3 1.6 %collective-permute-start.2 = (bf16[1,32,16,128]{3,2,1,0:T(8,128)(2,1)S(1)}, bf16[1,32,16,128]{3,2,1,0:T(8,128)(2,1)S(1)}, u32[]{:S(2)}, u32[]{:S(2)}) collective-permute-start(bf16[1,32,16,128]{3,2,1,0:T(8,128)(2,1)S(1)} %get-tuple-element.57), channel_id=1, source_target_pairs={{0,8},{2,10},{4,12},{6,14},{8,0},{10,2},{12,4},{14,6},{16,24},{18,... | collective-permute-start | bytes 393224 | tf_op jit(solution)/shard_map/ppermute | solution.py:21
  7.9 2.6 %collective-permute-start.1 = (bf16[1,32,16,128]{3,2,1,0:T(8,128)(2,1)S(1)}, bf16[1,32,16,128]{3,2,1,0:T(8,128)(2,1)S(1)}, u32[]{:S(2)}, u32[]{:S(2)}) collective-permute-start(bf16[1,32,16,128]{3,2,1,0:T(8,128)(2,1)S(1)} %get-tuple-element.57), channel_id=1, source_target_pairs={{0,16},{2,18},{4,20},{6,22},{8,24},{10,26},{12,28},{14,30},{16,0},... | collective-permute-start | bytes 393224 | tf_op jit(solution)/shard_map/ppermute | solution.py:21
  10.5 3.2 %collective-permute-done.2 = bf16[1,32,16,128]{3,2,1,0:T(8,128)(2,1)S(1)} collective-permute-done((bf16[1,32,16,128]{3,2,1,0:T(8,128)(2,1)S(1)}, bf16[1,32,16,128]{3,2,1,0:T(8,128)(2,1)S(1)}, u32[]{:S(2)}, u32[]{:S(2)}) %collective-permute-start.2) | collective-permute-done | bytes 131104 | tf_op jit(solution)/shard_map/ppermute | solution.py:21
  13.7 3.0 %collective-permute-done.1 = bf16[1,32,16,128]{3,2,1,0:T(8,128)(2,1)S(1)} collective-permute-done((bf16[1,32,16,128]{3,2,1,0:T(8,128)(2,1)S(1)}, bf16[1,32,16,128]{3,2,1,0:T(8,128)(2,1)S(1)}, u32[]{:S(2)}, u32[]{:S(2)}) %collective-permute-start.1) | collective-permute-done | bytes 131104 | tf_op jit(solution)/shard_map/ppermute | solution.py:21
  17.1 1.6 %collective-permute-start.5 = (bf16[2,32,16,128]{3,2,1,0:T(8,128)(2,1)S(1)}, bf16[2,32,16,128]{3,2,1,0:T(8,128)(2,1)S(1)}, u32[]{:S(2)}, u32[]{:S(2)}) collective-permute-start(bf16[2,32,16,128]{3,2,1,0:T(8,128)(2,1)S(1)} %pad_maximum_fusion), channel_id=1, source_target_pairs={{0,2},{1,5},{2,0},{3,7},{4,6},{5,1},{6,4},{7,3},{8,10},{9,13},{10,... | collective-permute-start | bytes 786440 | tf_op jit(solution)/shard_map/ppermute | solution.py:30
  18.7 0.7 constant_dynamic-update-slice_fusion.10
  19.4 0.7 constant_dynamic-update-slice_fusion.9
  20.1 1.5 %collective-permute-done.4 = bf16[1,32,16,128]{3,2,1,0:T(8,128)(2,1)S(1)} collective-permute-done((bf16[1,32,16,128]{3,2,1,0:T(8,128)(2,1)S(1)}, bf16[1,32,16,128]{3,2,1,0:T(8,128)(2,1)S(1)}, u32[]{:S(2)}, u32[]{:S(2)}) %collective-permute-start.4) | collective-permute-done | bytes 131104 | tf_op jit(solution)/shard_map/ppermute | solution.py:21
  21.6 1.9 %collective-permute-done.5 = bf16[2,32,16,128]{3,2,1,0:T(8,128)(2,1)S(1)} collective-permute-done((bf16[2,32,16,128]{3,2,1,0:T(8,128)(2,1)S(1)}, bf16[2,32,16,128]{3,2,1,0:T(8,128)(2,1)S(1)}, u32[]{:S(2)}, u32[]{:S(2)}) %collective-permute-start.5) | collective-permute-done | bytes 262176 | tf_op jit(solution)/shard_map/ppermute | solution.py:30
  23.6 0.7 constant_dynamic-update-slice_fusion.8
  24.2 0.8 constant_dynamic-update-slice_fusion.7
  25.1 0.6 collective-permute-start.7
  25.7 1.5 %collective-permute-start.6 = (bf16[1,32,16,128]{3,2,1,0:T(8,128)(2,1)S(1)}, bf16[1,32,16,128]{3,2,1,0:T(8,128)(2,1)S(1)}, u32[]{:S(2)}, u32[]{:S(2)}) collective-permute-start(bf16[1,32,16,128]{3,2,1,0:T(8,128)(2,1)S(1)} %collective-permute-done.4), channel_id=1, source_target_pairs={{0,2},{1,5},{2,0},{3,7},{4,6},{5,1},{6,4},{7,3},{8,10},{9,13},{10,... | collective-permute-start | bytes 393224 | tf_op jit(solution)/shard_map/ppermute | solution.py:30
  27.2 5.8 %collective-permute-done.7.rest_1_ = bf16[2,32,16,128]{3,2,1,0:T(8,128)(2,1)S(1)} collective-permute-done((bf16[2,32,16,128]{3,2,1,0:T(8,128)(2,1)S(1)}, bf16[2,32,16,128]{3,2,1,0:T(8,128)(2,1)S(1)}, u32[]{:S(2)}, u32[]{:S(2)}) %collective-permute-start.7) | collective-permute-done | bytes 262176 | tf_op jit(solution)/shard_map/ppermute | solution.py:30
  33.0 0.7 constant_dynamic-update-slice_fusion.6
  34.5 0.8 copy.7.partners_ref
  35.3 1.0 %copy-done = f32[64,16,64]{2,1,0:T(8,128)S(1)} copy-done((f32[64,16,64]{2,1,0:T(8,128)S(1)}, f32[64,16,64]{2,1,0:T(8,128)}, u32[]{:S(2)}) %copy-start) | copy-done | bytes 262168
  36.3 0.8 copy-done.1
  37.1 0.7 copy-done.2
  37.8 1.2 %prepare.1 = (s32[64,8]{1,0:T(8,128)S(1)}, bf16[64,4096]{1,0:T(8,128)(2,1)S(1)}, bf16[32,4096]{1,0:T(8,128)(2,1)S(1)}, f32[1,4096]{1,0:T(1,128)S(1)}, f32[16,48]{1,0:T(8,128)S(1)}) custom-call(f32[64,16,64]{2,1,0:T(8,128)S(1)} %copy-done, f32[64,64]{1,0:T(8,128)S(1)} %copy-done.1, s32[64,8]{1,0:T(8,128)S(1)} %copy.7.partners_ref, s32[8,128]{1,0:T(8,128)S(1)} %bitcast.11), custom_call_target="tpu_custom_call" | custom-call | tf_op jit(solution)/shard_map/prepare/pallas_call | solution.py:303
  38.9 7.0 %collective-permute-done.10 = bf16[6,32,16,128]{3,2,1,0:T(8,128)(2,1)} collective-permute-done((bf16[6,32,16,128]{3,2,1,0:T(8,128)(2,1)}, bf16[6,32,16,128]{3,2,1,0:T(8,128)(2,1)}, u32[]{:S(2)}, u32[]{:S(2)}) %collective-permute-start.10) | collective-permute-done | bytes 786464 | tf_op jit(solution)/shard_map/ppermute | solution.py:30
  46.0 1.3 %constant_dynamic-update-slice_fusion.11.rest_2_ = bf16[7,32,16,128]{3,2,1,0:T(8,128)(2,1)S(1)} fusion(bf16[7,32,16,128]{3,2,1,0:T(8,128)(2,1)S(1)} %constant_dynamic-update-slice_fusion.12, bf16[6,32,16,128]{3,2,1,0:T(8,128)(2,1)} %collective-permute-done.10), kind=kLoop, calls=%fused_computation.17 | loop fusion | bytes 1572864 | tf_op jit(solution)/shard_map/concatenate | solution.py:319
  47.4 2.5 %collective-permute-done.11.rest_5_ = bf16[7,32,16,128]{3,2,1,0:T(8,128)(2,1)S(1)} collective-permute-done((bf16[7,32,16,128]{3,2,1,0:T(8,128)(2,1)S(1)}, bf16[7,32,16,128]{3,2,1,0:T(8,128)(2,1)S(1)}, u32[]{:S(2)}, u32[]{:S(2)}) %collective-permute-start.11) | collective-permute-done | bytes 917536 | tf_op jit(solution)/shard_map/ppermute | solution.py:21
  49.8 8.6 %apply.1 = (bf16[32,4096]{1,0:T(8,128)(2,1)S(1)}, f32[16,128]{1,0:T(8,128)S(1)}) custom-call(s32[64,8]{1,0:T(8,128)S(1)} %get-tuple-element.41.rows_ref, bf16[64,8,64,128]{3,2,1,0:T(8,128)(2,1)} %ham_hbm.1, bf16[64,4096]{1,0:T(8,128)(2,1)S(1)} %get-tuple-element.42.zhm_ref, bf16[32,4096]{1,0:T(8,128)(2,1)S(1)} %get-tuple-element.43.zl_ref, ...), custom_call_target="tpu_custom_call" | custom-call | tf_op jit(solution)/shard_map/apply/pallas_call | solution.py:322
  58.6 1.0 %collective-permute-done.12 = f32[16,128]{1,0:T(8,128)S(1)} collective-permute-done((f32[16,128]{1,0:T(8,128)S(1)}, f32[16,128]{1,0:T(8,128)S(1)}, u32[]{:S(2)}, u32[]{:S(2)}) %collective-permute-start.12) | collective-permute-done | bytes 8224 | tf_op jit(solution)/shard_map/ppermute | solution.py:21
  59.7 8.9 %psum.14 = f32[16,128]{1,0:T(8,128)S(1)} all-reduce(f32[16,128]{1,0:T(8,128)S(1)} %add.16), channel_id=1, replica_groups={{0,2,4,6},{8,10,12,14},{16,18,20,22},{24,26,28,30},{1,3,5,7},{9,11,13,1..., use_global_device_ids=true, to_apply=%region_0.1 | all-reduce | flops 2048 | bytes 16384 | tf_op jit(solution)/shard_map/psum | solution.py:238
  68.5 10.7 %psum.15.sums_ref = f32[16,128]{1,0:T(8,128)S(1)} all-reduce(f32[16,128]{1,0:T(8,128)S(1)} %psum.14), channel_id=1, replica_groups={{0,8,16,24},{2,10,18,26},{4,12,20,28},{6,14,22,30},{1,9,17,25},{3,11,19..., use_global_device_ids=true, to_apply=%region_1.2 | all-reduce | flops 2048 | bytes 16384 | tf_op jit(solution)/shard_map/psum | solution.py:238
  79.3 3.0 %finish.1 = (f32[64,16,64]{2,1,0:T(8,128)}, f32[1,16]{1,0:T(1,128)}) custom-call(f32[16,128]{1,0:T(8,128)S(1)} %psum.15.sums_ref, bf16[32,4096]{1,0:T(8,128)(2,1)S(1)} %get-tuple-element.53.az_ref, bf16[64,4096]{1,0:T(8,128)(2,1)S(1)} %get-tuple-element.42.zhm_ref), custom_call_target="tpu_custom_call" | custom-call | tf_op jit(solution)/shard_map/finish/pallas_call | solution.py:341
  (22 shorter events, 1.9 us)
Async XLA Ops:
  1.7 1.5 %collective-permute-start = (bf16[32,16,64]{2,1,0:T(8,128)(2,1)S(1)}, bf16[32,16,64]{2,1,0:T(8,128)(2,1)S(1)}, u32[]{:S(2)}, u32[]{:S(2)}) collective-permute-start(bf16[32,16,64]{2,1,0:T(8,128)(2,1)S(1)} %dynamic-slice_bitcast_fusion), channel_id=1, source_target_pairs={{0,1},{1,0},{2,3},{3,2},{4,5},{5,4},{6,7},{7,6},{8,9},{9,8},{10,11... | collective-permute-start | bytes 196616 | tf_op jit(solution)/shard_map/ppermute | solution.py:21
  3.4 7.1 %collective-permute-start.3 = (bf16[1,32,16,128]{3,2,1,0:T(8,128)(2,1)S(1)}, bf16[1,32,16,128]{3,2,1,0:T(8,128)(2,1)S(1)}, u32[]{:S(2)}, u32[]{:S(2)}) collective-permute-start(bf16[1,32,16,128]{3,2,1,0:T(8,128)(2,1)S(1)} %get-tuple-element.57), channel_id=1, source_target_pairs={{0,2},{1,5},{2,0},{3,7},{4,6},{5,1},{6,4},{7,3},{8,10},{9,13},{10,... | collective-permute-start | bytes 393224 | tf_op jit(solution)/shard_map/ppermute | solution.py:30
  6.3 7.4 %collective-permute-start.2 = (bf16[1,32,16,128]{3,2,1,0:T(8,128)(2,1)S(1)}, bf16[1,32,16,128]{3,2,1,0:T(8,128)(2,1)S(1)}, u32[]{:S(2)}, u32[]{:S(2)}) collective-permute-start(bf16[1,32,16,128]{3,2,1,0:T(8,128)(2,1)S(1)} %get-tuple-element.57), channel_id=1, source_target_pairs={{0,8},{2,10},{4,12},{6,14},{8,0},{10,2},{12,4},{14,6},{16,24},{18,... | collective-permute-start | bytes 393224 | tf_op jit(solution)/shard_map/ppermute | solution.py:21
  7.9 8.8 %collective-permute-start.1 = (bf16[1,32,16,128]{3,2,1,0:T(8,128)(2,1)S(1)}, bf16[1,32,16,128]{3,2,1,0:T(8,128)(2,1)S(1)}, u32[]{:S(2)}, u32[]{:S(2)}) collective-permute-start(bf16[1,32,16,128]{3,2,1,0:T(8,128)(2,1)S(1)} %get-tuple-element.57), channel_id=1, source_target_pairs={{0,16},{2,18},{4,20},{6,22},{8,24},{10,26},{12,28},{14,30},{16,0},... | collective-permute-start | bytes 393224 | tf_op jit(solution)/shard_map/ppermute | solution.py:21
  16.7 5.0 %collective-permute-start.4 = (bf16[1,32,16,128]{3,2,1,0:T(8,128)(2,1)S(1)}, bf16[1,32,16,128]{3,2,1,0:T(8,128)(2,1)S(1)}, u32[]{:S(2)}, u32[]{:S(2)}) collective-permute-start(bf16[1,32,16,128]{3,2,1,0:T(8,128)(2,1)S(1)} %collective-permute-done.1), channel_id=1, source_target_pairs={{0,8},{2,10},{4,12},{6,14},{8,0},{10,2},{12,4},{14,6},{16,24},{18,... | collective-permute-start | bytes 393224 | tf_op jit(solution)/shard_map/ppermute | solution.py:21
  17.1 6.4 %collective-permute-start.5 = (bf16[2,32,16,128]{3,2,1,0:T(8,128)(2,1)S(1)}, bf16[2,32,16,128]{3,2,1,0:T(8,128)(2,1)S(1)}, u32[]{:S(2)}, u32[]{:S(2)}) collective-permute-start(bf16[2,32,16,128]{3,2,1,0:T(8,128)(2,1)S(1)} %pad_maximum_fusion), channel_id=1, source_target_pairs={{0,2},{1,5},{2,0},{3,7},{4,6},{5,1},{6,4},{7,3},{8,10},{9,13},{10,... | collective-permute-start | bytes 786440 | tf_op jit(solution)/shard_map/ppermute | solution.py:30
  25.0 8.0 %collective-permute-start.8 = (bf16[7,32,16,128]{3,2,1,0:T(8,128)(2,1)S(1)}, bf16[7,32,16,128]{3,2,1,0:T(8,128)(2,1)S(1)}, u32[]{:S(2)}, u32[]{:S(2)}) collective-permute-start(bf16[7,32,16,128]{3,2,1,0:T(8,128)(2,1)S(1)} %constant_dynamic-update-slice_fusion.rest_0_), channel_id=1, source_target_pairs={{0,1},{1,0},{2,3},{3,2},{4,5},{5,4},{6,7},{7,6},{8,9},{9,8},{10,11... | collective-permute-start | bytes 2752520 | tf_op jit(solution)/shard_map/ppermute | solution.py:21
  25.1 7.8 %collective-permute-start.7 = (bf16[2,32,16,128]{3,2,1,0:T(8,128)(2,1)S(1)}, bf16[2,32,16,128]{3,2,1,0:T(8,128)(2,1)S(1)}, u32[]{:S(2)}, u32[]{:S(2)}) collective-permute-start(bf16[2,32,16,128]{3,2,1,0:T(8,128)(2,1)S(1)} %pad_maximum_fusion.1), channel_id=1, source_target_pairs={{0,4},{1,3},{2,6},{3,1},{4,0},{5,7},{6,2},{7,5},{8,12},{9,11},{10,... | collective-permute-start | bytes 786440 | tf_op jit(solution)/shard_map/ppermute | solution.py:30
  25.7 7.3 %collective-permute-start.6 = (bf16[1,32,16,128]{3,2,1,0:T(8,128)(2,1)S(1)}, bf16[1,32,16,128]{3,2,1,0:T(8,128)(2,1)S(1)}, u32[]{:S(2)}, u32[]{:S(2)}) collective-permute-start(bf16[1,32,16,128]{3,2,1,0:T(8,128)(2,1)S(1)} %collective-permute-done.4), channel_id=1, source_target_pairs={{0,2},{1,5},{2,0},{3,7},{4,6},{5,1},{6,4},{7,3},{8,10},{9,13},{10,... | collective-permute-start | bytes 393224 | tf_op jit(solution)/shard_map/ppermute | solution.py:30
  33.7 12.3 %collective-permute-start.10 = (bf16[6,32,16,128]{3,2,1,0:T(8,128)(2,1)}, bf16[6,32,16,128]{3,2,1,0:T(8,128)(2,1)}, u32[]{:S(2)}, u32[]{:S(2)}) collective-permute-start(bf16[6,32,16,128]{3,2,1,0:T(8,128)(2,1)} %constant_dynamic-update-slice_fusion.6), channel_id=1, source_target_pairs={{0,4},{1,3},{2,6},{3,1},{4,0},{5,7},{6,2},{7,5},{8,12},{9,11},{10,... | collective-permute-start | bytes 2359304 | tf_op jit(solution)/shard_map/ppermute | solution.py:30
  34.2 4.8 %collective-permute-start.9 = (bf16[2,32,16,128]{3,2,1,0:T(8,128)(2,1)S(1)}, bf16[2,32,16,128]{3,2,1,0:T(8,128)(2,1)S(1)}, u32[]{:S(2)}, u32[]{:S(2)}) collective-permute-start(bf16[2,32,16,128]{3,2,1,0:T(8,128)(2,1)S(1)} %collective-permute-done.7.rest_1_), channel_id=1, source_target_pairs={{0,1},{1,0},{2,3},{3,2},{4,5},{5,4},{6,7},{7,6},{8,9},{9,8},{10,11... | collective-permute-start | bytes 786440 | tf_op jit(solution)/shard_map/ppermute | solution.py:21
  35.3 1.0 %copy-start = (f32[64,16,64]{2,1,0:T(8,128)S(1)}, f32[64,16,64]{2,1,0:T(8,128)}, u32[]{:S(2)}) copy-start(f32[64,16,64]{2,1,0:T(8,128)} %t_ref) | copy-start | bytes 786436
  36.3 0.8 copy-start.1
  37.1 0.7 copy-start.2
  47.3 2.5 %collective-permute-start.11 = (bf16[7,32,16,128]{3,2,1,0:T(8,128)(2,1)S(1)}, bf16[7,32,16,128]{3,2,1,0:T(8,128)(2,1)S(1)}, u32[]{:S(2)}, u32[]{:S(2)}) collective-permute-start(bf16[7,32,16,128]{3,2,1,0:T(8,128)(2,1)S(1)} %constant_dynamic-update-slice_fusion.11.rest_2_), channel_id=1, source_target_pairs={{0,1},{1,0},{2,3},{3,2},{4,5},{5,4},{6,7},{7,6},{8,9},{9,8},{10,11... | collective-permute-start | bytes 2752520 | tf_op jit(solution)/shard_map/ppermute | solution.py:21
  58.4 1.2 %collective-permute-start.12 = (f32[16,128]{1,0:T(8,128)S(1)}, f32[16,128]{1,0:T(8,128)S(1)}, u32[]{:S(2)}, u32[]{:S(2)}) collective-permute-start(f32[16,128]{1,0:T(8,128)S(1)} %get-tuple-element.52), channel_id=1, source_target_pairs={{0,1},{1,0},{2,3},{3,2},{4,5},{5,4},{6,7},{7,6},{8,9},{9,8},{10,11... | collective-permute-start | bytes 24584 | tf_op jit(solution)/shard_map/ppermute | solution.py:21

commit v7 on v5

--- a/solution.py
+++ b/solution.py
@@ -28,16 +28,6 @@
         for r in range(n_rad):
             pairs.append((c * n_rad + r, (c ^ order[r % 2]) * n_rad + r))
     return lax.ppermute(x, ("chan", "rad"), pairs)
-
-
-def z_groups(nz):
-    return [[0], [1], list(range(2, nz, 2)), list(range(3, nz, 2))]
-
-
-def z_place(z, nz):
-    if nz == 4:
-        return z
-    return jnp.where(z < 2, z, jnp.where((z & 1) == 1, (nz + z - 1) >> 1, 1 + (z >> 1)))
 
 
 def in_vmem(x):
@@ -86,12 +76,11 @@
 
     share, nz = ch // n_rad, n_chan // 4
     q = stored_ref[...]
-    slot = lax.div(q, ch) ^ lax.axis_index("chan")
-    local = lax.rem(q, ch)
+    owner, local = lax.div(q, ch), lax.rem(q, ch)
     core = lax.div(local, share)
-    near = slot & 3
-    part = jnp.where((core & 1) == 1, ((near & 1) << 1) | (near >> 1), near)
-    place = ((core ^ lax.axis_index("rad")) * nz + z_place(slot >> 2, nz)) * 4 + part
+    apart = (owner ^ lax.axis_index("chan")) & 3
+    part = jnp.where((core & 1) == 1, ((apart & 1) << 1) | (apart >> 1), apart)
+    place = ((core ^ lax.axis_index("rad")) * 4 + part) * nz + (owner >> 2)
     place = (place * share + lax.rem(local, share)).astype(F32)
     lane = lax.broadcasted_iota(jnp.int32, (ch, 128), 1)
     columns = []
@@ -128,7 +117,7 @@
         a0_ref[:, pl.ds(pl.multiple_of(g * 256, 256), 256)] = jnp.concatenate(own, axis=1) * SCALE
         return carry
 
-    lax.fori_loop(0, ch // group, work, 0)
+    lax.fori_loop(0, ch // group, work, 0, unroll=min(2, ch // group))
 
     lanes = ch * r
     block = min(lanes, 1024)
@@ -208,32 +197,26 @@
     lax.fori_loop(0, ch * r // block, result, 0)
 
 
-def chip_pairs(pick):
-    n_chan, n_rad = lax.axis_size("chan"), lax.axis_size("rad")
-    pairs = []
-    for c in range(n_chan):
-        for r in range(n_rad):
-            distance = pick[r % 2]
-            if distance:
-                pairs.append((c * n_rad + r, (c ^ distance) * n_rad + r))
-    return pairs
-
-
 def sum_everywhere(x):
     n_chan, n_rad = lax.axis_size("chan"), lax.axis_size("rad")
     step = 1
     while step < n_rad:
         x = x + swap(x, "rad", step)
         step *= 2
-    even = lax.axis_index("rad") % 2 == 0
-    step = 1
-    while step < n_chan:
-        first = lax.ppermute(x, ("chan", "rad"), chip_pairs((step, 2 * step)))
-        other = lax.ppermute(x, ("chan", "rad"), chip_pairs((0, 3 * step)))
-        x = first + jnp.where(even, x, other)
-        x = x + swap(x, "rad", 1)
-        step *= 4
-    return x
+    half = n_chan // 2
+    parts = []
+    for t in range(half):
+        pairs = []
+        for c in range(n_chan):
+            for r in range(n_rad):
+                distance = t + half * (r % 2)
+                if distance:
+                    pairs.append((c * n_rad + r, (c ^ distance) * n_rad + r))
+        parts.append(lax.ppermute(x, ("chan", "rad"), pairs))
+    parts[0] = jnp.where(lax.axis_index("rad") % 2 == 0, x, parts[0])
+    while len(parts) > 1:
+        parts = [parts[i] + parts[i + 1] for i in range(0, len(parts), 2)]
+    return parts[0] + swap(parts[0], "rad", 1)
 
 
 def own_share(trial_block):
@@ -262,40 +245,28 @@
     total = float(n_chan * n_rad * lanes)
     share, nz = ch // n_rad, n_chan // 4
 
-    own = own_share(trial_block)
     barrier = lax.optimization_barrier
     smem = pl.BlockSpec(memory_space=pltpu.SMEM)
     any_ = pl.BlockSpec(memory_space=pl.ANY)
     whole = pl.BlockSpec(memory_space=pltpu.VMEM)
 
-    def near_of(x):
-        return plane_swap(x, (1, 2))
-
-    def far_of(x, near):
-        half = jnp.stack([x, near], axis=1)
-        return half, plane_swap(half, (2, 1))
-
-    def to_cores(x):
-        return [swap(x, "rad", c) for c in range(1, n_rad)]
-
-    groups = z_groups(nz)
-    z1 = swap(own, "chan", 4)[None]
-    z2 = jnp.stack([swap(own, "chan", 4 * z) for z in groups[2]])
-    near0 = near_of(own[None])
-    near0, z1 = barrier((near0, z1))
-    half0, far0 = far_of(own[None], near0)
-    near1 = near_of(z1)
-    z2, near1 = barrier((z2, near1))
-    z3 = swap(z2, "chan", 4)
-    near2 = near_of(z2)
-    half1, far1 = far_of(z1, near1)
-    near2, far0 = barrier((near2, far0))
-    half2, far2 = far_of(z2, near2)
-    z3, far0 = barrier((z3, far0))
-    near3 = near_of(z3)
-    c_half0, c_far0, c_half1 = to_cores(half0), to_cores(far0), to_cores(half1)
+    def in_cores(x):
+        return [x] + [swap(x, "rad", c) for c in range(1, n_rad)]
+
+    own = own_share(trial_block)
+    column = lax.all_to_all(
+        jnp.broadcast_to(own, (nz,) + own.shape),
+        "chan",
+        split_axis=0,
+        concat_axis=0,
+        axis_index_groups=[[i + 4 * z for z in range(nz)] for i in range(4)],
+        tiled=True,
+    )
+    near = plane_swap(column, (1, 2))
+    far = plane_swap(column, (2, 1))
+    columns = in_cores(column)
     inputs = (trial_block, precond_diag, partners, stored_at, ham_blocks)
-    inputs, far1 = barrier((inputs, far1))
+    inputs, _ = barrier((inputs, column))
     trial_block, precond_diag, partners, stored_at, ham_blocks = inputs
     ham, rows, zhm, zl, dc, gram_t = pl.pallas_call(
         functools.partial(prepare_kernel, n_chan, n_rad),
@@ -313,22 +284,12 @@
         compiler_params=pltpu.CompilerParams(vmem_limit_bytes=VMEM_LIMIT),
         name="prepare",
     )(trial_block, precond_diag, partners, stored_at.reshape(-1, 128), in_hbm(ham_blocks))
-    near3, far1, c_half0, c_far0, c_half1 = barrier((near3, far1, c_half0, c_far0, c_half1))
-    half3, far3 = far_of(z3, near3)
-    c_far1, c_half2, c_half3 = to_cores(far1), to_cores(half2), to_cores(half3)
-    c_far2 = to_cores(far2)
-
-    late = jnp.zeros_like(half3)
-    table = [half0, far0, half1, far1, half2, far2, half3, late]
-    for c in range(n_rad - 1):
-        table += [c_half0[c], c_far0[c], c_half1[c], c_far1[c], c_half2[c], c_far2[c], c_half3[c], late]
-    table = jnp.concatenate(
-        [jnp.concatenate([table[i], table[i + 1]], axis=1) for i in range(0, len(table), 2)]
-    )
-    table, far3, ham, rows = barrier((table, far3, ham, rows))
-    for c, x in enumerate([far3] + to_cores(far3)):
-        at = c * nz + nz - len(groups[3])
-        table = lax.dynamic_update_slice(table, x, (at, 2, 0, 0, 0))
+    near, far, columns, rows = barrier((near, far, columns, rows))
+    both = plane_swap(near, (2, 1))
+    nears, fars = in_cores(near), in_cores(far)
+    both, nears, fars = barrier((both, nears, fars))
+    boths = in_cores(both)
+    table = jnp.concatenate([x for four in zip(columns, nears, fars, boths) for x in four])
     table = table.reshape(n_chan * ch, k, splines)
 
     az, sums = pl.pallas_call(

time: 72.3 us -> 79 us (1.093)
  blocking collectives: 0 us -> 20.8 us
  starting transfers between devices: 29.7 us -> 20.8 us
  other arithmetic: 5.59 us -> 1.23 us
  local copies, waits for them, and re-layouts: 0.36 us -> 3.86 us
  waiting for transfers between devices: 22.1 us -> 18.6 us
  Pallas kernels: 13.4 us -> 12.5 us
    all_to_all x0 -> x1, blocking collectives: none -> 20.8 us  [body(): lax.all_to_all(jnp.broadcast_to(own, (nz,) + own.shape), 'chan', split_ax...]
    ppermute x15 -> x7, starting transfers between devices: 15.2 us -> 7.26 us  [swap(): return lax.ppermute(x, axis, [(i, i ^ distance) for i in range(n)])]
    ppermute x8 -> x3, starting transfers between devices: 10.7 us -> 3.52 us  [plane_swap(): return lax.ppermute(x, ('chan', 'rad'), pairs)]
    ppermute x4 -> x8, starting transfers between devices: 3.75 us -> 9.99 us  [sum_everywhere(): parts.append(lax.ppermute(x, ('chan', 'rad'), pairs))]
    ppermute x15 -> x7, waiting for transfers between devices: 9.36 us -> 4.3 us  [swap(): return lax.ppermute(x, axis, [(i, i ^ distance) for i in range(n)])]
    unnamed x7 -> x0, other arithmetic: 4.2 us -> none
    ppermute x8 -> x3, waiting for transfers between devices: 9.17 us -> 12.3 us  [plane_swap(): return lax.ppermute(x, ('chan', 'rad'), pairs)]
    unnamed x10 -> x13, local copies, waits for them, and re-layouts: 0.02 us -> 2.94 us
  transfers between devices with their start and end apart: 27 -> 18, of which waited for: 13 -> 8; matrix products, arithmetic and copies ran while one was open for 6% -> 2% of each run, Pallas kernels for 5% -> 5%
where the time goes in v7:
time: 79 us; the launch traced here: 78.6 us
  starting transfers between devices  20.8 us (26%)
  blocking collectives  20.8 us (26%)
  waiting for transfers between devices  18.6 us (24%)
  Pallas kernels  12.5 us (16%)
  local copies, waits for them, and re-layouts  3.86 us (5%)
  other arithmetic  1.23 us (2%)
  between operations  0.8 us (1%)
    all_to_all x1, blocking collectives, body(): lax.all_to_all(jnp.broadcast_to(own, (nz,) + own.shape), 'chan', split_ax...  20.8 us
    ppermute x3, waiting for transfers between devices, plane_swap(): return lax.ppermute(x, ('chan', 'rad'), pairs)  12.3 us
    ppermute x8, starting transfers between devices, sum_everywhere(): parts.append(lax.ppermute(x, ('chan', 'rad'), pairs))  9.99 us
    ppermute x7, starting transfers between devices, swap(): return lax.ppermute(x, axis, [(i, i ^ distance) for i in range(n)])  7.26 us
    pallas_call x1, Pallas kernels, body(): pl.pallas_call(apply_kernel, in_specs=[smem] + [whole] * 6, out_specs=[wh...  5.78 us
    ppermute x7, waiting for transfers between devices, swap(): return lax.ppermute(x, axis, [(i, i ^ distance) for i in range(n)])  4.3 us
    pallas_call x1, Pallas kernels, body(): pl.pallas_call(functools.partial(prepare_kernel, n_chan, n_rad), in_specs...  3.68 us
    ppermute x3, starting transfers between devices, plane_swap(): return lax.ppermute(x, ('chan', 'rad'), pairs)  3.52 us
  transfers between devices with their start and end apart: 18, of which 8 were waited for; matrix products, arithmetic and copies ran while one was open for 2% of the time, Pallas kernels for 5%

profile of v7, /device:TPU:0, one launch (start us, length us, event | category | flops | bytes accessed | tf_op | source)
XLA Modules:
  0.0 78.6 jit_solution(838714551692513633)
XLA Ops:
  0.6 1.1 %convert_element_type.3 = bf16[64,16,64]{2,1,0:T(8,128)(2,1)S(1)} convert(f32[64,16,64]{2,1,0:T(8,128)} %t_ref) | non-fusion elementwise | flops 65536 | bytes 393216 | tf_op jit(solution)/shard_map/convert_element_type | solution.py:226
  1.7 0.5 collective-permute-start
  2.3 1.0 %collective-permute-done = bf16[32,16,64]{2,1,0:T(8,128)(2,1)S(1)} collective-permute-done((bf16[32,16,64]{2,1,0:T(8,128)(2,1)S(1)}, bf16[32,16,64]{2,1,0:T(8,128)(2,1)S(1)}, u32[]{:S(2)}, u32[]{:S(2)}) %collective-permute-start) | collective-permute-done | bytes 65568 | tf_op jit(solution)/shard_map/ppermute | solution.py:21
  3.3 0.1 pad_maximum_fusion
  3.5 20.8 %all_to_all.5 = bf16[4,32,16,128]{3,2,1,0:T(8,128)(2,1)S(1)} all-to-all(bf16[4,32,16,128]{3,2,1,0:T(8,128)(2,1)S(1)} %broadcast_in_dim.3), channel_id=1, replica_groups={{0,8,16,24},{2,10,18,26},{4,12,20,28},{6,14,22,30},{1,9,17,25},{3,11,19..., dimensions={0} | all-to-all | bytes 1048576 | tf_op jit(solution)/shard_map/all_to_all | solution.py:257
  24.3 1.5 %collective-permute-start.1 = (bf16[4,32,16,128]{3,2,1,0:T(8,128)(2,1)S(1)}, bf16[4,32,16,128]{3,2,1,0:T(8,128)(2,1)S(1)}, u32[]{:S(2)}, u32[]{:S(2)}) collective-permute-start(bf16[4,32,16,128]{3,2,1,0:T(8,128)(2,1)S(1)} %all_to_all.5), channel_id=1, source_target_pairs={{0,2},{1,5},{2,0},{3,7},{4,6},{5,1},{6,4},{7,3},{8,10},{9,13},{10,... | collective-permute-start | bytes 1572872 | tf_op jit(solution)/shard_map/ppermute | solution.py:30
  25.8 1.5 %collective-permute-start.2 = (bf16[4,32,16,128]{3,2,1,0:T(8,128)(2,1)S(1)}, bf16[4,32,16,128]{3,2,1,0:T(8,128)(2,1)S(1)}, u32[]{:S(2)}, u32[]{:S(2)}) collective-permute-start(bf16[4,32,16,128]{3,2,1,0:T(8,128)(2,1)S(1)} %all_to_all.5), channel_id=1, source_target_pairs={{0,4},{1,3},{2,6},{3,1},{4,0},{5,7},{6,2},{7,5},{8,12},{9,11},{10,... | collective-permute-start | bytes 1572872 | tf_op jit(solution)/shard_map/ppermute | solution.py:30
  27.3 0.8 copy.7.partners_ref
  28.1 1.0 %copy-done = f32[64,16,64]{2,1,0:T(8,128)S(1)} copy-done((f32[64,16,64]{2,1,0:T(8,128)S(1)}, f32[64,16,64]{2,1,0:T(8,128)}, u32[]{:S(2)}) %copy-start) | copy-done | bytes 262168
  29.1 0.8 copy-done.1
  29.9 0.7 copy-done.2
  30.6 3.7 %prepare.1 = (bf16[64,8,64,128]{3,2,1,0:T(8,128)(2,1)S(1)}, s32[64,8]{1,0:T(8,128)S(1)}, bf16[64,4096]{1,0:T(8,128)(2,1)S(1)}, bf16[32,4096]{1,0:T(8,128)(2,1)S(...) custom-call(f32[64,16,64]{2,1,0:T(8,128)S(1)} %copy-done, f32[64,64]{1,0:T(8,128)S(1)} %copy-done.1, ...), custom_call_target="tpu_custom_call" | custom-call | tf_op jit(solution)/shard_map/prepare/pallas_call | solution.py:271
  34.3 4.2 %collective-permute-done.1 = bf16[4,32,16,128]{3,2,1,0:T(8,128)(2,1)S(1)} collective-permute-done((bf16[4,32,16,128]{3,2,1,0:T(8,128)(2,1)S(1)}, bf16[4,32,16,128]{3,2,1,0:T(8,128)(2,1)S(1)}, u32[]{:S(2)}, u32[]{:S(2)}) %collective-permute-start.1) | collective-permute-done | bytes 524320 | tf_op jit(solution)/shard_map/ppermute | solution.py:30
  38.5 0.5 collective-permute-start.4
  39.0 0.2 collective-permute-start.5
  39.2 0.3 collective-permute-start.6
  39.5 8.1 %collective-permute-done.4 = bf16[4,32,16,128]{3,2,1,0:T(8,128)(2,1)S(1)} collective-permute-done((bf16[4,32,16,128]{3,2,1,0:T(8,128)(2,1)S(1)}, bf16[4,32,16,128]{3,2,1,0:T(8,128)(2,1)S(1)}, u32[]{:S(2)}, u32[]{:S(2)}) %collective-permute-start.4) | collective-permute-done | bytes 524320 | tf_op jit(solution)/shard_map/ppermute | solution.py:30
  48.2 1.4 %collective-permute-done.7 = bf16[4,32,16,128]{3,2,1,0:T(8,128)(2,1)S(1)} collective-permute-done((bf16[4,32,16,128]{3,2,1,0:T(8,128)(2,1)S(1)}, bf16[4,32,16,128]{3,2,1,0:T(8,128)(2,1)S(1)}, u32[]{:S(2)}, u32[]{:S(2)}) %collective-permute-start.7) | collective-permute-done | bytes 524320 | tf_op jit(solution)/shard_map/ppermute | solution.py:21
  49.7 5.8 %apply.1 = (bf16[32,4096]{1,0:T(8,128)(2,1)S(1)}, f32[16,128]{1,0:T(8,128)S(1)}) custom-call(s32[64,8]{1,0:T(8,128)S(1)} %get-tuple-element.33.rows_ref, bf16[64,8,64,128]{3,2,1,0:T(8,128)(2,1)S(1)} %get-tuple-element.34.ham_ref, bf16[1024,16,128]{2,1,0:T(8,128)(2,1)S(1)} %bitcast.9, bf16[64,4096]{1,0:T(8,128)(2,1)S(1)} %get-tuple-element.44.zhm_ref, ...), custom_call_target="tpu_custom_call" | custom-call | tf_op jit(solution)/shard_map/apply/pallas_call | solution.py:295
  55.4 0.1 collective-permute-start.8
  55.6 1.0 %collective-permute-done.8 = f32[16,128]{1,0:T(8,128)S(1)} collective-permute-done((f32[16,128]{1,0:T(8,128)S(1)}, f32[16,128]{1,0:T(8,128)S(1)}, u32[]{:S(2)}, u32[]{:S(2)}) %collective-permute-start.8) | collective-permute-done | bytes 8224 | tf_op jit(solution)/shard_map/ppermute | solution.py:21
  56.6 1.5 %collective-permute-start.10 = (f32[16,128]{1,0:T(8,128)S(1)}, f32[16,128]{1,0:T(8,128)S(1)}, u32[]{:S(2)}, u32[]{:S(2)}) collective-permute-start(f32[16,128]{1,0:T(8,128)S(1)} %add.41), channel_id=1, source_target_pairs={{0,2},{1,19},{2,0},{3,17},{4,6},{5,23},{6,4},{7,21},{8,10},{9,27},... | collective-permute-start | bytes 24584 | tf_op jit(solution)/shard_map/ppermute | solution.py:215
  58.1 0.5 collective-permute-start.11
  58.6 1.5 %collective-permute-start.12 = (f32[16,128]{1,0:T(8,128)S(1)}, f32[16,128]{1,0:T(8,128)S(1)}, u32[]{:S(2)}, u32[]{:S(2)}) collective-permute-start(f32[16,128]{1,0:T(8,128)S(1)} %add.41), channel_id=1, source_target_pairs={{0,6},{1,23},{2,4},{3,21},{4,2},{5,19},{6,0},{7,17},{8,14},{9,31},... | collective-permute-start | bytes 24584 | tf_op jit(solution)/shard_map/ppermute | solution.py:215
  60.1 2.9 %collective-permute-start.14 = (f32[16,128]{1,0:T(8,128)S(1)}, f32[16,128]{1,0:T(8,128)S(1)}, u32[]{:S(2)}, u32[]{:S(2)}) collective-permute-start(f32[16,128]{1,0:T(8,128)S(1)} %add.41), channel_id=1, source_target_pairs={{0,10},{1,27},{2,8},{3,25},{4,14},{5,31},{6,12},{7,29},{8,2},{9,19... | collective-permute-start | bytes 24584 | tf_op jit(solution)/shard_map/ppermute | solution.py:215
  63.1 2.9 %collective-permute-start.16 = (f32[16,128]{1,0:T(8,128)S(1)}, f32[16,128]{1,0:T(8,128)S(1)}, u32[]{:S(2)}, u32[]{:S(2)}) collective-permute-start(f32[16,128]{1,0:T(8,128)S(1)} %add.41), channel_id=1, source_target_pairs={{0,14},{1,31},{2,12},{3,29},{4,10},{5,27},{6,8},{7,25},{8,6},{9,23... | collective-permute-start | bytes 24584 | tf_op jit(solution)/shard_map/ppermute | solution.py:215
  66.0 0.7 collective-permute-start.9
  66.7 1.0 %collective-permute-done.15 = f32[16,128]{1,0:T(8,128)S(1)} collective-permute-done((f32[16,128]{1,0:T(8,128)S(1)}, f32[16,128]{1,0:T(8,128)S(1)}, u32[]{:S(2)}, u32[]{:S(2)}) %collective-permute-start.15) | collective-permute-done | bytes 8224 | tf_op jit(solution)/shard_map/ppermute | solution.py:215
  67.6 1.0 %collective-permute-done.16 = f32[16,128]{1,0:T(8,128)S(1)} collective-permute-done((f32[16,128]{1,0:T(8,128)S(1)}, f32[16,128]{1,0:T(8,128)S(1)}, u32[]{:S(2)}, u32[]{:S(2)}) %collective-permute-start.16) | collective-permute-done | bytes 8224 | tf_op jit(solution)/shard_map/ppermute | solution.py:215
  68.6 6.1 %collective-permute-start.17 = (f32[16,128]{1,0:T(8,128)S(1)}, f32[16,128]{1,0:T(8,128)S(1)}, u32[]{:S(2)}, u32[]{:S(2)}) collective-permute-start(f32[16,128]{1,0:T(8,128)S(1)} %add_add_fusion), channel_id=1, source_target_pairs={{0,1},{1,0},{2,3},{3,2},{4,5},{5,4},{6,7},{7,6},{8,9},{9,8},{10,11... | collective-permute-start | bytes 24584 | tf_op jit(solution)/shard_map/ppermute | solution.py:21
  74.7 0.8 %collective-permute-done.17 = f32[16,128]{1,0:T(8,128)S(1)} collective-permute-done((f32[16,128]{1,0:T(8,128)S(1)}, f32[16,128]{1,0:T(8,128)S(1)}, u32[]{:S(2)}, u32[]{:S(2)}) %collective-permute-start.17) | collective-permute-done | bytes 8224 | tf_op jit(solution)/shard_map/ppermute | solution.py:21
  75.5 3.0 %finish.1 = (f32[64,16,64]{2,1,0:T(8,128)}, f32[1,16]{1,0:T(1,128)}) custom-call(f32[16,128]{1,0:T(8,128)S(1)} %add.49.sums_ref, bf16[32,4096]{1,0:T(8,128)(2,1)S(1)} %get-tuple-element.49.az_ref, bf16[64,4096]{1,0:T(8,128)(2,1)S(1)} %get-tuple-element.44.zhm_ref), custom_call_target="tpu_custom_call" | custom-call | tf_op jit(solution)/shard_map/finish/pallas_call | solution.py:309
  (31 shorter events, 0.7 us)
Async XLA Ops:
  1.7 1.5 %collective-permute-start = (bf16[32,16,64]{2,1,0:T(8,128)(2,1)S(1)}, bf16[32,16,64]{2,1,0:T(8,128)(2,1)S(1)}, u32[]{:S(2)}, u32[]{:S(2)}) collective-permute-start(bf16[32,16,64]{2,1,0:T(8,128)(2,1)S(1)} %dynamic-slice_bitcast_fusion), channel_id=1, source_target_pairs={{0,1},{1,0},{2,3},{3,2},{4,5},{5,4},{6,7},{7,6},{8,9},{9,8},{10,11... | collective-permute-start | bytes 196616 | tf_op jit(solution)/shard_map/ppermute | solution.py:21
  24.3 14.2 %collective-permute-start.1 = (bf16[4,32,16,128]{3,2,1,0:T(8,128)(2,1)S(1)}, bf16[4,32,16,128]{3,2,1,0:T(8,128)(2,1)S(1)}, u32[]{:S(2)}, u32[]{:S(2)}) collective-permute-start(bf16[4,32,16,128]{3,2,1,0:T(8,128)(2,1)S(1)} %all_to_all.5), channel_id=1, source_target_pairs={{0,2},{1,5},{2,0},{3,7},{4,6},{5,1},{6,4},{7,3},{8,10},{9,13},{10,... | collective-permute-start | bytes 1572872 | tf_op jit(solution)/shard_map/ppermute | solution.py:30
  25.8 12.7 %collective-permute-start.2 = (bf16[4,32,16,128]{3,2,1,0:T(8,128)(2,1)S(1)}, bf16[4,32,16,128]{3,2,1,0:T(8,128)(2,1)S(1)}, u32[]{:S(2)}, u32[]{:S(2)}) collective-permute-start(bf16[4,32,16,128]{3,2,1,0:T(8,128)(2,1)S(1)} %all_to_all.5), channel_id=1, source_target_pairs={{0,4},{1,3},{2,6},{3,1},{4,0},{5,7},{6,2},{7,5},{8,12},{9,11},{10,... | collective-permute-start | bytes 1572872 | tf_op jit(solution)/shard_map/ppermute | solution.py:30
  27.3 11.2 %collective-permute-start.3 = (bf16[4,32,16,128]{3,2,1,0:T(8,128)(2,1)S(1)}, bf16[4,32,16,128]{3,2,1,0:T(8,128)(2,1)S(1)}, u32[]{:S(2)}, u32[]{:S(2)}) collective-permute-start(bf16[4,32,16,128]{3,2,1,0:T(8,128)(2,1)S(1)} %all_to_all.5), channel_id=1, source_target_pairs={{0,1},{1,0},{2,3},{3,2},{4,5},{5,4},{6,7},{7,6},{8,9},{9,8},{10,11... | collective-permute-start | bytes 1572872 | tf_op jit(solution)/shard_map/ppermute | solution.py:21
  28.1 1.0 %copy-start = (f32[64,16,64]{2,1,0:T(8,128)S(1)}, f32[64,16,64]{2,1,0:T(8,128)}, u32[]{:S(2)}) copy-start(f32[64,16,64]{2,1,0:T(8,128)} %t_ref) | copy-start | bytes 786436
  29.1 0.8 copy-start.1
  29.9 0.7 copy-start.2
  38.5 9.2 %collective-permute-start.4 = (bf16[4,32,16,128]{3,2,1,0:T(8,128)(2,1)S(1)}, bf16[4,32,16,128]{3,2,1,0:T(8,128)(2,1)S(1)}, u32[]{:S(2)}, u32[]{:S(2)}) collective-permute-start(bf16[4,32,16,128]{3,2,1,0:T(8,128)(2,1)S(1)} %collective-permute-done.1), channel_id=1, source_target_pairs={{0,4},{1,3},{2,6},{3,1},{4,0},{5,7},{6,2},{7,5},{8,12},{9,11},{10,... | collective-permute-start | bytes 1572872 | tf_op jit(solution)/shard_map/ppermute | solution.py:30
  39.0 8.7 %collective-permute-start.5 = (bf16[4,32,16,128]{3,2,1,0:T(8,128)(2,1)S(1)}, bf16[4,32,16,128]{3,2,1,0:T(8,128)(2,1)S(1)}, u32[]{:S(2)}, u32[]{:S(2)}) collective-permute-start(bf16[4,32,16,128]{3,2,1,0:T(8,128)(2,1)S(1)} %collective-permute-done.1), channel_id=1, source_target_pairs={{0,1},{1,0},{2,3},{3,2},{4,5},{5,4},{6,7},{7,6},{8,9},{9,8},{10,11... | collective-permute-start | bytes 1572872 | tf_op jit(solution)/shard_map/ppermute | solution.py:21
  39.2 8.4 %collective-permute-start.6 = (bf16[4,32,16,128]{3,2,1,0:T(8,128)(2,1)S(1)}, bf16[4,32,16,128]{3,2,1,0:T(8,128)(2,1)S(1)}, u32[]{:S(2)}, u32[]{:S(2)}) collective-permute-start(bf16[4,32,16,128]{3,2,1,0:T(8,128)(2,1)S(1)} %collective-permute-done.2), channel_id=1, source_target_pairs={{0,1},{1,0},{2,3},{3,2},{4,5},{5,4},{6,7},{7,6},{8,9},{9,8},{10,11... | collective-permute-start | bytes 1572872 | tf_op jit(solution)/shard_map/ppermute | solution.py:21
  47.7 1.9 %collective-permute-start.7 = (bf16[4,32,16,128]{3,2,1,0:T(8,128)(2,1)S(1)}, bf16[4,32,16,128]{3,2,1,0:T(8,128)(2,1)S(1)}, u32[]{:S(2)}, u32[]{:S(2)}) collective-permute-start(bf16[4,32,16,128]{3,2,1,0:T(8,128)(2,1)S(1)} %collective-permute-done.4), channel_id=1, source_target_pairs={{0,1},{1,0},{2,3},{3,2},{4,5},{5,4},{6,7},{7,6},{8,9},{9,8},{10,11... | collective-permute-start | bytes 1572872 | tf_op jit(solution)/shard_map/ppermute | solution.py:21
  55.4 1.2 %collective-permute-start.8 = (f32[16,128]{1,0:T(8,128)S(1)}, f32[16,128]{1,0:T(8,128)S(1)}, u32[]{:S(2)}, u32[]{:S(2)}) collective-permute-start(f32[16,128]{1,0:T(8,128)S(1)} %get-tuple-element.48), channel_id=1, source_target_pairs={{0,1},{1,0},{2,3},{3,2},{4,5},{5,4},{6,7},{7,6},{8,9},{9,8},{10,11... | collective-permute-start | bytes 24584 | tf_op jit(solution)/shard_map/ppermute | solution.py:21
  56.6 6.4 %collective-permute-start.10 = (f32[16,128]{1,0:T(8,128)S(1)}, f32[16,128]{1,0:T(8,128)S(1)}, u32[]{:S(2)}, u32[]{:S(2)}) collective-permute-start(f32[16,128]{1,0:T(8,128)S(1)} %add.41), channel_id=1, source_target_pairs={{0,2},{1,19},{2,0},{3,17},{4,6},{5,23},{6,4},{7,21},{8,10},{9,27},... | collective-permute-start | bytes 24584 | tf_op jit(solution)/shard_map/ppermute | solution.py:215
  58.1 5.0 %collective-permute-start.11 = (f32[16,128]{1,0:T(8,128)S(1)}, f32[16,128]{1,0:T(8,128)S(1)}, u32[]{:S(2)}, u32[]{:S(2)}) collective-permute-start(f32[16,128]{1,0:T(8,128)S(1)} %add.41), channel_id=1, source_target_pairs={{0,4},{1,21},{2,6},{3,23},{4,0},{5,17},{6,2},{7,19},{8,12},{9,29},... | collective-permute-start | bytes 24584 | tf_op jit(solution)/shard_map/ppermute | solution.py:215
  58.6 7.4 %collective-permute-start.12 = (f32[16,128]{1,0:T(8,128)S(1)}, f32[16,128]{1,0:T(8,128)S(1)}, u32[]{:S(2)}, u32[]{:S(2)}) collective-permute-start(f32[16,128]{1,0:T(8,128)S(1)} %add.41), channel_id=1, source_target_pairs={{0,6},{1,23},{2,4},{3,21},{4,2},{5,19},{6,0},{7,17},{8,14},{9,31},... | collective-permute-start | bytes 24584 | tf_op jit(solution)/shard_map/ppermute | solution.py:215
  60.1 6.5 %collective-permute-start.13 = (f32[16,128]{1,0:T(8,128)S(1)}, f32[16,128]{1,0:T(8,128)S(1)}, u32[]{:S(2)}, u32[]{:S(2)}) collective-permute-start(f32[16,128]{1,0:T(8,128)S(1)} %add.41), channel_id=1, source_target_pairs={{0,8},{1,25},{2,10},{3,27},{4,12},{5,29},{6,14},{7,31},{8,0},{9,17... | collective-permute-start | bytes 24584 | tf_op jit(solution)/shard_map/ppermute | solution.py:215
  60.1 6.5 %collective-permute-start.14 = (f32[16,128]{1,0:T(8,128)S(1)}, f32[16,128]{1,0:T(8,128)S(1)}, u32[]{:S(2)}, u32[]{:S(2)}) collective-permute-start(f32[16,128]{1,0:T(8,128)S(1)} %add.41), channel_id=1, source_target_pairs={{0,10},{1,27},{2,8},{3,25},{4,14},{5,31},{6,12},{7,29},{8,2},{9,19... | collective-permute-start | bytes 24584 | tf_op jit(solution)/shard_map/ppermute | solution.py:215
  63.1 4.6 %collective-permute-start.15 = (f32[16,128]{1,0:T(8,128)S(1)}, f32[16,128]{1,0:T(8,128)S(1)}, u32[]{:S(2)}, u32[]{:S(2)}) collective-permute-start(f32[16,128]{1,0:T(8,128)S(1)} %add.41), channel_id=1, source_target_pairs={{0,12},{1,29},{2,14},{3,31},{4,8},{5,25},{6,10},{7,27},{8,4},{9,21... | collective-permute-start | bytes 24584 | tf_op jit(solution)/shard_map/ppermute | solution.py:215
  63.1 5.5 %collective-permute-start.16 = (f32[16,128]{1,0:T(8,128)S(1)}, f32[16,128]{1,0:T(8,128)S(1)}, u32[]{:S(2)}, u32[]{:S(2)}) collective-permute-start(f32[16,128]{1,0:T(8,128)S(1)} %add.41), channel_id=1, source_target_pairs={{0,14},{1,31},{2,12},{3,29},{4,10},{5,27},{6,8},{7,25},{8,6},{9,23... | collective-permute-start | bytes 24584 | tf_op jit(solution)/shard_map/ppermute | solution.py:215
  66.0 2.6 %collective-permute-start.9 = (f32[16,128]{1,0:T(8,128)S(1)}, f32[16,128]{1,0:T(8,128)S(1)}, u32[]{:S(2)}, u32[]{:S(2)}) collective-permute-start(f32[16,128]{1,0:T(8,128)S(1)} %add.41), channel_id=1, source_target_pairs={{1,17},{3,19},{5,21},{7,23},{9,25},{11,27},{13,29},{15,31},{17,1},... | collective-permute-start | bytes 24584 | tf_op jit(solution)/shard_map/ppermute | solution.py:215
  68.6 6.9 %collective-permute-start.17 = (f32[16,128]{1,0:T(8,128)S(1)}, f32[16,128]{1,0:T(8,128)S(1)}, u32[]{:S(2)}, u32[]{:S(2)}) collective-permute-start(f32[16,128]{1,0:T(8,128)S(1)} %add_add_fusion), channel_id=1, source_target_pairs={{0,1},{1,0},{2,3},{3,2},{4,5},{5,4},{6,7},{7,6},{8,9},{9,8},{10,11... | collective-permute-start | bytes 24584 | tf_op jit(solution)/shard_map/ppermute | solution.py:21

commit v8 on v7

--- a/solution.py
+++ b/solution.py
@@ -28,6 +28,13 @@
         for r in range(n_rad):
             pairs.append((c * n_rad + r, (c ^ order[r % 2]) * n_rad + r))
     return lax.ppermute(x, ("chan", "rad"), pairs)
+
+
+def table_piece(z, part, nz):
+    z = z if nz == 4 else jnp.where(z < 2, z, jnp.where((z & 1) == 1, (nz + z - 1) >> 1, 1 + (z >> 1)))
+    near = jnp.where(z == 0, nz, nz + 2 + z)
+    far = (part & 1) + jnp.where(z == 0, nz + 1, 2 * nz + 1 + z + (part & 1) * (nz - 2))
+    return jnp.where(part == 0, z, jnp.where(part == 1, near, far))
 
 
 def in_vmem(x):
@@ -80,7 +87,8 @@
     core = lax.div(local, share)
     apart = (owner ^ lax.axis_index("chan")) & 3
     part = jnp.where((core & 1) == 1, ((apart & 1) << 1) | (apart >> 1), apart)
-    place = ((core ^ lax.axis_index("rad")) * 4 + part) * nz + (owner >> 2)
+    piece = table_piece((owner ^ lax.axis_index("chan")) >> 2, part, nz)
+    place = (core ^ lax.axis_index("rad")) * 4 * nz + piece
     place = (place * share + lax.rem(local, share)).astype(F32)
     lane = lax.broadcasted_iota(jnp.int32, (ch, 128), 1)
     columns = []
@@ -146,7 +154,7 @@
 
 def finish_kernel(total, sums_ref, az_ref, zhm_ref, out_ref, ritz_ref):
     ch, k, r = out_ref.shape
-    s = sums_ref[...]
+    s = jnp.sum(sums_ref[...], axis=0)
     row = lax.broadcasted_iota(jnp.int32, (k, 128), 0)
     cols = [spread(s, 2 * k + i) for i in range(k)]
     x = s
@@ -197,26 +205,14 @@
     lax.fori_loop(0, ch * r // block, result, 0)
 
 
-def sum_everywhere(x):
+def gather_sums(x):
     n_chan, n_rad = lax.axis_size("chan"), lax.axis_size("rad")
     step = 1
     while step < n_rad:
         x = x + swap(x, "rad", step)
         step *= 2
-    half = n_chan // 2
-    parts = []
-    for t in range(half):
-        pairs = []
-        for c in range(n_chan):
-            for r in range(n_rad):
-                distance = t + half * (r % 2)
-                if distance:
-                    pairs.append((c * n_rad + r, (c ^ distance) * n_rad + r))
-        parts.append(lax.ppermute(x, ("chan", "rad"), pairs))
-    parts[0] = jnp.where(lax.axis_index("rad") % 2 == 0, x, parts[0])
-    while len(parts) > 1:
-        parts = [parts[i] + parts[i + 1] for i in range(0, len(parts), 2)]
-    return parts[0] + swap(parts[0], "rad", 1)
+    every = jnp.broadcast_to(x, (n_chan,) + x.shape)
+    return lax.all_to_all(every, "chan", split_axis=0, concat_axis=0, tiled=True)
 
 
 def own_share(trial_block):
@@ -250,23 +246,35 @@
     any_ = pl.BlockSpec(memory_space=pl.ANY)
     whole = pl.BlockSpec(memory_space=pltpu.VMEM)
 
+    def near_of(x):
+        return plane_swap(x, (1, 2))
+
+    def far_of(x, near):
+        return plane_swap(jnp.concatenate([x, near]), (2, 1))
+
     def in_cores(x):
         return [x] + [swap(x, "rad", c) for c in range(1, n_rad)]
 
-    own = own_share(trial_block)
-    column = lax.all_to_all(
-        jnp.broadcast_to(own, (nz,) + own.shape),
-        "chan",
-        split_axis=0,
-        concat_axis=0,
-        axis_index_groups=[[i + 4 * z for z in range(nz)] for i in range(4)],
-        tiled=True,
-    )
-    near = plane_swap(column, (1, 2))
-    far = plane_swap(column, (2, 1))
-    columns = in_cores(column)
+    own = own_share(trial_block)[None]
+    z_even = jnp.concatenate([swap(own, "chan", 4 * z) for z in range(2, nz, 2)])
+    z1 = swap(own, "chan", 4)
+    near0 = near_of(own)
+    z_even, z1, near0 = barrier((z_even, z1, near0))
+    some = jnp.concatenate([z1, z_even])
+    near1 = near_of(some)
+    far0 = far_of(own, near0)
+    z_odd = swap(z_even, "chan", 4)
+    z_odd, near1, far0 = barrier((z_odd, near1, far0))
+    near2 = near_of(z_odd)
+    here = jnp.concatenate([some, z_odd])
+    early1 = jnp.concatenate([own, here, near0])
+    near2, near1, far0, here, early1 = barrier((near2, near1, far0, here, early1))
+    near = jnp.concatenate([near1, near2])
+    far = far_of(here, near)
+    early1, early2 = in_cores(early1), in_cores(jnp.concatenate([far0, near]))
+
     inputs = (trial_block, precond_diag, partners, stored_at, ham_blocks)
-    inputs, _ = barrier((inputs, column))
+    inputs, _ = barrier((inputs, near2))
     trial_block, precond_diag, partners, stored_at, ham_blocks = inputs
     ham, rows, zhm, zl, dc, gram_t = pl.pallas_call(
         functools.partial(prepare_kernel, n_chan, n_rad),
@@ -284,12 +292,8 @@
         compiler_params=pltpu.CompilerParams(vmem_limit_bytes=VMEM_LIMIT),
         name="prepare",
     )(trial_block, precond_diag, partners, stored_at.reshape(-1, 128), in_hbm(ham_blocks))
-    near, far, columns, rows = barrier((near, far, columns, rows))
-    both = plane_swap(near, (2, 1))
-    nears, fars = in_cores(near), in_cores(far)
-    both, nears, fars = barrier((both, nears, fars))
-    boths = in_cores(both)
-    table = jnp.concatenate([x for four in zip(columns, nears, fars, boths) for x in four])
+    far, early1, early2, rows = barrier((far, early1, early2, rows))
+    table = jnp.concatenate([x for three in zip(early1, early2, in_cores(far)) for x in three])
     table = table.reshape(n_chan * ch, k, splines)
 
     az, sums = pl.pallas_call(
@@ -305,7 +309,7 @@
         name="apply",
     )(rows, in_vmem(ham), in_vmem(table), in_vmem(zhm), in_vmem(zl), in_vmem(dc), gram_t)
 
-    sums = sum_everywhere(sums)
+    sums = gather_sums(sums)
     new_block, ritz = pl.pallas_call(
         functools.partial(finish_kernel, total),
         out_shape=[

time: 79 us -> 68.2 us (0.86)
  blocking collectives: 20.8 us -> 14.2 us
  starting transfers between devices: 20.8 us -> 15.8 us
  waiting for transfers between devices: 18.6 us -> 19.9 us
    ppermute x8 -> x0, starting transfers between devices: 9.99 us -> none  [sum_everywhere(): parts.append(lax.ppermute(x, ('chan', 'rad'), pairs))]
    all_to_all x1, blocking collectives: 20.8 us -> 14.2 us  [gather_sums(): lax.all_to_all(every, 'chan', split_axis=0, concat_axis=0, tiled=True)]
    ppermute x7 -> x8, waiting for transfers between devices: 4.3 us -> 9.15 us  [swap(): return lax.ppermute(x, axis, [(i, i ^ distance) for i in range(n)])]
    ppermute x3 -> x5, starting transfers between devices: 3.52 us -> 7.2 us  [plane_swap(): return lax.ppermute(x, ('chan', 'rad'), pairs)]
    ppermute x8 -> x0, waiting for transfers between devices: 1.94 us -> none  [sum_everywhere(): parts.append(lax.ppermute(x, ('chan', 'rad'), pairs))]
    ppermute x3 -> x5, waiting for transfers between devices: 12.3 us -> 10.7 us  [plane_swap(): return lax.ppermute(x, ('chan', 'rad'), pairs)]
    ppermute x7 -> x8, starting transfers between devices: 7.26 us -> 8.64 us  [swap(): return lax.ppermute(x, axis, [(i, i ^ distance) for i in range(n)])]
    unnamed x13 -> x18, local copies, waits for them, and re-layouts: 2.94 us -> 3.07 us
  transfers between devices with their start and end apart: 18 -> 13, of which waited for: 8 -> 8; matrix products, arithmetic and copies ran while one was open for 2% -> 5% of each run, Pallas kernels for 5% -> 5%
where the time goes in v8:
time: 68.2 us; the launch traced here: 67.9 us
  waiting for transfers between devices  19.9 us (29%)
  starting transfers between devices  15.8 us (23%)
  blocking collectives  14.2 us (21%)
  Pallas kernels  12.2 us (18%)
  local copies, waits for them, and re-layouts  3.41 us (5%)
  other arithmetic  1.46 us (2%)
  between operations  0.85 us (1%)
    all_to_all x1, blocking collectives, gather_sums(): lax.all_to_all(every, 'chan', split_axis=0, concat_axis=0, tiled=True)  14.2 us
    ppermute x5, waiting for transfers between devices, plane_swap(): return lax.ppermute(x, ('chan', 'rad'), pairs)  10.7 us
    ppermute x8, waiting for transfers between devices, swap(): return lax.ppermute(x, axis, [(i, i ^ distance) for i in range(n)])  9.15 us
    ppermute x8, starting transfers between devices, swap(): return lax.ppermute(x, axis, [(i, i ^ distance) for i in range(n)])  8.64 us
    ppermute x5, starting transfers between devices, plane_swap(): return lax.ppermute(x, ('chan', 'rad'), pairs)  7.2 us
    pallas_call x1, Pallas kernels, body(): pl.pallas_call(apply_kernel, in_specs=[smem] + [whole] * 6, out_specs=[wh...  5.78 us
    pallas_call x1, Pallas kernels, body(): pl.pallas_call(functools.partial(prepare_kernel, n_chan, n_rad), in_specs...  3.4 us
    unnamed x18, local copies, waits for them, and re-layouts  3.07 us
  transfers between devices with their start and end apart: 13, of which 8 were waited for; matrix products, arithmetic and copies ran while one was open for 5% of the time, Pallas kernels for 5%

profile of v8, /device:TPU:0, one launch (start us, length us, event | category | flops | bytes accessed | tf_op | source)
XLA Modules:
  0.0 67.9 jit_solution(10559672782151210666)
XLA Ops:
  0.7 1.1 %convert_element_type.3 = bf16[64,16,64]{2,1,0:T(8,128)(2,1)S(1)} convert(f32[64,16,64]{2,1,0:T(8,128)} %t_ref) | non-fusion elementwise | flops 65536 | bytes 393216 | tf_op jit(solution)/shard_map/convert_element_type | solution.py:222
  1.8 0.5 collective-permute-start
  2.4 1.0 %collective-permute-done = bf16[32,16,64]{2,1,0:T(8,128)(2,1)S(1)} collective-permute-done((bf16[32,16,64]{2,1,0:T(8,128)(2,1)S(1)}, bf16[32,16,64]{2,1,0:T(8,128)(2,1)S(1)}, u32[]{:S(2)}, u32[]{:S(2)}) %collective-permute-start) | collective-permute-done | bytes 65568 | tf_op jit(solution)/shard_map/ppermute | solution.py:21
  3.4 0.1 constant_dynamic-update-slice_fusion.4
  3.5 4.0 %collective-permute-start.1 = (bf16[1,32,16,128]{3,2,1,0:T(8,128)(2,1)S(1)}, bf16[1,32,16,128]{3,2,1,0:T(8,128)(2,1)S(1)}, u32[]{:S(2)}, u32[]{:S(2)}) collective-permute-start(bf16[1,32,16,128]{3,2,1,0:T(8,128)(2,1)S(1)} %get-tuple-element.67), channel_id=1, source_target_pairs={{0,16},{2,18},{4,20},{6,22},{8,24},{10,26},{12,28},{14,30},{16,0},... | collective-permute-start | bytes 393224 | tf_op jit(solution)/shard_map/ppermute | solution.py:21
  7.5 1.6 %collective-permute-start.2 = (bf16[1,32,16,128]{3,2,1,0:T(8,128)(2,1)S(1)}, bf16[1,32,16,128]{3,2,1,0:T(8,128)(2,1)S(1)}, u32[]{:S(2)}, u32[]{:S(2)}) collective-permute-start(bf16[1,32,16,128]{3,2,1,0:T(8,128)(2,1)S(1)} %get-tuple-element.67), channel_id=1, source_target_pairs={{0,8},{2,10},{4,12},{6,14},{8,0},{10,2},{12,4},{14,6},{16,24},{18,... | collective-permute-start | bytes 393224 | tf_op jit(solution)/shard_map/ppermute | solution.py:21
  9.1 1.5 %collective-permute-start.3 = (bf16[1,32,16,128]{3,2,1,0:T(8,128)(2,1)S(1)}, bf16[1,32,16,128]{3,2,1,0:T(8,128)(2,1)S(1)}, u32[]{:S(2)}, u32[]{:S(2)}) collective-permute-start(bf16[1,32,16,128]{3,2,1,0:T(8,128)(2,1)S(1)} %get-tuple-element.67), channel_id=1, source_target_pairs={{0,2},{1,5},{2,0},{3,7},{4,6},{5,1},{6,4},{7,3},{8,10},{9,13},{10,... | collective-permute-start | bytes 393224 | tf_op jit(solution)/shard_map/ppermute | solution.py:30
  10.6 3.7 %collective-permute-done.1 = bf16[1,32,16,128]{3,2,1,0:T(8,128)(2,1)S(1)} collective-permute-done((bf16[1,32,16,128]{3,2,1,0:T(8,128)(2,1)S(1)}, bf16[1,32,16,128]{3,2,1,0:T(8,128)(2,1)S(1)}, u32[]{:S(2)}, u32[]{:S(2)}) %collective-permute-start.1) | collective-permute-done | bytes 131104 | tf_op jit(solution)/shard_map/ppermute | solution.py:21
  14.2 0.2 collective-permute-done.2
  14.4 1.6 %collective-permute-start.6 = (bf16[2,32,16,128]{3,2,1,0:T(8,128)(2,1)S(1)}, bf16[2,32,16,128]{3,2,1,0:T(8,128)(2,1)S(1)}, u32[]{:S(2)}, u32[]{:S(2)}) collective-permute-start(bf16[2,32,16,128]{3,2,1,0:T(8,128)(2,1)S(1)} %pad_maximum_fusion.3), channel_id=1, source_target_pairs={{0,4},{1,3},{2,6},{3,1},{4,0},{5,7},{6,2},{7,5},{8,12},{9,11},{10,... | collective-permute-start | bytes 786440 | tf_op jit(solution)/shard_map/ppermute | solution.py:30
  16.1 1.6 %collective-permute-start.5 = (bf16[2,32,16,128]{3,2,1,0:T(8,128)(2,1)S(1)}, bf16[2,32,16,128]{3,2,1,0:T(8,128)(2,1)S(1)}, u32[]{:S(2)}, u32[]{:S(2)}) collective-permute-start(bf16[2,32,16,128]{3,2,1,0:T(8,128)(2,1)S(1)} %pad_maximum_fusion.2), channel_id=1, source_target_pairs={{0,2},{1,5},{2,0},{3,7},{4,6},{5,1},{6,4},{7,3},{8,10},{9,13},{10,... | collective-permute-start | bytes 786440 | tf_op jit(solution)/shard_map/ppermute | solution.py:30
  17.7 1.4 %collective-permute-start.4 = (bf16[1,32,16,128]{3,2,1,0:T(8,128)(2,1)S(1)}, bf16[1,32,16,128]{3,2,1,0:T(8,128)(2,1)S(1)}, u32[]{:S(2)}, u32[]{:S(2)}) collective-permute-start(bf16[1,32,16,128]{3,2,1,0:T(8,128)(2,1)S(1)} %collective-permute-done.1), channel_id=1, source_target_pairs={{0,8},{2,10},{4,12},{6,14},{8,0},{10,2},{12,4},{14,6},{16,24},{18,... | collective-permute-start | bytes 393224 | tf_op jit(solution)/shard_map/ppermute | solution.py:21
  19.2 3.5 %collective-permute-done.4 = bf16[1,32,16,128]{3,2,1,0:T(8,128)(2,1)S(1)} collective-permute-done((bf16[1,32,16,128]{3,2,1,0:T(8,128)(2,1)S(1)}, bf16[1,32,16,128]{3,2,1,0:T(8,128)(2,1)S(1)}, u32[]{:S(2)}, u32[]{:S(2)}) %collective-permute-start.4) | collective-permute-done | bytes 131104 | tf_op jit(solution)/shard_map/ppermute | solution.py:21
  22.6 0.5 collective-permute-done.6
  23.1 0.9 %collective-permute-start.7 = (bf16[1,32,16,128]{3,2,1,0:T(8,128)(2,1)S(1)}, bf16[1,32,16,128]{3,2,1,0:T(8,128)(2,1)S(1)}, u32[]{:S(2)}, u32[]{:S(2)}) collective-permute-start(bf16[1,32,16,128]{3,2,1,0:T(8,128)(2,1)S(1)} %collective-permute-done.4), channel_id=1, source_target_pairs={{0,2},{1,5},{2,0},{3,7},{4,6},{5,1},{6,4},{7,3},{8,10},{9,13},{10,... | collective-permute-start | bytes 393224 | tf_op jit(solution)/shard_map/ppermute | solution.py:30
  24.1 3.9 %collective-permute-done.7 = bf16[1,32,16,128]{3,2,1,0:T(8,128)(2,1)S(1)} collective-permute-done((bf16[1,32,16,128]{3,2,1,0:T(8,128)(2,1)S(1)}, bf16[1,32,16,128]{3,2,1,0:T(8,128)(2,1)S(1)}, u32[]{:S(2)}, u32[]{:S(2)}) %collective-permute-start.7) | collective-permute-done | bytes 131104 | tf_op jit(solution)/shard_map/ppermute | solution.py:30
  28.1 0.1 pad_maximum_fusion
  28.2 1.6 %collective-permute-start.8 = (bf16[6,32,16,128]{3,2,1,0:T(8,128)(2,1)S(1)}, bf16[6,32,16,128]{3,2,1,0:T(8,128)(2,1)S(1)}, u32[]{:S(2)}, u32[]{:S(2)}) collective-permute-start(bf16[6,32,16,128]{3,2,1,0:T(8,128)(2,1)S(1)} %pad_maximum_fusion), channel_id=1, source_target_pairs={{0,4},{1,3},{2,6},{3,1},{4,0},{5,7},{6,2},{7,5},{8,12},{9,11},{10,... | collective-permute-start | bytes 2359304 | tf_op jit(solution)/shard_map/ppermute | solution.py:30
  29.9 0.5 collective-permute-start.9
  30.5 3.4 %prepare.1 = (bf16[64,8,64,128]{3,2,1,0:T(8,128)(2,1)S(1)}, s32[64,8]{1,0:T(8,128)S(1)}, bf16[64,4096]{1,0:T(8,128)(2,1)S(1)}, bf16[32,4096]{1,0:T(8,128)(2,1)S(...) custom-call(f32[64,16,64]{2,1,0:T(8,128)S(1)} %copy-done, f32[64,64]{1,0:T(8,128)S(1)} %copy-done.1, ...), custom_call_target="tpu_custom_call" | custom-call | tf_op jit(solution)/shard_map/prepare/pallas_call | solution.py:279
  34.0 6.3 %collective-permute-done.8 = bf16[6,32,16,128]{3,2,1,0:T(8,128)(2,1)S(1)} collective-permute-done((bf16[6,32,16,128]{3,2,1,0:T(8,128)(2,1)S(1)}, bf16[6,32,16,128]{3,2,1,0:T(8,128)(2,1)S(1)}, u32[]{:S(2)}, u32[]{:S(2)}) %collective-permute-start.8) | collective-permute-done | bytes 786464 | tf_op jit(solution)/shard_map/ppermute | solution.py:30
  40.3 0.1 constant_dynamic-update-slice_fusion.13
  40.4 0.2 constant_dynamic-update-slice_fusion.12
  40.5 0.2 constant_dynamic-update-slice_fusion.11
  40.7 1.2 %constant_dynamic-update-slice_fusion.10 = bf16[32,32,16,128]{3,2,1,0:T(8,128)(2,1)S(1)} fusion(bf16[32,32,16,128]{3,2,1,0:T(8,128)(2,1)S(1)} %constant_dynamic-update-slice_fusion.11, bf16[5,32,16,128]{3,2,1,0:T(8,128)(2,1)} %collective-permute-done.9), kind=kLoop, calls=%fused_computation.18 | loop fusion | bytes 1310720
  42.0 1.2 %constant_dynamic-update-slice_fusion.9 = bf16[32,32,16,128]{3,2,1,0:T(8,128)(2,1)S(1)} fusion(bf16[32,32,16,128]{3,2,1,0:T(8,128)(2,1)S(1)} %constant_dynamic-update-slice_fusion.10, bf16[5,32,16,128]{3,2,1,0:T(8,128)(2,1)} %collective-permute-done.10), kind=kLoop, calls=%fused_computation.17 | loop fusion | bytes 1310720
  43.2 0.2 constant_dynamic-update-slice_fusion.8
  43.4 5.8 %apply.1 = (bf16[32,4096]{1,0:T(8,128)(2,1)S(1)}, f32[16,128]{1,0:T(8,128)S(1)}) custom-call(s32[64,8]{1,0:T(8,128)S(1)} %get-tuple-element.51.rows_ref, bf16[64,8,64,128]{3,2,1,0:T(8,128)(2,1)S(1)} %get-tuple-element.52.ham_ref, bf16[1024,16,128]{2,1,0:T(8,128)(2,1)S(1)} %bitcast.12, bf16[64,4096]{1,0:T(8,128)(2,1)S(1)} %get-tuple-element.58.zhm_ref, ...), custom_call_target="tpu_custom_call" | custom-call | tf_op jit(solution)/shard_map/apply/pallas_call | solution.py:299
  49.2 0.5 collective-permute-start.12
  49.8 0.8 %collective-permute-done.12 = f32[16,128]{1,0:T(8,128)S(1)} collective-permute-done((f32[16,128]{1,0:T(8,128)S(1)}, f32[16,128]{1,0:T(8,128)S(1)}, u32[]{:S(2)}, u32[]{:S(2)}) %collective-permute-start.12) | collective-permute-done | bytes 8224 | tf_op jit(solution)/shard_map/ppermute | solution.py:21
  50.6 14.2 %all_to_all.5.sums_ref = f32[16,16,128]{2,1,0:T(8,128)S(1)} all-to-all(f32[16,16,128]{2,1,0:T(8,128)S(1)} %broadcast_in_dim.7), channel_id=1, replica_groups=mesh['chan'=16,'rad'=2] {'chan'}, dimensions={0} | all-to-all | bytes 262144 | tf_op jit(solution)/shard_map/all_to_all | solution.py:215
  64.8 3.1 %finish.1 = (f32[64,16,64]{2,1,0:T(8,128)}, f32[1,16]{1,0:T(1,128)}) custom-call(f32[16,16,128]{2,1,0:T(8,128)S(1)} %all_to_all.5.sums_ref, bf16[32,4096]{1,0:T(8,128)(2,1)S(1)} %get-tuple-element.63.az_ref, bf16[64,4096]{1,0:T(8,128)(2,1)S(1)} %get-tuple-element.58.zhm_ref), custom_call_target="tpu_custom_call" | custom-call | tf_op jit(solution)/shard_map/finish/pallas_call | solution.py:313
  (30 shorter events, 0.5 us)
Async XLA Ops:
  0.6 29.9 %copy-start = (f32[64,16,64]{2,1,0:T(8,128)S(1)}, f32[64,16,64]{2,1,0:T(8,128)}, u32[]{:S(2)}) copy-start(f32[64,16,64]{2,1,0:T(8,128)} %t_ref) | copy-start | bytes 786436
  0.6 29.8 %copy-start.3 = (s32[64,8]{0,1:T(8,128)S(1)}, s32[64,8]{0,1:T(8,128)}, u32[]{:S(2)}) copy-start(s32[64,8]{0,1:T(8,128)} %param.7) | copy-start | bytes 6148
  0.7 29.9 %copy-start.2 = (s32[1024]{0:T(1024)S(1)}, s32[1024]{0:T(1024)}, u32[]{:S(2)}) copy-start(s32[1024]{0:T(1024)} %param.8) | copy-start | bytes 12292
  0.7 29.9 %copy-start.1 = (f32[64,64]{1,0:T(8,128)S(1)}, f32[64,64]{1,0:T(8,128)}, u32[]{:S(2)}) copy-start(f32[64,64]{1,0:T(8,128)} %d_ref) | copy-start | bytes 49156
  1.8 1.5 %collective-permute-start = (bf16[32,16,64]{2,1,0:T(8,128)(2,1)S(1)}, bf16[32,16,64]{2,1,0:T(8,128)(2,1)S(1)}, u32[]{:S(2)}, u32[]{:S(2)}) collective-permute-start(bf16[32,16,64]{2,1,0:T(8,128)(2,1)S(1)} %dynamic-slice_bitcast_fusion), channel_id=1, source_target_pairs={{0,1},{1,0},{2,3},{3,2},{4,5},{5,4},{6,7},{7,6},{8,9},{9,8},{10,11... | collective-permute-start | bytes 196616 | tf_op jit(solution)/shard_map/ppermute | solution.py:21
  3.5 10.7 %collective-permute-start.1 = (bf16[1,32,16,128]{3,2,1,0:T(8,128)(2,1)S(1)}, bf16[1,32,16,128]{3,2,1,0:T(8,128)(2,1)S(1)}, u32[]{:S(2)}, u32[]{:S(2)}) collective-permute-start(bf16[1,32,16,128]{3,2,1,0:T(8,128)(2,1)S(1)} %get-tuple-element.67), channel_id=1, source_target_pairs={{0,16},{2,18},{4,20},{6,22},{8,24},{10,26},{12,28},{14,30},{16,0},... | collective-permute-start | bytes 393224 | tf_op jit(solution)/shard_map/ppermute | solution.py:21
  7.5 6.9 %collective-permute-start.2 = (bf16[1,32,16,128]{3,2,1,0:T(8,128)(2,1)S(1)}, bf16[1,32,16,128]{3,2,1,0:T(8,128)(2,1)S(1)}, u32[]{:S(2)}, u32[]{:S(2)}) collective-permute-start(bf16[1,32,16,128]{3,2,1,0:T(8,128)(2,1)S(1)} %get-tuple-element.67), channel_id=1, source_target_pairs={{0,8},{2,10},{4,12},{6,14},{8,0},{10,2},{12,4},{14,6},{16,24},{18,... | collective-permute-start | bytes 393224 | tf_op jit(solution)/shard_map/ppermute | solution.py:21
  9.1 5.3 %collective-permute-start.3 = (bf16[1,32,16,128]{3,2,1,0:T(8,128)(2,1)S(1)}, bf16[1,32,16,128]{3,2,1,0:T(8,128)(2,1)S(1)}, u32[]{:S(2)}, u32[]{:S(2)}) collective-permute-start(bf16[1,32,16,128]{3,2,1,0:T(8,128)(2,1)S(1)} %get-tuple-element.67), channel_id=1, source_target_pairs={{0,2},{1,5},{2,0},{3,7},{4,6},{5,1},{6,4},{7,3},{8,10},{9,13},{10,... | collective-permute-start | bytes 393224 | tf_op jit(solution)/shard_map/ppermute | solution.py:30
  14.4 8.7 %collective-permute-start.6 = (bf16[2,32,16,128]{3,2,1,0:T(8,128)(2,1)S(1)}, bf16[2,32,16,128]{3,2,1,0:T(8,128)(2,1)S(1)}, u32[]{:S(2)}, u32[]{:S(2)}) collective-permute-start(bf16[2,32,16,128]{3,2,1,0:T(8,128)(2,1)S(1)} %pad_maximum_fusion.3), channel_id=1, source_target_pairs={{0,4},{1,3},{2,6},{3,1},{4,0},{5,7},{6,2},{7,5},{8,12},{9,11},{10,... | collective-permute-start | bytes 786440 | tf_op jit(solution)/shard_map/ppermute | solution.py:30
  16.1 7.0 %collective-permute-start.5 = (bf16[2,32,16,128]{3,2,1,0:T(8,128)(2,1)S(1)}, bf16[2,32,16,128]{3,2,1,0:T(8,128)(2,1)S(1)}, u32[]{:S(2)}, u32[]{:S(2)}) collective-permute-start(bf16[2,32,16,128]{3,2,1,0:T(8,128)(2,1)S(1)} %pad_maximum_fusion.2), channel_id=1, source_target_pairs={{0,2},{1,5},{2,0},{3,7},{4,6},{5,1},{6,4},{7,3},{8,10},{9,13},{10,... | collective-permute-start | bytes 786440 | tf_op jit(solution)/shard_map/ppermute | solution.py:30
  17.7 5.0 %collective-permute-start.4 = (bf16[1,32,16,128]{3,2,1,0:T(8,128)(2,1)S(1)}, bf16[1,32,16,128]{3,2,1,0:T(8,128)(2,1)S(1)}, u32[]{:S(2)}, u32[]{:S(2)}) collective-permute-start(bf16[1,32,16,128]{3,2,1,0:T(8,128)(2,1)S(1)} %collective-permute-done.1), channel_id=1, source_target_pairs={{0,8},{2,10},{4,12},{6,14},{8,0},{10,2},{12,4},{14,6},{16,24},{18,... | collective-permute-start | bytes 393224 | tf_op jit(solution)/shard_map/ppermute | solution.py:21
  23.1 5.0 %collective-permute-start.7 = (bf16[1,32,16,128]{3,2,1,0:T(8,128)(2,1)S(1)}, bf16[1,32,16,128]{3,2,1,0:T(8,128)(2,1)S(1)}, u32[]{:S(2)}, u32[]{:S(2)}) collective-permute-start(bf16[1,32,16,128]{3,2,1,0:T(8,128)(2,1)S(1)} %collective-permute-done.4), channel_id=1, source_target_pairs={{0,2},{1,5},{2,0},{3,7},{4,6},{5,1},{6,4},{7,3},{8,10},{9,13},{10,... | collective-permute-start | bytes 393224 | tf_op jit(solution)/shard_map/ppermute | solution.py:30
  28.2 12.1 %collective-permute-start.8 = (bf16[6,32,16,128]{3,2,1,0:T(8,128)(2,1)S(1)}, bf16[6,32,16,128]{3,2,1,0:T(8,128)(2,1)S(1)}, u32[]{:S(2)}, u32[]{:S(2)}) collective-permute-start(bf16[6,32,16,128]{3,2,1,0:T(8,128)(2,1)S(1)} %pad_maximum_fusion), channel_id=1, source_target_pairs={{0,4},{1,3},{2,6},{3,1},{4,0},{5,7},{6,2},{7,5},{8,12},{9,11},{10,... | collective-permute-start | bytes 2359304 | tf_op jit(solution)/shard_map/ppermute | solution.py:30
  29.9 4.1 %collective-permute-start.10 = (bf16[5,32,16,128]{3,2,1,0:T(8,128)(2,1)S(1)}, bf16[5,32,16,128]{3,2,1,0:T(8,128)(2,1)}, u32[]{:S(2)}, u32[]{:S(2)}) collective-permute-start(bf16[5,32,16,128]{3,2,1,0:T(8,128)(2,1)S(1)} %constant_dynamic-update-slice_fusion.5), channel_id=1, source_target_pairs={{0,1},{1,0},{2,3},{3,2},{4,5},{5,4},{6,7},{7,6},{8,9},{9,8},{10,11... | collective-permute-start | bytes 1966088 | tf_op jit(solution)/shard_map/ppermute | solution.py:21
  29.9 4.0 %collective-permute-start.9 = (bf16[5,32,16,128]{3,2,1,0:T(8,128)(2,1)S(1)}, bf16[5,32,16,128]{3,2,1,0:T(8,128)(2,1)}, u32[]{:S(2)}, u32[]{:S(2)}) collective-permute-start(bf16[5,32,16,128]{3,2,1,0:T(8,128)(2,1)S(1)} %constant_dynamic-update-slice_fusion), channel_id=1, source_target_pairs={{0,1},{1,0},{2,3},{3,2},{4,5},{5,4},{6,7},{7,6},{8,9},{9,8},{10,11... | collective-permute-start | bytes 1966088 | tf_op jit(solution)/shard_map/ppermute | solution.py:21
  40.3 3.0 %collective-permute-start.11 = (bf16[6,32,16,128]{3,2,1,0:T(8,128)(2,1)S(1)}, bf16[6,32,16,128]{3,2,1,0:T(8,128)(2,1)S(1)}, u32[]{:S(2)}, u32[]{:S(2)}) collective-permute-start(bf16[6,32,16,128]{3,2,1,0:T(8,128)(2,1)S(1)} %collective-permute-done.8), channel_id=1, source_target_pairs={{0,1},{1,0},{2,3},{3,2},{4,5},{5,4},{6,7},{7,6},{8,9},{9,8},{10,11... | collective-permute-start | bytes 2359304 | tf_op jit(solution)/shard_map/ppermute | solution.py:21
  49.2 1.4 %collective-permute-start.12 = (f32[16,128]{1,0:T(8,128)S(1)}, f32[16,128]{1,0:T(8,128)S(1)}, u32[]{:S(2)}, u32[]{:S(2)}) collective-permute-start(f32[16,128]{1,0:T(8,128)S(1)} %get-tuple-element.62), channel_id=1, source_target_pairs={{0,1},{1,0},{2,3},{3,2},{4,5},{5,4},{6,7},{7,6},{8,9},{9,8},{10,11... | collective-permute-start | bytes 24584 | tf_op jit(solution)/shard_map/ppermute | solution.py:21

commit v9 on v8

--- a/solution.py
+++ b/solution.py
@@ -102,17 +102,56 @@
     copy.wait()
 
 
-def apply_kernel(rows_ref, ham_ref, table_ref, zhm_ref, zl_ref, dc_ref, gt_ref, az_ref, sums_ref, a0_ref):
+def assemble_kernel(*refs):
+    pieces, table_ref, sems = refs[:-2], refs[-2], refs[-1]
+    cores = len(pieces) // 2
+    copies = []
+    for i, piece in enumerate(pieces):
+        at = (i // 2) * (table_ref.shape[0] // cores) + (i % 2) * pieces[0].shape[0]
+        copies.append(
+            pltpu.make_async_copy(piece, table_ref.at[pl.ds(at, piece.shape[0])], sems.at[i])
+        )
+        copies[-1].start()
+    for copy in copies:
+        copy.wait()
+
+
+def terms_kernel(a0_ref, dc_ref, az_ref):
+    lanes = a0_ref.shape[1]
+    block = min(lanes, 1024)
+
+    def terms(i, carry):
+        at = pl.ds(pl.multiple_of(i * block, block), block)
+        az_ref[:, at] = jnp.concatenate(split3(a0_ref[:, at] / dc_ref[:, at])[:2], axis=0)
+        return carry
+
+    lax.fori_loop(0, lanes // block, terms, 0)
+
+
+def apply_kernel(rows_ref, ham_ref, _, zhm_ref, zl_ref, dc_ref, gt_ref, *rest):
+    last, (a0_ref, sums_ref, table_ref) = rest[:-3], rest[-3:]
+    share = table_ref.shape[1]
+    for c, piece in enumerate(last):
+        start = (c + 1) * (table_ref.shape[0] // len(last)) - piece.shape[0]
+
+        def put(i, carry, piece=piece, start=start):
+            table_ref[start + i] = piece[i]
+            return carry
+
+        lax.fori_loop(0, piece.shape[0], put, 0)
     ch, ncoup, r, splines = ham_ref.shape
     k = zl_ref.shape[0] // 2
     group = 256 // r
+
+    def row_of(n):
+        return table_ref[lax.div(n, share), lax.rem(n, share)]
 
     def work(g, carry):
         left, right = [], []
         for i in range(group):
             p = g * group + i
             left.append(
-                jnp.concatenate([table_ref[rows_ref[p, j]] for j in range(ncoup)], axis=1)
+                jnp.concatenate([row_of(rows_ref[p, j]) for j in range(ncoup)], axis=1)
             )
             right.append(jnp.concatenate([ham_ref[p, j] for j in range(ncoup)], axis=1))
         product = lax.dot_general(
@@ -134,7 +173,6 @@
         at = pl.ds(pl.multiple_of(i * block, block), block)
         a0 = a0_ref[:, at]
         a1_terms = split3(a0 / dc_ref[:, at])
-        az_ref[:, at] = jnp.concatenate(a1_terms[:2], axis=0)
         right = jnp.concatenate(a1_terms + split3(a0), axis=0)
         left = jnp.concatenate([zhm_ref[:, at], zl_ref[:, at], right[: 3 * k]], axis=0)
         return gram + lax.dot_general(left, right, NT, preferred_element_type=F32)
@@ -292,23 +330,41 @@
         compiler_params=pltpu.CompilerParams(vmem_limit_bytes=VMEM_LIMIT),
         name="prepare",
     )(trial_block, precond_diag, partners, stored_at.reshape(-1, 128), in_hbm(ham_blocks))
-    far, early1, early2, rows = barrier((far, early1, early2, rows))
-    table = jnp.concatenate([x for three in zip(early1, early2, in_cores(far)) for x in three])
-    table = table.reshape(n_chan * ch, k, splines)
-
-    az, sums = pl.pallas_call(
+    pieces = [x for pair in zip(early1, early2) for x in pair]
+    table = pl.pallas_call(
+        assemble_kernel,
+        in_specs=[any_] * len(pieces),
+        out_specs=whole,
+        out_shape=pltpu.VMEM((4 * nz * n_rad,) + own.shape[1:], BF16),
+        scratch_shapes=[pltpu.SemaphoreType.DMA((len(pieces),))],
+        compiler_params=pltpu.CompilerParams(vmem_limit_bytes=VMEM_LIMIT),
+        name="assemble",
+    )(*pieces)
+    far, table, rows = barrier((far, table, rows))
+    last = [in_vmem(x) for x in in_cores(far)]
+
+    a0, sums, _ = pl.pallas_call(
         apply_kernel,
-        in_specs=[smem] + [whole] * 6,
-        out_specs=[whole, whole],
+        in_specs=[smem] + [whole] * (6 + n_rad),
+        out_specs=[whole, whole, whole],
         out_shape=[
-            pltpu.VMEM((2 * k, lanes), BF16),
+            pltpu.VMEM((k, lanes), F32),
             jax.ShapeDtypeStruct((k, 8 * k), F32),
+            pltpu.VMEM(table.shape, BF16),
         ],
-        scratch_shapes=[pltpu.VMEM((k, lanes), F32)],
+        input_output_aliases={2: 2},
         compiler_params=pltpu.CompilerParams(vmem_limit_bytes=VMEM_LIMIT),
         name="apply",
-    )(rows, in_vmem(ham), in_vmem(table), in_vmem(zhm), in_vmem(zl), in_vmem(dc), gram_t)
-
+    )(rows, in_vmem(ham), in_vmem(table), in_vmem(zhm), in_vmem(zl), in_vmem(dc), gram_t, *last)
+
+    az = pl.pallas_call(
+        terms_kernel,
+        in_specs=[whole, whole],
+        out_specs=whole,
+        out_shape=pltpu.VMEM((2 * k, lanes), BF16),
+        compiler_params=pltpu.CompilerParams(vmem_limit_bytes=VMEM_LIMIT),
+        name="terms",
+    )(in_vmem(a0), in_vmem(dc))
     sums = gather_sums(sums)
     new_block, ritz = pl.pallas_call(
         functools.partial(finish_kernel, total),

time: 68.2 us -> 70.2 us (1.029)
  blocking collectives: 14.2 us -> 0 us
  waiting for transfers between devices: 19.9 us -> 33.8 us
  Pallas kernels: 12.2 us -> 13.9 us
  starting transfers between devices: 15.8 us -> 14.8 us
  other arithmetic: 1.46 us -> 2.31 us
    all_to_all x1 -> x0, blocking collectives: 14.2 us -> none  [gather_sums(): lax.all_to_all(every, 'chan', split_axis=0, concat_axis=0, tiled=True)]
    all_to_all x0 -> x1, waiting for transfers between devices: none -> 7.75 us  [gather_sums(): lax.all_to_all(every, 'chan', split_axis=0, concat_axis=0, tiled=True)]
    ppermute x8, waiting for transfers between devices: 9.15 us -> 15 us  [swap(): return lax.ppermute(x, axis, [(i, i ^ distance) for i in range(n)])]
    all_to_all x0 -> x1, starting transfers between devices: none -> 3.69 us  [gather_sums(): lax.all_to_all(every, 'chan', split_axis=0, concat_axis=0, tiled=True)]
    ppermute x8, starting transfers between devices: 8.64 us -> 5.86 us  [swap(): return lax.ppermute(x, axis, [(i, i ^ distance) for i in range(n)])]
    ppermute x5, starting transfers between devices: 7.2 us -> 5.22 us  [plane_swap(): return lax.ppermute(x, ('chan', 'rad'), pairs)]
    pallas_call x1 -> x3, Pallas kernels: 5.78 us -> 7.46 us  [the longest x1 5.85 us: body(): pl.pallas_call(apply_kernel, in_specs=[smem] + [whole] * (6 + n_rad), out...]
    concatenate x2, other arithmetic: 0.12 us -> 1.01 us  [far_of(): return plane_swap(jnp.concatenate([x, near]), (2, 1))]
  transfers between devices with their start and end apart: 13 -> 14, of which waited for: 8 -> 10; matrix products, arithmetic and copies ran while one was open for 5% -> 1% of each run, Pallas kernels for 5% -> 7%
where the time goes in v9:
time: 70.2 us; the launch traced here: 69.7 us
  waiting for transfers between devices  33.8 us (48%)
  starting transfers between devices  14.8 us (21%)
  Pallas kernels  13.9 us (20%)
  local copies, waits for them, and re-layouts  4.09 us (6%)
  other arithmetic  2.31 us (3%)
  between operations  0.79 us (1%)
    ppermute x8, waiting for transfers between devices, swap(): return lax.ppermute(x, axis, [(i, i ^ distance) for i in range(n)])  15 us
    ppermute x5, waiting for transfers between devices, plane_swap(): return lax.ppermute(x, ('chan', 'rad'), pairs)  11.1 us
    all_to_all x1, waiting for transfers between devices, gather_sums(): lax.all_to_all(every, 'chan', split_axis=0, concat_axis=0, tiled=True)  7.75 us
    ppermute x8, starting transfers between devices, swap(): return lax.ppermute(x, axis, [(i, i ^ distance) for i in range(n)])  5.86 us
    pallas_call x1, Pallas kernels, body(): pl.pallas_call(apply_kernel, in_specs=[smem] + [whole] * (6 + n_rad), out...  5.85 us
    ppermute x5, starting transfers between devices, plane_swap(): return lax.ppermute(x, ('chan', 'rad'), pairs)  5.22 us
    all_to_all x1, starting transfers between devices, gather_sums(): lax.all_to_all(every, 'chan', split_axis=0, concat_axis=0, tiled=True)  3.69 us
    pallas_call x1, Pallas kernels, body(): pl.pallas_call(functools.partial(prepare_kernel, n_chan, n_rad), in_specs...  3.39 us
  transfers between devices with their start and end apart: 14, of which 10 were waited for; matrix products, arithmetic and copies ran while one was open for 1% of the time, Pallas kernels for 7%

profile of v9, /device:TPU:0, one launch (start us, length us, event | category | flops | bytes accessed | tf_op | source)
XLA Modules:
  0.0 69.7 jit_solution(5777847578716492966)
XLA Ops:
  0.6 1.1 %convert_element_type.3 = bf16[64,16,64]{2,1,0:T(8,128)(2,1)S(1)} convert(f32[64,16,64]{2,1,0:T(8,128)} %t_ref) | non-fusion elementwise | flops 65536 | bytes 393216 | tf_op jit(solution)/shard_map/convert_element_type | solution.py:260
  1.7 0.5 collective-permute-start
  2.3 1.0 %collective-permute-done = bf16[32,16,64]{2,1,0:T(8,128)(2,1)S(1)} collective-permute-done((bf16[32,16,64]{2,1,0:T(8,128)(2,1)S(1)}, bf16[32,16,64]{2,1,0:T(8,128)(2,1)S(1)}, u32[]{:S(2)}, u32[]{:S(2)}) %collective-permute-start) | collective-permute-done | bytes 65568 | tf_op jit(solution)/shard_map/ppermute | solution.py:21
  3.4 2.9 %collective-permute-start.3 = (bf16[1,32,16,128]{3,2,1,0:T(8,128)(2,1)S(1)}, bf16[1,32,16,128]{3,2,1,0:T(8,128)(2,1)S(1)}, u32[]{:S(2)}, u32[]{:S(2)}) collective-permute-start(bf16[1,32,16,128]{3,2,1,0:T(8,128)(2,1)S(1)} %get-tuple-element.61), channel_id=1, source_target_pairs={{0,2},{1,5},{2,0},{3,7},{4,6},{5,1},{6,4},{7,3},{8,10},{9,13},{10,... | collective-permute-start | bytes 393224 | tf_op jit(solution)/shard_map/ppermute | solution.py:30
  6.3 1.6 %collective-permute-start.2 = (bf16[1,32,16,128]{3,2,1,0:T(8,128)(2,1)S(1)}, bf16[1,32,16,128]{3,2,1,0:T(8,128)(2,1)S(1)}, u32[]{:S(2)}, u32[]{:S(2)}) collective-permute-start(bf16[1,32,16,128]{3,2,1,0:T(8,128)(2,1)S(1)} %get-tuple-element.61), channel_id=1, source_target_pairs={{0,8},{2,10},{4,12},{6,14},{8,0},{10,2},{12,4},{14,6},{16,24},{18,... | collective-permute-start | bytes 393224 | tf_op jit(solution)/shard_map/ppermute | solution.py:21
  7.9 2.6 %collective-permute-start.1 = (bf16[1,32,16,128]{3,2,1,0:T(8,128)(2,1)S(1)}, bf16[1,32,16,128]{3,2,1,0:T(8,128)(2,1)S(1)}, u32[]{:S(2)}, u32[]{:S(2)}) collective-permute-start(bf16[1,32,16,128]{3,2,1,0:T(8,128)(2,1)S(1)} %get-tuple-element.61), channel_id=1, source_target_pairs={{0,16},{2,18},{4,20},{6,22},{8,24},{10,26},{12,28},{14,30},{16,0},... | collective-permute-start | bytes 393224 | tf_op jit(solution)/shard_map/ppermute | solution.py:21
  10.5 3.2 %collective-permute-done.2 = bf16[1,32,16,128]{3,2,1,0:T(8,128)(2,1)S(1)} collective-permute-done((bf16[1,32,16,128]{3,2,1,0:T(8,128)(2,1)S(1)}, bf16[1,32,16,128]{3,2,1,0:T(8,128)(2,1)S(1)}, u32[]{:S(2)}, u32[]{:S(2)}) %collective-permute-start.2) | collective-permute-done | bytes 131104 | tf_op jit(solution)/shard_map/ppermute | solution.py:21
  13.7 3.0 %collective-permute-done.1 = bf16[1,32,16,128]{3,2,1,0:T(8,128)(2,1)S(1)} collective-permute-done((bf16[1,32,16,128]{3,2,1,0:T(8,128)(2,1)S(1)}, bf16[1,32,16,128]{3,2,1,0:T(8,128)(2,1)S(1)}, u32[]{:S(2)}, u32[]{:S(2)}) %collective-permute-start.1) | collective-permute-done | bytes 131104 | tf_op jit(solution)/shard_map/ppermute | solution.py:21
  16.7 1.6 %collective-permute-start.5 = (bf16[2,32,16,128]{3,2,1,0:T(8,128)(2,1)S(1)}, bf16[2,32,16,128]{3,2,1,0:T(8,128)(2,1)S(1)}, u32[]{:S(2)}, u32[]{:S(2)}) collective-permute-start(bf16[2,32,16,128]{3,2,1,0:T(8,128)(2,1)S(1)} %pad_maximum_fusion.2), channel_id=1, source_target_pairs={{0,2},{1,5},{2,0},{3,7},{4,6},{5,1},{6,4},{7,3},{8,10},{9,13},{10,... | collective-permute-start | bytes 786440 | tf_op jit(solution)/shard_map/ppermute | solution.py:30
  18.3 0.5 collective-permute-start.6
  18.8 0.4 collective-permute-start.4
  19.3 4.5 %collective-permute-done.4 = bf16[1,32,16,128]{3,2,1,0:T(8,128)(2,1)S(1)} collective-permute-done((bf16[1,32,16,128]{3,2,1,0:T(8,128)(2,1)S(1)}, bf16[1,32,16,128]{3,2,1,0:T(8,128)(2,1)S(1)}, u32[]{:S(2)}, u32[]{:S(2)}) %collective-permute-start.4) | collective-permute-done | bytes 131104 | tf_op jit(solution)/shard_map/ppermute | solution.py:21
  23.8 2.0 %collective-permute-done.6 = bf16[2,32,16,128]{3,2,1,0:T(8,128)(2,1)S(1)} collective-permute-done((bf16[2,32,16,128]{3,2,1,0:T(8,128)(2,1)S(1)}, bf16[2,32,16,128]{3,2,1,0:T(8,128)(2,1)S(1)}, u32[]{:S(2)}, u32[]{:S(2)}) %collective-permute-start.6) | collective-permute-done | bytes 262176 | tf_op jit(solution)/shard_map/ppermute | solution.py:30
  25.8 0.2 collective-permute-start.7
  26.1 5.8 %collective-permute-done.7 = bf16[1,32,16,128]{3,2,1,0:T(8,128)(2,1)S(1)} collective-permute-done((bf16[1,32,16,128]{3,2,1,0:T(8,128)(2,1)S(1)}, bf16[1,32,16,128]{3,2,1,0:T(8,128)(2,1)S(1)}, u32[]{:S(2)}, u32[]{:S(2)}) %collective-permute-start.7) | collective-permute-done | bytes 131104 | tf_op jit(solution)/shard_map/ppermute | solution.py:30
  31.9 1.0 %pad_maximum_fusion = bf16[6,32,16,128]{3,2,1,0:T(8,128)(2,1)} fusion(bf16[1,32,16,128]{3,2,1,0:T(8,128)(2,1)S(1)} %collective-permute-done.7, bf16[2,32,16,128]{3,2,1,0:T(8,128)(2,1)S(1)} %collective-permute-done.5, bf16[3,32,16,128]{3,2,1,0:T(8,128)(2,1)S(1)} %pad_maximum_fusion.1), kind=kLoop, calls=%fused_computation | loop fusion | flops 786432 | bytes 1572864 | tf_op jit(solution)/shard_map/concatenate | solution.py:291
  33.1 0.5 collective-permute-start.9
  33.6 0.8 %copy.8.partners_ref = s32[64,8]{1,0:T(8,128)S(1)} copy(s32[64,8]{0,1:T(8,128)} %param.7) | data formatting | bytes 4096 | tf_op jit(solution)/shard_map/optimization_barrier | solution.py:315
  34.3 1.0 %copy-done = f32[64,16,64]{2,1,0:T(8,128)S(1)} copy-done((f32[64,16,64]{2,1,0:T(8,128)S(1)}, f32[64,16,64]{2,1,0:T(8,128)}, u32[]{:S(2)}) %copy-start) | copy-done | bytes 262168
  35.4 0.8 %copy-done.1 = f32[64,64]{1,0:T(8,128)S(1)} copy-done((f32[64,64]{1,0:T(8,128)S(1)}, f32[64,64]{1,0:T(8,128)}, u32[]{:S(2)}) %copy-start.1) | copy-done | bytes 16408
  36.1 0.7 copy-done.2
  36.8 3.4 %prepare.1 = (bf16[64,8,64,128]{3,2,1,0:T(8,128)(2,1)S(1)}, s32[64,8]{1,0:T(8,128)S(1)}, bf16[64,4096]{1,0:T(8,128)(2,1)S(1)}, bf16[32,4096]{1,0:T(8,128)(2,1)S(...) custom-call(f32[64,16,64]{2,1,0:T(8,128)S(1)} %copy-done, f32[64,64]{1,0:T(8,128)S(1)} %copy-done.1, ...), custom_call_target="tpu_custom_call" | custom-call | tf_op jit(solution)/shard_map/prepare/pallas_call | solution.py:317
  40.2 1.5 %assemble.1._ = bf16[32,32,16,128]{3,2,1,0:T(8,128)(2,1)S(1)} custom-call(bf16[5,32,16,128]{3,2,1,0:T(8,128)(2,1)S(1)} %constant_dynamic-update-slice_fusion.refs_0_, bf16[5,32,16,128]{3,2,1,0:T(8,128)(2,1)S(1)} %constant_dynamic-update-slice_fusion.5.refs_1_, bf16[5,32,16,128]{3,2,1,0:T(8,128)(2,1)} %collective-permute-done.9.refs_2_, ...), custom_call_target="tpu_custom_call" | custom-call | tf_op jit(solution)/shard_map/assemble/pallas_call | solution.py:334
  41.8 3.3 %collective-permute-done.8.rest_0_ = bf16[6,32,16,128]{3,2,1,0:T(8,128)(2,1)S(1)} collective-permute-done((bf16[6,32,16,128]{3,2,1,0:T(8,128)(2,1)}, bf16[6,32,16,128]{3,2,1,0:T(8,128)(2,1)S(1)}, u32[]{:S(2)}, u32[]{:S(2)}) %collective-permute-start.8) | collective-permute-done | bytes 786464 | tf_op jit(solution)/shard_map/ppermute | solution.py:30
  45.1 2.3 %collective-permute-done.11.rest_1_ = bf16[6,32,16,128]{3,2,1,0:T(8,128)(2,1)S(1)} collective-permute-done((bf16[6,32,16,128]{3,2,1,0:T(8,128)(2,1)S(1)}, bf16[6,32,16,128]{3,2,1,0:T(8,128)(2,1)S(1)}, u32[]{:S(2)}, u32[]{:S(2)}) %collective-permute-start.11) | collective-permute-done | bytes 786464 | tf_op jit(solution)/shard_map/ppermute | solution.py:21
  47.4 5.8 %apply.1 = (f32[16,4096]{1,0:T(8,128)S(1)}, f32[16,128]{1,0:T(8,128)S(1)}, bf16[32,32,16,128]{3,2,1,0:T(8,128)(2,1)S(1)}) custom-call(s32[64,8]{1,0:T(8,128)S(1)} %get-tuple-element.48.rows_ref, bf16[64,8,64,128]{3,2,1,0:T(8,128)(2,1)S(1)} %get-tuple-element.49.ham_ref, bf16[32,32,16,128]{3,2,1,0:T(8,128)(2,1)S(1)} %assemble.1._, ...), custom_call_target="tpu_custom_call", output_to_operand_aliasing={{2}: (2, {})} | custom-call | tf_op jit(solution)/shard_map/apply/pallas_call | solution.py:346
  53.2 0.2 collective-permute-start.12
  53.4 1.0 %collective-permute-done.12 = f32[16,128]{1,0:T(8,128)S(1)} collective-permute-done((f32[16,128]{1,0:T(8,128)S(1)}, f32[16,128]{1,0:T(8,128)S(1)}, u32[]{:S(2)}, u32[]{:S(2)}) %collective-permute-start.12) | collective-permute-done | bytes 8224 | tf_op jit(solution)/shard_map/ppermute | solution.py:21
  54.4 0.7 broadcast_in_dim.7
  55.1 3.7 %all-to-all-start = ((f32[16,16,128]{2,1,0:T(8,128)}), f32[16,16,128]{2,1,0:T(8,128)S(1)}, u32[]{:S(2)}, u32[]{:S(2)}) async-start(f32[16,16,128]{2,1,0:T(8,128)} %broadcast_in_dim.7), calls=%async_computation | async-start | bytes 262144 | tf_op jit(solution)/shard_map/all_to_all | solution.py:253
  58.9 7.7 %all-to-all-done.sums_ref = f32[16,16,128]{2,1,0:T(8,128)S(1)} async-done(((f32[16,16,128]{2,1,0:T(8,128)}), f32[16,16,128]{2,1,0:T(8,128)S(1)}, u32[]{:S(2)}, u32[]{:S(2)}) %all-to-all-start) | async-done | bytes 131104 | tf_op jit(solution)/shard_map/all_to_all | solution.py:253
  66.6 3.1 %finish.1 = (f32[64,16,64]{2,1,0:T(8,128)}, f32[1,16]{1,0:T(1,128)}) custom-call(f32[16,16,128]{2,1,0:T(8,128)S(1)} %all-to-all-done.sums_ref, bf16[32,4096]{1,0:T(8,128)(2,1)S(1)} %terms.1.az_ref, bf16[64,4096]{1,0:T(8,128)(2,1)S(1)} %get-tuple-element.51.zhm_ref), custom_call_target="tpu_custom_call" | custom-call | tf_op jit(solution)/shard_map/finish/pallas_call | solution.py:369
  (25 shorter events, 0.6 us)
Async XLA Ops:
  1.7 1.5 %collective-permute-start = (bf16[32,16,64]{2,1,0:T(8,128)(2,1)S(1)}, bf16[32,16,64]{2,1,0:T(8,128)(2,1)S(1)}, u32[]{:S(2)}, u32[]{:S(2)}) collective-permute-start(bf16[32,16,64]{2,1,0:T(8,128)(2,1)S(1)} %dynamic-slice_bitcast_fusion), channel_id=1, source_target_pairs={{0,1},{1,0},{2,3},{3,2},{4,5},{5,4},{6,7},{7,6},{8,9},{9,8},{10,11... | collective-permute-start | bytes 196616 | tf_op jit(solution)/shard_map/ppermute | solution.py:21
  3.4 7.1 %collective-permute-start.3 = (bf16[1,32,16,128]{3,2,1,0:T(8,128)(2,1)S(1)}, bf16[1,32,16,128]{3,2,1,0:T(8,128)(2,1)S(1)}, u32[]{:S(2)}, u32[]{:S(2)}) collective-permute-start(bf16[1,32,16,128]{3,2,1,0:T(8,128)(2,1)S(1)} %get-tuple-element.61), channel_id=1, source_target_pairs={{0,2},{1,5},{2,0},{3,7},{4,6},{5,1},{6,4},{7,3},{8,10},{9,13},{10,... | collective-permute-start | bytes 393224 | tf_op jit(solution)/shard_map/ppermute | solution.py:30
  6.3 7.4 %collective-permute-start.2 = (bf16[1,32,16,128]{3,2,1,0:T(8,128)(2,1)S(1)}, bf16[1,32,16,128]{3,2,1,0:T(8,128)(2,1)S(1)}, u32[]{:S(2)}, u32[]{:S(2)}) collective-permute-start(bf16[1,32,16,128]{3,2,1,0:T(8,128)(2,1)S(1)} %get-tuple-element.61), channel_id=1, source_target_pairs={{0,8},{2,10},{4,12},{6,14},{8,0},{10,2},{12,4},{14,6},{16,24},{18,... | collective-permute-start | bytes 393224 | tf_op jit(solution)/shard_map/ppermute | solution.py:21
  7.9 8.8 %collective-permute-start.1 = (bf16[1,32,16,128]{3,2,1,0:T(8,128)(2,1)S(1)}, bf16[1,32,16,128]{3,2,1,0:T(8,128)(2,1)S(1)}, u32[]{:S(2)}, u32[]{:S(2)}) collective-permute-start(bf16[1,32,16,128]{3,2,1,0:T(8,128)(2,1)S(1)} %get-tuple-element.61), channel_id=1, source_target_pairs={{0,16},{2,18},{4,20},{6,22},{8,24},{10,26},{12,28},{14,30},{16,0},... | collective-permute-start | bytes 393224 | tf_op jit(solution)/shard_map/ppermute | solution.py:21
  16.7 7.0 %collective-permute-start.5 = (bf16[2,32,16,128]{3,2,1,0:T(8,128)(2,1)S(1)}, bf16[2,32,16,128]{3,2,1,0:T(8,128)(2,1)S(1)}, u32[]{:S(2)}, u32[]{:S(2)}) collective-permute-start(bf16[2,32,16,128]{3,2,1,0:T(8,128)(2,1)S(1)} %pad_maximum_fusion.2), channel_id=1, source_target_pairs={{0,2},{1,5},{2,0},{3,7},{4,6},{5,1},{6,4},{7,3},{8,10},{9,13},{10,... | collective-permute-start | bytes 786440 | tf_op jit(solution)/shard_map/ppermute | solution.py:30
  18.3 7.5 %collective-permute-start.6 = (bf16[2,32,16,128]{3,2,1,0:T(8,128)(2,1)S(1)}, bf16[2,32,16,128]{3,2,1,0:T(8,128)(2,1)S(1)}, u32[]{:S(2)}, u32[]{:S(2)}) collective-permute-start(bf16[2,32,16,128]{3,2,1,0:T(8,128)(2,1)S(1)} %pad_maximum_fusion.3), channel_id=1, source_target_pairs={{0,4},{1,3},{2,6},{3,1},{4,0},{5,7},{6,2},{7,5},{8,12},{9,11},{10,... | collective-permute-start | bytes 786440 | tf_op jit(solution)/shard_map/ppermute | solution.py:30
  18.8 5.0 %collective-permute-start.4 = (bf16[1,32,16,128]{3,2,1,0:T(8,128)(2,1)S(1)}, bf16[1,32,16,128]{3,2,1,0:T(8,128)(2,1)S(1)}, u32[]{:S(2)}, u32[]{:S(2)}) collective-permute-start(bf16[1,32,16,128]{3,2,1,0:T(8,128)(2,1)S(1)} %collective-permute-done.1), channel_id=1, source_target_pairs={{0,8},{2,10},{4,12},{6,14},{8,0},{10,2},{12,4},{14,6},{16,24},{18,... | collective-permute-start | bytes 393224 | tf_op jit(solution)/shard_map/ppermute | solution.py:21
  25.8 6.1 %collective-permute-start.7 = (bf16[1,32,16,128]{3,2,1,0:T(8,128)(2,1)S(1)}, bf16[1,32,16,128]{3,2,1,0:T(8,128)(2,1)S(1)}, u32[]{:S(2)}, u32[]{:S(2)}) collective-permute-start(bf16[1,32,16,128]{3,2,1,0:T(8,128)(2,1)S(1)} %collective-permute-done.4), channel_id=1, source_target_pairs={{0,2},{1,5},{2,0},{3,7},{4,6},{5,1},{6,4},{7,3},{8,10},{9,13},{10,... | collective-permute-start | bytes 393224 | tf_op jit(solution)/shard_map/ppermute | solution.py:30
  32.9 12.2 %collective-permute-start.8 = (bf16[6,32,16,128]{3,2,1,0:T(8,128)(2,1)}, bf16[6,32,16,128]{3,2,1,0:T(8,128)(2,1)S(1)}, u32[]{:S(2)}, u32[]{:S(2)}) collective-permute-start(bf16[6,32,16,128]{3,2,1,0:T(8,128)(2,1)} %pad_maximum_fusion), channel_id=1, source_target_pairs={{0,4},{1,3},{2,6},{3,1},{4,0},{5,7},{6,2},{7,5},{8,12},{9,11},{10,... | collective-permute-start | bytes 2359304 | tf_op jit(solution)/shard_map/ppermute | solution.py:30
  33.0 7.2 %collective-permute-start.10 = (bf16[5,32,16,128]{3,2,1,0:T(8,128)(2,1)S(1)}, bf16[5,32,16,128]{3,2,1,0:T(8,128)(2,1)S(1)}, u32[]{:S(2)}, u32[]{:S(2)}) collective-permute-start(bf16[5,32,16,128]{3,2,1,0:T(8,128)(2,1)S(1)} %constant_dynamic-update-slice_fusion.5.refs_1_), channel_id=1, source_target_pairs={{0,1},{1,0},{2,3},{3,2},{4,5},{5,4},{6,7},{7,6},{8,9},{9,8},{10,11... | collective-permute-start | bytes 1966088 | tf_op jit(solution)/shard_map/ppermute | solution.py:21
  33.1 7.2 %collective-permute-start.9 = (bf16[5,32,16,128]{3,2,1,0:T(8,128)(2,1)S(1)}, bf16[5,32,16,128]{3,2,1,0:T(8,128)(2,1)}, u32[]{:S(2)}, u32[]{:S(2)}) collective-permute-start(bf16[5,32,16,128]{3,2,1,0:T(8,128)(2,1)S(1)} %constant_dynamic-update-slice_fusion.refs_0_), channel_id=1, source_target_pairs={{0,1},{1,0},{2,3},{3,2},{4,5},{5,4},{6,7},{7,6},{8,9},{9,8},{10,11... | collective-permute-start | bytes 1966088 | tf_op jit(solution)/shard_map/ppermute | solution.py:21
  34.3 1.0 %copy-start = (f32[64,16,64]{2,1,0:T(8,128)S(1)}, f32[64,16,64]{2,1,0:T(8,128)}, u32[]{:S(2)}) copy-start(f32[64,16,64]{2,1,0:T(8,128)} %t_ref) | copy-start | bytes 786436
  35.4 0.8 %copy-start.1 = (f32[64,64]{1,0:T(8,128)S(1)}, f32[64,64]{1,0:T(8,128)}, u32[]{:S(2)}) copy-start(f32[64,64]{1,0:T(8,128)} %d_ref) | copy-start | bytes 49156
  36.1 0.7 copy-start.2
  45.1 2.3 %collective-permute-start.11 = (bf16[6,32,16,128]{3,2,1,0:T(8,128)(2,1)S(1)}, bf16[6,32,16,128]{3,2,1,0:T(8,128)(2,1)S(1)}, u32[]{:S(2)}, u32[]{:S(2)}) collective-permute-start(bf16[6,32,16,128]{3,2,1,0:T(8,128)(2,1)S(1)} %collective-permute-done.8.rest_0_), channel_id=1, source_target_pairs={{0,1},{1,0},{2,3},{3,2},{4,5},{5,4},{6,7},{7,6},{8,9},{9,8},{10,11... | collective-permute-start | bytes 2359304 | tf_op jit(solution)/shard_map/ppermute | solution.py:21
  53.2 1.2 %collective-permute-start.12 = (f32[16,128]{1,0:T(8,128)S(1)}, f32[16,128]{1,0:T(8,128)S(1)}, u32[]{:S(2)}, u32[]{:S(2)}) collective-permute-start(f32[16,128]{1,0:T(8,128)S(1)} %get-tuple-element.56), channel_id=1, source_target_pairs={{0,1},{1,0},{2,3},{3,2},{4,5},{5,4},{6,7},{7,6},{8,9},{9,8},{10,11... | collective-permute-start | bytes 24584 | tf_op jit(solution)/shard_map/ppermute | solution.py:21
  55.1 11.5 %all-to-all-start = ((f32[16,16,128]{2,1,0:T(8,128)}), f32[16,16,128]{2,1,0:T(8,128)S(1)}, u32[]{:S(2)}, u32[]{:S(2)}) async-start(f32[16,16,128]{2,1,0:T(8,128)} %broadcast_in_dim.7), calls=%async_computation | async-start | bytes 262144 | tf_op jit(solution)/shard_map/all_to_all | solution.py:253

commit v10 on v9

--- a/solution.py
+++ b/solution.py
@@ -33,7 +33,8 @@
 def table_piece(z, part, nz):
     z = z if nz == 4 else jnp.where(z < 2, z, jnp.where((z & 1) == 1, (nz + z - 1) >> 1, 1 + (z >> 1)))
     near = jnp.where(z == 0, nz, nz + 2 + z)
-    far = (part & 1) + jnp.where(z == 0, nz + 1, 2 * nz + 1 + z + (part & 1) * (nz - 2))
+    second = part & 1
+    far = jnp.where(z == 0, nz + 1, jnp.where(z == 1, 4 * nz - 2, 2 * nz + z + second * (nz - 3))) + second
     return jnp.where(part == 0, z, jnp.where(part == 1, near, far))
 
 
@@ -62,11 +63,17 @@
 
 
 def prepare_kernel(
-    n_chan, n_rad, t_ref, d_ref, partners_ref, stored_ref, ham_hbm,
-    ham_ref, rows_ref, zhm_ref, zl_ref, dc_ref, gram_ref, sem,
+    n_chan, n_rad, t_hbm, d_hbm, partners_hbm, stored_hbm, ham_hbm,
+    rows_ref, ham_ref, zhm_ref, zl_ref, dc_ref, gram_ref, t_ref, d_ref, partners_ref, stored_ref, sems,
 ):
-    copy = pltpu.make_async_copy(ham_hbm, ham_ref, sem)
-    copy.start()
+    moves = (
+        (t_hbm, t_ref), (d_hbm, d_ref), (partners_hbm, partners_ref), (stored_hbm, stored_ref), (ham_hbm, ham_ref)
+    )
+    copies = [pltpu.make_async_copy(x, y, sems.at[i]) for i, (x, y) in enumerate(moves)]
+    for copy in copies:
+        copy.start()
+    for copy in copies[:4]:
+        copy.wait()
     ch, k, r = t_ref.shape
     group = 128 // r
     for i in range(ch // group):
@@ -92,14 +99,15 @@
     place = (place * share + lax.rem(local, share)).astype(F32)
     lane = lax.broadcasted_iota(jnp.int32, (ch, 128), 1)
     columns = []
-    for j in range(partners_ref.shape[1]):
-        wanted = jnp.broadcast_to(partners_ref[:, j : j + 1], (ch, 128)) - lane
+    partners = partners_ref[...].astype(F32).T.astype(jnp.int32)
+    for j in range(partners.shape[1]):
+        wanted = jnp.broadcast_to(partners[:, j : j + 1], (ch, 128)) - lane
         found = jnp.zeros((ch, 128), F32)
         for c in range(place.shape[0]):
             found = found + jnp.where(wanted == 128 * c, place[c : c + 1], 0.0)
         columns.append(jnp.sum(found, axis=1, keepdims=True))
     rows_ref[...] = jnp.concatenate(columns, axis=1).astype(jnp.int32)
-    copy.wait()
+    copies[4].wait()
 
 
 def assemble_kernel(*refs):
@@ -116,20 +124,8 @@
         copy.wait()
 
 
-def terms_kernel(a0_ref, dc_ref, az_ref):
-    lanes = a0_ref.shape[1]
-    block = min(lanes, 1024)
-
-    def terms(i, carry):
-        at = pl.ds(pl.multiple_of(i * block, block), block)
-        az_ref[:, at] = jnp.concatenate(split3(a0_ref[:, at] / dc_ref[:, at])[:2], axis=0)
-        return carry
-
-    lax.fori_loop(0, lanes // block, terms, 0)
-
-
 def apply_kernel(rows_ref, ham_ref, _, zhm_ref, zl_ref, dc_ref, gt_ref, *rest):
-    last, (a0_ref, sums_ref, table_ref) = rest[:-3], rest[-3:]
+    last, (az_ref, sums_ref, table_ref, a0_ref) = rest[:-4], rest[-4:]
     share = table_ref.shape[1]
     for c, piece in enumerate(last):
         start = (c + 1) * (table_ref.shape[0] // len(last)) - piece.shape[0]
@@ -173,6 +169,7 @@
         at = pl.ds(pl.multiple_of(i * block, block), block)
         a0 = a0_ref[:, at]
         a1_terms = split3(a0 / dc_ref[:, at])
+        az_ref[:, at] = jnp.concatenate(a1_terms[:2], axis=0)
         right = jnp.concatenate(a1_terms + split3(a0), axis=0)
         left = jnp.concatenate([zhm_ref[:, at], zl_ref[:, at], right[: 3 * k]], axis=0)
         return gram + lax.dot_general(left, right, NT, preferred_element_type=F32)
@@ -287,50 +284,56 @@
     def near_of(x):
         return plane_swap(x, (1, 2))
 
-    def far_of(x, near):
-        return plane_swap(jnp.concatenate([x, near]), (2, 1))
+    def far_of(x):
+        return plane_swap(x, (2, 1))
 
     def in_cores(x):
         return [x] + [swap(x, "rad", c) for c in range(1, n_rad)]
 
     own = own_share(trial_block)[None]
+    near0, far_own = near_of(own), far_of(own)
+    z1 = swap(own, "chan", 4)
     z_even = jnp.concatenate([swap(own, "chan", 4 * z) for z in range(2, nz, 2)])
-    z1 = swap(own, "chan", 4)
-    near0 = near_of(own)
-    z_even, z1, near0 = barrier((z_even, z1, near0))
-    some = jnp.concatenate([z1, z_even])
-    near1 = near_of(some)
-    far0 = far_of(own, near0)
-    z_odd = swap(z_even, "chan", 4)
-    z_odd, near1, far0 = barrier((z_odd, near1, far0))
-    near2 = near_of(z_odd)
-    here = jnp.concatenate([some, z_odd])
-    early1 = jnp.concatenate([own, here, near0])
-    near2, near1, far0, here, early1 = barrier((near2, near1, far0, here, early1))
-    near = jnp.concatenate([near1, near2])
-    far = far_of(here, near)
-    early1, early2 = in_cores(early1), in_cores(jnp.concatenate([far0, near]))
-
-    inputs = (trial_block, precond_diag, partners, stored_at, ham_blocks)
-    inputs, _ = barrier((inputs, near2))
-    trial_block, precond_diag, partners, stored_at, ham_blocks = inputs
-    ham, rows, zhm, zl, dc, gram_t = pl.pallas_call(
+    rows, ham, zhm, zl, dc, gram_t = pl.pallas_call(
         functools.partial(prepare_kernel, n_chan, n_rad),
-        in_specs=[whole] * 4 + [any_],
+        in_specs=[any_] * 5,
         out_specs=[whole] * 6,
         out_shape=[
+            jax.ShapeDtypeStruct((ch, ncoup), jnp.int32),
             pltpu.VMEM(ham_blocks.shape, BF16),
-            jax.ShapeDtypeStruct((ch, ncoup), jnp.int32),
             pltpu.VMEM((4 * k, lanes), BF16),
             pltpu.VMEM((2 * k, lanes), BF16),
             pltpu.VMEM((1, lanes), F32),
             pltpu.VMEM((k, 3 * k), F32),
         ],
-        scratch_shapes=[pltpu.SemaphoreType.DMA],
+        scratch_shapes=[
+            pltpu.VMEM(trial_block.shape, F32),
+            pltpu.VMEM(precond_diag.shape, F32),
+            pltpu.VMEM((ncoup, ch), jnp.int32),
+            pltpu.VMEM((stored_at.shape[0] // 128, 128), jnp.int32),
+            pltpu.SemaphoreType.DMA((5,)),
+        ],
         compiler_params=pltpu.CompilerParams(vmem_limit_bytes=VMEM_LIMIT),
         name="prepare",
-    )(trial_block, precond_diag, partners, stored_at.reshape(-1, 128), in_hbm(ham_blocks))
-    pieces = [x for pair in zip(early1, early2) for x in pair]
+    )(
+        in_hbm(trial_block),
+        in_hbm(precond_diag),
+        in_hbm(partners.T),
+        in_hbm(stored_at.reshape(-1, 128)),
+        in_hbm(ham_blocks),
+    )
+    far_own, near0, z1, z_even, rows = barrier((far_own, near0, z1, z_even, rows))
+    z_odd = swap(z_even, "chan", 4)
+    near1 = near_of(jnp.concatenate([z1, z_even]))
+    far_near = far_of(near0)
+    z_odd, near1, far_near = barrier((z_odd, near1, far_near))
+    near2 = near_of(z_odd)
+    early = in_cores(jnp.concatenate([own, z1, z_even, z_odd, near0, far_own, far_near, near1]))
+    near2, near1, early, far_own, far_near = barrier((near2, near1, early, far_own, far_near))
+    far = far_of(jnp.concatenate([z_even, z_odd, near1[1:], near2]))
+    far1 = swap(jnp.concatenate([far_own, far_near]), "chan", 4)
+    near2 = in_cores(near2)
+    pieces = [x for pair in zip(early, near2) for x in pair]
     table = pl.pallas_call(
         assemble_kernel,
         in_specs=[any_] * len(pieces),
@@ -340,31 +343,24 @@
         compiler_params=pltpu.CompilerParams(vmem_limit_bytes=VMEM_LIMIT),
         name="assemble",
     )(*pieces)
-    far, table, rows = barrier((far, table, rows))
-    last = [in_vmem(x) for x in in_cores(far)]
-
-    a0, sums, _ = pl.pallas_call(
+    far, far1, table = barrier((far, far1, table))
+    last = [in_vmem(x) for x in in_cores(jnp.concatenate([far, far1]))]
+
+    az, sums, _ = pl.pallas_call(
         apply_kernel,
         in_specs=[smem] + [whole] * (6 + n_rad),
         out_specs=[whole, whole, whole],
         out_shape=[
-            pltpu.VMEM((k, lanes), F32),
+            pltpu.VMEM((2 * k, lanes), BF16),
             jax.ShapeDtypeStruct((k, 8 * k), F32),
             pltpu.VMEM(table.shape, BF16),
         ],
         input_output_aliases={2: 2},
+        scratch_shapes=[pltpu.VMEM((k, lanes), F32)],
         compiler_params=pltpu.CompilerParams(vmem_limit_bytes=VMEM_LIMIT),
         name="apply",
     )(rows, in_vmem(ham), in_vmem(table), in_vmem(zhm), in_vmem(zl), in_vmem(dc), gram_t, *last)
 
-    az = pl.pallas_call(
-        terms_kernel,
-        in_specs=[whole, whole],
-        out_specs=whole,
-        out_shape=pltpu.VMEM((2 * k, lanes), BF16),
-        compiler_params=pltpu.CompilerParams(vmem_limit_bytes=VMEM_LIMIT),
-        name="terms",
-    )(in_vmem(a0), in_vmem(dc))
     sums = gather_sums(sums)
     new_block, ritz = pl.pallas_call(
         functools.partial(finish_kernel, total),

time: 70.2 us -> 63 us (0.90)
  waiting for transfers between devices: 33.8 us -> 17.7 us
  blocking collectives: 0 us -> 12.6 us
  local copies, waits for them, and re-layouts: 4.09 us -> 0.26 us
  starting transfers between devices: 14.8 us -> 16.6 us
  other arithmetic: 2.31 us -> 1.34 us
    all_to_all x0 -> x1, blocking collectives: none -> 12.6 us  [gather_sums(): lax.all_to_all(every, 'chan', split_axis=0, concat_axis=0, tiled=True)]
    all_to_all x1 -> x0, waiting for transfers between devices: 7.75 us -> none  [gather_sums(): lax.all_to_all(every, 'chan', split_axis=0, concat_axis=0, tiled=True)]
    ppermute x8 -> x9, waiting for transfers between devices: 15 us -> 10.1 us  [swap(): return lax.ppermute(x, axis, [(i, i ^ distance) for i in range(n)])]
    all_to_all x1 -> x0, starting transfers between devices: 3.69 us -> none  [gather_sums(): lax.all_to_all(every, 'chan', split_axis=0, concat_axis=0, tiled=True)]
    ppermute x5 -> x6, waiting for transfers between devices: 11.1 us -> 7.59 us  [plane_swap(): return lax.ppermute(x, ('chan', 'rad'), pairs)]
    ppermute x5 -> x6, starting transfers between devices: 5.22 us -> 8.22 us  [plane_swap(): return lax.ppermute(x, ('chan', 'rad'), pairs)]
    ppermute x8 -> x9, starting transfers between devices: 5.86 us -> 8.35 us  [swap(): return lax.ppermute(x, axis, [(i, i ^ distance) for i in range(n)])]
    unnamed x11 -> x7, local copies, waits for them, and re-layouts: 2.59 us -> 0.15 us
  transfers between devices with their start and end apart: 14 -> 15, of which waited for: 10 -> 9; matrix products, arithmetic and copies ran while one was open for 1% -> 0% of each run, Pallas kernels for 7% -> 7%
where the time goes in v10:
time: 63 us; the launch traced here: 62.8 us
  waiting for transfers between devices  17.7 us (28%)
  starting transfers between devices  16.6 us (26%)
  Pallas kernels  13.4 us (21%)
  blocking collectives  12.6 us (20%)
  other arithmetic  1.34 us (2%)
  between operations  0.82 us (1%)
    all_to_all x1, blocking collectives, gather_sums(): lax.all_to_all(every, 'chan', split_axis=0, concat_axis=0, tiled=True)  12.6 us
    ppermute x9, waiting for transfers between devices, swap(): return lax.ppermute(x, axis, [(i, i ^ distance) for i in range(n)])  10.1 us
    ppermute x9, starting transfers between devices, swap(): return lax.ppermute(x, axis, [(i, i ^ distance) for i in range(n)])  8.35 us
    ppermute x6, starting transfers between devices, plane_swap(): return lax.ppermute(x, ('chan', 'rad'), pairs)  8.22 us
    ppermute x6, waiting for transfers between devices, plane_swap(): return lax.ppermute(x, ('chan', 'rad'), pairs)  7.59 us
    pallas_call x1, Pallas kernels, body(): pl.pallas_call(apply_kernel, in_specs=[smem] + [whole] * (6 + n_rad), out...  5.85 us
    pallas_call x1, Pallas kernels, body(): pl.pallas_call(functools.partial(prepare_kernel, n_chan, n_rad), in_specs...  3.66 us
    pallas_call x1, Pallas kernels, body(): pl.pallas_call(functools.partial(finish_kernel, total), out_shape=[jax.Sh...  3.07 us
  transfers between devices with their start and end apart: 15, of which 9 were waited for; matrix products, arithmetic and copies ran while one was open for 0% of the time, Pallas kernels for 7%

profile of v10, /device:TPU:0, one launch (start us, length us, event | category | flops | bytes accessed | tf_op | source)
XLA Modules:
  0.0 62.8 jit_solution(10236466669611578947)
XLA Ops:
  0.6 1.1 %convert_element_type.3 = bf16[64,16,64]{2,1,0:T(8,128)(2,1)S(1)} convert(f32[64,16,64]{2,1,0:T(8,128)} %t_hbm.1) | non-fusion elementwise | flops 65536 | bytes 393216 | tf_op jit(solution)/shard_map/convert_element_type | solution.py:257
  1.7 0.5 collective-permute-start
  2.3 1.0 %collective-permute-done = bf16[32,16,64]{2,1,0:T(8,128)(2,1)S(1)} collective-permute-done((bf16[32,16,64]{2,1,0:T(8,128)(2,1)S(1)}, bf16[32,16,64]{2,1,0:T(8,128)(2,1)S(1)}, u32[]{:S(2)}, u32[]{:S(2)}) %collective-permute-start) | collective-permute-done | bytes 65568 | tf_op jit(solution)/shard_map/ppermute | solution.py:21
  3.3 0.1 constant_dynamic-update-slice_fusion.7
  3.4 4.0 %collective-permute-start.4 = (bf16[1,32,16,128]{3,2,1,0:T(8,128)(2,1)S(1)}, bf16[1,32,16,128]{3,2,1,0:T(8,128)(2,1)S(1)}, u32[]{:S(2)}, u32[]{:S(2)}) collective-permute-start(bf16[1,32,16,128]{3,2,1,0:T(8,128)(2,1)S(1)} %get-tuple-element.57), channel_id=1, source_target_pairs={{0,16},{2,18},{4,20},{6,22},{8,24},{10,26},{12,28},{14,30},{16,0},... | collective-permute-start | bytes 393224 | tf_op jit(solution)/shard_map/ppermute | solution.py:21
  7.4 1.6 %collective-permute-start.3 = (bf16[1,32,16,128]{3,2,1,0:T(8,128)(2,1)S(1)}, bf16[1,32,16,128]{3,2,1,0:T(8,128)(2,1)S(1)}, u32[]{:S(2)}, u32[]{:S(2)}) collective-permute-start(bf16[1,32,16,128]{3,2,1,0:T(8,128)(2,1)S(1)} %get-tuple-element.57), channel_id=1, source_target_pairs={{0,8},{2,10},{4,12},{6,14},{8,0},{10,2},{12,4},{14,6},{16,24},{18,... | collective-permute-start | bytes 393224 | tf_op jit(solution)/shard_map/ppermute | solution.py:21
  9.0 1.5 %collective-permute-start.2 = (bf16[1,32,16,128]{3,2,1,0:T(8,128)(2,1)S(1)}, bf16[1,32,16,128]{3,2,1,0:T(8,128)(2,1)S(1)}, u32[]{:S(2)}, u32[]{:S(2)}) collective-permute-start(bf16[1,32,16,128]{3,2,1,0:T(8,128)(2,1)S(1)} %get-tuple-element.57), channel_id=1, source_target_pairs={{0,2},{1,5},{2,0},{3,7},{4,6},{5,1},{6,4},{7,3},{8,10},{9,13},{10,... | collective-permute-start | bytes 393224 | tf_op jit(solution)/shard_map/ppermute | solution.py:30
  10.5 1.5 %collective-permute-start.1 = (bf16[1,32,16,128]{3,2,1,0:T(8,128)(2,1)S(1)}, bf16[1,32,16,128]{3,2,1,0:T(8,128)(2,1)S(1)}, u32[]{:S(2)}, u32[]{:S(2)}) collective-permute-start(bf16[1,32,16,128]{3,2,1,0:T(8,128)(2,1)S(1)} %get-tuple-element.57), channel_id=1, source_target_pairs={{0,4},{1,3},{2,6},{3,1},{4,0},{5,7},{6,2},{7,5},{8,12},{9,11},{10,... | collective-permute-start | bytes 393224 | tf_op jit(solution)/shard_map/ppermute | solution.py:30
  12.0 3.7 %prepare.1 = (s32[64,8]{1,0:T(8,128)S(1)}, bf16[64,8,64,128]{3,2,1,0:T(8,128)(2,1)S(1)}, bf16[64,4096]{1,0:T(8,128)(2,1)S(1)}, bf16[32,4096]{1,0:T(8,128)(2,1)S(...) custom-call(f32[64,16,64]{2,1,0:T(8,128)} %t_hbm.1, f32[64,64]{1,0:T(8,128)} %d_hbm.1, s32[8,64]{1,0:T(8,128)} %bitcast.14, ...), custom_call_target="tpu_custom_call" | custom-call | tf_op jit(solution)/shard_map/prepare/pallas_call | solution.py:297
  15.7 0.0 collective-permute-done.3
  15.7 1.1 %collective-permute-start.6 = (bf16[2,32,16,128]{3,2,1,0:T(8,128)(2,1)S(1)}, bf16[2,32,16,128]{3,2,1,0:T(8,128)(2,1)S(1)}, u32[]{:S(2)}, u32[]{:S(2)}) collective-permute-start(bf16[2,32,16,128]{3,2,1,0:T(8,128)(2,1)S(1)} %pad_maximum_fusion.1), channel_id=1, source_target_pairs={{0,2},{1,5},{2,0},{3,7},{4,6},{5,1},{6,4},{7,3},{8,10},{9,13},{10,... | collective-permute-start | bytes 786440 | tf_op jit(solution)/shard_map/ppermute | solution.py:30
  16.8 0.6 collective-permute-start.5
  17.4 1.5 %collective-permute-start.7 = (bf16[1,32,16,128]{3,2,1,0:T(8,128)(2,1)S(1)}, bf16[1,32,16,128]{3,2,1,0:T(8,128)(2,1)S(1)}, u32[]{:S(2)}, u32[]{:S(2)}) collective-permute-start(bf16[1,32,16,128]{3,2,1,0:T(8,128)(2,1)S(1)} %collective-permute-done.2), channel_id=1, source_target_pairs={{0,4},{1,3},{2,6},{3,1},{4,0},{5,7},{6,2},{7,5},{8,12},{9,11},{10,... | collective-permute-start | bytes 393224 | tf_op jit(solution)/shard_map/ppermute | solution.py:30
  19.0 3.4 %collective-permute-done.7 = bf16[1,32,16,128]{3,2,1,0:T(8,128)(2,1)S(1)} collective-permute-done((bf16[1,32,16,128]{3,2,1,0:T(8,128)(2,1)S(1)}, bf16[1,32,16,128]{3,2,1,0:T(8,128)(2,1)S(1)}, u32[]{:S(2)}, u32[]{:S(2)}) %collective-permute-start.7) | collective-permute-done | bytes 131104 | tf_op jit(solution)/shard_map/ppermute | solution.py:30
  22.4 0.6 collective-permute-done.6
  23.1 0.1 collective-permute-start.9
  23.2 1.6 %collective-permute-start.8 = (bf16[1,32,16,128]{3,2,1,0:T(8,128)(2,1)S(1)}, bf16[1,32,16,128]{3,2,1,0:T(8,128)(2,1)S(1)}, u32[]{:S(2)}, u32[]{:S(2)}) collective-permute-start(bf16[1,32,16,128]{3,2,1,0:T(8,128)(2,1)S(1)} %collective-permute-done.5), channel_id=1, source_target_pairs={{0,2},{1,5},{2,0},{3,7},{4,6},{5,1},{6,4},{7,3},{8,10},{9,13},{10,... | collective-permute-start | bytes 393224 | tf_op jit(solution)/shard_map/ppermute | solution.py:30
  24.8 3.5 %collective-permute-done.8.refs_1_ = bf16[1,32,16,128]{3,2,1,0:T(8,128)(2,1)S(1)} collective-permute-done((bf16[1,32,16,128]{3,2,1,0:T(8,128)(2,1)S(1)}, bf16[1,32,16,128]{3,2,1,0:T(8,128)(2,1)S(1)}, u32[]{:S(2)}, u32[]{:S(2)}) %collective-permute-start.8) | collective-permute-done | bytes 131104 | tf_op jit(solution)/shard_map/ppermute | solution.py:30
  28.3 0.1 pad_maximum_fusion
  28.4 1.1 %collective-permute-start.10 = (bf16[4,32,16,128]{3,2,1,0:T(8,128)(2,1)S(1)}, bf16[4,32,16,128]{3,2,1,0:T(8,128)(2,1)S(1)}, u32[]{:S(2)}, u32[]{:S(2)}) collective-permute-start(bf16[4,32,16,128]{3,2,1,0:T(8,128)(2,1)S(1)} %pad_maximum_fusion), channel_id=1, source_target_pairs={{0,4},{1,3},{2,6},{3,1},{4,0},{5,7},{6,2},{7,5},{8,12},{9,11},{10,... | collective-permute-start | bytes 1572872 | tf_op jit(solution)/shard_map/ppermute | solution.py:30
  29.5 1.3 %collective-permute-start.11 = (bf16[2,32,16,128]{3,2,1,0:T(8,128)(2,1)S(1)}, bf16[2,32,16,128]{3,2,1,0:T(8,128)(2,1)S(1)}, u32[]{:S(2)}, u32[]{:S(2)}) collective-permute-start(bf16[2,32,16,128]{3,2,1,0:T(8,128)(2,1)S(1)} %pad_maximum_fusion.2), channel_id=1, source_target_pairs={{0,8},{2,10},{4,12},{6,14},{8,0},{10,2},{12,4},{14,6},{16,24},{18,... | collective-permute-start | bytes 786440 | tf_op jit(solution)/shard_map/ppermute | solution.py:21
  30.8 1.3 %collective-permute-done.12.refs_3_ = bf16[1,32,16,128]{3,2,1,0:T(8,128)(2,1)S(1)} collective-permute-done((bf16[1,32,16,128]{3,2,1,0:T(8,128)(2,1)S(1)}, bf16[1,32,16,128]{3,2,1,0:T(8,128)(2,1)S(1)}, u32[]{:S(2)}, u32[]{:S(2)}) %collective-permute-start.12) | collective-permute-done | bytes 131104 | tf_op jit(solution)/shard_map/ppermute | solution.py:21
  32.2 0.9 %assemble.1._ = bf16[32,32,16,128]{3,2,1,0:T(8,128)(2,1)S(1)} custom-call(bf16[9,32,16,128]{3,2,1,0:T(8,128)(2,1)S(1)} %constant_dynamic-update-slice_fusion.refs_0_, bf16[1,32,16,128]{3,2,1,0:T(8,128)(2,1)S(1)} %collective-permute-done.8.refs_1_, bf16[9,32,16,128]{3,2,1,0:T(8,128)(2,1)S(1)} %collective-permute-done.9.refs_2_, ...), custom_call_target="tpu_custom_call" | custom-call | tf_op jit(solution)/shard_map/assemble/pallas_call | solution.py:337
  33.0 4.5 %collective-permute-done.11 = bf16[2,32,16,128]{3,2,1,0:T(8,128)(2,1)S(1)} collective-permute-done((bf16[2,32,16,128]{3,2,1,0:T(8,128)(2,1)S(1)}, bf16[2,32,16,128]{3,2,1,0:T(8,128)(2,1)S(1)}, u32[]{:S(2)}, u32[]{:S(2)}) %collective-permute-start.11) | collective-permute-done | bytes 262176 | tf_op jit(solution)/shard_map/ppermute | solution.py:21
  37.5 0.1 collective-permute-done.10
  37.7 0.1 collective-permute-start.13
  37.8 2.3 %collective-permute-done.13.rest_1_ = bf16[6,32,16,128]{3,2,1,0:T(8,128)(2,1)S(1)} collective-permute-done((bf16[6,32,16,128]{3,2,1,0:T(8,128)(2,1)S(1)}, bf16[6,32,16,128]{3,2,1,0:T(8,128)(2,1)S(1)}, u32[]{:S(2)}, u32[]{:S(2)}) %collective-permute-start.13) | collective-permute-done | bytes 786464 | tf_op jit(solution)/shard_map/ppermute | solution.py:21
  40.0 5.8 %apply.1 = (bf16[32,4096]{1,0:T(8,128)(2,1)S(1)}, f32[16,128]{1,0:T(8,128)S(1)}, bf16[32,32,16,128]{3,2,1,0:T(8,128)(2,1)S(1)}) custom-call(s32[64,8]{1,0:T(8,128)S(1)} %get-tuple-element.30.rows_ref, bf16[64,8,64,128]{3,2,1,0:T(8,128)(2,1)S(1)} %get-tuple-element.31.ham_ref, ...), custom_call_target="tpu_custom_call", output_to_operand_aliasing={{2}: (2, {})} | custom-call | tf_op jit(solution)/shard_map/apply/pallas_call | solution.py:349
  45.9 0.2 collective-permute-start.14
  46.0 1.0 %collective-permute-done.14 = f32[16,128]{1,0:T(8,128)S(1)} collective-permute-done((f32[16,128]{1,0:T(8,128)S(1)}, f32[16,128]{1,0:T(8,128)S(1)}, u32[]{:S(2)}, u32[]{:S(2)}) %collective-permute-start.14) | collective-permute-done | bytes 8224 | tf_op jit(solution)/shard_map/ppermute | solution.py:21
  47.1 12.6 %all_to_all.5.sums_ref = f32[16,16,128]{2,1,0:T(8,128)S(1)} all-to-all(f32[16,16,128]{2,1,0:T(8,128)S(1)} %broadcast_in_dim.7), channel_id=1, replica_groups=mesh['chan'=16,'rad'=2] {'chan'}, dimensions={0} | all-to-all | bytes 262144 | tf_op jit(solution)/shard_map/all_to_all | solution.py:250
  59.7 3.1 %finish.1 = (f32[64,16,64]{2,1,0:T(8,128)}, f32[1,16]{1,0:T(1,128)}) custom-call(f32[16,16,128]{2,1,0:T(8,128)S(1)} %all_to_all.5.sums_ref, bf16[32,4096]{1,0:T(8,128)(2,1)S(1)} %get-tuple-element.53.az_ref, bf16[64,4096]{1,0:T(8,128)(2,1)S(1)} %get-tuple-element.46.zhm_ref), custom_call_target="tpu_custom_call" | custom-call | tf_op jit(solution)/shard_map/finish/pallas_call | solution.py:365
  (22 shorter events, 0.4 us)
Async XLA Ops:
  1.7 1.5 %collective-permute-start = (bf16[32,16,64]{2,1,0:T(8,128)(2,1)S(1)}, bf16[32,16,64]{2,1,0:T(8,128)(2,1)S(1)}, u32[]{:S(2)}, u32[]{:S(2)}) collective-permute-start(bf16[32,16,64]{2,1,0:T(8,128)(2,1)S(1)} %dynamic-slice_bitcast_fusion), channel_id=1, source_target_pairs={{0,1},{1,0},{2,3},{3,2},{4,5},{5,4},{6,7},{7,6},{8,9},{9,8},{10,11... | collective-permute-start | bytes 196616 | tf_op jit(solution)/shard_map/ppermute | solution.py:21
  3.4 12.3 %collective-permute-start.4 = (bf16[1,32,16,128]{3,2,1,0:T(8,128)(2,1)S(1)}, bf16[1,32,16,128]{3,2,1,0:T(8,128)(2,1)S(1)}, u32[]{:S(2)}, u32[]{:S(2)}) collective-permute-start(bf16[1,32,16,128]{3,2,1,0:T(8,128)(2,1)S(1)} %get-tuple-element.57), channel_id=1, source_target_pairs={{0,16},{2,18},{4,20},{6,22},{8,24},{10,26},{12,28},{14,30},{16,0},... | collective-permute-start | bytes 393224 | tf_op jit(solution)/shard_map/ppermute | solution.py:21
  7.4 8.3 %collective-permute-start.3 = (bf16[1,32,16,128]{3,2,1,0:T(8,128)(2,1)S(1)}, bf16[1,32,16,128]{3,2,1,0:T(8,128)(2,1)S(1)}, u32[]{:S(2)}, u32[]{:S(2)}) collective-permute-start(bf16[1,32,16,128]{3,2,1,0:T(8,128)(2,1)S(1)} %get-tuple-element.57), channel_id=1, source_target_pairs={{0,8},{2,10},{4,12},{6,14},{8,0},{10,2},{12,4},{14,6},{16,24},{18,... | collective-permute-start | bytes 393224 | tf_op jit(solution)/shard_map/ppermute | solution.py:21
  9.0 6.7 %collective-permute-start.2 = (bf16[1,32,16,128]{3,2,1,0:T(8,128)(2,1)S(1)}, bf16[1,32,16,128]{3,2,1,0:T(8,128)(2,1)S(1)}, u32[]{:S(2)}, u32[]{:S(2)}) collective-permute-start(bf16[1,32,16,128]{3,2,1,0:T(8,128)(2,1)S(1)} %get-tuple-element.57), channel_id=1, source_target_pairs={{0,2},{1,5},{2,0},{3,7},{4,6},{5,1},{6,4},{7,3},{8,10},{9,13},{10,... | collective-permute-start | bytes 393224 | tf_op jit(solution)/shard_map/ppermute | solution.py:30
  10.5 5.2 %collective-permute-start.1 = (bf16[1,32,16,128]{3,2,1,0:T(8,128)(2,1)S(1)}, bf16[1,32,16,128]{3,2,1,0:T(8,128)(2,1)S(1)}, u32[]{:S(2)}, u32[]{:S(2)}) collective-permute-start(bf16[1,32,16,128]{3,2,1,0:T(8,128)(2,1)S(1)} %get-tuple-element.57), channel_id=1, source_target_pairs={{0,4},{1,3},{2,6},{3,1},{4,0},{5,7},{6,2},{7,5},{8,12},{9,11},{10,... | collective-permute-start | bytes 393224 | tf_op jit(solution)/shard_map/ppermute | solution.py:30
  15.7 7.3 %collective-permute-start.6 = (bf16[2,32,16,128]{3,2,1,0:T(8,128)(2,1)S(1)}, bf16[2,32,16,128]{3,2,1,0:T(8,128)(2,1)S(1)}, u32[]{:S(2)}, u32[]{:S(2)}) collective-permute-start(bf16[2,32,16,128]{3,2,1,0:T(8,128)(2,1)S(1)} %pad_maximum_fusion.1), channel_id=1, source_target_pairs={{0,2},{1,5},{2,0},{3,7},{4,6},{5,1},{6,4},{7,3},{8,10},{9,13},{10,... | collective-permute-start | bytes 786440 | tf_op jit(solution)/shard_map/ppermute | solution.py:30
  16.8 5.6 %collective-permute-start.5 = (bf16[1,32,16,128]{3,2,1,0:T(8,128)(2,1)S(1)}, bf16[1,32,16,128]{3,2,1,0:T(8,128)(2,1)S(1)}, u32[]{:S(2)}, u32[]{:S(2)}) collective-permute-start(bf16[1,32,16,128]{3,2,1,0:T(8,128)(2,1)S(1)} %collective-permute-done.4), channel_id=1, source_target_pairs={{0,8},{2,10},{4,12},{6,14},{8,0},{10,2},{12,4},{14,6},{16,24},{18,... | collective-permute-start | bytes 393224 | tf_op jit(solution)/shard_map/ppermute | solution.py:21
  17.4 5.0 %collective-permute-start.7 = (bf16[1,32,16,128]{3,2,1,0:T(8,128)(2,1)S(1)}, bf16[1,32,16,128]{3,2,1,0:T(8,128)(2,1)S(1)}, u32[]{:S(2)}, u32[]{:S(2)}) collective-permute-start(bf16[1,32,16,128]{3,2,1,0:T(8,128)(2,1)S(1)} %collective-permute-done.2), channel_id=1, source_target_pairs={{0,4},{1,3},{2,6},{3,1},{4,0},{5,7},{6,2},{7,5},{8,12},{9,11},{10,... | collective-permute-start | bytes 393224 | tf_op jit(solution)/shard_map/ppermute | solution.py:30
  23.1 5.1 %collective-permute-start.9 = (bf16[9,32,16,128]{3,2,1,0:T(8,128)(2,1)S(1)}, bf16[9,32,16,128]{3,2,1,0:T(8,128)(2,1)S(1)}, u32[]{:S(2)}, u32[]{:S(2)}) collective-permute-start(bf16[9,32,16,128]{3,2,1,0:T(8,128)(2,1)S(1)} %constant_dynamic-update-slice_fusion.refs_0_), channel_id=1, source_target_pairs={{0,1},{1,0},{2,3},{3,2},{4,5},{5,4},{6,7},{7,6},{8,9},{9,8},{10,11... | collective-permute-start | bytes 3538952 | tf_op jit(solution)/shard_map/ppermute | solution.py:21
  23.2 5.0 %collective-permute-start.8 = (bf16[1,32,16,128]{3,2,1,0:T(8,128)(2,1)S(1)}, bf16[1,32,16,128]{3,2,1,0:T(8,128)(2,1)S(1)}, u32[]{:S(2)}, u32[]{:S(2)}) collective-permute-start(bf16[1,32,16,128]{3,2,1,0:T(8,128)(2,1)S(1)} %collective-permute-done.5), channel_id=1, source_target_pairs={{0,2},{1,5},{2,0},{3,7},{4,6},{5,1},{6,4},{7,3},{8,10},{9,13},{10,... | collective-permute-start | bytes 393224 | tf_op jit(solution)/shard_map/ppermute | solution.py:30
  28.4 9.2 %collective-permute-start.10 = (bf16[4,32,16,128]{3,2,1,0:T(8,128)(2,1)S(1)}, bf16[4,32,16,128]{3,2,1,0:T(8,128)(2,1)S(1)}, u32[]{:S(2)}, u32[]{:S(2)}) collective-permute-start(bf16[4,32,16,128]{3,2,1,0:T(8,128)(2,1)S(1)} %pad_maximum_fusion), channel_id=1, source_target_pairs={{0,4},{1,3},{2,6},{3,1},{4,0},{5,7},{6,2},{7,5},{8,12},{9,11},{10,... | collective-permute-start | bytes 1572872 | tf_op jit(solution)/shard_map/ppermute | solution.py:30
  29.5 8.1 %collective-permute-start.11 = (bf16[2,32,16,128]{3,2,1,0:T(8,128)(2,1)S(1)}, bf16[2,32,16,128]{3,2,1,0:T(8,128)(2,1)S(1)}, u32[]{:S(2)}, u32[]{:S(2)}) collective-permute-start(bf16[2,32,16,128]{3,2,1,0:T(8,128)(2,1)S(1)} %pad_maximum_fusion.2), channel_id=1, source_target_pairs={{0,8},{2,10},{4,12},{6,14},{8,0},{10,2},{12,4},{14,6},{16,24},{18,... | collective-permute-start | bytes 786440 | tf_op jit(solution)/shard_map/ppermute | solution.py:21
  30.8 1.3 %collective-permute-start.12 = (bf16[1,32,16,128]{3,2,1,0:T(8,128)(2,1)S(1)}, bf16[1,32,16,128]{3,2,1,0:T(8,128)(2,1)S(1)}, u32[]{:S(2)}, u32[]{:S(2)}) collective-permute-start(bf16[1,32,16,128]{3,2,1,0:T(8,128)(2,1)S(1)} %collective-permute-done.8.refs_1_), channel_id=1, source_target_pairs={{0,1},{1,0},{2,3},{3,2},{4,5},{5,4},{6,7},{7,6},{8,9},{9,8},{10,11... | collective-permute-start | bytes 393224 | tf_op jit(solution)/shard_map/ppermute | solution.py:21
  37.7 2.4 %collective-permute-start.13 = (bf16[6,32,16,128]{3,2,1,0:T(8,128)(2,1)S(1)}, bf16[6,32,16,128]{3,2,1,0:T(8,128)(2,1)S(1)}, u32[]{:S(2)}, u32[]{:S(2)}) collective-permute-start(bf16[6,32,16,128]{3,2,1,0:T(8,128)(2,1)S(1)} %constant_dynamic-update-slice_fusion.8.rest_0_), channel_id=1, source_target_pairs={{0,1},{1,0},{2,3},{3,2},{4,5},{5,4},{6,7},{7,6},{8,9},{9,8},{10,11... | collective-permute-start | bytes 2359304 | tf_op jit(solution)/shard_map/ppermute | solution.py:21
  45.9 1.2 %collective-permute-start.14 = (f32[16,128]{1,0:T(8,128)S(1)}, f32[16,128]{1,0:T(8,128)S(1)}, u32[]{:S(2)}, u32[]{:S(2)}) collective-permute-start(f32[16,128]{1,0:T(8,128)S(1)} %get-tuple-element.52), channel_id=1, source_target_pairs={{0,1},{1,0},{2,3},{3,2},{4,5},{5,4},{6,7},{7,6},{8,9},{9,8},{10,11... | collective-permute-start | bytes 24584 | tf_op jit(solution)/shard_map/ppermute | solution.py:21

commit v11 on v10

--- a/solution.py
+++ b/solution.py
@@ -31,11 +31,19 @@
 
 
 def table_piece(z, part, nz):
-    z = z if nz == 4 else jnp.where(z < 2, z, jnp.where((z & 1) == 1, (nz + z - 1) >> 1, 1 + (z >> 1)))
-    near = jnp.where(z == 0, nz, nz + 2 + z)
-    second = part & 1
-    far = jnp.where(z == 0, nz + 1, jnp.where(z == 1, 4 * nz - 2, 2 * nz + z + second * (nz - 3))) + second
-    return jnp.where(part == 0, z, jnp.where(part == 1, near, far))
+    some, odd = nz // 2, nz // 2 - 1
+    is_odd = (z & 1 == 1) & (z > 1)
+    i = jnp.where(is_odd, (z - 3) >> 1, jnp.where(z == 1, 0, z >> 1))
+    base = 2 * some + odd + 4
+
+    def pick(own, of_some, of_odd):
+        return jnp.where(z == 0, own, jnp.where(is_odd, of_odd + i, of_some + i))
+
+    here = pick(0, 1, 2 * some + 4)
+    near = pick(some + 1, some + 4, base + odd + some)
+    far = pick(some + 2, base + odd, base + 2 * odd + some)
+    both = pick(some + 3, base + 3 * odd + some, base)
+    return jnp.where(part == 0, here, jnp.where(part == 1, near, jnp.where(part == 2, far, both)))
 
 
 def in_vmem(x):
@@ -112,13 +120,11 @@
 
 def assemble_kernel(*refs):
     pieces, table_ref, sems = refs[:-2], refs[-2], refs[-1]
-    cores = len(pieces) // 2
+    each = table_ref.shape[0] // len(pieces)
     copies = []
     for i, piece in enumerate(pieces):
-        at = (i // 2) * (table_ref.shape[0] // cores) + (i % 2) * pieces[0].shape[0]
-        copies.append(
-            pltpu.make_async_copy(piece, table_ref.at[pl.ds(at, piece.shape[0])], sems.at[i])
-        )
+        place = table_ref.at[pl.ds(i * each, piece.shape[0])]
+        copies.append(pltpu.make_async_copy(piece, place, sems.at[i]))
         copies[-1].start()
     for copy in copies:
         copy.wait()
@@ -254,10 +260,10 @@
     n_rad = lax.axis_size("rad")
     ch, k, r = trial_block.shape
     me = lax.axis_index("rad")
-    rounded = trial_block.astype(BF16).reshape(n_rad, ch // n_rad, k, r)
+    shares = trial_block.reshape(n_rad, ch // n_rad, k, r)
     got = []
     for d in range(n_rad):
-        part = lax.dynamic_index_in_dim(rounded, me ^ d, 0, keepdims=False)
+        part = lax.dynamic_index_in_dim(shares, me ^ d, 0, keepdims=False).astype(BF16)
         got.append(swap(part, "rad", d) if d else part)
     lanes = []
     for c in range(n_rad):
@@ -291,7 +297,7 @@
         return [x] + [swap(x, "rad", c) for c in range(1, n_rad)]
 
     own = own_share(trial_block)[None]
-    near0, far_own = near_of(own), far_of(own)
+    near0, far_own, diag0 = near_of(own), far_of(own), swap(own, "chan", 3)
     z1 = swap(own, "chan", 4)
     z_even = jnp.concatenate([swap(own, "chan", 4 * z) for z in range(2, nz, 2)])
     rows, ham, zhm, zl, dc, gram_t = pl.pallas_call(
@@ -322,29 +328,27 @@
         in_hbm(stored_at.reshape(-1, 128)),
         in_hbm(ham_blocks),
     )
-    far_own, near0, z1, z_even, rows = barrier((far_own, near0, z1, z_even, rows))
+    far_own, near0, diag0, z1, z_even, rows = barrier((far_own, near0, diag0, z1, z_even, rows))
+    some = jnp.concatenate([z1, z_even])
+    near1, far1 = near_of(some), far_of(some)
     z_odd = swap(z_even, "chan", 4)
-    near1 = near_of(jnp.concatenate([z1, z_even]))
-    far_near = far_of(near0)
-    z_odd, near1, far_near = barrier((z_odd, near1, far_near))
-    near2 = near_of(z_odd)
-    early = in_cores(jnp.concatenate([own, z1, z_even, z_odd, near0, far_own, far_near, near1]))
-    near2, near1, early, far_own, far_near = barrier((near2, near1, early, far_own, far_near))
-    far = far_of(jnp.concatenate([z_even, z_odd, near1[1:], near2]))
-    far1 = swap(jnp.concatenate([far_own, far_near]), "chan", 4)
-    near2 = in_cores(near2)
-    pieces = [x for pair in zip(early, near2) for x in pair]
+    diag_odd = jnp.concatenate([swap(diag0, "chan", 4 * z) for z in range(3, nz, 2)])
+    near1, z_odd = barrier((near1, z_odd))
+    early = in_cores(jnp.concatenate([own, z1, z_even, near0, far_own, diag0, near1, z_odd]))
+    near_odd = near_of(z_odd)
+    far2 = far_of(jnp.concatenate([z_odd, near1]))
     table = pl.pallas_call(
         assemble_kernel,
-        in_specs=[any_] * len(pieces),
+        in_specs=[any_] * n_rad,
         out_specs=whole,
         out_shape=pltpu.VMEM((4 * nz * n_rad,) + own.shape[1:], BF16),
-        scratch_shapes=[pltpu.SemaphoreType.DMA((len(pieces),))],
+        scratch_shapes=[pltpu.SemaphoreType.DMA((n_rad,))],
         compiler_params=pltpu.CompilerParams(vmem_limit_bytes=VMEM_LIMIT),
         name="assemble",
-    )(*pieces)
-    far, far1, table = barrier((far, far1, table))
-    last = [in_vmem(x) for x in in_cores(jnp.concatenate([far, far1]))]
+    )(*early)
+    last = barrier((diag_odd, far1, near_odd, far2, table))
+    table = last[4]
+    last = [in_vmem(x) for x in in_cores(jnp.concatenate(last[:4]))]
 
     az, sums, _ = pl.pallas_call(
         apply_kernel,

time: 63 us -> 62.6 us (level)
  local copies, waits for them, and re-layouts: 0.26 us -> 1.32 us
  blocking collectives: 12.6 us -> 11.7 us
    ppermute x9, starting transfers between devices: 8.35 us -> 10.7 us  [swap(): return lax.ppermute(x, axis, [(i, i ^ distance) for i in range(n)])]
    ppermute x6, starting transfers between devices: 8.22 us -> 6.27 us  [plane_swap(): return lax.ppermute(x, ('chan', 'rad'), pairs)]
    ppermute x6, waiting for transfers between devices: 7.59 us -> 6.32 us  [plane_swap(): return lax.ppermute(x, ('chan', 'rad'), pairs)]
    convert_element_type x1 -> x0, other arithmetic: 1.08 us -> none  [own_share(): rounded = trial_block.astype(BF16).reshape(n_rad, ch // n_rad, k, r)]
    convert_element_type x0 -> x1, local copies, waits for them, and re-layouts: none -> 0.97 us  [own_share(): lax.dynamic_index_in_dim(shares, me ^ d, 0, keepdims=False).astype(BF16)]
    select_n x1, other arithmetic: 0.02 us -> 0.97 us  [own_share(): x = jnp.where(me ^ d == c, got[d], x)]
    all_to_all x1, blocking collectives: 12.6 us -> 11.7 us  [gather_sums(): lax.all_to_all(every, 'chan', split_axis=0, concat_axis=0, tiled=True)]
    ppermute x9, waiting for transfers between devices: 10.1 us -> 11 us  [swap(): return lax.ppermute(x, axis, [(i, i ^ distance) for i in range(n)])]
  transfers between devices with their start and end apart: 15 -> 15, of which waited for: 9 -> 8; matrix products, arithmetic and copies ran while one was open for 0% -> 0% of each run, Pallas kernels for 7% -> 7%
where the time goes in v11:
time: 62.6 us; the launch traced here: 62.3 us
  waiting for transfers between devices  17.4 us (28%)
  starting transfers between devices  16.9 us (27%)
  Pallas kernels  13.1 us (21%)
  blocking collectives  11.7 us (19%)
  local copies, waits for them, and re-layouts  1.32 us (2%)
  other arithmetic  1.13 us (2%)
  between operations  0.8 us (1%)
    all_to_all x1, blocking collectives, gather_sums(): lax.all_to_all(every, 'chan', split_axis=0, concat_axis=0, tiled=True)  11.7 us
    ppermute x9, waiting for transfers between devices, swap(): return lax.ppermute(x, axis, [(i, i ^ distance) for i in range(n)])  11 us
    ppermute x9, starting transfers between devices, swap(): return lax.ppermute(x, axis, [(i, i ^ distance) for i in range(n)])  10.7 us
    ppermute x6, waiting for transfers between devices, plane_swap(): return lax.ppermute(x, ('chan', 'rad'), pairs)  6.32 us
    ppermute x6, starting transfers between devices, plane_swap(): return lax.ppermute(x, ('chan', 'rad'), pairs)  6.27 us
    pallas_call x1, Pallas kernels, body(): pl.pallas_call(apply_kernel, in_specs=[smem] + [whole] * (6 + n_rad), out...  5.87 us
    pallas_call x1, Pallas kernels, body(): pl.pallas_call(functools.partial(prepare_kernel, n_chan, n_rad), in_specs...  3.66 us
    pallas_call x1, Pallas kernels, body(): pl.pallas_call(functools.partial(finish_kernel, total), out_shape=[jax.Sh...  3.07 us
  transfers between devices with their start and end apart: 15, of which 8 were waited for; matrix products, arithmetic and copies ran while one was open for 0% of the time, Pallas kernels for 7%

profile of v11, /device:TPU:0, one launch (start us, length us, event | category | flops | bytes accessed | tf_op | source)
XLA Modules:
  0.0 62.3 jit_solution(5767197545467608045)
XLA Ops:
  0.6 1.0 %fusion = bf16[32,16,64]{2,1,0:T(8,128)(2,1)S(1)} fusion(f32[2,32,16,64]{3,2,1,0:T(8,128)} %bitcast.15, s32[]{:T(128)S(6)} %select_n.22), kind=kLoop, calls=%fused_computation.3 | loop fusion | bytes 131076 | tf_op jit(solution)/shard_map/convert_element_type | solution.py:266
  1.6 0.5 collective-permute-start
  2.1 1.0 %collective-permute-done = bf16[32,16,64]{2,1,0:T(8,128)(2,1)S(1)} collective-permute-done((bf16[32,16,64]{2,1,0:T(8,128)(2,1)S(1)}, bf16[32,16,64]{2,1,0:T(8,128)(2,1)S(1)}, u32[]{:S(2)}, u32[]{:S(2)}) %collective-permute-start) | collective-permute-done | bytes 65568 | tf_op jit(solution)/shard_map/ppermute | solution.py:21
  3.1 1.0 %broadcast_select_fusion.1 = (bf16[32,16,64]{2,1,0:T(8,128)(2,1)S(1)}, bf16[32,16,64]{2,1,0:T(8,128)(2,1)S(1)}) fusion(bf16[32,16,64]{2,1,0:T(8,128)(2,1)S(1)} %collective-permute-done, pred[]{:T(512)S(6)} %eq.6, f32[2,32,16,64]{3,2,1,0:T(8,128)} %bitcast.16, s32[]{:T(128)S(6)} %select_n.23, pred[]{:T(512)S(6)} %eq.7), kind=kLoop, calls=%fused_computation.7 | loop fusion | flops 65536 | bytes 262150 | tf_op jit(solution)/shard_map/jit(_where)/select_n | solution.py:272
  4.1 0.1 constant_dynamic-update-slice_fusion.9
  4.2 4.0 %collective-permute-start.5 = (bf16[1,32,16,128]{3,2,1,0:T(8,128)(2,1)S(1)}, bf16[1,32,16,128]{3,2,1,0:T(8,128)(2,1)S(1)}, u32[]{:S(2)}, u32[]{:S(2)}) collective-permute-start(bf16[1,32,16,128]{3,2,1,0:T(8,128)(2,1)S(1)} %get-tuple-element.49), channel_id=1, source_target_pairs={{0,16},{2,18},{4,20},{6,22},{8,24},{10,26},{12,28},{14,30},{16,0},... | collective-permute-start | bytes 393224 | tf_op jit(solution)/shard_map/ppermute | solution.py:21
  8.2 1.6 %collective-permute-start.4 = (bf16[1,32,16,128]{3,2,1,0:T(8,128)(2,1)S(1)}, bf16[1,32,16,128]{3,2,1,0:T(8,128)(2,1)S(1)}, u32[]{:S(2)}, u32[]{:S(2)}) collective-permute-start(bf16[1,32,16,128]{3,2,1,0:T(8,128)(2,1)S(1)} %get-tuple-element.49), channel_id=1, source_target_pairs={{0,8},{2,10},{4,12},{6,14},{8,0},{10,2},{12,4},{14,6},{16,24},{18,... | collective-permute-start | bytes 393224 | tf_op jit(solution)/shard_map/ppermute | solution.py:21
  9.8 2.4 %collective-permute-start.3 = (bf16[1,32,16,128]{3,2,1,0:T(8,128)(2,1)S(1)}, bf16[1,32,16,128]{3,2,1,0:T(8,128)(2,1)S(1)}, u32[]{:S(2)}, u32[]{:S(2)}) collective-permute-start(bf16[1,32,16,128]{3,2,1,0:T(8,128)(2,1)S(1)} %get-tuple-element.49), channel_id=1, source_target_pairs={{0,6},{2,4},{4,2},{6,0},{8,14},{10,12},{12,10},{14,8},{16,22},{18,... | collective-permute-start | bytes 393224 | tf_op jit(solution)/shard_map/ppermute | solution.py:21
  12.3 0.5 collective-permute-start.2
  12.8 0.5 collective-permute-start.1
  13.3 3.7 %prepare.1 = (s32[64,8]{1,0:T(8,128)S(1)}, bf16[64,8,64,128]{3,2,1,0:T(8,128)(2,1)S(1)}, bf16[64,4096]{1,0:T(8,128)(2,1)S(1)}, bf16[32,4096]{1,0:T(8,128)(2,1)S(...) custom-call(f32[64,16,64]{2,1,0:T(8,128)} %t_hbm.1, f32[64,64]{1,0:T(8,128)} %d_hbm.1, s32[8,64]{1,0:T(8,128)} %bitcast.17, ...), custom_call_target="tpu_custom_call" | custom-call | tf_op jit(solution)/shard_map/prepare/pallas_call | solution.py:303
  17.0 1.6 %collective-permute-done.2 = bf16[1,32,16,128]{3,2,1,0:T(8,128)(2,1)S(1)} collective-permute-done((bf16[1,32,16,128]{3,2,1,0:T(8,128)(2,1)S(1)}, bf16[1,32,16,128]{3,2,1,0:T(8,128)(2,1)S(1)}, u32[]{:S(2)}, u32[]{:S(2)}) %collective-permute-start.2) | collective-permute-done | bytes 131104 | tf_op jit(solution)/shard_map/ppermute | solution.py:30
  18.6 0.5 collective-permute-start.9
  19.1 0.1 constant_dynamic-update-slice_fusion.7
  19.1 1.6 %collective-permute-start.8 = (bf16[2,32,16,128]{3,2,1,0:T(8,128)(2,1)S(1)}, bf16[2,32,16,128]{3,2,1,0:T(8,128)(2,1)S(1)}, u32[]{:S(2)}, u32[]{:S(2)}) collective-permute-start(bf16[2,32,16,128]{3,2,1,0:T(8,128)(2,1)S(1)} %get-tuple-element.53), channel_id=1, source_target_pairs={{0,2},{1,5},{2,0},{3,7},{4,6},{5,1},{6,4},{7,3},{8,10},{9,13},{10,... | collective-permute-start | bytes 786440 | tf_op jit(solution)/shard_map/ppermute | solution.py:30
  20.8 2.7 %collective-permute-done.9 = bf16[1,32,16,128]{3,2,1,0:T(8,128)(2,1)S(1)} collective-permute-done((bf16[1,32,16,128]{3,2,1,0:T(8,128)(2,1)S(1)}, bf16[1,32,16,128]{3,2,1,0:T(8,128)(2,1)S(1)}, u32[]{:S(2)}, u32[]{:S(2)}) %collective-permute-start.9) | collective-permute-done | bytes 131104 | tf_op jit(solution)/shard_map/ppermute | solution.py:21
  23.5 2.0 %collective-permute-done.8 = bf16[2,32,16,128]{3,2,1,0:T(8,128)(2,1)S(1)} collective-permute-done((bf16[2,32,16,128]{3,2,1,0:T(8,128)(2,1)S(1)}, bf16[2,32,16,128]{3,2,1,0:T(8,128)(2,1)S(1)}, u32[]{:S(2)}, u32[]{:S(2)}) %collective-permute-start.8) | collective-permute-done | bytes 262176 | tf_op jit(solution)/shard_map/ppermute | solution.py:30
  25.6 0.1 collective-permute-start.12
  25.7 1.5 %collective-permute-start.11 = (bf16[3,32,16,128]{3,2,1,0:T(8,128)(2,1)S(1)}, bf16[3,32,16,128]{3,2,1,0:T(8,128)(2,1)S(1)}, u32[]{:S(2)}, u32[]{:S(2)}) collective-permute-start(bf16[3,32,16,128]{3,2,1,0:T(8,128)(2,1)S(1)} %pad_maximum_fusion), channel_id=1, source_target_pairs={{0,4},{1,3},{2,6},{3,1},{4,0},{5,7},{6,2},{7,5},{8,12},{9,11},{10,... | collective-permute-start | bytes 1179656 | tf_op jit(solution)/shard_map/ppermute | solution.py:30
  27.3 0.6 collective-permute-start.7
  27.8 1.4 %collective-permute-start.6 = (bf16[1,32,16,128]{3,2,1,0:T(8,128)(2,1)S(1)}, bf16[1,32,16,128]{3,2,1,0:T(8,128)(2,1)S(1)}, u32[]{:S(2)}, u32[]{:S(2)}) collective-permute-start(bf16[1,32,16,128]{3,2,1,0:T(8,128)(2,1)S(1)} %collective-permute-done.3), channel_id=1, source_target_pairs={{0,24},{2,26},{4,28},{6,30},{8,16},{10,18},{12,20},{14,22},{16,8},... | collective-permute-start | bytes 393224 | tf_op jit(solution)/shard_map/ppermute | solution.py:21
  29.2 1.5 %collective-permute-start.10 = (bf16[1,32,16,128]{3,2,1,0:T(8,128)(2,1)S(1)}, bf16[1,32,16,128]{3,2,1,0:T(8,128)(2,1)S(1)}, u32[]{:S(2)}, u32[]{:S(2)}) collective-permute-start(bf16[1,32,16,128]{3,2,1,0:T(8,128)(2,1)S(1)} %collective-permute-done.9), channel_id=1, source_target_pairs={{0,2},{1,5},{2,0},{3,7},{4,6},{5,1},{6,4},{7,3},{8,10},{9,13},{10,... | collective-permute-start | bytes 393224 | tf_op jit(solution)/shard_map/ppermute | solution.py:30
  30.8 0.5 assemble.1._
  31.3 3.8 %collective-permute-done.6 = bf16[1,32,16,128]{3,2,1,0:T(8,128)(2,1)S(1)} collective-permute-done((bf16[1,32,16,128]{3,2,1,0:T(8,128)(2,1)S(1)}, bf16[1,32,16,128]{3,2,1,0:T(8,128)(2,1)S(1)}, u32[]{:S(2)}, u32[]{:S(2)}) %collective-permute-start.6) | collective-permute-done | bytes 131104 | tf_op jit(solution)/shard_map/ppermute | solution.py:21
  35.1 2.7 %collective-permute-done.7 = bf16[2,32,16,128]{3,2,1,0:T(8,128)(2,1)S(1)} collective-permute-done((bf16[2,32,16,128]{3,2,1,0:T(8,128)(2,1)S(1)}, bf16[2,32,16,128]{3,2,1,0:T(8,128)(2,1)S(1)}, u32[]{:S(2)}, u32[]{:S(2)}) %collective-permute-start.7) | collective-permute-done | bytes 262176 | tf_op jit(solution)/shard_map/ppermute | solution.py:30
  38.0 0.1 collective-permute-start.13
  38.0 2.5 %collective-permute-done.13.rest_1_ = bf16[7,32,16,128]{3,2,1,0:T(8,128)(2,1)S(1)} collective-permute-done((bf16[7,32,16,128]{3,2,1,0:T(8,128)(2,1)S(1)}, bf16[7,32,16,128]{3,2,1,0:T(8,128)(2,1)S(1)}, u32[]{:S(2)}, u32[]{:S(2)}) %collective-permute-start.13) | collective-permute-done | bytes 917536 | tf_op jit(solution)/shard_map/ppermute | solution.py:21
  40.5 5.9 %apply.1 = (bf16[32,4096]{1,0:T(8,128)(2,1)S(1)}, f32[16,128]{1,0:T(8,128)S(1)}, bf16[32,32,16,128]{3,2,1,0:T(8,128)(2,1)S(1)}) custom-call(s32[64,8]{1,0:T(8,128)S(1)} %get-tuple-element.26.rows_ref, bf16[64,8,64,128]{3,2,1,0:T(8,128)(2,1)S(1)} %get-tuple-element.27.ham_ref, ...), custom_call_target="tpu_custom_call", output_to_operand_aliasing={{2}: (2, {})} | custom-call | tf_op jit(solution)/shard_map/apply/pallas_call | solution.py:353
  46.4 0.2 collective-permute-start.14
  46.5 1.0 %collective-permute-done.14 = f32[16,128]{1,0:T(8,128)S(1)} collective-permute-done((f32[16,128]{1,0:T(8,128)S(1)}, f32[16,128]{1,0:T(8,128)S(1)}, u32[]{:S(2)}, u32[]{:S(2)}) %collective-permute-start.14) | collective-permute-done | bytes 8224 | tf_op jit(solution)/shard_map/ppermute | solution.py:21
  47.6 11.7 %all_to_all.5.sums_ref = f32[16,16,128]{2,1,0:T(8,128)S(1)} all-to-all(f32[16,16,128]{2,1,0:T(8,128)S(1)} %broadcast_in_dim.7), channel_id=1, replica_groups=mesh['chan'=16,'rad'=2] {'chan'}, dimensions={0} | all-to-all | bytes 262144 | tf_op jit(solution)/shard_map/all_to_all | solution.py:256
  59.3 3.1 %finish.1 = (f32[64,16,64]{2,1,0:T(8,128)}, f32[1,16]{1,0:T(1,128)}) custom-call(f32[16,16,128]{2,1,0:T(8,128)S(1)} %all_to_all.5.sums_ref, bf16[32,4096]{1,0:T(8,128)(2,1)S(1)} %get-tuple-element.45.az_ref, bf16[64,4096]{1,0:T(8,128)(2,1)S(1)} %get-tuple-element.36.zhm_ref), custom_call_target="tpu_custom_call" | custom-call | tf_op jit(solution)/shard_map/finish/pallas_call | solution.py:369
  (20 shorter events, 0.3 us)
Async XLA Ops:
  1.6 1.5 %collective-permute-start = (bf16[32,16,64]{2,1,0:T(8,128)(2,1)S(1)}, bf16[32,16,64]{2,1,0:T(8,128)(2,1)S(1)}, u32[]{:S(2)}, u32[]{:S(2)}) collective-permute-start(bf16[32,16,64]{2,1,0:T(8,128)(2,1)S(1)} %fusion), channel_id=1, source_target_pairs={{0,1},{1,0},{2,3},{3,2},{4,5},{5,4},{6,7},{7,6},{8,9},{9,8},{10,11... | collective-permute-start | bytes 196616 | tf_op jit(solution)/shard_map/ppermute | solution.py:21
  4.2 12.7 %collective-permute-start.5 = (bf16[1,32,16,128]{3,2,1,0:T(8,128)(2,1)S(1)}, bf16[1,32,16,128]{3,2,1,0:T(8,128)(2,1)S(1)}, u32[]{:S(2)}, u32[]{:S(2)}) collective-permute-start(bf16[1,32,16,128]{3,2,1,0:T(8,128)(2,1)S(1)} %get-tuple-element.49), channel_id=1, source_target_pairs={{0,16},{2,18},{4,20},{6,22},{8,24},{10,26},{12,28},{14,30},{16,0},... | collective-permute-start | bytes 393224 | tf_op jit(solution)/shard_map/ppermute | solution.py:21
  8.2 8.7 %collective-permute-start.4 = (bf16[1,32,16,128]{3,2,1,0:T(8,128)(2,1)S(1)}, bf16[1,32,16,128]{3,2,1,0:T(8,128)(2,1)S(1)}, u32[]{:S(2)}, u32[]{:S(2)}) collective-permute-start(bf16[1,32,16,128]{3,2,1,0:T(8,128)(2,1)S(1)} %get-tuple-element.49), channel_id=1, source_target_pairs={{0,8},{2,10},{4,12},{6,14},{8,0},{10,2},{12,4},{14,6},{16,24},{18,... | collective-permute-start | bytes 393224 | tf_op jit(solution)/shard_map/ppermute | solution.py:21
  9.8 7.2 %collective-permute-start.3 = (bf16[1,32,16,128]{3,2,1,0:T(8,128)(2,1)S(1)}, bf16[1,32,16,128]{3,2,1,0:T(8,128)(2,1)S(1)}, u32[]{:S(2)}, u32[]{:S(2)}) collective-permute-start(bf16[1,32,16,128]{3,2,1,0:T(8,128)(2,1)S(1)} %get-tuple-element.49), channel_id=1, source_target_pairs={{0,6},{2,4},{4,2},{6,0},{8,14},{10,12},{12,10},{14,8},{16,22},{18,... | collective-permute-start | bytes 393224 | tf_op jit(solution)/shard_map/ppermute | solution.py:21
  12.3 6.3 %collective-permute-start.2 = (bf16[1,32,16,128]{3,2,1,0:T(8,128)(2,1)S(1)}, bf16[1,32,16,128]{3,2,1,0:T(8,128)(2,1)S(1)}, u32[]{:S(2)}, u32[]{:S(2)}) collective-permute-start(bf16[1,32,16,128]{3,2,1,0:T(8,128)(2,1)S(1)} %get-tuple-element.49), channel_id=1, source_target_pairs={{0,2},{1,5},{2,0},{3,7},{4,6},{5,1},{6,4},{7,3},{8,10},{9,13},{10,... | collective-permute-start | bytes 393224 | tf_op jit(solution)/shard_map/ppermute | solution.py:30
  12.8 5.8 %collective-permute-start.1 = (bf16[1,32,16,128]{3,2,1,0:T(8,128)(2,1)S(1)}, bf16[1,32,16,128]{3,2,1,0:T(8,128)(2,1)S(1)}, u32[]{:S(2)}, u32[]{:S(2)}) collective-permute-start(bf16[1,32,16,128]{3,2,1,0:T(8,128)(2,1)S(1)} %get-tuple-element.49), channel_id=1, source_target_pairs={{0,4},{1,3},{2,6},{3,1},{4,0},{5,7},{6,2},{7,5},{8,12},{9,11},{10,... | collective-permute-start | bytes 393224 | tf_op jit(solution)/shard_map/ppermute | solution.py:30
  18.6 5.0 %collective-permute-start.9 = (bf16[1,32,16,128]{3,2,1,0:T(8,128)(2,1)S(1)}, bf16[1,32,16,128]{3,2,1,0:T(8,128)(2,1)S(1)}, u32[]{:S(2)}, u32[]{:S(2)}) collective-permute-start(bf16[1,32,16,128]{3,2,1,0:T(8,128)(2,1)S(1)} %collective-permute-done.5), channel_id=1, source_target_pairs={{0,8},{2,10},{4,12},{6,14},{8,0},{10,2},{12,4},{14,6},{16,24},{18,... | collective-permute-start | bytes 393224 | tf_op jit(solution)/shard_map/ppermute | solution.py:21
  19.1 6.4 %collective-permute-start.8 = (bf16[2,32,16,128]{3,2,1,0:T(8,128)(2,1)S(1)}, bf16[2,32,16,128]{3,2,1,0:T(8,128)(2,1)S(1)}, u32[]{:S(2)}, u32[]{:S(2)}) collective-permute-start(bf16[2,32,16,128]{3,2,1,0:T(8,128)(2,1)S(1)} %get-tuple-element.53), channel_id=1, source_target_pairs={{0,2},{1,5},{2,0},{3,7},{4,6},{5,1},{6,4},{7,3},{8,10},{9,13},{10,... | collective-permute-start | bytes 786440 | tf_op jit(solution)/shard_map/ppermute | solution.py:30
  25.6 5.1 %collective-permute-start.12 = (bf16[9,32,16,128]{3,2,1,0:T(8,128)(2,1)S(1)}, bf16[9,32,16,128]{3,2,1,0:T(8,128)(2,1)S(1)}, u32[]{:S(2)}, u32[]{:S(2)}) collective-permute-start(bf16[9,32,16,128]{3,2,1,0:T(8,128)(2,1)S(1)} %constant_dynamic-update-slice_fusion.2.refs_0_), channel_id=1, source_target_pairs={{0,1},{1,0},{2,3},{3,2},{4,5},{5,4},{6,7},{7,6},{8,9},{9,8},{10,11... | collective-permute-start | bytes 3538952 | tf_op jit(solution)/shard_map/ppermute | solution.py:21
  25.7 12.1 %collective-permute-start.11 = (bf16[3,32,16,128]{3,2,1,0:T(8,128)(2,1)S(1)}, bf16[3,32,16,128]{3,2,1,0:T(8,128)(2,1)S(1)}, u32[]{:S(2)}, u32[]{:S(2)}) collective-permute-start(bf16[3,32,16,128]{3,2,1,0:T(8,128)(2,1)S(1)} %pad_maximum_fusion), channel_id=1, source_target_pairs={{0,4},{1,3},{2,6},{3,1},{4,0},{5,7},{6,2},{7,5},{8,12},{9,11},{10,... | collective-permute-start | bytes 1179656 | tf_op jit(solution)/shard_map/ppermute | solution.py:30
  27.3 10.5 %collective-permute-start.7 = (bf16[2,32,16,128]{3,2,1,0:T(8,128)(2,1)S(1)}, bf16[2,32,16,128]{3,2,1,0:T(8,128)(2,1)S(1)}, u32[]{:S(2)}, u32[]{:S(2)}) collective-permute-start(bf16[2,32,16,128]{3,2,1,0:T(8,128)(2,1)S(1)} %get-tuple-element.53), channel_id=1, source_target_pairs={{0,4},{1,3},{2,6},{3,1},{4,0},{5,7},{6,2},{7,5},{8,12},{9,11},{10,... | collective-permute-start | bytes 786440 | tf_op jit(solution)/shard_map/ppermute | solution.py:30
  27.8 7.2 %collective-permute-start.6 = (bf16[1,32,16,128]{3,2,1,0:T(8,128)(2,1)S(1)}, bf16[1,32,16,128]{3,2,1,0:T(8,128)(2,1)S(1)}, u32[]{:S(2)}, u32[]{:S(2)}) collective-permute-start(bf16[1,32,16,128]{3,2,1,0:T(8,128)(2,1)S(1)} %collective-permute-done.3), channel_id=1, source_target_pairs={{0,24},{2,26},{4,28},{6,30},{8,16},{10,18},{12,20},{14,22},{16,8},... | collective-permute-start | bytes 393224 | tf_op jit(solution)/shard_map/ppermute | solution.py:21
  29.2 8.6 %collective-permute-start.10 = (bf16[1,32,16,128]{3,2,1,0:T(8,128)(2,1)S(1)}, bf16[1,32,16,128]{3,2,1,0:T(8,128)(2,1)S(1)}, u32[]{:S(2)}, u32[]{:S(2)}) collective-permute-start(bf16[1,32,16,128]{3,2,1,0:T(8,128)(2,1)S(1)} %collective-permute-done.9), channel_id=1, source_target_pairs={{0,2},{1,5},{2,0},{3,7},{4,6},{5,1},{6,4},{7,3},{8,10},{9,13},{10,... | collective-permute-start | bytes 393224 | tf_op jit(solution)/shard_map/ppermute | solution.py:30
  38.0 2.5 %collective-permute-start.13 = (bf16[7,32,16,128]{3,2,1,0:T(8,128)(2,1)S(1)}, bf16[7,32,16,128]{3,2,1,0:T(8,128)(2,1)S(1)}, u32[]{:S(2)}, u32[]{:S(2)}) collective-permute-start(bf16[7,32,16,128]{3,2,1,0:T(8,128)(2,1)S(1)} %constant_dynamic-update-slice_fusion.10.rest_0_), channel_id=1, source_target_pairs={{0,1},{1,0},{2,3},{3,2},{4,5},{5,4},{6,7},{7,6},{8,9},{9,8},{10,11... | collective-permute-start | bytes 2752520 | tf_op jit(solution)/shard_map/ppermute | solution.py:21
  46.4 1.2 %collective-permute-start.14 = (f32[16,128]{1,0:T(8,128)S(1)}, f32[16,128]{1,0:T(8,128)S(1)}, u32[]{:S(2)}, u32[]{:S(2)}) collective-permute-start(f32[16,128]{1,0:T(8,128)S(1)} %get-tuple-element.44), channel_id=1, source_target_pairs={{0,1},{1,0},{2,3},{3,2},{4,5},{5,4},{6,7},{7,6},{8,9},{9,8},{10,11... | collective-permute-start | bytes 24584 | tf_op jit(solution)/shard_map/ppermute | solution.py:21

commit v12 on v11

--- a/solution.py
+++ b/solution.py
@@ -166,7 +166,7 @@
         a0_ref[:, pl.ds(pl.multiple_of(g * 256, 256), 256)] = jnp.concatenate(own, axis=1) * SCALE
         return carry
 
-    lax.fori_loop(0, ch // group, work, 0, unroll=min(2, ch // group))
+    lax.fori_loop(0, ch // group, work, 0, unroll=min(4, ch // group))
 
     lanes = ch * r
     block = min(lanes, 1024)
@@ -260,10 +260,10 @@
     n_rad = lax.axis_size("rad")
     ch, k, r = trial_block.shape
     me = lax.axis_index("rad")
-    shares = trial_block.reshape(n_rad, ch // n_rad, k, r)
+    rounded = trial_block.astype(BF16).reshape(n_rad, ch // n_rad, k, r)
     got = []
     for d in range(n_rad):
-        part = lax.dynamic_index_in_dim(shares, me ^ d, 0, keepdims=False).astype(BF16)
+        part = lax.dynamic_index_in_dim(rounded, me ^ d, 0, keepdims=False)
         got.append(swap(part, "rad", d) if d else part)
     lanes = []
     for c in range(n_rad):
@@ -300,6 +300,19 @@
     near0, far_own, diag0 = near_of(own), far_of(own), swap(own, "chan", 3)
     z1 = swap(own, "chan", 4)
     z_even = jnp.concatenate([swap(own, "chan", 4 * z) for z in range(2, nz, 2)])
+    z1, far_own, near0, diag0, z_even = barrier((z1, far_own, near0, diag0, z_even))
+    some = jnp.concatenate([z1, z_even])
+    near1, far1 = near_of(some), far_of(some)
+    z_odd = swap(z_even, "chan", 4)
+    diag_odd = jnp.concatenate([swap(diag0, "chan", 4 * z) for z in range(3, nz, 2)])
+    inputs = (trial_block, precond_diag, partners, stored_at, ham_blocks)
+    diag_odd, z_odd, far1, near1, inputs = barrier((diag_odd, z_odd, far1, near1, inputs))
+    trial_block, precond_diag, partners, stored_at, ham_blocks = inputs
+    early = in_cores(
+        jnp.concatenate([own, z1, z_even, near0, far_own, diag0, near1, z_odd, diag_odd, far1])
+    )
+    near_odd = near_of(z_odd)
+    far2 = far_of(jnp.concatenate([z_odd, near1]))
     rows, ham, zhm, zl, dc, gram_t = pl.pallas_call(
         functools.partial(prepare_kernel, n_chan, n_rad),
         in_specs=[any_] * 5,
@@ -328,15 +341,6 @@
         in_hbm(stored_at.reshape(-1, 128)),
         in_hbm(ham_blocks),
     )
-    far_own, near0, diag0, z1, z_even, rows = barrier((far_own, near0, diag0, z1, z_even, rows))
-    some = jnp.concatenate([z1, z_even])
-    near1, far1 = near_of(some), far_of(some)
-    z_odd = swap(z_even, "chan", 4)
-    diag_odd = jnp.concatenate([swap(diag0, "chan", 4 * z) for z in range(3, nz, 2)])
-    near1, z_odd = barrier((near1, z_odd))
-    early = in_cores(jnp.concatenate([own, z1, z_even, near0, far_own, diag0, near1, z_odd]))
-    near_odd = near_of(z_odd)
-    far2 = far_of(jnp.concatenate([z_odd, near1]))
     table = pl.pallas_call(
         assemble_kernel,
         in_specs=[any_] * n_rad,
@@ -346,9 +350,8 @@
         compiler_params=pltpu.CompilerParams(vmem_limit_bytes=VMEM_LIMIT),
         name="assemble",
     )(*early)
-    last = barrier((diag_odd, far1, near_odd, far2, table))
-    table = last[4]
-    last = [in_vmem(x) for x in in_cores(jnp.concatenate(last[:4]))]
+    near_odd, far2, table, rows = barrier((near_odd, far2, table, rows))
+    last = [in_vmem(x) for x in in_cores(jnp.concatenate([near_odd, far2]))]
 
     az, sums, _ = pl.pallas_call(
         apply_kernel,

time: 62.6 us -> 59.9 us (0.957)
  local copies, waits for them, and re-layouts: 1.32 us -> 0.36 us
  Pallas kernels: 13.1 us -> 12.3 us
  blocking collectives: 11.7 us -> 11 us
  waiting for transfers between devices: 17.4 us -> 16.7 us
    ppermute x9, starting transfers between devices: 10.7 us -> 12 us  [swap(): return lax.ppermute(x, axis, [(i, i ^ distance) for i in range(n)])]
    convert_element_type x0 -> x1, other arithmetic: none -> 1.08 us  [own_share(): rounded = trial_block.astype(BF16).reshape(n_rad, ch // n_rad, k, r)]
    ppermute x6, starting transfers between devices: 6.27 us -> 5.22 us  [plane_swap(): return lax.ppermute(x, ('chan', 'rad'), pairs)]
    convert_element_type x1 -> x0, local copies, waits for them, and re-layouts: 0.97 us -> none  [own_share(): lax.dynamic_index_in_dim(shares, me ^ d, 0, keepdims=False).astype(BF16)]
    select_n x1, other arithmetic: 0.97 us -> 0.02 us  [own_share(): x = jnp.where(me ^ d == c, got[d], x)]
    all_to_all x1, blocking collectives: 11.7 us -> 11 us  [gather_sums(): lax.all_to_all(every, 'chan', split_axis=0, concat_axis=0, tiled=True)]
  transfers between devices with their start and end apart: 15 -> 15, of which waited for: 8 -> 9; matrix products, arithmetic and copies ran while one was open for 0% -> 0% of each run, Pallas kernels for 7% -> 7%
where the time goes in v12:
time: 59.9 us; the launch traced here: 59.7 us
  starting transfers between devices  17.2 us (29%)
  waiting for transfers between devices  16.7 us (28%)
  Pallas kernels  12.3 us (21%)
  blocking collectives  11 us (18%)
  other arithmetic  1.26 us (2%)
  between operations  0.8 us (1%)
    ppermute x9, starting transfers between devices, swap(): return lax.ppermute(x, axis, [(i, i ^ distance) for i in range(n)])  12 us
    all_to_all x1, blocking collectives, gather_sums(): lax.all_to_all(every, 'chan', split_axis=0, concat_axis=0, tiled=True)  11 us
    ppermute x9, waiting for transfers between devices, swap(): return lax.ppermute(x, axis, [(i, i ^ distance) for i in range(n)])  10.8 us
    ppermute x6, waiting for transfers between devices, plane_swap(): return lax.ppermute(x, ('chan', 'rad'), pairs)  5.95 us
    pallas_call x1, Pallas kernels, body(): pl.pallas_call(apply_kernel, in_specs=[smem] + [whole] * (6 + n_rad), out...  5.31 us
    ppermute x6, starting transfers between devices, plane_swap(): return lax.ppermute(x, ('chan', 'rad'), pairs)  5.22 us
    pallas_call x1, Pallas kernels, body(): pl.pallas_call(functools.partial(prepare_kernel, n_chan, n_rad), in_specs...  3.66 us
    pallas_call x1, Pallas kernels, body(): pl.pallas_call(functools.partial(finish_kernel, total), out_shape=[jax.Sh...  3.07 us
  transfers between devices with their start and end apart: 15, of which 9 were waited for; matrix products, arithmetic and copies ran while one was open for 0% of the time, Pallas kernels for 7%

profile of v12, /device:TPU:0, one launch (start us, length us, event | category | flops | bytes accessed | tf_op | source)
XLA Modules:
  0.0 59.7 jit_solution(95482784051542168)
XLA Ops:
  0.6 1.1 %convert_element_type.3 = bf16[64,16,64]{2,1,0:T(8,128)(2,1)S(1)} convert(f32[64,16,64]{2,1,0:T(8,128)} %t_hbm) | non-fusion elementwise | flops 65536 | bytes 393216 | tf_op jit(solution)/shard_map/convert_element_type | solution.py:263
  1.7 0.5 collective-permute-start
  2.3 1.0 %collective-permute-done = bf16[32,16,64]{2,1,0:T(8,128)(2,1)S(1)} collective-permute-done((bf16[32,16,64]{2,1,0:T(8,128)(2,1)S(1)}, bf16[32,16,64]{2,1,0:T(8,128)(2,1)S(1)}, u32[]{:S(2)}, u32[]{:S(2)}) %collective-permute-start) | collective-permute-done | bytes 65568 | tf_op jit(solution)/shard_map/ppermute | solution.py:21
  3.3 0.1 constant_dynamic-update-slice_fusion.11
  3.4 4.0 %collective-permute-start.5 = (bf16[1,32,16,128]{3,2,1,0:T(8,128)(2,1)S(1)}, bf16[1,32,16,128]{3,2,1,0:T(8,128)(2,1)S(1)}, u32[]{:S(2)}, u32[]{:S(2)}) collective-permute-start(bf16[1,32,16,128]{3,2,1,0:T(8,128)(2,1)S(1)} %get-tuple-element.59), channel_id=1, source_target_pairs={{0,16},{2,18},{4,20},{6,22},{8,24},{10,26},{12,28},{14,30},{16,0},... | collective-permute-start | bytes 393224 | tf_op jit(solution)/shard_map/ppermute | solution.py:21
  7.4 2.4 %collective-permute-start.4 = (bf16[1,32,16,128]{3,2,1,0:T(8,128)(2,1)S(1)}, bf16[1,32,16,128]{3,2,1,0:T(8,128)(2,1)S(1)}, u32[]{:S(2)}, u32[]{:S(2)}) collective-permute-start(bf16[1,32,16,128]{3,2,1,0:T(8,128)(2,1)S(1)} %get-tuple-element.59), channel_id=1, source_target_pairs={{0,6},{2,4},{4,2},{6,0},{8,14},{10,12},{12,10},{14,8},{16,22},{18,... | collective-permute-start | bytes 393224 | tf_op jit(solution)/shard_map/ppermute | solution.py:21
  9.9 0.5 collective-permute-start.3
  10.4 0.5 collective-permute-start.2
  10.9 1.6 %collective-permute-start.1 = (bf16[1,32,16,128]{3,2,1,0:T(8,128)(2,1)S(1)}, bf16[1,32,16,128]{3,2,1,0:T(8,128)(2,1)S(1)}, u32[]{:S(2)}, u32[]{:S(2)}) collective-permute-start(bf16[1,32,16,128]{3,2,1,0:T(8,128)(2,1)S(1)} %get-tuple-element.59), channel_id=1, source_target_pairs={{0,8},{2,10},{4,12},{6,14},{8,0},{10,2},{12,4},{14,6},{16,24},{18,... | collective-permute-start | bytes 393224 | tf_op jit(solution)/shard_map/ppermute | solution.py:21
  12.5 1.7 %collective-permute-done.5 = bf16[1,32,16,128]{3,2,1,0:T(8,128)(2,1)S(1)} collective-permute-done((bf16[1,32,16,128]{3,2,1,0:T(8,128)(2,1)S(1)}, bf16[1,32,16,128]{3,2,1,0:T(8,128)(2,1)S(1)}, u32[]{:S(2)}, u32[]{:S(2)}) %collective-permute-start.5) | collective-permute-done | bytes 131104 | tf_op jit(solution)/shard_map/ppermute | solution.py:21
  14.1 2.3 %collective-permute-done.3 = bf16[1,32,16,128]{3,2,1,0:T(8,128)(2,1)S(1)} collective-permute-done((bf16[1,32,16,128]{3,2,1,0:T(8,128)(2,1)S(1)}, bf16[1,32,16,128]{3,2,1,0:T(8,128)(2,1)S(1)}, u32[]{:S(2)}, u32[]{:S(2)}) %collective-permute-start.3) | collective-permute-done | bytes 131104 | tf_op jit(solution)/shard_map/ppermute | solution.py:30
  16.4 0.4 collective-permute-done.1
  16.8 1.2 %collective-permute-start.7 = (bf16[1,32,16,128]{3,2,1,0:T(8,128)(2,1)S(1)}, bf16[1,32,16,128]{3,2,1,0:T(8,128)(2,1)S(1)}, u32[]{:S(2)}, u32[]{:S(2)}) collective-permute-start(bf16[1,32,16,128]{3,2,1,0:T(8,128)(2,1)S(1)} %collective-permute-done.5), channel_id=1, source_target_pairs={{0,8},{2,10},{4,12},{6,14},{8,0},{10,2},{12,4},{14,6},{16,24},{18,... | collective-permute-start | bytes 393224 | tf_op jit(solution)/shard_map/ppermute | solution.py:21
  18.1 0.1 constant_dynamic-update-slice_fusion.9
  18.1 1.6 %collective-permute-start.9 = (bf16[2,32,16,128]{3,2,1,0:T(8,128)(2,1)S(1)}, bf16[2,32,16,128]{3,2,1,0:T(8,128)(2,1)S(1)}, u32[]{:S(2)}, u32[]{:S(2)}) collective-permute-start(bf16[2,32,16,128]{3,2,1,0:T(8,128)(2,1)S(1)} %get-tuple-element.63), channel_id=1, source_target_pairs={{0,2},{1,5},{2,0},{3,7},{4,6},{5,1},{6,4},{7,3},{8,10},{9,13},{10,... | collective-permute-start | bytes 786440 | tf_op jit(solution)/shard_map/ppermute | solution.py:30
  19.7 0.9 %collective-permute-start.8 = (bf16[2,32,16,128]{3,2,1,0:T(8,128)(2,1)S(1)}, bf16[2,32,16,128]{3,2,1,0:T(8,128)(2,1)S(1)}, u32[]{:S(2)}, u32[]{:S(2)}) collective-permute-start(bf16[2,32,16,128]{3,2,1,0:T(8,128)(2,1)S(1)} %get-tuple-element.63), channel_id=1, source_target_pairs={{0,4},{1,3},{2,6},{3,1},{4,0},{5,7},{6,2},{7,5},{8,12},{9,11},{10,... | collective-permute-start | bytes 786440 | tf_op jit(solution)/shard_map/ppermute | solution.py:30
  20.6 2.0 %collective-permute-start.6 = (bf16[1,32,16,128]{3,2,1,0:T(8,128)(2,1)S(1)}, bf16[1,32,16,128]{3,2,1,0:T(8,128)(2,1)S(1)}, u32[]{:S(2)}, u32[]{:S(2)}) collective-permute-start(bf16[1,32,16,128]{3,2,1,0:T(8,128)(2,1)S(1)} %collective-permute-done.4), channel_id=1, source_target_pairs={{0,24},{2,26},{4,28},{6,30},{8,16},{10,18},{12,20},{14,22},{16,8},... | collective-permute-start | bytes 393224 | tf_op jit(solution)/shard_map/ppermute | solution.py:21
  22.7 4.8 %collective-permute-done.6 = bf16[1,32,16,128]{3,2,1,0:T(8,128)(2,1)S(1)} collective-permute-done((bf16[1,32,16,128]{3,2,1,0:T(8,128)(2,1)S(1)}, bf16[1,32,16,128]{3,2,1,0:T(8,128)(2,1)S(1)}, u32[]{:S(2)}, u32[]{:S(2)}) %collective-permute-start.6) | collective-permute-done | bytes 131104 | tf_op jit(solution)/shard_map/ppermute | solution.py:21
  27.7 0.1 collective-permute-start.12
  27.8 1.2 %collective-permute-start.11 = (bf16[3,32,16,128]{3,2,1,0:T(8,128)(2,1)S(1)}, bf16[3,32,16,128]{3,2,1,0:T(8,128)(2,1)S(1)}, u32[]{:S(2)}, u32[]{:S(2)}) collective-permute-start(bf16[3,32,16,128]{3,2,1,0:T(8,128)(2,1)S(1)} %pad_maximum_fusion), channel_id=1, source_target_pairs={{0,4},{1,3},{2,6},{3,1},{4,0},{5,7},{6,2},{7,5},{8,12},{9,11},{10,... | collective-permute-start | bytes 1179656 | tf_op jit(solution)/shard_map/ppermute | solution.py:30
  29.0 0.5 collective-permute-start.10
  29.5 3.7 %prepare.1 = (s32[64,8]{1,0:T(8,128)S(1)}, bf16[64,8,64,128]{3,2,1,0:T(8,128)(2,1)S(1)}, bf16[64,4096]{1,0:T(8,128)(2,1)S(1)}, bf16[32,4096]{1,0:T(8,128)(2,1)S(...) custom-call(f32[64,16,64]{2,1,0:T(8,128)} %t_hbm, f32[64,64]{1,0:T(8,128)} %d_hbm, s32[8,64]{1,0:T(8,128)} %bitcast.14, ...), custom_call_target="tpu_custom_call" | custom-call | tf_op jit(solution)/shard_map/prepare/pallas_call | solution.py:316
  33.2 0.2 assemble.1._
  33.4 2.0 %collective-permute-done.10 = bf16[1,32,16,128]{3,2,1,0:T(8,128)(2,1)S(1)} collective-permute-done((bf16[1,32,16,128]{3,2,1,0:T(8,128)(2,1)S(1)}, bf16[1,32,16,128]{3,2,1,0:T(8,128)(2,1)S(1)}, u32[]{:S(2)}, u32[]{:S(2)}) %collective-permute-start.10) | collective-permute-done | bytes 131104 | tf_op jit(solution)/shard_map/ppermute | solution.py:30
  35.4 1.6 %collective-permute-done.11 = bf16[3,32,16,128]{3,2,1,0:T(8,128)(2,1)S(1)} collective-permute-done((bf16[3,32,16,128]{3,2,1,0:T(8,128)(2,1)S(1)}, bf16[3,32,16,128]{3,2,1,0:T(8,128)(2,1)S(1)}, u32[]{:S(2)}, u32[]{:S(2)}) %collective-permute-start.11) | collective-permute-done | bytes 393248 | tf_op jit(solution)/shard_map/ppermute | solution.py:30
  37.1 0.1 collective-permute-start.13
  37.2 1.9 %collective-permute-done.13.rest_1_ = bf16[4,32,16,128]{3,2,1,0:T(8,128)(2,1)S(1)} collective-permute-done((bf16[4,32,16,128]{3,2,1,0:T(8,128)(2,1)S(1)}, bf16[4,32,16,128]{3,2,1,0:T(8,128)(2,1)S(1)}, u32[]{:S(2)}, u32[]{:S(2)}) %collective-permute-start.13) | collective-permute-done | bytes 524320 | tf_op jit(solution)/shard_map/ppermute | solution.py:21
  39.1 5.3 %apply.1 = (bf16[32,4096]{1,0:T(8,128)(2,1)S(1)}, f32[16,128]{1,0:T(8,128)S(1)}, bf16[32,32,16,128]{3,2,1,0:T(8,128)(2,1)S(1)}) custom-call(s32[64,8]{1,0:T(8,128)S(1)} %get-tuple-element.45.rows_ref, bf16[64,8,64,128]{3,2,1,0:T(8,128)(2,1)S(1)} %get-tuple-element.46.ham_ref, ...), custom_call_target="tpu_custom_call", output_to_operand_aliasing={{2}: (2, {})} | custom-call | tf_op jit(solution)/shard_map/apply/pallas_call | solution.py:356
  44.4 0.2 collective-permute-start.14
  44.5 1.0 %collective-permute-done.14 = f32[16,128]{1,0:T(8,128)S(1)} collective-permute-done((f32[16,128]{1,0:T(8,128)S(1)}, f32[16,128]{1,0:T(8,128)S(1)}, u32[]{:S(2)}, u32[]{:S(2)}) %collective-permute-start.14) | collective-permute-done | bytes 8224 | tf_op jit(solution)/shard_map/ppermute | solution.py:21
  45.6 11.0 %all_to_all.5.sums_ref = f32[16,16,128]{2,1,0:T(8,128)S(1)} all-to-all(f32[16,16,128]{2,1,0:T(8,128)S(1)} %broadcast_in_dim.7), channel_id=1, replica_groups=mesh['chan'=16,'rad'=2] {'chan'}, dimensions={0} | all-to-all | bytes 262144 | tf_op jit(solution)/shard_map/all_to_all | solution.py:256
  56.6 3.1 %finish.1 = (f32[64,16,64]{2,1,0:T(8,128)}, f32[1,16]{1,0:T(1,128)}) custom-call(f32[16,16,128]{2,1,0:T(8,128)S(1)} %all_to_all.5.sums_ref, bf16[32,4096]{1,0:T(8,128)(2,1)S(1)} %get-tuple-element.55.az_ref, bf16[64,4096]{1,0:T(8,128)(2,1)S(1)} %get-tuple-element.48.zhm_ref), custom_call_target="tpu_custom_call" | custom-call | tf_op jit(solution)/shard_map/finish/pallas_call | solution.py:372
  (21 shorter events, 0.4 us)
Async XLA Ops:
  1.7 1.5 %collective-permute-start = (bf16[32,16,64]{2,1,0:T(8,128)(2,1)S(1)}, bf16[32,16,64]{2,1,0:T(8,128)(2,1)S(1)}, u32[]{:S(2)}, u32[]{:S(2)}) collective-permute-start(bf16[32,16,64]{2,1,0:T(8,128)(2,1)S(1)} %dynamic-slice_bitcast_fusion), channel_id=1, source_target_pairs={{0,1},{1,0},{2,3},{3,2},{4,5},{5,4},{6,7},{7,6},{8,9},{9,8},{10,11... | collective-permute-start | bytes 196616 | tf_op jit(solution)/shard_map/ppermute | solution.py:21
  3.4 10.7 %collective-permute-start.5 = (bf16[1,32,16,128]{3,2,1,0:T(8,128)(2,1)S(1)}, bf16[1,32,16,128]{3,2,1,0:T(8,128)(2,1)S(1)}, u32[]{:S(2)}, u32[]{:S(2)}) collective-permute-start(bf16[1,32,16,128]{3,2,1,0:T(8,128)(2,1)S(1)} %get-tuple-element.59), channel_id=1, source_target_pairs={{0,16},{2,18},{4,20},{6,22},{8,24},{10,26},{12,28},{14,30},{16,0},... | collective-permute-start | bytes 393224 | tf_op jit(solution)/shard_map/ppermute | solution.py:21
  7.4 6.7 %collective-permute-start.4 = (bf16[1,32,16,128]{3,2,1,0:T(8,128)(2,1)S(1)}, bf16[1,32,16,128]{3,2,1,0:T(8,128)(2,1)S(1)}, u32[]{:S(2)}, u32[]{:S(2)}) collective-permute-start(bf16[1,32,16,128]{3,2,1,0:T(8,128)(2,1)S(1)} %get-tuple-element.59), channel_id=1, source_target_pairs={{0,6},{2,4},{4,2},{6,0},{8,14},{10,12},{12,10},{14,8},{16,22},{18,... | collective-permute-start | bytes 393224 | tf_op jit(solution)/shard_map/ppermute | solution.py:21
  9.9 6.6 %collective-permute-start.3 = (bf16[1,32,16,128]{3,2,1,0:T(8,128)(2,1)S(1)}, bf16[1,32,16,128]{3,2,1,0:T(8,128)(2,1)S(1)}, u32[]{:S(2)}, u32[]{:S(2)}) collective-permute-start(bf16[1,32,16,128]{3,2,1,0:T(8,128)(2,1)S(1)} %get-tuple-element.59), channel_id=1, source_target_pairs={{0,2},{1,5},{2,0},{3,7},{4,6},{5,1},{6,4},{7,3},{8,10},{9,13},{10,... | collective-permute-start | bytes 393224 | tf_op jit(solution)/shard_map/ppermute | solution.py:30
  10.4 6.1 %collective-permute-start.2 = (bf16[1,32,16,128]{3,2,1,0:T(8,128)(2,1)S(1)}, bf16[1,32,16,128]{3,2,1,0:T(8,128)(2,1)S(1)}, u32[]{:S(2)}, u32[]{:S(2)}) collective-permute-start(bf16[1,32,16,128]{3,2,1,0:T(8,128)(2,1)S(1)} %get-tuple-element.59), channel_id=1, source_target_pairs={{0,4},{1,3},{2,6},{3,1},{4,0},{5,7},{6,2},{7,5},{8,12},{9,11},{10,... | collective-permute-start | bytes 393224 | tf_op jit(solution)/shard_map/ppermute | solution.py:30
  10.9 5.9 %collective-permute-start.1 = (bf16[1,32,16,128]{3,2,1,0:T(8,128)(2,1)S(1)}, bf16[1,32,16,128]{3,2,1,0:T(8,128)(2,1)S(1)}, u32[]{:S(2)}, u32[]{:S(2)}) collective-permute-start(bf16[1,32,16,128]{3,2,1,0:T(8,128)(2,1)S(1)} %get-tuple-element.59), channel_id=1, source_target_pairs={{0,8},{2,10},{4,12},{6,14},{8,0},{10,2},{12,4},{14,6},{16,24},{18,... | collective-permute-start | bytes 393224 | tf_op jit(solution)/shard_map/ppermute | solution.py:21
  16.8 10.7 %collective-permute-start.7 = (bf16[1,32,16,128]{3,2,1,0:T(8,128)(2,1)S(1)}, bf16[1,32,16,128]{3,2,1,0:T(8,128)(2,1)S(1)}, u32[]{:S(2)}, u32[]{:S(2)}) collective-permute-start(bf16[1,32,16,128]{3,2,1,0:T(8,128)(2,1)S(1)} %collective-permute-done.5), channel_id=1, source_target_pairs={{0,8},{2,10},{4,12},{6,14},{8,0},{10,2},{12,4},{14,6},{16,24},{18,... | collective-permute-start | bytes 393224 | tf_op jit(solution)/shard_map/ppermute | solution.py:21
  18.1 9.4 %collective-permute-start.9 = (bf16[2,32,16,128]{3,2,1,0:T(8,128)(2,1)S(1)}, bf16[2,32,16,128]{3,2,1,0:T(8,128)(2,1)S(1)}, u32[]{:S(2)}, u32[]{:S(2)}) collective-permute-start(bf16[2,32,16,128]{3,2,1,0:T(8,128)(2,1)S(1)} %get-tuple-element.63), channel_id=1, source_target_pairs={{0,2},{1,5},{2,0},{3,7},{4,6},{5,1},{6,4},{7,3},{8,10},{9,13},{10,... | collective-permute-start | bytes 786440 | tf_op jit(solution)/shard_map/ppermute | solution.py:30
  19.7 7.8 %collective-permute-start.8 = (bf16[2,32,16,128]{3,2,1,0:T(8,128)(2,1)S(1)}, bf16[2,32,16,128]{3,2,1,0:T(8,128)(2,1)S(1)}, u32[]{:S(2)}, u32[]{:S(2)}) collective-permute-start(bf16[2,32,16,128]{3,2,1,0:T(8,128)(2,1)S(1)} %get-tuple-element.63), channel_id=1, source_target_pairs={{0,4},{1,3},{2,6},{3,1},{4,0},{5,7},{6,2},{7,5},{8,12},{9,11},{10,... | collective-permute-start | bytes 786440 | tf_op jit(solution)/shard_map/ppermute | solution.py:30
  20.6 6.9 %collective-permute-start.6 = (bf16[1,32,16,128]{3,2,1,0:T(8,128)(2,1)S(1)}, bf16[1,32,16,128]{3,2,1,0:T(8,128)(2,1)S(1)}, u32[]{:S(2)}, u32[]{:S(2)}) collective-permute-start(bf16[1,32,16,128]{3,2,1,0:T(8,128)(2,1)S(1)} %collective-permute-done.4), channel_id=1, source_target_pairs={{0,24},{2,26},{4,28},{6,30},{8,16},{10,18},{12,20},{14,22},{16,8},... | collective-permute-start | bytes 393224 | tf_op jit(solution)/shard_map/ppermute | solution.py:21
  27.7 5.5 %collective-permute-start.12 = (bf16[12,32,16,128]{3,2,1,0:T(8,128)(2,1)S(1)}, bf16[12,32,16,128]{3,2,1,0:T(8,128)(2,1)S(1)}, u32[]{:S(2)}, u32[]{:S(2)}) collective-permute-start(bf16[12,32,16,128]{3,2,1,0:T(8,128)(2,1)S(1)} %constant_dynamic-update-slice_fusion.2.refs_0_), channel_id=1, source_target_pairs={{0,1},{1,0},{2,3},{3,2},{4,5},{5,4},{6,7},{7,6},{8,9},{9,8},{10,11... | collective-permute-start | bytes 4718600 | tf_op jit(solution)/shard_map/ppermute | solution.py:21
  27.8 9.2 %collective-permute-start.11 = (bf16[3,32,16,128]{3,2,1,0:T(8,128)(2,1)S(1)}, bf16[3,32,16,128]{3,2,1,0:T(8,128)(2,1)S(1)}, u32[]{:S(2)}, u32[]{:S(2)}) collective-permute-start(bf16[3,32,16,128]{3,2,1,0:T(8,128)(2,1)S(1)} %pad_maximum_fusion), channel_id=1, source_target_pairs={{0,4},{1,3},{2,6},{3,1},{4,0},{5,7},{6,2},{7,5},{8,12},{9,11},{10,... | collective-permute-start | bytes 1179656 | tf_op jit(solution)/shard_map/ppermute | solution.py:30
  29.0 6.4 %collective-permute-start.10 = (bf16[1,32,16,128]{3,2,1,0:T(8,128)(2,1)S(1)}, bf16[1,32,16,128]{3,2,1,0:T(8,128)(2,1)S(1)}, u32[]{:S(2)}, u32[]{:S(2)}) collective-permute-start(bf16[1,32,16,128]{3,2,1,0:T(8,128)(2,1)S(1)} %collective-permute-done.7), channel_id=1, source_target_pairs={{0,2},{1,5},{2,0},{3,7},{4,6},{5,1},{6,4},{7,3},{8,10},{9,13},{10,... | collective-permute-start | bytes 393224 | tf_op jit(solution)/shard_map/ppermute | solution.py:30
  37.1 2.0 %collective-permute-start.13 = (bf16[4,32,16,128]{3,2,1,0:T(8,128)(2,1)S(1)}, bf16[4,32,16,128]{3,2,1,0:T(8,128)(2,1)S(1)}, u32[]{:S(2)}, u32[]{:S(2)}) collective-permute-start(bf16[4,32,16,128]{3,2,1,0:T(8,128)(2,1)S(1)} %constant_dynamic-update-slice_fusion.12.rest_0_), channel_id=1, source_target_pairs={{0,1},{1,0},{2,3},{3,2},{4,5},{5,4},{6,7},{7,6},{8,9},{9,8},{10,11... | collective-permute-start | bytes 1572872 | tf_op jit(solution)/shard_map/ppermute | solution.py:21
  44.4 1.2 %collective-permute-start.14 = (f32[16,128]{1,0:T(8,128)S(1)}, f32[16,128]{1,0:T(8,128)S(1)}, u32[]{:S(2)}, u32[]{:S(2)}) collective-permute-start(f32[16,128]{1,0:T(8,128)S(1)} %get-tuple-element.54), channel_id=1, source_target_pairs={{0,1},{1,0},{2,3},{3,2},{4,5},{5,4},{6,7},{7,6},{8,9},{9,8},{10,11... | collective-permute-start | bytes 24584 | tf_op jit(solution)/shard_map/ppermute | solution.py:21

commit v13 on v12

--- a/solution.py
+++ b/solution.py
@@ -42,7 +42,7 @@
     here = pick(0, 1, 2 * some + 4)
     near = pick(some + 1, some + 4, base + odd + some)
     far = pick(some + 2, base + odd, base + 2 * odd + some)
-    both = pick(some + 3, base + 3 * odd + some, base)
+    both = jnp.where(z == 1, 4 * nz - 1, pick(some + 3, base + 3 * odd + some - 1, base))
     return jnp.where(part == 0, here, jnp.where(part == 1, near, jnp.where(part == 2, far, both)))
 
 
@@ -132,28 +132,25 @@
 
 def apply_kernel(rows_ref, ham_ref, _, zhm_ref, zl_ref, dc_ref, gt_ref, *rest):
     last, (az_ref, sums_ref, table_ref, a0_ref) = rest[:-4], rest[-4:]
-    share = table_ref.shape[1]
     for c, piece in enumerate(last):
         start = (c + 1) * (table_ref.shape[0] // len(last)) - piece.shape[0]
-
-        def put(i, carry, piece=piece, start=start):
-            table_ref[start + i] = piece[i]
+        step = min(32, piece.shape[0])
+
+        def put(i, carry, piece=piece, start=start, step=step):
+            table_ref[pl.ds(start + i * step, step)] = piece[pl.ds(i * step, step)]
             return carry
 
-        lax.fori_loop(0, piece.shape[0], put, 0)
+        lax.fori_loop(0, piece.shape[0] // step, put, 0)
     ch, ncoup, r, splines = ham_ref.shape
     k = zl_ref.shape[0] // 2
     group = 256 // r
-
-    def row_of(n):
-        return table_ref[lax.div(n, share), lax.rem(n, share)]
 
     def work(g, carry):
         left, right = [], []
         for i in range(group):
             p = g * group + i
             left.append(
-                jnp.concatenate([row_of(rows_ref[p, j]) for j in range(ncoup)], axis=1)
+                jnp.concatenate([table_ref[rows_ref[p, j]] for j in range(ncoup)], axis=1)
             )
             right.append(jnp.concatenate([ham_ref[p, j] for j in range(ncoup)], axis=1))
         product = lax.dot_general(
@@ -293,6 +290,9 @@
     def far_of(x):
         return plane_swap(x, (2, 1))
 
+    def flat(x):
+        return x.reshape((-1,) + x.shape[2:])
+
     def in_cores(x):
         return [x] + [swap(x, "rad", c) for c in range(1, n_rad)]
 
@@ -301,18 +301,20 @@
     z1 = swap(own, "chan", 4)
     z_even = jnp.concatenate([swap(own, "chan", 4 * z) for z in range(2, nz, 2)])
     z1, far_own, near0, diag0, z_even = barrier((z1, far_own, near0, diag0, z_even))
-    some = jnp.concatenate([z1, z_even])
+    some, z_even, diag0 = barrier((jnp.concatenate([z1, z_even]), z_even, diag0))
     near1, far1 = near_of(some), far_of(some)
     z_odd = swap(z_even, "chan", 4)
     diag_odd = jnp.concatenate([swap(diag0, "chan", 4 * z) for z in range(3, nz, 2)])
     inputs = (trial_block, precond_diag, partners, stored_at, ham_blocks)
-    diag_odd, z_odd, far1, near1, inputs = barrier((diag_odd, z_odd, far1, near1, inputs))
+    diag_odd, z_odd, far1, near1, diag0, inputs = barrier(
+        (diag_odd, z_odd, far1, near1, diag0, inputs)
+    )
     trial_block, precond_diag, partners, stored_at, ham_blocks = inputs
     early = in_cores(
         jnp.concatenate([own, z1, z_even, near0, far_own, diag0, near1, z_odd, diag_odd, far1])
     )
-    near_odd = near_of(z_odd)
-    far2 = far_of(jnp.concatenate([z_odd, near1]))
+    near_odd, diag1 = near_of(z_odd), swap(diag0, "chan", 4)
+    far2 = far_of(jnp.concatenate([z_odd, near1[1:]]))
     rows, ham, zhm, zl, dc, gram_t = pl.pallas_call(
         functools.partial(prepare_kernel, n_chan, n_rad),
         in_specs=[any_] * 5,
@@ -345,13 +347,13 @@
         assemble_kernel,
         in_specs=[any_] * n_rad,
         out_specs=whole,
-        out_shape=pltpu.VMEM((4 * nz * n_rad,) + own.shape[1:], BF16),
+        out_shape=pltpu.VMEM((n_chan * ch, k, splines), BF16),
         scratch_shapes=[pltpu.SemaphoreType.DMA((n_rad,))],
         compiler_params=pltpu.CompilerParams(vmem_limit_bytes=VMEM_LIMIT),
         name="assemble",
-    )(*early)
-    near_odd, far2, table, rows = barrier((near_odd, far2, table, rows))
-    last = [in_vmem(x) for x in in_cores(jnp.concatenate([near_odd, far2]))]
+    )(*[flat(x) for x in early])
+    diag1, near_odd, far2, table, rows = barrier((diag1, near_odd, far2, table, rows))
+    last = [in_vmem(flat(x)) for x in in_cores(jnp.concatenate([near_odd, far2, diag1]))]
 
     az, sums, _ = pl.pallas_call(
         apply_kernel,

time: 59.9 us -> 59.5 us (level)
  waiting for transfers between devices: 16.7 us -> 14.7 us
  starting transfers between devices: 17.2 us -> 18.4 us
    ppermute x6, waiting for transfers between devices: 5.95 us -> 3.42 us  [plane_swap(): return lax.ppermute(x, ('chan', 'rad'), pairs)]
    ppermute x6, starting transfers between devices: 5.22 us -> 5.87 us  [plane_swap(): return lax.ppermute(x, ('chan', 'rad'), pairs)]
    ppermute x9 -> x10, starting transfers between devices: 12 us -> 12.5 us  [swap(): return lax.ppermute(x, axis, [(i, i ^ distance) for i in range(n)])]
    ppermute x9 -> x10, waiting for transfers between devices: 10.8 us -> 11.2 us  [swap(): return lax.ppermute(x, axis, [(i, i ^ distance) for i in range(n)])]
  transfers between devices with their start and end apart: 15 -> 16, of which waited for: 9 -> 10; matrix products, arithmetic and copies ran while one was open for 0% -> 0% of each run, Pallas kernels for 7% -> 7%
where the time goes in v13:
time: 59.5 us; the launch traced here: 59.3 us
  starting transfers between devices  18.4 us (31%)
  waiting for transfers between devices  14.7 us (25%)
  Pallas kernels  12.3 us (21%)
  blocking collectives  11.5 us (19%)
  other arithmetic  1.27 us (2%)
  between operations  0.81 us (1%)
    ppermute x10, starting transfers between devices, swap(): return lax.ppermute(x, axis, [(i, i ^ distance) for i in range(n)])  12.5 us
    all_to_all x1, blocking collectives, gather_sums(): lax.all_to_all(every, 'chan', split_axis=0, concat_axis=0, tiled=True)  11.5 us
    ppermute x10, waiting for transfers between devices, swap(): return lax.ppermute(x, axis, [(i, i ^ distance) for i in range(n)])  11.2 us
    ppermute x6, starting transfers between devices, plane_swap(): return lax.ppermute(x, ('chan', 'rad'), pairs)  5.87 us
    pallas_call x1, Pallas kernels, body(): pl.pallas_call(apply_kernel, in_specs=[smem] + [whole] * (6 + n_rad), out...  5.33 us
    pallas_call x1, Pallas kernels, body(): pl.pallas_call(functools.partial(prepare_kernel, n_chan, n_rad), in_specs...  3.66 us
    ppermute x6, waiting for transfers between devices, plane_swap(): return lax.ppermute(x, ('chan', 'rad'), pairs)  3.42 us
    pallas_call x1, Pallas kernels, body(): pl.pallas_call(functools.partial(finish_kernel, total), out_shape=[jax.Sh...  3.07 us
  transfers between devices with their start and end apart: 16, of which 10 were waited for; matrix products, arithmetic and copies ran while one was open for 0% of the time, Pallas kernels for 7%

profile of v13, /device:TPU:0, one launch (start us, length us, event | category | flops | bytes accessed | tf_op | source)
XLA Modules:
  0.0 59.3 jit_solution(14002201301141982515)
XLA Ops:
  0.6 1.1 %convert_element_type.3 = bf16[64,16,64]{2,1,0:T(8,128)(2,1)S(1)} convert(f32[64,16,64]{2,1,0:T(8,128)} %t_hbm) | non-fusion elementwise | flops 65536 | bytes 393216 | tf_op jit(solution)/shard_map/convert_element_type | solution.py:260
  1.7 0.5 collective-permute-start
  2.3 1.0 %collective-permute-done = bf16[32,16,64]{2,1,0:T(8,128)(2,1)S(1)} collective-permute-done((bf16[32,16,64]{2,1,0:T(8,128)(2,1)S(1)}, bf16[32,16,64]{2,1,0:T(8,128)(2,1)S(1)}, u32[]{:S(2)}, u32[]{:S(2)}) %collective-permute-start) | collective-permute-done | bytes 65568 | tf_op jit(solution)/shard_map/ppermute | solution.py:21
  3.3 0.1 constant_dynamic-update-slice_fusion.9
  3.4 4.0 %collective-permute-start.5 = (bf16[1,32,16,128]{3,2,1,0:T(8,128)(2,1)S(1)}, bf16[1,32,16,128]{3,2,1,0:T(8,128)(2,1)S(1)}, u32[]{:S(2)}, u32[]{:S(2)}) collective-permute-start(bf16[1,32,16,128]{3,2,1,0:T(8,128)(2,1)S(1)} %get-tuple-element.69), channel_id=1, source_target_pairs={{0,16},{2,18},{4,20},{6,22},{8,24},{10,26},{12,28},{14,30},{16,0},... | collective-permute-start | bytes 393224 | tf_op jit(solution)/shard_map/ppermute | solution.py:21
  7.4 2.4 %collective-permute-start.4 = (bf16[1,32,16,128]{3,2,1,0:T(8,128)(2,1)S(1)}, bf16[1,32,16,128]{3,2,1,0:T(8,128)(2,1)S(1)}, u32[]{:S(2)}, u32[]{:S(2)}) collective-permute-start(bf16[1,32,16,128]{3,2,1,0:T(8,128)(2,1)S(1)} %get-tuple-element.69), channel_id=1, source_target_pairs={{0,6},{2,4},{4,2},{6,0},{8,14},{10,12},{12,10},{14,8},{16,22},{18,... | collective-permute-start | bytes 393224 | tf_op jit(solution)/shard_map/ppermute | solution.py:21
  9.9 0.5 collective-permute-start.3
  10.4 0.5 collective-permute-start.2
  10.9 1.6 %collective-permute-start.1 = (bf16[1,32,16,128]{3,2,1,0:T(8,128)(2,1)S(1)}, bf16[1,32,16,128]{3,2,1,0:T(8,128)(2,1)S(1)}, u32[]{:S(2)}, u32[]{:S(2)}) collective-permute-start(bf16[1,32,16,128]{3,2,1,0:T(8,128)(2,1)S(1)} %get-tuple-element.69), channel_id=1, source_target_pairs={{0,8},{2,10},{4,12},{6,14},{8,0},{10,2},{12,4},{14,6},{16,24},{18,... | collective-permute-start | bytes 393224 | tf_op jit(solution)/shard_map/ppermute | solution.py:21
  12.5 1.7 %collective-permute-done.5 = bf16[1,32,16,128]{3,2,1,0:T(8,128)(2,1)S(1)} collective-permute-done((bf16[1,32,16,128]{3,2,1,0:T(8,128)(2,1)S(1)}, bf16[1,32,16,128]{3,2,1,0:T(8,128)(2,1)S(1)}, u32[]{:S(2)}, u32[]{:S(2)}) %collective-permute-start.5) | collective-permute-done | bytes 131104 | tf_op jit(solution)/shard_map/ppermute | solution.py:21
  14.1 2.3 %collective-permute-done.3 = bf16[1,32,16,128]{3,2,1,0:T(8,128)(2,1)S(1)} collective-permute-done((bf16[1,32,16,128]{3,2,1,0:T(8,128)(2,1)S(1)}, bf16[1,32,16,128]{3,2,1,0:T(8,128)(2,1)S(1)}, u32[]{:S(2)}, u32[]{:S(2)}) %collective-permute-start.3) | collective-permute-done | bytes 131104 | tf_op jit(solution)/shard_map/ppermute | solution.py:30
  16.4 0.4 collective-permute-done.1
  16.9 1.6 %collective-permute-start.9 = (bf16[2,32,16,128]{3,2,1,0:T(8,128)(2,1)S(1)}, bf16[2,32,16,128]{3,2,1,0:T(8,128)(2,1)S(1)}, u32[]{:S(2)}, u32[]{:S(2)}) collective-permute-start(bf16[2,32,16,128]{3,2,1,0:T(8,128)(2,1)S(1)} %pad_maximum_fusion), channel_id=1, source_target_pairs={{0,2},{1,5},{2,0},{3,7},{4,6},{5,1},{6,4},{7,3},{8,10},{9,13},{10,... | collective-permute-start | bytes 786440 | tf_op jit(solution)/shard_map/ppermute | solution.py:30
  18.5 1.5 %collective-permute-start.8 = (bf16[2,32,16,128]{3,2,1,0:T(8,128)(2,1)S(1)}, bf16[2,32,16,128]{3,2,1,0:T(8,128)(2,1)S(1)}, u32[]{:S(2)}, u32[]{:S(2)}) collective-permute-start(bf16[2,32,16,128]{3,2,1,0:T(8,128)(2,1)S(1)} %pad_maximum_fusion), channel_id=1, source_target_pairs={{0,4},{1,3},{2,6},{3,1},{4,0},{5,7},{6,2},{7,5},{8,12},{9,11},{10,... | collective-permute-start | bytes 786440 | tf_op jit(solution)/shard_map/ppermute | solution.py:30
  20.0 0.6 %collective-permute-start.7 = (bf16[1,32,16,128]{3,2,1,0:T(8,128)(2,1)S(1)}, bf16[1,32,16,128]{3,2,1,0:T(8,128)(2,1)S(1)}, u32[]{:S(2)}, u32[]{:S(2)}) collective-permute-start(bf16[1,32,16,128]{3,2,1,0:T(8,128)(2,1)S(1)} %collective-permute-done.5), channel_id=1, source_target_pairs={{0,8},{2,10},{4,12},{6,14},{8,0},{10,2},{12,4},{14,6},{16,24},{18,... | collective-permute-start | bytes 393224 | tf_op jit(solution)/shard_map/ppermute | solution.py:21
  20.7 2.1 %collective-permute-start.6 = (bf16[1,32,16,128]{3,2,1,0:T(8,128)(2,1)S(1)}, bf16[1,32,16,128]{3,2,1,0:T(8,128)(2,1)S(1)}, u32[]{:S(2)}, u32[]{:S(2)}) collective-permute-start(bf16[1,32,16,128]{3,2,1,0:T(8,128)(2,1)S(1)} %collective-permute-done.4), channel_id=1, source_target_pairs={{0,24},{2,26},{4,28},{6,30},{8,16},{10,18},{12,20},{14,22},{16,8},... | collective-permute-start | bytes 393224 | tf_op jit(solution)/shard_map/ppermute | solution.py:21
  22.8 5.2 %collective-permute-done.6 = bf16[1,32,16,128]{3,2,1,0:T(8,128)(2,1)S(1)} collective-permute-done((bf16[1,32,16,128]{3,2,1,0:T(8,128)(2,1)S(1)}, bf16[1,32,16,128]{3,2,1,0:T(8,128)(2,1)S(1)}, u32[]{:S(2)}, u32[]{:S(2)}) %collective-permute-start.6) | collective-permute-done | bytes 131104 | tf_op jit(solution)/shard_map/ppermute | solution.py:21
  28.1 0.1 collective-permute-start.13
  28.3 1.0 %collective-permute-start.12 = (bf16[2,32,16,128]{3,2,1,0:T(8,128)(2,1)S(1)}, bf16[2,32,16,128]{3,2,1,0:T(8,128)(2,1)S(1)}, u32[]{:S(2)}, u32[]{:S(2)}) collective-permute-start(bf16[2,32,16,128]{3,2,1,0:T(8,128)(2,1)S(1)} %pad_maximum_fusion.1), channel_id=1, source_target_pairs={{0,4},{1,3},{2,6},{3,1},{4,0},{5,7},{6,2},{7,5},{8,12},{9,11},{10,... | collective-permute-start | bytes 786440 | tf_op jit(solution)/shard_map/ppermute | solution.py:30
  29.3 1.0 %collective-permute-start.10 = (bf16[1,32,16,128]{3,2,1,0:T(8,128)(2,1)S(1)}, bf16[1,32,16,128]{3,2,1,0:T(8,128)(2,1)S(1)}, u32[]{:S(2)}, u32[]{:S(2)}) collective-permute-start(bf16[1,32,16,128]{3,2,1,0:T(8,128)(2,1)S(1)} %collective-permute-done.4), channel_id=1, source_target_pairs={{0,8},{2,10},{4,12},{6,14},{8,0},{10,2},{12,4},{14,6},{16,24},{18,... | collective-permute-start | bytes 393224 | tf_op jit(solution)/shard_map/ppermute | solution.py:21
  30.3 0.7 %collective-permute-start.11 = (bf16[1,32,16,128]{3,2,1,0:T(8,128)(2,1)S(1)}, bf16[1,32,16,128]{3,2,1,0:T(8,128)(2,1)S(1)}, u32[]{:S(2)}, u32[]{:S(2)}) collective-permute-start(bf16[1,32,16,128]{3,2,1,0:T(8,128)(2,1)S(1)} %collective-permute-done.7), channel_id=1, source_target_pairs={{0,2},{1,5},{2,0},{3,7},{4,6},{5,1},{6,4},{7,3},{8,10},{9,13},{10,... | collective-permute-start | bytes 393224 | tf_op jit(solution)/shard_map/ppermute | solution.py:30
  31.0 3.7 %prepare.1 = (s32[64,8]{1,0:T(8,128)S(1)}, bf16[64,8,64,128]{3,2,1,0:T(8,128)(2,1)S(1)}, bf16[64,4096]{1,0:T(8,128)(2,1)S(1)}, bf16[32,4096]{1,0:T(8,128)(2,1)S(...) custom-call(f32[64,16,64]{2,1,0:T(8,128)} %t_hbm, f32[64,64]{1,0:T(8,128)} %d_hbm, s32[8,64]{1,0:T(8,128)} %bitcast.22, ...), custom_call_target="tpu_custom_call" | custom-call | tf_op jit(solution)/shard_map/prepare/pallas_call | solution.py:318
  34.7 0.2 assemble.1._
  34.9 0.1 collective-permute-done.10
  35.0 0.6 %collective-permute-done.11 = bf16[1,32,16,128]{3,2,1,0:T(8,128)(2,1)S(1)} collective-permute-done((bf16[1,32,16,128]{3,2,1,0:T(8,128)(2,1)S(1)}, bf16[1,32,16,128]{3,2,1,0:T(8,128)(2,1)S(1)}, u32[]{:S(2)}, u32[]{:S(2)}) %collective-permute-start.11) | collective-permute-done | bytes 131104 | tf_op jit(solution)/shard_map/ppermute | solution.py:30
  35.6 0.5 collective-permute-done.12
  36.3 1.9 %collective-permute-done.14 = bf16[4,32,16,128]{3,2,1,0:T(8,128)(2,1)S(1)} collective-permute-done((bf16[4,32,16,128]{3,2,1,0:T(8,128)(2,1)S(1)}, bf16[4,32,16,128]{3,2,1,0:T(8,128)(2,1)S(1)}, u32[]{:S(2)}, u32[]{:S(2)}) %collective-permute-start.14) | collective-permute-done | bytes 524320 | tf_op jit(solution)/shard_map/ppermute | solution.py:21
  38.2 5.3 %apply.1 = (bf16[32,4096]{1,0:T(8,128)(2,1)S(1)}, f32[16,128]{1,0:T(8,128)S(1)}, bf16[1024,16,128]{2,1,0:T(8,128)(2,1)S(1)}) custom-call(s32[64,8]{1,0:T(8,128)S(1)} %get-tuple-element.54.rows_ref, bf16[64,8,64,128]{3,2,1,0:T(8,128)(2,1)S(1)} %get-tuple-element.55.ham_ref, bf16[1024,16,128]{2,1,0:T(8,128)(2,1)S(1)} %assemble.1._, ...), custom_call_target="tpu_custom_call", output_to_operand_aliasing={{2}: (2, {})} | custom-call | tf_op jit(solution)/shard_map/apply/pallas_call | solution.py:358
  43.5 0.2 collective-permute-start.15
  43.7 1.0 %collective-permute-done.15 = f32[16,128]{1,0:T(8,128)S(1)} collective-permute-done((f32[16,128]{1,0:T(8,128)S(1)}, f32[16,128]{1,0:T(8,128)S(1)}, u32[]{:S(2)}, u32[]{:S(2)}) %collective-permute-start.15) | collective-permute-done | bytes 8224 | tf_op jit(solution)/shard_map/ppermute | solution.py:21
  44.7 11.5 %all_to_all.5.sums_ref = f32[16,16,128]{2,1,0:T(8,128)S(1)} all-to-all(f32[16,16,128]{2,1,0:T(8,128)S(1)} %broadcast_in_dim.7), channel_id=1, replica_groups=mesh['chan'=16,'rad'=2] {'chan'}, dimensions={0} | all-to-all | bytes 262144 | tf_op jit(solution)/shard_map/all_to_all | solution.py:253
  56.3 3.1 %finish.1 = (f32[64,16,64]{2,1,0:T(8,128)}, f32[1,16]{1,0:T(1,128)}) custom-call(f32[16,16,128]{2,1,0:T(8,128)S(1)} %all_to_all.5.sums_ref, bf16[32,4096]{1,0:T(8,128)(2,1)S(1)} %get-tuple-element.65.az_ref, bf16[64,4096]{1,0:T(8,128)(2,1)S(1)} %get-tuple-element.57.zhm_ref), custom_call_target="tpu_custom_call" | custom-call | tf_op jit(solution)/shard_map/finish/pallas_call | solution.py:374
  (26 shorter events, 0.5 us)
Async XLA Ops:
  1.7 1.5 %collective-permute-start = (bf16[32,16,64]{2,1,0:T(8,128)(2,1)S(1)}, bf16[32,16,64]{2,1,0:T(8,128)(2,1)S(1)}, u32[]{:S(2)}, u32[]{:S(2)}) collective-permute-start(bf16[32,16,64]{2,1,0:T(8,128)(2,1)S(1)} %dynamic-slice_bitcast_fusion), channel_id=1, source_target_pairs={{0,1},{1,0},{2,3},{3,2},{4,5},{5,4},{6,7},{7,6},{8,9},{9,8},{10,11... | collective-permute-start | bytes 196616 | tf_op jit(solution)/shard_map/ppermute | solution.py:21
  3.4 10.7 %collective-permute-start.5 = (bf16[1,32,16,128]{3,2,1,0:T(8,128)(2,1)S(1)}, bf16[1,32,16,128]{3,2,1,0:T(8,128)(2,1)S(1)}, u32[]{:S(2)}, u32[]{:S(2)}) collective-permute-start(bf16[1,32,16,128]{3,2,1,0:T(8,128)(2,1)S(1)} %get-tuple-element.69), channel_id=1, source_target_pairs={{0,16},{2,18},{4,20},{6,22},{8,24},{10,26},{12,28},{14,30},{16,0},... | collective-permute-start | bytes 393224 | tf_op jit(solution)/shard_map/ppermute | solution.py:21
  7.4 6.7 %collective-permute-start.4 = (bf16[1,32,16,128]{3,2,1,0:T(8,128)(2,1)S(1)}, bf16[1,32,16,128]{3,2,1,0:T(8,128)(2,1)S(1)}, u32[]{:S(2)}, u32[]{:S(2)}) collective-permute-start(bf16[1,32,16,128]{3,2,1,0:T(8,128)(2,1)S(1)} %get-tuple-element.69), channel_id=1, source_target_pairs={{0,6},{2,4},{4,2},{6,0},{8,14},{10,12},{12,10},{14,8},{16,22},{18,... | collective-permute-start | bytes 393224 | tf_op jit(solution)/shard_map/ppermute | solution.py:21
  9.9 6.6 %collective-permute-start.3 = (bf16[1,32,16,128]{3,2,1,0:T(8,128)(2,1)S(1)}, bf16[1,32,16,128]{3,2,1,0:T(8,128)(2,1)S(1)}, u32[]{:S(2)}, u32[]{:S(2)}) collective-permute-start(bf16[1,32,16,128]{3,2,1,0:T(8,128)(2,1)S(1)} %get-tuple-element.69), channel_id=1, source_target_pairs={{0,2},{1,5},{2,0},{3,7},{4,6},{5,1},{6,4},{7,3},{8,10},{9,13},{10,... | collective-permute-start | bytes 393224 | tf_op jit(solution)/shard_map/ppermute | solution.py:30
  10.4 6.1 %collective-permute-start.2 = (bf16[1,32,16,128]{3,2,1,0:T(8,128)(2,1)S(1)}, bf16[1,32,16,128]{3,2,1,0:T(8,128)(2,1)S(1)}, u32[]{:S(2)}, u32[]{:S(2)}) collective-permute-start(bf16[1,32,16,128]{3,2,1,0:T(8,128)(2,1)S(1)} %get-tuple-element.69), channel_id=1, source_target_pairs={{0,4},{1,3},{2,6},{3,1},{4,0},{5,7},{6,2},{7,5},{8,12},{9,11},{10,... | collective-permute-start | bytes 393224 | tf_op jit(solution)/shard_map/ppermute | solution.py:30
  10.9 5.9 %collective-permute-start.1 = (bf16[1,32,16,128]{3,2,1,0:T(8,128)(2,1)S(1)}, bf16[1,32,16,128]{3,2,1,0:T(8,128)(2,1)S(1)}, u32[]{:S(2)}, u32[]{:S(2)}) collective-permute-start(bf16[1,32,16,128]{3,2,1,0:T(8,128)(2,1)S(1)} %get-tuple-element.69), channel_id=1, source_target_pairs={{0,8},{2,10},{4,12},{6,14},{8,0},{10,2},{12,4},{14,6},{16,24},{18,... | collective-permute-start | bytes 393224 | tf_op jit(solution)/shard_map/ppermute | solution.py:21
  16.9 11.1 %collective-permute-start.9 = (bf16[2,32,16,128]{3,2,1,0:T(8,128)(2,1)S(1)}, bf16[2,32,16,128]{3,2,1,0:T(8,128)(2,1)S(1)}, u32[]{:S(2)}, u32[]{:S(2)}) collective-permute-start(bf16[2,32,16,128]{3,2,1,0:T(8,128)(2,1)S(1)} %pad_maximum_fusion), channel_id=1, source_target_pairs={{0,2},{1,5},{2,0},{3,7},{4,6},{5,1},{6,4},{7,3},{8,10},{9,13},{10,... | collective-permute-start | bytes 786440 | tf_op jit(solution)/shard_map/ppermute | solution.py:30
  18.5 9.5 %collective-permute-start.8 = (bf16[2,32,16,128]{3,2,1,0:T(8,128)(2,1)S(1)}, bf16[2,32,16,128]{3,2,1,0:T(8,128)(2,1)S(1)}, u32[]{:S(2)}, u32[]{:S(2)}) collective-permute-start(bf16[2,32,16,128]{3,2,1,0:T(8,128)(2,1)S(1)} %pad_maximum_fusion), channel_id=1, source_target_pairs={{0,4},{1,3},{2,6},{3,1},{4,0},{5,7},{6,2},{7,5},{8,12},{9,11},{10,... | collective-permute-start | bytes 786440 | tf_op jit(solution)/shard_map/ppermute | solution.py:30
  20.0 7.9 %collective-permute-start.7 = (bf16[1,32,16,128]{3,2,1,0:T(8,128)(2,1)S(1)}, bf16[1,32,16,128]{3,2,1,0:T(8,128)(2,1)S(1)}, u32[]{:S(2)}, u32[]{:S(2)}) collective-permute-start(bf16[1,32,16,128]{3,2,1,0:T(8,128)(2,1)S(1)} %collective-permute-done.5), channel_id=1, source_target_pairs={{0,8},{2,10},{4,12},{6,14},{8,0},{10,2},{12,4},{14,6},{16,24},{18,... | collective-permute-start | bytes 393224 | tf_op jit(solution)/shard_map/ppermute | solution.py:21
  20.7 7.3 %collective-permute-start.6 = (bf16[1,32,16,128]{3,2,1,0:T(8,128)(2,1)S(1)}, bf16[1,32,16,128]{3,2,1,0:T(8,128)(2,1)S(1)}, u32[]{:S(2)}, u32[]{:S(2)}) collective-permute-start(bf16[1,32,16,128]{3,2,1,0:T(8,128)(2,1)S(1)} %collective-permute-done.4), channel_id=1, source_target_pairs={{0,24},{2,26},{4,28},{6,30},{8,16},{10,18},{12,20},{14,22},{16,8},... | collective-permute-start | bytes 393224 | tf_op jit(solution)/shard_map/ppermute | solution.py:21
  28.1 6.5 %collective-permute-start.13 = (bf16[12,32,16,128]{3,2,1,0:T(8,128)(2,1)S(1)}, bf16[12,32,16,128]{3,2,1,0:T(8,128)(2,1)S(1)}, u32[]{:S(2)}, u32[]{:S(2)}) collective-permute-start(bf16[12,32,16,128]{3,2,1,0:T(8,128)(2,1)S(1)} %constant_dynamic-update-slice_fusion), channel_id=1, source_target_pairs={{0,1},{1,0},{2,3},{3,2},{4,5},{5,4},{6,7},{7,6},{8,9},{9,8},{10,11... | collective-permute-start | bytes 4718600 | tf_op jit(solution)/shard_map/ppermute | solution.py:21
  28.3 7.8 %collective-permute-start.12 = (bf16[2,32,16,128]{3,2,1,0:T(8,128)(2,1)S(1)}, bf16[2,32,16,128]{3,2,1,0:T(8,128)(2,1)S(1)}, u32[]{:S(2)}, u32[]{:S(2)}) collective-permute-start(bf16[2,32,16,128]{3,2,1,0:T(8,128)(2,1)S(1)} %pad_maximum_fusion.1), channel_id=1, source_target_pairs={{0,4},{1,3},{2,6},{3,1},{4,0},{5,7},{6,2},{7,5},{8,12},{9,11},{10,... | collective-permute-start | bytes 786440 | tf_op jit(solution)/shard_map/ppermute | solution.py:30
  29.3 5.7 %collective-permute-start.10 = (bf16[1,32,16,128]{3,2,1,0:T(8,128)(2,1)S(1)}, bf16[1,32,16,128]{3,2,1,0:T(8,128)(2,1)S(1)}, u32[]{:S(2)}, u32[]{:S(2)}) collective-permute-start(bf16[1,32,16,128]{3,2,1,0:T(8,128)(2,1)S(1)} %collective-permute-done.4), channel_id=1, source_target_pairs={{0,8},{2,10},{4,12},{6,14},{8,0},{10,2},{12,4},{14,6},{16,24},{18,... | collective-permute-start | bytes 393224 | tf_op jit(solution)/shard_map/ppermute | solution.py:21
  30.3 5.3 %collective-permute-start.11 = (bf16[1,32,16,128]{3,2,1,0:T(8,128)(2,1)S(1)}, bf16[1,32,16,128]{3,2,1,0:T(8,128)(2,1)S(1)}, u32[]{:S(2)}, u32[]{:S(2)}) collective-permute-start(bf16[1,32,16,128]{3,2,1,0:T(8,128)(2,1)S(1)} %collective-permute-done.7), channel_id=1, source_target_pairs={{0,2},{1,5},{2,0},{3,7},{4,6},{5,1},{6,4},{7,3},{8,10},{9,13},{10,... | collective-permute-start | bytes 393224 | tf_op jit(solution)/shard_map/ppermute | solution.py:30
  36.2 2.0 %collective-permute-start.14 = (bf16[4,32,16,128]{3,2,1,0:T(8,128)(2,1)S(1)}, bf16[4,32,16,128]{3,2,1,0:T(8,128)(2,1)S(1)}, u32[]{:S(2)}, u32[]{:S(2)}) collective-permute-start(bf16[4,32,16,128]{3,2,1,0:T(8,128)(2,1)S(1)} %constant_dynamic-update-slice_fusion.10), channel_id=1, source_target_pairs={{0,1},{1,0},{2,3},{3,2},{4,5},{5,4},{6,7},{7,6},{8,9},{9,8},{10,11... | collective-permute-start | bytes 1572872 | tf_op jit(solution)/shard_map/ppermute | solution.py:21
  43.5 1.2 %collective-permute-start.15 = (f32[16,128]{1,0:T(8,128)S(1)}, f32[16,128]{1,0:T(8,128)S(1)}, u32[]{:S(2)}, u32[]{:S(2)}) collective-permute-start(f32[16,128]{1,0:T(8,128)S(1)} %get-tuple-element.64), channel_id=1, source_target_pairs={{0,1},{1,0},{2,3},{3,2},{4,5},{5,4},{6,7},{7,6},{8,9},{9,8},{10,11... | collective-permute-start | bytes 24584 | tf_op jit(solution)/shard_map/ppermute | solution.py:21

commit v14 on v13

--- a/solution.py
+++ b/solution.py
@@ -30,6 +30,17 @@
     return lax.ppermute(x, ("chan", "rad"), pairs)
 
 
+def early_pieces(nz):
+    some, odd = [1] + list(range(2, nz, 2)), list(range(3, nz, 2))
+    order = [(0, 0)] + [(z, 0) for z in some] + [(0, 1), (0, 2), (0, 3)] + [(z, 1) for z in some]
+    return order + [(z, 0) for z in odd] + [(z, 3) for z in odd] + [(z, 2) for z in some]
+
+
+def late_pieces(nz):
+    even, odd = list(range(2, nz, 2)), list(range(3, nz, 2))
+    return [(z, 1) for z in odd] + [(z, 2) for z in odd] + [(z, 3) for z in even] + [(1, 3)]
+
+
 def table_piece(z, part, nz):
     some, odd = nz // 2, nz // 2 - 1
     is_odd = (z & 1 == 1) & (z > 1)
@@ -44,6 +55,29 @@
     far = pick(some + 2, base + odd, base + 2 * odd + some)
     both = jnp.where(z == 1, 4 * nz - 1, pick(some + 3, base + 3 * odd + some - 1, base))
     return jnp.where(part == 0, here, jnp.where(part == 1, near, jnp.where(part == 2, far, both)))
+
+
+def merge(refs, table_ref, order, start, share):
+    n_rad = len(refs)
+    r = 128 // n_rad
+    me = lax.axis_index("rad")
+
+    def rows(n, carry):
+        for i, (z, part) in enumerate(order):
+            other = order.index((z, (0, 2, 1, 3)[part]))
+            tiles = [ref[(other if s % 2 else i) * share + n] for s, ref in enumerate(refs)]
+            by_core = []
+            for c in range(n_rad):
+                x = tiles[0]
+                for s in range(1, n_rad):
+                    x = jnp.where((me ^ s) == c, tiles[s], x)
+                by_core.append(x)
+            for g in range(n_rad):
+                row = jnp.concatenate([x[:, g * r : (g + 1) * r] for x in by_core], axis=1)
+                table_ref[((start + i) * n_rad + g) * share + n] = row
+        return carry
+
+    lax.fori_loop(0, share, rows, 0)
 
 
 def in_vmem(x):
@@ -99,12 +133,11 @@
     share, nz = ch // n_rad, n_chan // 4
     q = stored_ref[...]
     owner, local = lax.div(q, ch), lax.rem(q, ch)
-    core = lax.div(local, share)
     apart = (owner ^ lax.axis_index("chan")) & 3
-    part = jnp.where((core & 1) == 1, ((apart & 1) << 1) | (apart >> 1), apart)
+    turned = ((apart & 1) << 1) | (apart >> 1)
+    part = jnp.where((lax.axis_index("rad") & 1) == 1, turned, apart)
     piece = table_piece((owner ^ lax.axis_index("chan")) >> 2, part, nz)
-    place = (core ^ lax.axis_index("rad")) * 4 * nz + piece
-    place = (place * share + lax.rem(local, share)).astype(F32)
+    place = (piece * ch + local).astype(F32)
     lane = lax.broadcasted_iota(jnp.int32, (ch, 128), 1)
     columns = []
     partners = partners_ref[...].astype(F32).T.astype(jnp.int32)
@@ -118,34 +151,18 @@
     copies[4].wait()
 
 
-def assemble_kernel(*refs):
-    pieces, table_ref, sems = refs[:-2], refs[-2], refs[-1]
-    each = table_ref.shape[0] // len(pieces)
-    copies = []
-    for i, piece in enumerate(pieces):
-        place = table_ref.at[pl.ds(i * each, piece.shape[0])]
-        copies.append(pltpu.make_async_copy(piece, place, sems.at[i]))
-        copies[-1].start()
-    for copy in copies:
-        copy.wait()
-
-
-def apply_kernel(rows_ref, ham_ref, _, zhm_ref, zl_ref, dc_ref, gt_ref, *rest):
-    last, (az_ref, sums_ref, table_ref, a0_ref) = rest[:-4], rest[-4:]
-    for c, piece in enumerate(last):
-        start = (c + 1) * (table_ref.shape[0] // len(last)) - piece.shape[0]
-        step = min(32, piece.shape[0])
-
-        def put(i, carry, piece=piece, start=start, step=step):
-            table_ref[pl.ds(start + i * step, step)] = piece[pl.ds(i * step, step)]
-            return carry
-
-        lax.fori_loop(0, piece.shape[0] // step, put, 0)
+def assemble_kernel(nz, share, *refs):
+    merge(refs[:-1], refs[-1], early_pieces(nz), 0, share)
+
+
+def apply_kernel(nz, share, rows_ref, ham_ref, _, zhm_ref, zl_ref, dc_ref, gt_ref, *rest):
+    last, (az_ref, sums_ref, table_ref) = rest[:-3], rest[-3:]
+    merge(last, table_ref, late_pieces(nz), len(early_pieces(nz)), share)
     ch, ncoup, r, splines = ham_ref.shape
     k = zl_ref.shape[0] // 2
     group = 256 // r
 
-    def work(g, carry):
+    def work(g, gram):
         left, right = [], []
         for i in range(group):
             p = g * group + i
@@ -160,24 +177,16 @@
             preferred_element_type=F32,
         )
         own = [product[i * k : (i + 1) * k, i * r : (i + 1) * r] for i in range(group)]
-        a0_ref[:, pl.ds(pl.multiple_of(g * 256, 256), 256)] = jnp.concatenate(own, axis=1) * SCALE
-        return carry
-
-    lax.fori_loop(0, ch // group, work, 0, unroll=min(4, ch // group))
-
-    lanes = ch * r
-    block = min(lanes, 1024)
-
-    def gram_block(i, gram):
-        at = pl.ds(pl.multiple_of(i * block, block), block)
-        a0 = a0_ref[:, at]
+        at = pl.ds(pl.multiple_of(g * 256, 256), 256)
+        a0 = jnp.concatenate(own, axis=1) * SCALE
         a1_terms = split3(a0 / dc_ref[:, at])
         az_ref[:, at] = jnp.concatenate(a1_terms[:2], axis=0)
         right = jnp.concatenate(a1_terms + split3(a0), axis=0)
         left = jnp.concatenate([zhm_ref[:, at], zl_ref[:, at], right[: 3 * k]], axis=0)
         return gram + lax.dot_general(left, right, NT, preferred_element_type=F32)
 
-    gram = lax.fori_loop(0, lanes // block, gram_block, jnp.zeros((9 * k, 6 * k), F32))
+    groups = ch // group
+    gram = lax.fori_loop(0, groups, work, jnp.zeros((9 * k, 6 * k), F32), unroll=min(4, groups))
     ta1 = block_sum(gram[: 6 * k, : 3 * k], 2 * k, k)
     ta0 = block_sum(gram[: 6 * k, 3 * k :], 2 * k, k)
     aa = block_sum(gram[6 * k :, : 3 * k], k, k)
@@ -253,24 +262,6 @@
     return lax.all_to_all(every, "chan", split_axis=0, concat_axis=0, tiled=True)
 
 
-def own_share(trial_block):
-    n_rad = lax.axis_size("rad")
-    ch, k, r = trial_block.shape
-    me = lax.axis_index("rad")
-    rounded = trial_block.astype(BF16).reshape(n_rad, ch // n_rad, k, r)
-    got = []
-    for d in range(n_rad):
-        part = lax.dynamic_index_in_dim(rounded, me ^ d, 0, keepdims=False)
-        got.append(swap(part, "rad", d) if d else part)
-    lanes = []
-    for c in range(n_rad):
-        x = got[0]
-        for d in range(1, n_rad):
-            x = jnp.where(me ^ d == c, got[d], x)
-        lanes.append(x)
-    return jnp.concatenate(lanes, axis=2)
-
-
 def body(trial_block, ham_blocks, partners, stored_at, precond_diag):
     n_chan, n_rad = lax.axis_size("chan"), lax.axis_size("rad")
     ch, k, r = trial_block.shape
@@ -296,25 +287,10 @@
     def in_cores(x):
         return [x] + [swap(x, "rad", c) for c in range(1, n_rad)]
 
-    own = own_share(trial_block)[None]
+    own = jnp.concatenate(jnp.split(trial_block.astype(BF16), n_rad), axis=2)[None]
     near0, far_own, diag0 = near_of(own), far_of(own), swap(own, "chan", 3)
     z1 = swap(own, "chan", 4)
     z_even = jnp.concatenate([swap(own, "chan", 4 * z) for z in range(2, nz, 2)])
-    z1, far_own, near0, diag0, z_even = barrier((z1, far_own, near0, diag0, z_even))
-    some, z_even, diag0 = barrier((jnp.concatenate([z1, z_even]), z_even, diag0))
-    near1, far1 = near_of(some), far_of(some)
-    z_odd = swap(z_even, "chan", 4)
-    diag_odd = jnp.concatenate([swap(diag0, "chan", 4 * z) for z in range(3, nz, 2)])
-    inputs = (trial_block, precond_diag, partners, stored_at, ham_blocks)
-    diag_odd, z_odd, far1, near1, diag0, inputs = barrier(
-        (diag_odd, z_odd, far1, near1, diag0, inputs)
-    )
-    trial_block, precond_diag, partners, stored_at, ham_blocks = inputs
-    early = in_cores(
-        jnp.concatenate([own, z1, z_even, near0, far_own, diag0, near1, z_odd, diag_odd, far1])
-    )
-    near_odd, diag1 = near_of(z_odd), swap(diag0, "chan", 4)
-    far2 = far_of(jnp.concatenate([z_odd, near1[1:]]))
     rows, ham, zhm, zl, dc, gram_t = pl.pallas_call(
         functools.partial(prepare_kernel, n_chan, n_rad),
         in_specs=[any_] * 5,
@@ -343,20 +319,32 @@
         in_hbm(stored_at.reshape(-1, 128)),
         in_hbm(ham_blocks),
     )
+    far_own, near0, z1, z_even, diag0, rows = barrier((far_own, near0, z1, z_even, diag0, rows))
+    some, z_even, diag0 = barrier((jnp.concatenate([z1, z_even]), z_even, diag0))
+    near1, far1 = near_of(some), far_of(some)
+    z_odd = swap(z_even, "chan", 4)
+    diag_odd = jnp.concatenate([swap(diag0, "chan", 4 * z) for z in range(3, nz, 2)])
+    diag_odd, z_odd, far1, near1, diag0 = barrier(
+        (diag_odd, z_odd, far1, near1, diag0)
+    )
+    early = in_cores(
+        jnp.concatenate([own, z1, z_even, near0, far_own, diag0, near1, z_odd, diag_odd, far1])
+    )
+    near_odd, diag1 = near_of(z_odd), swap(diag0, "chan", 4)
+    far2 = far_of(jnp.concatenate([z_odd, near1[1:]]))
     table = pl.pallas_call(
-        assemble_kernel,
-        in_specs=[any_] * n_rad,
+        functools.partial(assemble_kernel, nz, share),
+        in_specs=[whole] * n_rad,
         out_specs=whole,
         out_shape=pltpu.VMEM((n_chan * ch, k, splines), BF16),
-        scratch_shapes=[pltpu.SemaphoreType.DMA((n_rad,))],
         compiler_params=pltpu.CompilerParams(vmem_limit_bytes=VMEM_LIMIT),
         name="assemble",
-    )(*[flat(x) for x in early])
+    )(*[in_vmem(flat(x)) for x in early])
     diag1, near_odd, far2, table, rows = barrier((diag1, near_odd, far2, table, rows))
     last = [in_vmem(flat(x)) for x in in_cores(jnp.concatenate([near_odd, far2, diag1]))]
 
     az, sums, _ = pl.pallas_call(
-        apply_kernel,
+        functools.partial(apply_kernel, nz, share),
         in_specs=[smem] + [whole] * (6 + n_rad),
         out_specs=[whole, whole, whole],
         out_shape=[
@@ -365,7 +353,6 @@
             pltpu.VMEM(table.shape, BF16),
         ],
         input_output_aliases={2: 2},
-        scratch_shapes=[pltpu.VMEM((k, lanes), F32)],
         compiler_params=pltpu.CompilerParams(vmem_limit_bytes=VMEM_LIMIT),
         name="apply",
     )(rows, in_vmem(ham), in_vmem(table), in_vmem(zhm), in_vmem(zl), in_vmem(dc), gram_t, *last)

time: 59.5 us -> 62.3 us (1.047)
  Pallas kernels: 12.3 us -> 19.3 us
  waiting for transfers between devices: 14.7 us -> 9.78 us
  blocking collectives: 11.5 us -> 12.8 us
    pallas_call x2, Pallas kernels: 5.57 us -> 12.6 us  [the longest x1 9.49 us: body(): pl.pallas_call(functools.partial(apply_kernel, nz, share), in_specs=[smem...]
    ppermute x10 -> x9, waiting for transfers between devices: 11.2 us -> 8.39 us  [swap(): return lax.ppermute(x, axis, [(i, i ^ distance) for i in range(n)])]
    ppermute x6, waiting for transfers between devices: 3.42 us -> 1.38 us  [plane_swap(): return lax.ppermute(x, ('chan', 'rad'), pairs)]
    all_to_all x1, blocking collectives: 11.5 us -> 12.8 us  [gather_sums(): lax.all_to_all(every, 'chan', split_axis=0, concat_axis=0, tiled=True)]
    ppermute x10 -> x9, starting transfers between devices: 12.5 us -> 11.8 us  [swap(): return lax.ppermute(x, axis, [(i, i ^ distance) for i in range(n)])]
  transfers between devices with their start and end apart: 16 -> 15, of which waited for: 10 -> 7; matrix products, arithmetic and copies ran while one was open for 0% -> 0% of each run, Pallas kernels for 7% -> 11%
where the time goes in v14:
time: 62.3 us; the launch traced here: 62.1 us
  Pallas kernels  19.3 us (31%)
  starting transfers between devices  17.8 us (29%)
  blocking collectives  12.8 us (21%)
  waiting for transfers between devices  9.78 us (16%)
  other arithmetic  1.25 us (2%)
  between operations  0.8 us (1%)
    all_to_all x1, blocking collectives, gather_sums(): lax.all_to_all(every, 'chan', split_axis=0, concat_axis=0, tiled=True)  12.8 us
    ppermute x9, starting transfers between devices, swap(): return lax.ppermute(x, axis, [(i, i ^ distance) for i in range(n)])  11.8 us
    pallas_call x1, Pallas kernels, body(): pl.pallas_call(functools.partial(apply_kernel, nz, share), in_specs=[smem...  9.49 us
    ppermute x9, waiting for transfers between devices, swap(): return lax.ppermute(x, axis, [(i, i ^ distance) for i in range(n)])  8.39 us
    ppermute x6, starting transfers between devices, plane_swap(): return lax.ppermute(x, ('chan', 'rad'), pairs)  6.01 us
    pallas_call x1, Pallas kernels, body(): pl.pallas_call(functools.partial(prepare_kernel, n_chan, n_rad), in_specs...  3.66 us
    pallas_call x1, Pallas kernels, body(): pl.pallas_call(functools.partial(assemble_kernel, nz, share), in_specs=[w...  3.11 us
    pallas_call x1, Pallas kernels, body(): pl.pallas_call(functools.partial(finish_kernel, total), out_shape=[jax.Sh...  3.07 us
  transfers between devices with their start and end apart: 15, of which 7 were waited for; matrix products, arithmetic and copies ran while one was open for 0% of the time, Pallas kernels for 11%

profile of v14, /device:TPU:0, one launch (start us, length us, event | category | flops | bytes accessed | tf_op | source)
XLA Modules:
  0.0 62.1 jit_solution(4235690423530582211)
XLA Ops:
  0.6 1.1 %convert_element_type.3 = bf16[64,16,64]{2,1,0:T(8,128)(2,1)S(1)} convert(f32[64,16,64]{2,1,0:T(8,128)} %t_hbm.1) | non-fusion elementwise | flops 65536 | bytes 393216 | tf_op jit(solution)/shard_map/convert_element_type | solution.py:290
  1.7 0.1 constant_dynamic-update-slice_fusion.9
  1.9 4.0 %collective-permute-start.4 = (bf16[1,32,16,128]{3,2,1,0:T(8,128)(2,1)S(1)}, bf16[1,32,16,128]{3,2,1,0:T(8,128)(2,1)S(1)}, u32[]{:S(2)}, u32[]{:S(2)}) collective-permute-start(bf16[1,32,16,128]{3,2,1,0:T(8,128)(2,1)S(1)} %get-tuple-element.61), channel_id=1, source_target_pairs={{0,6},{2,4},{4,2},{6,0},{8,14},{10,12},{12,10},{14,8},{16,22},{18,... | collective-permute-start | bytes 393224 | tf_op jit(solution)/shard_map/ppermute | solution.py:21
  5.8 2.6 %collective-permute-start.3 = (bf16[1,32,16,128]{3,2,1,0:T(8,128)(2,1)S(1)}, bf16[1,32,16,128]{3,2,1,0:T(8,128)(2,1)S(1)}, u32[]{:S(2)}, u32[]{:S(2)}) collective-permute-start(bf16[1,32,16,128]{3,2,1,0:T(8,128)(2,1)S(1)} %get-tuple-element.61), channel_id=1, source_target_pairs={{0,16},{2,18},{4,20},{6,22},{8,24},{10,26},{12,28},{14,30},{16,0},... | collective-permute-start | bytes 393224 | tf_op jit(solution)/shard_map/ppermute | solution.py:21
  8.4 1.6 %collective-permute-start.2 = (bf16[1,32,16,128]{3,2,1,0:T(8,128)(2,1)S(1)}, bf16[1,32,16,128]{3,2,1,0:T(8,128)(2,1)S(1)}, u32[]{:S(2)}, u32[]{:S(2)}) collective-permute-start(bf16[1,32,16,128]{3,2,1,0:T(8,128)(2,1)S(1)} %get-tuple-element.61), channel_id=1, source_target_pairs={{0,8},{2,10},{4,12},{6,14},{8,0},{10,2},{12,4},{14,6},{16,24},{18,... | collective-permute-start | bytes 393224 | tf_op jit(solution)/shard_map/ppermute | solution.py:21
  10.0 0.5 collective-permute-start.1
  10.5 0.5 collective-permute-start
  11.0 3.7 %prepare.1 = (s32[64,8]{1,0:T(8,128)S(1)}, bf16[64,8,64,128]{3,2,1,0:T(8,128)(2,1)S(1)}, bf16[64,4096]{1,0:T(8,128)(2,1)S(1)}, bf16[32,4096]{1,0:T(8,128)(2,1)S(...) custom-call(f32[64,16,64]{2,1,0:T(8,128)} %t_hbm.1, f32[64,64]{1,0:T(8,128)} %d_hbm.1, s32[8,64]{1,0:T(8,128)} %bitcast.14, ...), custom_call_target="tpu_custom_call" | custom-call | tf_op jit(solution)/shard_map/prepare/pallas_call | solution.py:294
  14.7 0.0 collective-permute-done.4
  14.7 0.0 collective-permute-done.3
  14.7 0.1 collective-permute-done.2
  14.8 0.2 collective-permute-done.1
  14.9 0.5 collective-permute-done
  15.5 1.6 %collective-permute-start.8 = (bf16[2,32,16,128]{3,2,1,0:T(8,128)(2,1)S(1)}, bf16[2,32,16,128]{3,2,1,0:T(8,128)(2,1)S(1)}, u32[]{:S(2)}, u32[]{:S(2)}) collective-permute-start(bf16[2,32,16,128]{3,2,1,0:T(8,128)(2,1)S(1)} %pad_maximum_fusion), channel_id=1, source_target_pairs={{0,2},{1,5},{2,0},{3,7},{4,6},{5,1},{6,4},{7,3},{8,10},{9,13},{10,... | collective-permute-start | bytes 786440 | tf_op jit(solution)/shard_map/ppermute | solution.py:30
  17.1 0.8 %collective-permute-start.7 = (bf16[2,32,16,128]{3,2,1,0:T(8,128)(2,1)S(1)}, bf16[2,32,16,128]{3,2,1,0:T(8,128)(2,1)S(1)}, u32[]{:S(2)}, u32[]{:S(2)}) collective-permute-start(bf16[2,32,16,128]{3,2,1,0:T(8,128)(2,1)S(1)} %pad_maximum_fusion), channel_id=1, source_target_pairs={{0,4},{1,3},{2,6},{3,1},{4,0},{5,7},{6,2},{7,5},{8,12},{9,11},{10,... | collective-permute-start | bytes 786440 | tf_op jit(solution)/shard_map/ppermute | solution.py:30
  17.9 0.5 collective-permute-start.6
  18.4 1.4 %collective-permute-start.5 = (bf16[1,32,16,128]{3,2,1,0:T(8,128)(2,1)S(1)}, bf16[1,32,16,128]{3,2,1,0:T(8,128)(2,1)S(1)}, u32[]{:S(2)}, u32[]{:S(2)}) collective-permute-start(bf16[1,32,16,128]{3,2,1,0:T(8,128)(2,1)S(1)} %collective-permute-done.4), channel_id=1, source_target_pairs={{0,24},{2,26},{4,28},{6,30},{8,16},{10,18},{12,20},{14,22},{16,8},... | collective-permute-start | bytes 393224 | tf_op jit(solution)/shard_map/ppermute | solution.py:21
  19.9 5.5 %collective-permute-done.5 = bf16[1,32,16,128]{3,2,1,0:T(8,128)(2,1)S(1)} collective-permute-done((bf16[1,32,16,128]{3,2,1,0:T(8,128)(2,1)S(1)}, bf16[1,32,16,128]{3,2,1,0:T(8,128)(2,1)S(1)}, u32[]{:S(2)}, u32[]{:S(2)}) %collective-permute-start.5) | collective-permute-done | bytes 131104 | tf_op jit(solution)/shard_map/ppermute | solution.py:21
  25.4 0.0 collective-permute-done.6
  25.5 0.1 collective-permute-start.12
  25.7 1.5 %collective-permute-start.11 = (bf16[2,32,16,128]{3,2,1,0:T(8,128)(2,1)S(1)}, bf16[2,32,16,128]{3,2,1,0:T(8,128)(2,1)S(1)}, u32[]{:S(2)}, u32[]{:S(2)}) collective-permute-start(bf16[2,32,16,128]{3,2,1,0:T(8,128)(2,1)S(1)} %pad_maximum_fusion.1), channel_id=1, source_target_pairs={{0,4},{1,3},{2,6},{3,1},{4,0},{5,7},{6,2},{7,5},{8,12},{9,11},{10,... | collective-permute-start | bytes 786440 | tf_op jit(solution)/shard_map/ppermute | solution.py:30
  27.1 1.3 %collective-permute-start.9 = (bf16[1,32,16,128]{3,2,1,0:T(8,128)(2,1)S(1)}, bf16[1,32,16,128]{3,2,1,0:T(8,128)(2,1)S(1)}, u32[]{:S(2)}, u32[]{:S(2)}) collective-permute-start(bf16[1,32,16,128]{3,2,1,0:T(8,128)(2,1)S(1)} %collective-permute-done.4), channel_id=1, source_target_pairs={{0,8},{2,10},{4,12},{6,14},{8,0},{10,2},{12,4},{14,6},{16,24},{18,... | collective-permute-start | bytes 393224 | tf_op jit(solution)/shard_map/ppermute | solution.py:21
  28.5 1.2 %collective-permute-start.10 = (bf16[1,32,16,128]{3,2,1,0:T(8,128)(2,1)S(1)}, bf16[1,32,16,128]{3,2,1,0:T(8,128)(2,1)S(1)}, u32[]{:S(2)}, u32[]{:S(2)}) collective-permute-start(bf16[1,32,16,128]{3,2,1,0:T(8,128)(2,1)S(1)} %collective-permute-done.6), channel_id=1, source_target_pairs={{0,2},{1,5},{2,0},{3,7},{4,6},{5,1},{6,4},{7,3},{8,10},{9,13},{10,... | collective-permute-start | bytes 393224 | tf_op jit(solution)/shard_map/ppermute | solution.py:30
  29.6 3.1 %assemble.1._ = bf16[1024,16,128]{2,1,0:T(8,128)(2,1)S(1)} custom-call(bf16[384,16,128]{2,1,0:T(8,128)(2,1)S(1)} %bitcast.10, bf16[384,16,128]{2,1,0:T(8,128)(2,1)S(1)} %bitcast.11), custom_call_target="tpu_custom_call" | custom-call | tf_op jit(solution)/shard_map/assemble/pallas_call | solution.py:335
  32.7 0.7 %collective-permute-done.10 = bf16[1,32,16,128]{3,2,1,0:T(8,128)(2,1)S(1)} collective-permute-done((bf16[1,32,16,128]{3,2,1,0:T(8,128)(2,1)S(1)}, bf16[1,32,16,128]{3,2,1,0:T(8,128)(2,1)S(1)}, u32[]{:S(2)}, u32[]{:S(2)}) %collective-permute-start.10) | collective-permute-done | bytes 131104 | tf_op jit(solution)/shard_map/ppermute | solution.py:30
  33.5 0.2 collective-permute-start.13
  33.7 1.8 %collective-permute-done.13 = bf16[4,32,16,128]{3,2,1,0:T(8,128)(2,1)S(1)} collective-permute-done((bf16[4,32,16,128]{3,2,1,0:T(8,128)(2,1)S(1)}, bf16[4,32,16,128]{3,2,1,0:T(8,128)(2,1)S(1)}, u32[]{:S(2)}, u32[]{:S(2)}) %collective-permute-start.13) | collective-permute-done | bytes 524320 | tf_op jit(solution)/shard_map/ppermute | solution.py:21
  35.5 9.5 %apply.1 = (bf16[32,4096]{1,0:T(8,128)(2,1)S(1)}, f32[16,128]{1,0:T(8,128)S(1)}, bf16[1024,16,128]{2,1,0:T(8,128)(2,1)S(1)}) custom-call(s32[64,8]{1,0:T(8,128)S(1)} %get-tuple-element.46.rows_ref, bf16[64,8,64,128]{3,2,1,0:T(8,128)(2,1)S(1)} %get-tuple-element.47.ham_ref, bf16[1024,16,128]{2,1,0:T(8,128)(2,1)S(1)} %assemble.1._, ...), custom_call_target="tpu_custom_call", output_to_operand_aliasing={{2}: (2, {})} | custom-call | tf_op jit(solution)/shard_map/apply/pallas_call | solution.py:346
  45.0 0.2 collective-permute-start.14
  45.1 1.0 %collective-permute-done.14 = f32[16,128]{1,0:T(8,128)S(1)} collective-permute-done((f32[16,128]{1,0:T(8,128)S(1)}, f32[16,128]{1,0:T(8,128)S(1)}, u32[]{:S(2)}, u32[]{:S(2)}) %collective-permute-start.14) | collective-permute-done | bytes 8224 | tf_op jit(solution)/shard_map/ppermute | solution.py:21
  46.2 12.8 %all_to_all.5.sums_ref = f32[16,16,128]{2,1,0:T(8,128)S(1)} all-to-all(f32[16,16,128]{2,1,0:T(8,128)S(1)} %broadcast_in_dim.7), channel_id=1, replica_groups=mesh['chan'=16,'rad'=2] {'chan'}, dimensions={0} | all-to-all | bytes 262144 | tf_op jit(solution)/shard_map/all_to_all | solution.py:262
  59.0 3.1 %finish.1 = (f32[64,16,64]{2,1,0:T(8,128)}, f32[1,16]{1,0:T(1,128)}) custom-call(f32[16,16,128]{2,1,0:T(8,128)S(1)} %all_to_all.5.sums_ref, bf16[32,4096]{1,0:T(8,128)(2,1)S(1)} %get-tuple-element.57.az_ref, bf16[64,4096]{1,0:T(8,128)(2,1)S(1)} %get-tuple-element.49.zhm_ref), custom_call_target="tpu_custom_call" | custom-call | tf_op jit(solution)/shard_map/finish/pallas_call | solution.py:361
  (23 shorter events, 0.4 us)
Async XLA Ops:
  1.9 12.8 %collective-permute-start.4 = (bf16[1,32,16,128]{3,2,1,0:T(8,128)(2,1)S(1)}, bf16[1,32,16,128]{3,2,1,0:T(8,128)(2,1)S(1)}, u32[]{:S(2)}, u32[]{:S(2)}) collective-permute-start(bf16[1,32,16,128]{3,2,1,0:T(8,128)(2,1)S(1)} %get-tuple-element.61), channel_id=1, source_target_pairs={{0,6},{2,4},{4,2},{6,0},{8,14},{10,12},{12,10},{14,8},{16,22},{18,... | collective-permute-start | bytes 393224 | tf_op jit(solution)/shard_map/ppermute | solution.py:21
  5.8 8.9 %collective-permute-start.3 = (bf16[1,32,16,128]{3,2,1,0:T(8,128)(2,1)S(1)}, bf16[1,32,16,128]{3,2,1,0:T(8,128)(2,1)S(1)}, u32[]{:S(2)}, u32[]{:S(2)}) collective-permute-start(bf16[1,32,16,128]{3,2,1,0:T(8,128)(2,1)S(1)} %get-tuple-element.61), channel_id=1, source_target_pairs={{0,16},{2,18},{4,20},{6,22},{8,24},{10,26},{12,28},{14,30},{16,0},... | collective-permute-start | bytes 393224 | tf_op jit(solution)/shard_map/ppermute | solution.py:21
  8.4 6.4 %collective-permute-start.2 = (bf16[1,32,16,128]{3,2,1,0:T(8,128)(2,1)S(1)}, bf16[1,32,16,128]{3,2,1,0:T(8,128)(2,1)S(1)}, u32[]{:S(2)}, u32[]{:S(2)}) collective-permute-start(bf16[1,32,16,128]{3,2,1,0:T(8,128)(2,1)S(1)} %get-tuple-element.61), channel_id=1, source_target_pairs={{0,8},{2,10},{4,12},{6,14},{8,0},{10,2},{12,4},{14,6},{16,24},{18,... | collective-permute-start | bytes 393224 | tf_op jit(solution)/shard_map/ppermute | solution.py:21
  10.0 5.0 %collective-permute-start.1 = (bf16[1,32,16,128]{3,2,1,0:T(8,128)(2,1)S(1)}, bf16[1,32,16,128]{3,2,1,0:T(8,128)(2,1)S(1)}, u32[]{:S(2)}, u32[]{:S(2)}) collective-permute-start(bf16[1,32,16,128]{3,2,1,0:T(8,128)(2,1)S(1)} %get-tuple-element.61), channel_id=1, source_target_pairs={{0,2},{1,5},{2,0},{3,7},{4,6},{5,1},{6,4},{7,3},{8,10},{9,13},{10,... | collective-permute-start | bytes 393224 | tf_op jit(solution)/shard_map/ppermute | solution.py:30
  10.5 5.0 %collective-permute-start = (bf16[1,32,16,128]{3,2,1,0:T(8,128)(2,1)S(1)}, bf16[1,32,16,128]{3,2,1,0:T(8,128)(2,1)S(1)}, u32[]{:S(2)}, u32[]{:S(2)}) collective-permute-start(bf16[1,32,16,128]{3,2,1,0:T(8,128)(2,1)S(1)} %get-tuple-element.61), channel_id=1, source_target_pairs={{0,4},{1,3},{2,6},{3,1},{4,0},{5,7},{6,2},{7,5},{8,12},{9,11},{10,... | collective-permute-start | bytes 393224 | tf_op jit(solution)/shard_map/ppermute | solution.py:30
  15.5 9.8 %collective-permute-start.8 = (bf16[2,32,16,128]{3,2,1,0:T(8,128)(2,1)S(1)}, bf16[2,32,16,128]{3,2,1,0:T(8,128)(2,1)S(1)}, u32[]{:S(2)}, u32[]{:S(2)}) collective-permute-start(bf16[2,32,16,128]{3,2,1,0:T(8,128)(2,1)S(1)} %pad_maximum_fusion), channel_id=1, source_target_pairs={{0,2},{1,5},{2,0},{3,7},{4,6},{5,1},{6,4},{7,3},{8,10},{9,13},{10,... | collective-permute-start | bytes 786440 | tf_op jit(solution)/shard_map/ppermute | solution.py:30
  17.1 8.3 %collective-permute-start.7 = (bf16[2,32,16,128]{3,2,1,0:T(8,128)(2,1)S(1)}, bf16[2,32,16,128]{3,2,1,0:T(8,128)(2,1)S(1)}, u32[]{:S(2)}, u32[]{:S(2)}) collective-permute-start(bf16[2,32,16,128]{3,2,1,0:T(8,128)(2,1)S(1)} %pad_maximum_fusion), channel_id=1, source_target_pairs={{0,4},{1,3},{2,6},{3,1},{4,0},{5,7},{6,2},{7,5},{8,12},{9,11},{10,... | collective-permute-start | bytes 786440 | tf_op jit(solution)/shard_map/ppermute | solution.py:30
  17.9 7.5 %collective-permute-start.6 = (bf16[1,32,16,128]{3,2,1,0:T(8,128)(2,1)S(1)}, bf16[1,32,16,128]{3,2,1,0:T(8,128)(2,1)S(1)}, u32[]{:S(2)}, u32[]{:S(2)}) collective-permute-start(bf16[1,32,16,128]{3,2,1,0:T(8,128)(2,1)S(1)} %collective-permute-done.3), channel_id=1, source_target_pairs={{0,8},{2,10},{4,12},{6,14},{8,0},{10,2},{12,4},{14,6},{16,24},{18,... | collective-permute-start | bytes 393224 | tf_op jit(solution)/shard_map/ppermute | solution.py:21
  18.4 6.9 %collective-permute-start.5 = (bf16[1,32,16,128]{3,2,1,0:T(8,128)(2,1)S(1)}, bf16[1,32,16,128]{3,2,1,0:T(8,128)(2,1)S(1)}, u32[]{:S(2)}, u32[]{:S(2)}) collective-permute-start(bf16[1,32,16,128]{3,2,1,0:T(8,128)(2,1)S(1)} %collective-permute-done.4), channel_id=1, source_target_pairs={{0,24},{2,26},{4,28},{6,30},{8,16},{10,18},{12,20},{14,22},{16,8},... | collective-permute-start | bytes 393224 | tf_op jit(solution)/shard_map/ppermute | solution.py:21
  25.5 4.1 %collective-permute-start.12 = (bf16[12,32,16,128]{3,2,1,0:T(8,128)(2,1)S(1)}, bf16[12,32,16,128]{3,2,1,0:T(8,128)(2,1)S(1)}, u32[]{:S(2)}, u32[]{:S(2)}) collective-permute-start(bf16[12,32,16,128]{3,2,1,0:T(8,128)(2,1)S(1)} %constant_dynamic-update-slice_fusion), channel_id=1, source_target_pairs={{0,1},{1,0},{2,3},{3,2},{4,5},{5,4},{6,7},{7,6},{8,9},{9,8},{10,11... | collective-permute-start | bytes 4718600 | tf_op jit(solution)/shard_map/ppermute | solution.py:21
  25.7 7.8 %collective-permute-start.11 = (bf16[2,32,16,128]{3,2,1,0:T(8,128)(2,1)S(1)}, bf16[2,32,16,128]{3,2,1,0:T(8,128)(2,1)S(1)}, u32[]{:S(2)}, u32[]{:S(2)}) collective-permute-start(bf16[2,32,16,128]{3,2,1,0:T(8,128)(2,1)S(1)} %pad_maximum_fusion.1), channel_id=1, source_target_pairs={{0,4},{1,3},{2,6},{3,1},{4,0},{5,7},{6,2},{7,5},{8,12},{9,11},{10,... | collective-permute-start | bytes 786440 | tf_op jit(solution)/shard_map/ppermute | solution.py:30
  27.1 5.6 %collective-permute-start.9 = (bf16[1,32,16,128]{3,2,1,0:T(8,128)(2,1)S(1)}, bf16[1,32,16,128]{3,2,1,0:T(8,128)(2,1)S(1)}, u32[]{:S(2)}, u32[]{:S(2)}) collective-permute-start(bf16[1,32,16,128]{3,2,1,0:T(8,128)(2,1)S(1)} %collective-permute-done.4), channel_id=1, source_target_pairs={{0,8},{2,10},{4,12},{6,14},{8,0},{10,2},{12,4},{14,6},{16,24},{18,... | collective-permute-start | bytes 393224 | tf_op jit(solution)/shard_map/ppermute | solution.py:21
  28.5 5.0 %collective-permute-start.10 = (bf16[1,32,16,128]{3,2,1,0:T(8,128)(2,1)S(1)}, bf16[1,32,16,128]{3,2,1,0:T(8,128)(2,1)S(1)}, u32[]{:S(2)}, u32[]{:S(2)}) collective-permute-start(bf16[1,32,16,128]{3,2,1,0:T(8,128)(2,1)S(1)} %collective-permute-done.6), channel_id=1, source_target_pairs={{0,2},{1,5},{2,0},{3,7},{4,6},{5,1},{6,4},{7,3},{8,10},{9,13},{10,... | collective-permute-start | bytes 393224 | tf_op jit(solution)/shard_map/ppermute | solution.py:30
  33.5 2.0 %collective-permute-start.13 = (bf16[4,32,16,128]{3,2,1,0:T(8,128)(2,1)S(1)}, bf16[4,32,16,128]{3,2,1,0:T(8,128)(2,1)S(1)}, u32[]{:S(2)}, u32[]{:S(2)}) collective-permute-start(bf16[4,32,16,128]{3,2,1,0:T(8,128)(2,1)S(1)} %constant_dynamic-update-slice_fusion.10), channel_id=1, source_target_pairs={{0,1},{1,0},{2,3},{3,2},{4,5},{5,4},{6,7},{7,6},{8,9},{9,8},{10,11... | collective-permute-start | bytes 1572872 | tf_op jit(solution)/shard_map/ppermute | solution.py:21
  45.0 1.2 %collective-permute-start.14 = (f32[16,128]{1,0:T(8,128)S(1)}, f32[16,128]{1,0:T(8,128)S(1)}, u32[]{:S(2)}, u32[]{:S(2)}) collective-permute-start(f32[16,128]{1,0:T(8,128)S(1)} %get-tuple-element.56), channel_id=1, source_target_pairs={{0,1},{1,0},{2,3},{3,2},{4,5},{5,4},{6,7},{7,6},{8,9},{9,8},{10,11... | collective-permute-start | bytes 24584 | tf_op jit(solution)/shard_map/ppermute | solution.py:21

commit v15 on v14

--- a/solution.py
+++ b/solution.py
@@ -33,12 +33,12 @@
 def early_pieces(nz):
     some, odd = [1] + list(range(2, nz, 2)), list(range(3, nz, 2))
     order = [(0, 0)] + [(z, 0) for z in some] + [(0, 1), (0, 2), (0, 3)] + [(z, 1) for z in some]
-    return order + [(z, 0) for z in odd] + [(z, 3) for z in odd] + [(z, 2) for z in some]
+    return order + [(z, 0) for z in odd] + [(z, 2) for z in some]
 
 
 def late_pieces(nz):
     even, odd = list(range(2, nz, 2)), list(range(3, nz, 2))
-    return [(z, 1) for z in odd] + [(z, 2) for z in odd] + [(z, 3) for z in even] + [(1, 3)]
+    return [(z, 1) for z in odd] + [(z, 2) for z in odd] + [(z, 3) for z in even + [1] + odd]
 
 
 def table_piece(z, part, nz):
@@ -51,33 +51,37 @@
         return jnp.where(z == 0, own, jnp.where(is_odd, of_odd + i, of_some + i))
 
     here = pick(0, 1, 2 * some + 4)
-    near = pick(some + 1, some + 4, base + odd + some)
-    far = pick(some + 2, base + odd, base + 2 * odd + some)
-    both = jnp.where(z == 1, 4 * nz - 1, pick(some + 3, base + 3 * odd + some - 1, base))
+    near = pick(some + 1, some + 4, base + some)
+    far = pick(some + 2, base, base + some + odd)
+    last = base + 2 * some + 2 * odd
+    both = jnp.where(z == 1, last - 1, pick(some + 3, last - some - 1, last))
     return jnp.where(part == 0, here, jnp.where(part == 1, near, jnp.where(part == 2, far, both)))
 
 
 def merge(refs, table_ref, order, start, share):
     n_rad = len(refs)
     r = 128 // n_rad
-    me = lax.axis_index("rad")
-
-    def rows(n, carry):
-        for i, (z, part) in enumerate(order):
-            other = order.index((z, (0, 2, 1, 3)[part]))
-            tiles = [ref[(other if s % 2 else i) * share + n] for s, ref in enumerate(refs)]
-            by_core = []
-            for c in range(n_rad):
-                x = tiles[0]
-                for s in range(1, n_rad):
-                    x = jnp.where((me ^ s) == c, tiles[s], x)
-                by_core.append(x)
-            for g in range(n_rad):
-                row = jnp.concatenate([x[:, g * r : (g + 1) * r] for x in by_core], axis=1)
-                table_ref[((start + i) * n_rad + g) * share + n] = row
-        return carry
-
-    lax.fori_loop(0, share, rows, 0)
+    lane = lax.broadcasted_iota(jnp.int32, (1, 128), 1)
+    masks = [jnp.where(lane // r == c, 1.0, 0.0).astype(BF16) for c in range(n_rad)]
+
+    for me in range(n_rad):
+
+        @pl.when(lax.axis_index("rad") == me)
+        def _():
+            def rows(n, carry):
+                for i, (z, part) in enumerate(order):
+                    other = order.index((z, (0, 2, 1, 3)[part]))
+                    tiles = [refs[me ^ c][((other if (me ^ c) % 2 else i) * share) + n] for c in range(n_rad)]
+                    for g in range(n_rad):
+                        row = None
+                        for c, x in enumerate(tiles):
+                            if c != g:
+                                x = pltpu.roll(x, (c - g) % n_rad * r, 1)
+                            row = x * masks[c] if row is None else row + x * masks[c]
+                        table_ref[((start + i) * n_rad + g) * share + n] = row
+                return carry
+
+            lax.fori_loop(0, share, rows, 0)
 
 
 def in_vmem(x):
@@ -156,13 +160,13 @@
 
 
 def apply_kernel(nz, share, rows_ref, ham_ref, _, zhm_ref, zl_ref, dc_ref, gt_ref, *rest):
-    last, (az_ref, sums_ref, table_ref) = rest[:-3], rest[-3:]
+    last, (az_ref, sums_ref, table_ref, a0_ref) = rest[:-4], rest[-4:]
     merge(last, table_ref, late_pieces(nz), len(early_pieces(nz)), share)
     ch, ncoup, r, splines = ham_ref.shape
     k = zl_ref.shape[0] // 2
     group = 256 // r
 
-    def work(g, gram):
+    def work(g, carry):
         left, right = [], []
         for i in range(group):
             p = g * group + i
@@ -177,16 +181,26 @@
             preferred_element_type=F32,
         )
         own = [product[i * k : (i + 1) * k, i * r : (i + 1) * r] for i in range(group)]
-        at = pl.ds(pl.multiple_of(g * 256, 256), 256)
-        a0 = jnp.concatenate(own, axis=1) * SCALE
+        a0_ref[:, pl.ds(pl.multiple_of(g * 256, 256), 256)] = jnp.concatenate(own, axis=1) * SCALE
+        return carry
+
+    lax.fori_loop(0, ch // group, work, 0, unroll=min(8, ch // group))
+
+    lanes = ch * r
+    block = min(lanes, 1024)
+
+    def gram_block(i, gram):
+        at = pl.ds(pl.multiple_of(i * block, block), block)
+        a0 = a0_ref[:, at]
         a1_terms = split3(a0 / dc_ref[:, at])
         az_ref[:, at] = jnp.concatenate(a1_terms[:2], axis=0)
         right = jnp.concatenate(a1_terms + split3(a0), axis=0)
         left = jnp.concatenate([zhm_ref[:, at], zl_ref[:, at], right[: 3 * k]], axis=0)
         return gram + lax.dot_general(left, right, NT, preferred_element_type=F32)
 
-    groups = ch // group
-    gram = lax.fori_loop(0, groups, work, jnp.zeros((9 * k, 6 * k), F32), unroll=min(4, groups))
+    gram = lax.fori_loop(
+        0, lanes // block, gram_block, jnp.zeros((9 * k, 6 * k), F32), unroll=min(2, lanes // block)
+    )
     ta1 = block_sum(gram[: 6 * k, : 3 * k], 2 * k, k)
     ta0 = block_sum(gram[: 6 * k, 3 * k :], 2 * k, k)
     aa = block_sum(gram[6 * k :, : 3 * k], k, k)
@@ -323,13 +337,11 @@
     some, z_even, diag0 = barrier((jnp.concatenate([z1, z_even]), z_even, diag0))
     near1, far1 = near_of(some), far_of(some)
     z_odd = swap(z_even, "chan", 4)
+    z_odd, far1, near1, diag0 = barrier((z_odd, far1, near1, diag0))
+    early = in_cores(
+        jnp.concatenate([own, z1, z_even, near0, far_own, diag0, near1, z_odd, far1])
+    )
     diag_odd = jnp.concatenate([swap(diag0, "chan", 4 * z) for z in range(3, nz, 2)])
-    diag_odd, z_odd, far1, near1, diag0 = barrier(
-        (diag_odd, z_odd, far1, near1, diag0)
-    )
-    early = in_cores(
-        jnp.concatenate([own, z1, z_even, near0, far_own, diag0, near1, z_odd, diag_odd, far1])
-    )
     near_odd, diag1 = near_of(z_odd), swap(diag0, "chan", 4)
     far2 = far_of(jnp.concatenate([z_odd, near1[1:]]))
     table = pl.pallas_call(
@@ -340,8 +352,8 @@
         compiler_params=pltpu.CompilerParams(vmem_limit_bytes=VMEM_LIMIT),
         name="assemble",
     )(*[in_vmem(flat(x)) for x in early])
-    diag1, near_odd, far2, table, rows = barrier((diag1, near_odd, far2, table, rows))
-    last = [in_vmem(flat(x)) for x in in_cores(jnp.concatenate([near_odd, far2, diag1]))]
+    diag1, near_odd, diag_odd, far2, table = barrier((diag1, near_odd, diag_odd, far2, table))
+    last = [in_vmem(flat(x)) for x in in_cores(jnp.concatenate([near_odd, far2, diag1, diag_odd]))]
 
     az, sums, _ = pl.pallas_call(
         functools.partial(apply_kernel, nz, share),
@@ -353,6 +365,7 @@
             pltpu.VMEM(table.shape, BF16),
         ],
         input_output_aliases={2: 2},
+        scratch_shapes=[pltpu.VMEM((k, lanes), F32)],
         compiler_params=pltpu.CompilerParams(vmem_limit_bytes=VMEM_LIMIT),
         name="apply",
     )(rows, in_vmem(ham), in_vmem(table), in_vmem(zhm), in_vmem(zl), in_vmem(dc), gram_t, *last)

time: 62.3 us -> 60.5 us (0.971)
  waiting for transfers between devices: 9.78 us -> 12.4 us
  Pallas kernels: 19.3 us -> 17 us
  blocking collectives: 12.8 us -> 11.5 us
  starting transfers between devices: 17.8 us -> 16.9 us
    ppermute x9, waiting for transfers between devices: 8.39 us -> 11 us  [swap(): return lax.ppermute(x, axis, [(i, i ^ distance) for i in range(n)])]
    pallas_call x1, Pallas kernels: 9.49 us -> 7.28 us  [body(): pl.pallas_call(functools.partial(apply_kernel, nz, share), in_specs=[smem...]
    ppermute x6, starting transfers between devices: 6.01 us -> 4.64 us  [plane_swap(): return lax.ppermute(x, ('chan', 'rad'), pairs)]
    all_to_all x1, blocking collectives: 12.8 us -> 11.5 us  [gather_sums(): lax.all_to_all(every, 'chan', split_axis=0, concat_axis=0, tiled=True)]
  transfers between devices with their start and end apart: 15 -> 15, of which waited for: 7 -> 9; matrix products, arithmetic and copies ran while one was open for 0% -> 0% of each run, Pallas kernels for 11% -> 11%
where the time goes in v15:
time: 60.5 us; the launch traced here: 60.2 us
  Pallas kernels  17 us (28%)
  starting transfers between devices  16.9 us (28%)
  waiting for transfers between devices  12.4 us (20%)
  blocking collectives  11.5 us (19%)
  other arithmetic  1.25 us (2%)
  between operations  0.8 us (1%)
    ppermute x9, starting transfers between devices, swap(): return lax.ppermute(x, axis, [(i, i ^ distance) for i in range(n)])  12.3 us
    all_to_all x1, blocking collectives, gather_sums(): lax.all_to_all(every, 'chan', split_axis=0, concat_axis=0, tiled=True)  11.5 us
    ppermute x9, waiting for transfers between devices, swap(): return lax.ppermute(x, axis, [(i, i ^ distance) for i in range(n)])  11 us
    pallas_call x1, Pallas kernels, body(): pl.pallas_call(functools.partial(apply_kernel, nz, share), in_specs=[smem...  7.28 us
    ppermute x6, starting transfers between devices, plane_swap(): return lax.ppermute(x, ('chan', 'rad'), pairs)  4.64 us
    pallas_call x1, Pallas kernels, body(): pl.pallas_call(functools.partial(prepare_kernel, n_chan, n_rad), in_specs...  3.66 us
    pallas_call x1, Pallas kernels, body(): pl.pallas_call(functools.partial(finish_kernel, total), out_shape=[jax.Sh...  3.06 us
    pallas_call x1, Pallas kernels, body(): pl.pallas_call(functools.partial(assemble_kernel, nz, share), in_specs=[w...  3.02 us
  transfers between devices with their start and end apart: 15, of which 9 were waited for; matrix products, arithmetic and copies ran while one was open for 0% of the time, Pallas kernels for 11%

profile of v15, /device:TPU:0, one launch (start us, length us, event | category | flops | bytes accessed | tf_op | source)
XLA Modules:
  0.0 60.2 jit_solution(11433599999427409656)
XLA Ops:
  0.6 1.1 %convert_element_type.3 = bf16[64,16,64]{2,1,0:T(8,128)(2,1)S(1)} convert(f32[64,16,64]{2,1,0:T(8,128)} %t_hbm.1) | non-fusion elementwise | flops 65536 | bytes 393216 | tf_op jit(solution)/shard_map/convert_element_type | solution.py:304
  1.7 0.1 constant_dynamic-update-slice_fusion.8
  1.9 4.0 %collective-permute-start.4 = (bf16[1,32,16,128]{3,2,1,0:T(8,128)(2,1)S(1)}, bf16[1,32,16,128]{3,2,1,0:T(8,128)(2,1)S(1)}, u32[]{:S(2)}, u32[]{:S(2)}) collective-permute-start(bf16[1,32,16,128]{3,2,1,0:T(8,128)(2,1)S(1)} %get-tuple-element.59), channel_id=1, source_target_pairs={{0,6},{2,4},{4,2},{6,0},{8,14},{10,12},{12,10},{14,8},{16,22},{18,... | collective-permute-start | bytes 393224 | tf_op jit(solution)/shard_map/ppermute | solution.py:21
  5.8 2.6 %collective-permute-start.3 = (bf16[1,32,16,128]{3,2,1,0:T(8,128)(2,1)S(1)}, bf16[1,32,16,128]{3,2,1,0:T(8,128)(2,1)S(1)}, u32[]{:S(2)}, u32[]{:S(2)}) collective-permute-start(bf16[1,32,16,128]{3,2,1,0:T(8,128)(2,1)S(1)} %get-tuple-element.59), channel_id=1, source_target_pairs={{0,16},{2,18},{4,20},{6,22},{8,24},{10,26},{12,28},{14,30},{16,0},... | collective-permute-start | bytes 393224 | tf_op jit(solution)/shard_map/ppermute | solution.py:21
  8.4 1.6 %collective-permute-start.2 = (bf16[1,32,16,128]{3,2,1,0:T(8,128)(2,1)S(1)}, bf16[1,32,16,128]{3,2,1,0:T(8,128)(2,1)S(1)}, u32[]{:S(2)}, u32[]{:S(2)}) collective-permute-start(bf16[1,32,16,128]{3,2,1,0:T(8,128)(2,1)S(1)} %get-tuple-element.59), channel_id=1, source_target_pairs={{0,8},{2,10},{4,12},{6,14},{8,0},{10,2},{12,4},{14,6},{16,24},{18,... | collective-permute-start | bytes 393224 | tf_op jit(solution)/shard_map/ppermute | solution.py:21
  10.0 0.5 collective-permute-start.1
  10.5 0.5 collective-permute-start
  11.0 3.7 %prepare.1 = (s32[64,8]{1,0:T(8,128)S(1)}, bf16[64,8,64,128]{3,2,1,0:T(8,128)(2,1)S(1)}, bf16[64,4096]{1,0:T(8,128)(2,1)S(1)}, bf16[32,4096]{1,0:T(8,128)(2,1)S(...) custom-call(f32[64,16,64]{2,1,0:T(8,128)} %t_hbm.1, f32[64,64]{1,0:T(8,128)} %d_hbm.1, s32[8,64]{1,0:T(8,128)} %bitcast.14, ...), custom_call_target="tpu_custom_call" | custom-call | tf_op jit(solution)/shard_map/prepare/pallas_call | solution.py:308
  14.7 0.0 collective-permute-done.4
  14.7 0.0 collective-permute-done.3
  14.7 0.1 collective-permute-done.2
  14.8 0.2 collective-permute-done.1
  14.9 0.5 collective-permute-done
  15.5 1.6 %collective-permute-start.7 = (bf16[2,32,16,128]{3,2,1,0:T(8,128)(2,1)S(1)}, bf16[2,32,16,128]{3,2,1,0:T(8,128)(2,1)S(1)}, u32[]{:S(2)}, u32[]{:S(2)}) collective-permute-start(bf16[2,32,16,128]{3,2,1,0:T(8,128)(2,1)S(1)} %pad_maximum_fusion), channel_id=1, source_target_pairs={{0,2},{1,5},{2,0},{3,7},{4,6},{5,1},{6,4},{7,3},{8,10},{9,13},{10,... | collective-permute-start | bytes 786440 | tf_op jit(solution)/shard_map/ppermute | solution.py:30
  17.1 0.8 %collective-permute-start.6 = (bf16[2,32,16,128]{3,2,1,0:T(8,128)(2,1)S(1)}, bf16[2,32,16,128]{3,2,1,0:T(8,128)(2,1)S(1)}, u32[]{:S(2)}, u32[]{:S(2)}) collective-permute-start(bf16[2,32,16,128]{3,2,1,0:T(8,128)(2,1)S(1)} %pad_maximum_fusion), channel_id=1, source_target_pairs={{0,4},{1,3},{2,6},{3,1},{4,0},{5,7},{6,2},{7,5},{8,12},{9,11},{10,... | collective-permute-start | bytes 786440 | tf_op jit(solution)/shard_map/ppermute | solution.py:30
  17.9 0.5 collective-permute-start.5
  18.5 4.4 %collective-permute-done.5 = bf16[1,32,16,128]{3,2,1,0:T(8,128)(2,1)S(1)} collective-permute-done((bf16[1,32,16,128]{3,2,1,0:T(8,128)(2,1)S(1)}, bf16[1,32,16,128]{3,2,1,0:T(8,128)(2,1)S(1)}, u32[]{:S(2)}, u32[]{:S(2)}) %collective-permute-start.5) | collective-permute-done | bytes 131104 | tf_op jit(solution)/shard_map/ppermute | solution.py:21
  22.9 0.7 %collective-permute-done.7 = bf16[2,32,16,128]{3,2,1,0:T(8,128)(2,1)S(1)} collective-permute-done((bf16[2,32,16,128]{3,2,1,0:T(8,128)(2,1)S(1)}, bf16[2,32,16,128]{3,2,1,0:T(8,128)(2,1)S(1)}, u32[]{:S(2)}, u32[]{:S(2)}) %collective-permute-start.7) | collective-permute-done | bytes 262176 | tf_op jit(solution)/shard_map/ppermute | solution.py:30
  23.7 0.1 collective-permute-start.12
  23.8 0.7 %collective-permute-start.11 = (bf16[2,32,16,128]{3,2,1,0:T(8,128)(2,1)S(1)}, bf16[2,32,16,128]{3,2,1,0:T(8,128)(2,1)S(1)}, u32[]{:S(2)}, u32[]{:S(2)}) collective-permute-start(bf16[2,32,16,128]{3,2,1,0:T(8,128)(2,1)S(1)} %pad_maximum_fusion.1), channel_id=1, source_target_pairs={{0,4},{1,3},{2,6},{3,1},{4,0},{5,7},{6,2},{7,5},{8,12},{9,11},{10,... | collective-permute-start | bytes 786440 | tf_op jit(solution)/shard_map/ppermute | solution.py:30
  24.6 3.3 %collective-permute-start.10 = (bf16[1,32,16,128]{3,2,1,0:T(8,128)(2,1)S(1)}, bf16[1,32,16,128]{3,2,1,0:T(8,128)(2,1)S(1)}, u32[]{:S(2)}, u32[]{:S(2)}) collective-permute-start(bf16[1,32,16,128]{3,2,1,0:T(8,128)(2,1)S(1)} %collective-permute-done.4), channel_id=1, source_target_pairs={{0,24},{2,26},{4,28},{6,30},{8,16},{10,18},{12,20},{14,22},{16,8},... | collective-permute-start | bytes 393224 | tf_op jit(solution)/shard_map/ppermute | solution.py:21
  27.9 0.5 collective-permute-start.9
  28.5 3.0 %assemble.1._ = bf16[1024,16,128]{2,1,0:T(8,128)(2,1)S(1)} custom-call(bf16[352,16,128]{2,1,0:T(8,128)(2,1)S(1)} %bitcast.10, bf16[352,16,128]{2,1,0:T(8,128)(2,1)S(1)} %bitcast.11), custom_call_target="tpu_custom_call" | custom-call | tf_op jit(solution)/shard_map/assemble/pallas_call | solution.py:347
  31.5 1.3 %collective-permute-done.10 = bf16[1,32,16,128]{3,2,1,0:T(8,128)(2,1)S(1)} collective-permute-done((bf16[1,32,16,128]{3,2,1,0:T(8,128)(2,1)S(1)}, bf16[1,32,16,128]{3,2,1,0:T(8,128)(2,1)S(1)}, u32[]{:S(2)}, u32[]{:S(2)}) %collective-permute-start.10) | collective-permute-done | bytes 131104 | tf_op jit(solution)/shard_map/ppermute | solution.py:21
  32.7 2.1 %collective-permute-done.8 = bf16[1,32,16,128]{3,2,1,0:T(8,128)(2,1)S(1)} collective-permute-done((bf16[1,32,16,128]{3,2,1,0:T(8,128)(2,1)S(1)}, bf16[1,32,16,128]{3,2,1,0:T(8,128)(2,1)S(1)}, u32[]{:S(2)}, u32[]{:S(2)}) %collective-permute-start.8) | collective-permute-done | bytes 131104 | tf_op jit(solution)/shard_map/ppermute | solution.py:21
  35.0 0.1 collective-permute-start.13
  35.1 2.1 %collective-permute-done.13 = bf16[5,32,16,128]{3,2,1,0:T(8,128)(2,1)S(1)} collective-permute-done((bf16[5,32,16,128]{3,2,1,0:T(8,128)(2,1)S(1)}, bf16[5,32,16,128]{3,2,1,0:T(8,128)(2,1)S(1)}, u32[]{:S(2)}, u32[]{:S(2)}) %collective-permute-start.13) | collective-permute-done | bytes 655392 | tf_op jit(solution)/shard_map/ppermute | solution.py:21
  37.2 7.3 %apply.1 = (bf16[32,4096]{1,0:T(8,128)(2,1)S(1)}, f32[16,128]{1,0:T(8,128)S(1)}, bf16[1024,16,128]{2,1,0:T(8,128)(2,1)S(1)}) custom-call(s32[64,8]{1,0:T(8,128)S(1)} %get-tuple-element.31.rows_ref, bf16[64,8,64,128]{3,2,1,0:T(8,128)(2,1)S(1)} %get-tuple-element.32.ham_ref, bf16[1024,16,128]{2,1,0:T(8,128)(2,1)S(1)} %assemble.1._, ...), custom_call_target="tpu_custom_call", output_to_operand_aliasing={{2}: (2, {})} | custom-call | tf_op jit(solution)/shard_map/apply/pallas_call | solution.py:358
  44.4 0.2 collective-permute-start.14
  44.6 1.0 %collective-permute-done.14 = f32[16,128]{1,0:T(8,128)S(1)} collective-permute-done((f32[16,128]{1,0:T(8,128)S(1)}, f32[16,128]{1,0:T(8,128)S(1)}, u32[]{:S(2)}, u32[]{:S(2)}) %collective-permute-start.14) | collective-permute-done | bytes 8224 | tf_op jit(solution)/shard_map/ppermute | solution.py:21
  45.7 11.5 %all_to_all.5.sums_ref = f32[16,16,128]{2,1,0:T(8,128)S(1)} all-to-all(f32[16,16,128]{2,1,0:T(8,128)S(1)} %broadcast_in_dim.7), channel_id=1, replica_groups=mesh['chan'=16,'rad'=2] {'chan'}, dimensions={0} | all-to-all | bytes 262144 | tf_op jit(solution)/shard_map/all_to_all | solution.py:276
  57.2 3.1 %finish.1 = (f32[64,16,64]{2,1,0:T(8,128)}, f32[1,16]{1,0:T(1,128)}) custom-call(f32[16,16,128]{2,1,0:T(8,128)S(1)} %all_to_all.5.sums_ref, bf16[32,4096]{1,0:T(8,128)(2,1)S(1)} %get-tuple-element.55.az_ref, bf16[64,4096]{1,0:T(8,128)(2,1)S(1)} %get-tuple-element.46.zhm_ref), custom_call_target="tpu_custom_call" | custom-call | tf_op jit(solution)/shard_map/finish/pallas_call | solution.py:374
  (23 shorter events, 0.4 us)
Async XLA Ops:
  1.9 12.8 %collective-permute-start.4 = (bf16[1,32,16,128]{3,2,1,0:T(8,128)(2,1)S(1)}, bf16[1,32,16,128]{3,2,1,0:T(8,128)(2,1)S(1)}, u32[]{:S(2)}, u32[]{:S(2)}) collective-permute-start(bf16[1,32,16,128]{3,2,1,0:T(8,128)(2,1)S(1)} %get-tuple-element.59), channel_id=1, source_target_pairs={{0,6},{2,4},{4,2},{6,0},{8,14},{10,12},{12,10},{14,8},{16,22},{18,... | collective-permute-start | bytes 393224 | tf_op jit(solution)/shard_map/ppermute | solution.py:21
  5.8 8.9 %collective-permute-start.3 = (bf16[1,32,16,128]{3,2,1,0:T(8,128)(2,1)S(1)}, bf16[1,32,16,128]{3,2,1,0:T(8,128)(2,1)S(1)}, u32[]{:S(2)}, u32[]{:S(2)}) collective-permute-start(bf16[1,32,16,128]{3,2,1,0:T(8,128)(2,1)S(1)} %get-tuple-element.59), channel_id=1, source_target_pairs={{0,16},{2,18},{4,20},{6,22},{8,24},{10,26},{12,28},{14,30},{16,0},... | collective-permute-start | bytes 393224 | tf_op jit(solution)/shard_map/ppermute | solution.py:21
  8.4 6.4 %collective-permute-start.2 = (bf16[1,32,16,128]{3,2,1,0:T(8,128)(2,1)S(1)}, bf16[1,32,16,128]{3,2,1,0:T(8,128)(2,1)S(1)}, u32[]{:S(2)}, u32[]{:S(2)}) collective-permute-start(bf16[1,32,16,128]{3,2,1,0:T(8,128)(2,1)S(1)} %get-tuple-element.59), channel_id=1, source_target_pairs={{0,8},{2,10},{4,12},{6,14},{8,0},{10,2},{12,4},{14,6},{16,24},{18,... | collective-permute-start | bytes 393224 | tf_op jit(solution)/shard_map/ppermute | solution.py:21
  10.0 5.0 %collective-permute-start.1 = (bf16[1,32,16,128]{3,2,1,0:T(8,128)(2,1)S(1)}, bf16[1,32,16,128]{3,2,1,0:T(8,128)(2,1)S(1)}, u32[]{:S(2)}, u32[]{:S(2)}) collective-permute-start(bf16[1,32,16,128]{3,2,1,0:T(8,128)(2,1)S(1)} %get-tuple-element.59), channel_id=1, source_target_pairs={{0,2},{1,5},{2,0},{3,7},{4,6},{5,1},{6,4},{7,3},{8,10},{9,13},{10,... | collective-permute-start | bytes 393224 | tf_op jit(solution)/shard_map/ppermute | solution.py:30
  10.5 5.0 %collective-permute-start = (bf16[1,32,16,128]{3,2,1,0:T(8,128)(2,1)S(1)}, bf16[1,32,16,128]{3,2,1,0:T(8,128)(2,1)S(1)}, u32[]{:S(2)}, u32[]{:S(2)}) collective-permute-start(bf16[1,32,16,128]{3,2,1,0:T(8,128)(2,1)S(1)} %get-tuple-element.59), channel_id=1, source_target_pairs={{0,4},{1,3},{2,6},{3,1},{4,0},{5,7},{6,2},{7,5},{8,12},{9,11},{10,... | collective-permute-start | bytes 393224 | tf_op jit(solution)/shard_map/ppermute | solution.py:30
  15.5 8.0 %collective-permute-start.7 = (bf16[2,32,16,128]{3,2,1,0:T(8,128)(2,1)S(1)}, bf16[2,32,16,128]{3,2,1,0:T(8,128)(2,1)S(1)}, u32[]{:S(2)}, u32[]{:S(2)}) collective-permute-start(bf16[2,32,16,128]{3,2,1,0:T(8,128)(2,1)S(1)} %pad_maximum_fusion), channel_id=1, source_target_pairs={{0,2},{1,5},{2,0},{3,7},{4,6},{5,1},{6,4},{7,3},{8,10},{9,13},{10,... | collective-permute-start | bytes 786440 | tf_op jit(solution)/shard_map/ppermute | solution.py:30
  17.1 6.5 %collective-permute-start.6 = (bf16[2,32,16,128]{3,2,1,0:T(8,128)(2,1)S(1)}, bf16[2,32,16,128]{3,2,1,0:T(8,128)(2,1)S(1)}, u32[]{:S(2)}, u32[]{:S(2)}) collective-permute-start(bf16[2,32,16,128]{3,2,1,0:T(8,128)(2,1)S(1)} %pad_maximum_fusion), channel_id=1, source_target_pairs={{0,4},{1,3},{2,6},{3,1},{4,0},{5,7},{6,2},{7,5},{8,12},{9,11},{10,... | collective-permute-start | bytes 786440 | tf_op jit(solution)/shard_map/ppermute | solution.py:30
  17.9 5.0 %collective-permute-start.5 = (bf16[1,32,16,128]{3,2,1,0:T(8,128)(2,1)S(1)}, bf16[1,32,16,128]{3,2,1,0:T(8,128)(2,1)S(1)}, u32[]{:S(2)}, u32[]{:S(2)}) collective-permute-start(bf16[1,32,16,128]{3,2,1,0:T(8,128)(2,1)S(1)} %collective-permute-done.3), channel_id=1, source_target_pairs={{0,8},{2,10},{4,12},{6,14},{8,0},{10,2},{12,4},{14,6},{16,24},{18,... | collective-permute-start | bytes 393224 | tf_op jit(solution)/shard_map/ppermute | solution.py:21
  23.7 4.7 %collective-permute-start.12 = (bf16[11,32,16,128]{3,2,1,0:T(8,128)(2,1)S(1)}, bf16[11,32,16,128]{3,2,1,0:T(8,128)(2,1)S(1)}, u32[]{:S(2)}, u32[]{:S(2)}) collective-permute-start(bf16[11,32,16,128]{3,2,1,0:T(8,128)(2,1)S(1)} %constant_dynamic-update-slice_fusion), channel_id=1, source_target_pairs={{0,1},{1,0},{2,3},{3,2},{4,5},{5,4},{6,7},{7,6},{8,9},{9,8},{10,11... | collective-permute-start | bytes 4325384 | tf_op jit(solution)/shard_map/ppermute | solution.py:21
  23.8 11.1 %collective-permute-start.11 = (bf16[2,32,16,128]{3,2,1,0:T(8,128)(2,1)S(1)}, bf16[2,32,16,128]{3,2,1,0:T(8,128)(2,1)S(1)}, u32[]{:S(2)}, u32[]{:S(2)}) collective-permute-start(bf16[2,32,16,128]{3,2,1,0:T(8,128)(2,1)S(1)} %pad_maximum_fusion.1), channel_id=1, source_target_pairs={{0,4},{1,3},{2,6},{3,1},{4,0},{5,7},{6,2},{7,5},{8,12},{9,11},{10,... | collective-permute-start | bytes 786440 | tf_op jit(solution)/shard_map/ppermute | solution.py:30
  24.6 8.2 %collective-permute-start.10 = (bf16[1,32,16,128]{3,2,1,0:T(8,128)(2,1)S(1)}, bf16[1,32,16,128]{3,2,1,0:T(8,128)(2,1)S(1)}, u32[]{:S(2)}, u32[]{:S(2)}) collective-permute-start(bf16[1,32,16,128]{3,2,1,0:T(8,128)(2,1)S(1)} %collective-permute-done.4), channel_id=1, source_target_pairs={{0,24},{2,26},{4,28},{6,30},{8,16},{10,18},{12,20},{14,22},{16,8},... | collective-permute-start | bytes 393224 | tf_op jit(solution)/shard_map/ppermute | solution.py:21
  27.9 7.0 %collective-permute-start.8 = (bf16[1,32,16,128]{3,2,1,0:T(8,128)(2,1)S(1)}, bf16[1,32,16,128]{3,2,1,0:T(8,128)(2,1)S(1)}, u32[]{:S(2)}, u32[]{:S(2)}) collective-permute-start(bf16[1,32,16,128]{3,2,1,0:T(8,128)(2,1)S(1)} %collective-permute-done.4), channel_id=1, source_target_pairs={{0,8},{2,10},{4,12},{6,14},{8,0},{10,2},{12,4},{14,6},{16,24},{18,... | collective-permute-start | bytes 393224 | tf_op jit(solution)/shard_map/ppermute | solution.py:21
  27.9 7.0 %collective-permute-start.9 = (bf16[1,32,16,128]{3,2,1,0:T(8,128)(2,1)S(1)}, bf16[1,32,16,128]{3,2,1,0:T(8,128)(2,1)S(1)}, u32[]{:S(2)}, u32[]{:S(2)}) collective-permute-start(bf16[1,32,16,128]{3,2,1,0:T(8,128)(2,1)S(1)} %collective-permute-done.5), channel_id=1, source_target_pairs={{0,2},{1,5},{2,0},{3,7},{4,6},{5,1},{6,4},{7,3},{8,10},{9,13},{10,... | collective-permute-start | bytes 393224 | tf_op jit(solution)/shard_map/ppermute | solution.py:30
  35.0 2.2 %collective-permute-start.13 = (bf16[5,32,16,128]{3,2,1,0:T(8,128)(2,1)S(1)}, bf16[5,32,16,128]{3,2,1,0:T(8,128)(2,1)S(1)}, u32[]{:S(2)}, u32[]{:S(2)}) collective-permute-start(bf16[5,32,16,128]{3,2,1,0:T(8,128)(2,1)S(1)} %constant_dynamic-update-slice_fusion.9), channel_id=1, source_target_pairs={{0,1},{1,0},{2,3},{3,2},{4,5},{5,4},{6,7},{7,6},{8,9},{9,8},{10,11... | collective-permute-start | bytes 1966088 | tf_op jit(solution)/shard_map/ppermute | solution.py:21
  44.4 1.2 %collective-permute-start.14 = (f32[16,128]{1,0:T(8,128)S(1)}, f32[16,128]{1,0:T(8,128)S(1)}, u32[]{:S(2)}, u32[]{:S(2)}) collective-permute-start(f32[16,128]{1,0:T(8,128)S(1)} %get-tuple-element.54), channel_id=1, source_target_pairs={{0,1},{1,0},{2,3},{3,2},{4,5},{5,4},{6,7},{7,6},{8,9},{9,8},{10,11... | collective-permute-start | bytes 24584 | tf_op jit(solution)/shard_map/ppermute | solution.py:21

commit v16 on v13

--- a/solution.py
+++ b/solution.py
@@ -40,9 +40,9 @@
         return jnp.where(z == 0, own, jnp.where(is_odd, of_odd + i, of_some + i))
 
     here = pick(0, 1, 2 * some + 4)
-    near = pick(some + 1, some + 4, base + odd + some)
-    far = pick(some + 2, base + odd, base + 2 * odd + some)
-    both = jnp.where(z == 1, 4 * nz - 1, pick(some + 3, base + 3 * odd + some - 1, base))
+    near = pick(some + 1, some + 4, base + some)
+    far = pick(some + 2, base, base + some + odd)
+    both = pick(some + 3, base + some + 2 * odd, base + 2 * some + 2 * odd)
     return jnp.where(part == 0, here, jnp.where(part == 1, near, jnp.where(part == 2, far, both)))
 
 
@@ -114,7 +114,7 @@
         for c in range(place.shape[0]):
             found = found + jnp.where(wanted == 128 * c, place[c : c + 1], 0.0)
         columns.append(jnp.sum(found, axis=1, keepdims=True))
-    rows_ref[...] = jnp.concatenate(columns, axis=1).astype(jnp.int32)
+    rows_ref[...] = jnp.concatenate(columns, axis=1).T.astype(jnp.int32)
     copies[4].wait()
 
 
@@ -150,7 +150,7 @@
         for i in range(group):
             p = g * group + i
             left.append(
-                jnp.concatenate([table_ref[rows_ref[p, j]] for j in range(ncoup)], axis=1)
+                jnp.concatenate([table_ref[rows_ref[j, p]] for j in range(ncoup)], axis=1)
             )
             right.append(jnp.concatenate([ham_ref[p, j] for j in range(ncoup)], axis=1))
         product = lax.dot_general(
@@ -300,27 +300,12 @@
     near0, far_own, diag0 = near_of(own), far_of(own), swap(own, "chan", 3)
     z1 = swap(own, "chan", 4)
     z_even = jnp.concatenate([swap(own, "chan", 4 * z) for z in range(2, nz, 2)])
-    z1, far_own, near0, diag0, z_even = barrier((z1, far_own, near0, diag0, z_even))
-    some, z_even, diag0 = barrier((jnp.concatenate([z1, z_even]), z_even, diag0))
-    near1, far1 = near_of(some), far_of(some)
-    z_odd = swap(z_even, "chan", 4)
-    diag_odd = jnp.concatenate([swap(diag0, "chan", 4 * z) for z in range(3, nz, 2)])
-    inputs = (trial_block, precond_diag, partners, stored_at, ham_blocks)
-    diag_odd, z_odd, far1, near1, diag0, inputs = barrier(
-        (diag_odd, z_odd, far1, near1, diag0, inputs)
-    )
-    trial_block, precond_diag, partners, stored_at, ham_blocks = inputs
-    early = in_cores(
-        jnp.concatenate([own, z1, z_even, near0, far_own, diag0, near1, z_odd, diag_odd, far1])
-    )
-    near_odd, diag1 = near_of(z_odd), swap(diag0, "chan", 4)
-    far2 = far_of(jnp.concatenate([z_odd, near1[1:]]))
     rows, ham, zhm, zl, dc, gram_t = pl.pallas_call(
         functools.partial(prepare_kernel, n_chan, n_rad),
         in_specs=[any_] * 5,
         out_specs=[whole] * 6,
         out_shape=[
-            jax.ShapeDtypeStruct((ch, ncoup), jnp.int32),
+            jax.ShapeDtypeStruct((ncoup, ch), jnp.int32),
             pltpu.VMEM(ham_blocks.shape, BF16),
             pltpu.VMEM((4 * k, lanes), BF16),
             pltpu.VMEM((2 * k, lanes), BF16),
@@ -343,6 +328,17 @@
         in_hbm(stored_at.reshape(-1, 128)),
         in_hbm(ham_blocks),
     )
+    far_own, near0, z1, z_even, diag0, rows = barrier((far_own, near0, z1, z_even, diag0, rows))
+    some, z_even, diag0 = barrier((jnp.concatenate([z1, z_even]), z_even, diag0))
+    near1, far1 = near_of(some), far_of(some)
+    z_odd = swap(z_even, "chan", 4)
+    z_odd, far1, near1, diag0 = barrier((z_odd, far1, near1, diag0))
+    early = in_cores(
+        jnp.concatenate([own, z1, z_even, near0, far_own, diag0, near1, z_odd, far1])
+    )
+    near_odd = near_of(z_odd)
+    diag_odd = jnp.concatenate([swap(diag0, "chan", 4 * z) for z in range(3, nz, 2)])
+    far2 = far_of(jnp.concatenate([z_odd, near1]))
     table = pl.pallas_call(
         assemble_kernel,
         in_specs=[any_] * n_rad,
@@ -352,8 +348,8 @@
         compiler_params=pltpu.CompilerParams(vmem_limit_bytes=VMEM_LIMIT),
         name="assemble",
     )(*[flat(x) for x in early])
-    diag1, near_odd, far2, table, rows = barrier((diag1, near_odd, far2, table, rows))
-    last = [in_vmem(flat(x)) for x in in_cores(jnp.concatenate([near_odd, far2, diag1]))]
+    near_odd, diag_odd, far2, table = barrier((near_odd, diag_odd, far2, table))
+    last = [in_vmem(flat(x)) for x in in_cores(jnp.concatenate([near_odd, far2, diag_odd]))]
 
     az, sums, _ = pl.pallas_call(
         apply_kernel,

time: 59.5 us -> 58.9 us (0.990)
  starting transfers between devices: 18.4 us -> 17 us
  blocking collectives: 11.5 us -> 12.1 us
    ppermute x6, starting transfers between devices: 5.87 us -> 4.34 us  [plane_swap(): return lax.ppermute(x, ('chan', 'rad'), pairs)]
    ppermute x10 -> x9, waiting for transfers between devices: 11.2 us -> 12.3 us  [swap(): return lax.ppermute(x, axis, [(i, i ^ distance) for i in range(n)])]
    ppermute x10 -> x9, starting transfers between devices: 12.5 us -> 12.6 us  [swap(): return lax.ppermute(x, axis, [(i, i ^ distance) for i in range(n)])]
  transfers between devices with their start and end apart: 16 -> 15, of which waited for: 10 -> 11; matrix products, arithmetic and copies ran while one was open for 0% -> 0% of each run, Pallas kernels for 7% -> 7%
where the time goes in v16:
time: 58.9 us; the launch traced here: 58.7 us
  starting transfers between devices  17 us (29%)
  waiting for transfers between devices  15.1 us (26%)
  Pallas kernels  12.1 us (21%)
  blocking collectives  12.1 us (21%)
  other arithmetic  1.28 us (2%)
  between operations  0.79 us (1%)
    ppermute x9, starting transfers between devices, swap(): return lax.ppermute(x, axis, [(i, i ^ distance) for i in range(n)])  12.6 us
    ppermute x9, waiting for transfers between devices, swap(): return lax.ppermute(x, axis, [(i, i ^ distance) for i in range(n)])  12.3 us
    all_to_all x1, blocking collectives, gather_sums(): lax.all_to_all(every, 'chan', split_axis=0, concat_axis=0, tiled=True)  12.1 us
    pallas_call x1, Pallas kernels, body(): pl.pallas_call(apply_kernel, in_specs=[smem] + [whole] * (6 + n_rad), out...  4.87 us
    ppermute x6, starting transfers between devices, plane_swap(): return lax.ppermute(x, ('chan', 'rad'), pairs)  4.34 us
    pallas_call x1, Pallas kernels, body(): pl.pallas_call(functools.partial(prepare_kernel, n_chan, n_rad), in_specs...  3.66 us
    pallas_call x1, Pallas kernels, body(): pl.pallas_call(functools.partial(finish_kernel, total), out_shape=[jax.Sh...  3.06 us
    ppermute x6, waiting for transfers between devices, plane_swap(): return lax.ppermute(x, ('chan', 'rad'), pairs)  2.85 us
  transfers between devices with their start and end apart: 15, of which 11 were waited for; matrix products, arithmetic and copies ran while one was open for 0% of the time, Pallas kernels for 7%

profile of v16, /device:TPU:0, one launch (start us, length us, event | category | flops | bytes accessed | tf_op | source)
XLA Modules:
  0.0 58.7 jit_solution(6950388527406861744)
XLA Ops:
  0.6 1.1 %convert_element_type.3 = bf16[64,16,64]{2,1,0:T(8,128)(2,1)S(1)} convert(f32[64,16,64]{2,1,0:T(8,128)} %t_hbm.1) | non-fusion elementwise | flops 65536 | bytes 393216 | tf_op jit(solution)/shard_map/convert_element_type | solution.py:260
  1.7 0.5 collective-permute-start
  2.3 1.0 %collective-permute-done = bf16[32,16,64]{2,1,0:T(8,128)(2,1)S(1)} collective-permute-done((bf16[32,16,64]{2,1,0:T(8,128)(2,1)S(1)}, bf16[32,16,64]{2,1,0:T(8,128)(2,1)S(1)}, u32[]{:S(2)}, u32[]{:S(2)}) %collective-permute-start) | collective-permute-done | bytes 65568 | tf_op jit(solution)/shard_map/ppermute | solution.py:21
  3.3 0.1 constant_dynamic-update-slice_fusion.8
  3.4 3.9 %collective-permute-start.5 = (bf16[1,32,16,128]{3,2,1,0:T(8,128)(2,1)S(1)}, bf16[1,32,16,128]{3,2,1,0:T(8,128)(2,1)S(1)}, u32[]{:S(2)}, u32[]{:S(2)}) collective-permute-start(bf16[1,32,16,128]{3,2,1,0:T(8,128)(2,1)S(1)} %get-tuple-element.57), channel_id=1, source_target_pairs={{0,6},{2,4},{4,2},{6,0},{8,14},{10,12},{12,10},{14,8},{16,22},{18,... | collective-permute-start | bytes 393224 | tf_op jit(solution)/shard_map/ppermute | solution.py:21
  7.3 2.6 %collective-permute-start.4 = (bf16[1,32,16,128]{3,2,1,0:T(8,128)(2,1)S(1)}, bf16[1,32,16,128]{3,2,1,0:T(8,128)(2,1)S(1)}, u32[]{:S(2)}, u32[]{:S(2)}) collective-permute-start(bf16[1,32,16,128]{3,2,1,0:T(8,128)(2,1)S(1)} %get-tuple-element.57), channel_id=1, source_target_pairs={{0,16},{2,18},{4,20},{6,22},{8,24},{10,26},{12,28},{14,30},{16,0},... | collective-permute-start | bytes 393224 | tf_op jit(solution)/shard_map/ppermute | solution.py:21
  9.9 1.6 %collective-permute-start.3 = (bf16[1,32,16,128]{3,2,1,0:T(8,128)(2,1)S(1)}, bf16[1,32,16,128]{3,2,1,0:T(8,128)(2,1)S(1)}, u32[]{:S(2)}, u32[]{:S(2)}) collective-permute-start(bf16[1,32,16,128]{3,2,1,0:T(8,128)(2,1)S(1)} %get-tuple-element.57), channel_id=1, source_target_pairs={{0,8},{2,10},{4,12},{6,14},{8,0},{10,2},{12,4},{14,6},{16,24},{18,... | collective-permute-start | bytes 393224 | tf_op jit(solution)/shard_map/ppermute | solution.py:21
  11.4 0.5 collective-permute-start.2
  12.0 0.5 collective-permute-start.1
  12.5 3.7 %prepare.1 = (s32[8,64]{1,0:T(8,128)S(1)}, bf16[64,8,64,128]{3,2,1,0:T(8,128)(2,1)S(1)}, bf16[64,4096]{1,0:T(8,128)(2,1)S(1)}, bf16[32,4096]{1,0:T(8,128)(2,1)S(...) custom-call(f32[64,16,64]{2,1,0:T(8,128)} %t_hbm.1, f32[64,64]{1,0:T(8,128)} %d_hbm.1, s32[8,64]{1,0:T(8,128)} %bitcast.22, ...), custom_call_target="tpu_custom_call" | custom-call | tf_op jit(solution)/shard_map/prepare/pallas_call | solution.py:303
  16.2 0.2 collective-permute-done.4
  16.3 0.2 collective-permute-done.3
  16.5 0.4 collective-permute-done.1
  17.0 1.6 %collective-permute-start.8 = (bf16[2,32,16,128]{3,2,1,0:T(8,128)(2,1)S(1)}, bf16[2,32,16,128]{3,2,1,0:T(8,128)(2,1)S(1)}, u32[]{:S(2)}, u32[]{:S(2)}) collective-permute-start(bf16[2,32,16,128]{3,2,1,0:T(8,128)(2,1)S(1)} %pad_maximum_fusion.1), channel_id=1, source_target_pairs={{0,2},{1,5},{2,0},{3,7},{4,6},{5,1},{6,4},{7,3},{8,10},{9,13},{10,... | collective-permute-start | bytes 786440 | tf_op jit(solution)/shard_map/ppermute | solution.py:30
  18.5 0.8 %collective-permute-start.7 = (bf16[2,32,16,128]{3,2,1,0:T(8,128)(2,1)S(1)}, bf16[2,32,16,128]{3,2,1,0:T(8,128)(2,1)S(1)}, u32[]{:S(2)}, u32[]{:S(2)}) collective-permute-start(bf16[2,32,16,128]{3,2,1,0:T(8,128)(2,1)S(1)} %pad_maximum_fusion.1), channel_id=1, source_target_pairs={{0,4},{1,3},{2,6},{3,1},{4,0},{5,7},{6,2},{7,5},{8,12},{9,11},{10,... | collective-permute-start | bytes 786440 | tf_op jit(solution)/shard_map/ppermute | solution.py:30
  19.3 0.5 collective-permute-start.6
  19.9 4.4 %collective-permute-done.6 = bf16[1,32,16,128]{3,2,1,0:T(8,128)(2,1)S(1)} collective-permute-done((bf16[1,32,16,128]{3,2,1,0:T(8,128)(2,1)S(1)}, bf16[1,32,16,128]{3,2,1,0:T(8,128)(2,1)S(1)}, u32[]{:S(2)}, u32[]{:S(2)}) %collective-permute-start.6) | collective-permute-done | bytes 131104 | tf_op jit(solution)/shard_map/ppermute | solution.py:21
  24.4 1.3 %collective-permute-done.8 = bf16[2,32,16,128]{3,2,1,0:T(8,128)(2,1)S(1)} collective-permute-done((bf16[2,32,16,128]{3,2,1,0:T(8,128)(2,1)S(1)}, bf16[2,32,16,128]{3,2,1,0:T(8,128)(2,1)S(1)}, u32[]{:S(2)}, u32[]{:S(2)}) %collective-permute-start.8) | collective-permute-done | bytes 262176 | tf_op jit(solution)/shard_map/ppermute | solution.py:30
  26.0 0.4 collective-permute-start.11
  26.4 3.3 %collective-permute-start.10 = (bf16[1,32,16,128]{3,2,1,0:T(8,128)(2,1)S(1)}, bf16[1,32,16,128]{3,2,1,0:T(8,128)(2,1)S(1)}, u32[]{:S(2)}, u32[]{:S(2)}) collective-permute-start(bf16[1,32,16,128]{3,2,1,0:T(8,128)(2,1)S(1)} %collective-permute-done.5), channel_id=1, source_target_pairs={{0,24},{2,26},{4,28},{6,30},{8,16},{10,18},{12,20},{14,22},{16,8},... | collective-permute-start | bytes 393224 | tf_op jit(solution)/shard_map/ppermute | solution.py:21
  29.7 0.5 collective-permute-start.9
  30.2 0.5 assemble.1._
  30.7 3.3 %collective-permute-done.10 = bf16[1,32,16,128]{3,2,1,0:T(8,128)(2,1)S(1)} collective-permute-done((bf16[1,32,16,128]{3,2,1,0:T(8,128)(2,1)S(1)}, bf16[1,32,16,128]{3,2,1,0:T(8,128)(2,1)S(1)}, u32[]{:S(2)}, u32[]{:S(2)}) %collective-permute-start.10) | collective-permute-done | bytes 131104 | tf_op jit(solution)/shard_map/ppermute | solution.py:21
  34.1 0.6 %collective-permute-done.9 = bf16[1,32,16,128]{3,2,1,0:T(8,128)(2,1)S(1)} collective-permute-done((bf16[1,32,16,128]{3,2,1,0:T(8,128)(2,1)S(1)}, bf16[1,32,16,128]{3,2,1,0:T(8,128)(2,1)S(1)}, u32[]{:S(2)}, u32[]{:S(2)}) %collective-permute-start.9) | collective-permute-done | bytes 131104 | tf_op jit(solution)/shard_map/ppermute | solution.py:30
  34.7 0.5 collective-permute-done.11
  35.3 0.1 collective-permute-start.13
  35.4 2.1 %collective-permute-done.13 = bf16[5,32,16,128]{3,2,1,0:T(8,128)(2,1)S(1)} collective-permute-done((bf16[5,32,16,128]{3,2,1,0:T(8,128)(2,1)S(1)}, bf16[5,32,16,128]{3,2,1,0:T(8,128)(2,1)S(1)}, u32[]{:S(2)}, u32[]{:S(2)}) %collective-permute-start.13) | collective-permute-done | bytes 655392 | tf_op jit(solution)/shard_map/ppermute | solution.py:21
  37.5 4.9 %apply.1 = (bf16[32,4096]{1,0:T(8,128)(2,1)S(1)}, f32[16,128]{1,0:T(8,128)S(1)}, bf16[1024,16,128]{2,1,0:T(8,128)(2,1)S(1)}) custom-call(s32[8,64]{1,0:T(8,128)S(1)} %get-tuple-element.30.rows_ref, bf16[64,8,64,128]{3,2,1,0:T(8,128)(2,1)S(1)} %get-tuple-element.31.ham_ref, bf16[1024,16,128]{2,1,0:T(8,128)(2,1)S(1)} %assemble.1._, ...), custom_call_target="tpu_custom_call", output_to_operand_aliasing={{2}: (2, {})} | custom-call | tf_op jit(solution)/shard_map/apply/pallas_call | solution.py:354
  42.3 0.2 collective-permute-start.14
  42.5 1.0 %collective-permute-done.14 = f32[16,128]{1,0:T(8,128)S(1)} collective-permute-done((f32[16,128]{1,0:T(8,128)S(1)}, f32[16,128]{1,0:T(8,128)S(1)}, u32[]{:S(2)}, u32[]{:S(2)}) %collective-permute-start.14) | collective-permute-done | bytes 8224 | tf_op jit(solution)/shard_map/ppermute | solution.py:21
  43.6 12.1 %all_to_all.5.sums_ref = f32[16,16,128]{2,1,0:T(8,128)S(1)} all-to-all(f32[16,16,128]{2,1,0:T(8,128)S(1)} %broadcast_in_dim.7), channel_id=1, replica_groups=mesh['chan'=16,'rad'=2] {'chan'}, dimensions={0} | all-to-all | bytes 262144 | tf_op jit(solution)/shard_map/all_to_all | solution.py:253
  55.6 3.1 %finish.1 = (f32[64,16,64]{2,1,0:T(8,128)}, f32[1,16]{1,0:T(1,128)}) custom-call(f32[16,16,128]{2,1,0:T(8,128)S(1)} %all_to_all.5.sums_ref, bf16[32,4096]{1,0:T(8,128)(2,1)S(1)} %get-tuple-element.53.az_ref, bf16[64,4096]{1,0:T(8,128)(2,1)S(1)} %get-tuple-element.45.zhm_ref), custom_call_target="tpu_custom_call" | custom-call | tf_op jit(solution)/shard_map/finish/pallas_call | solution.py:370
  (22 shorter events, 0.5 us)
Async XLA Ops:
  1.7 1.5 %collective-permute-start = (bf16[32,16,64]{2,1,0:T(8,128)(2,1)S(1)}, bf16[32,16,64]{2,1,0:T(8,128)(2,1)S(1)}, u32[]{:S(2)}, u32[]{:S(2)}) collective-permute-start(bf16[32,16,64]{2,1,0:T(8,128)(2,1)S(1)} %dynamic-slice_bitcast_fusion), channel_id=1, source_target_pairs={{0,1},{1,0},{2,3},{3,2},{4,5},{5,4},{6,7},{7,6},{8,9},{9,8},{10,11... | collective-permute-start | bytes 196616 | tf_op jit(solution)/shard_map/ppermute | solution.py:21
  3.4 12.7 %collective-permute-start.5 = (bf16[1,32,16,128]{3,2,1,0:T(8,128)(2,1)S(1)}, bf16[1,32,16,128]{3,2,1,0:T(8,128)(2,1)S(1)}, u32[]{:S(2)}, u32[]{:S(2)}) collective-permute-start(bf16[1,32,16,128]{3,2,1,0:T(8,128)(2,1)S(1)} %get-tuple-element.57), channel_id=1, source_target_pairs={{0,6},{2,4},{4,2},{6,0},{8,14},{10,12},{12,10},{14,8},{16,22},{18,... | collective-permute-start | bytes 393224 | tf_op jit(solution)/shard_map/ppermute | solution.py:21
  7.3 9.1 %collective-permute-start.4 = (bf16[1,32,16,128]{3,2,1,0:T(8,128)(2,1)S(1)}, bf16[1,32,16,128]{3,2,1,0:T(8,128)(2,1)S(1)}, u32[]{:S(2)}, u32[]{:S(2)}) collective-permute-start(bf16[1,32,16,128]{3,2,1,0:T(8,128)(2,1)S(1)} %get-tuple-element.57), channel_id=1, source_target_pairs={{0,16},{2,18},{4,20},{6,22},{8,24},{10,26},{12,28},{14,30},{16,0},... | collective-permute-start | bytes 393224 | tf_op jit(solution)/shard_map/ppermute | solution.py:21
  9.9 6.7 %collective-permute-start.3 = (bf16[1,32,16,128]{3,2,1,0:T(8,128)(2,1)S(1)}, bf16[1,32,16,128]{3,2,1,0:T(8,128)(2,1)S(1)}, u32[]{:S(2)}, u32[]{:S(2)}) collective-permute-start(bf16[1,32,16,128]{3,2,1,0:T(8,128)(2,1)S(1)} %get-tuple-element.57), channel_id=1, source_target_pairs={{0,8},{2,10},{4,12},{6,14},{8,0},{10,2},{12,4},{14,6},{16,24},{18,... | collective-permute-start | bytes 393224 | tf_op jit(solution)/shard_map/ppermute | solution.py:21
  11.4 5.1 %collective-permute-start.2 = (bf16[1,32,16,128]{3,2,1,0:T(8,128)(2,1)S(1)}, bf16[1,32,16,128]{3,2,1,0:T(8,128)(2,1)S(1)}, u32[]{:S(2)}, u32[]{:S(2)}) collective-permute-start(bf16[1,32,16,128]{3,2,1,0:T(8,128)(2,1)S(1)} %get-tuple-element.57), channel_id=1, source_target_pairs={{0,2},{1,5},{2,0},{3,7},{4,6},{5,1},{6,4},{7,3},{8,10},{9,13},{10,... | collective-permute-start | bytes 393224 | tf_op jit(solution)/shard_map/ppermute | solution.py:30
  12.0 5.0 %collective-permute-start.1 = (bf16[1,32,16,128]{3,2,1,0:T(8,128)(2,1)S(1)}, bf16[1,32,16,128]{3,2,1,0:T(8,128)(2,1)S(1)}, u32[]{:S(2)}, u32[]{:S(2)}) collective-permute-start(bf16[1,32,16,128]{3,2,1,0:T(8,128)(2,1)S(1)} %get-tuple-element.57), channel_id=1, source_target_pairs={{0,4},{1,3},{2,6},{3,1},{4,0},{5,7},{6,2},{7,5},{8,12},{9,11},{10,... | collective-permute-start | bytes 393224 | tf_op jit(solution)/shard_map/ppermute | solution.py:30
  17.0 8.7 %collective-permute-start.8 = (bf16[2,32,16,128]{3,2,1,0:T(8,128)(2,1)S(1)}, bf16[2,32,16,128]{3,2,1,0:T(8,128)(2,1)S(1)}, u32[]{:S(2)}, u32[]{:S(2)}) collective-permute-start(bf16[2,32,16,128]{3,2,1,0:T(8,128)(2,1)S(1)} %pad_maximum_fusion.1), channel_id=1, source_target_pairs={{0,2},{1,5},{2,0},{3,7},{4,6},{5,1},{6,4},{7,3},{8,10},{9,13},{10,... | collective-permute-start | bytes 786440 | tf_op jit(solution)/shard_map/ppermute | solution.py:30
  18.5 7.2 %collective-permute-start.7 = (bf16[2,32,16,128]{3,2,1,0:T(8,128)(2,1)S(1)}, bf16[2,32,16,128]{3,2,1,0:T(8,128)(2,1)S(1)}, u32[]{:S(2)}, u32[]{:S(2)}) collective-permute-start(bf16[2,32,16,128]{3,2,1,0:T(8,128)(2,1)S(1)} %pad_maximum_fusion.1), channel_id=1, source_target_pairs={{0,4},{1,3},{2,6},{3,1},{4,0},{5,7},{6,2},{7,5},{8,12},{9,11},{10,... | collective-permute-start | bytes 786440 | tf_op jit(solution)/shard_map/ppermute | solution.py:30
  19.3 5.0 %collective-permute-start.6 = (bf16[1,32,16,128]{3,2,1,0:T(8,128)(2,1)S(1)}, bf16[1,32,16,128]{3,2,1,0:T(8,128)(2,1)S(1)}, u32[]{:S(2)}, u32[]{:S(2)}) collective-permute-start(bf16[1,32,16,128]{3,2,1,0:T(8,128)(2,1)S(1)} %collective-permute-done.4), channel_id=1, source_target_pairs={{0,8},{2,10},{4,12},{6,14},{8,0},{10,2},{12,4},{14,6},{16,24},{18,... | collective-permute-start | bytes 393224 | tf_op jit(solution)/shard_map/ppermute | solution.py:21
  25.8 4.4 %collective-permute-start.12 = (bf16[11,32,16,128]{3,2,1,0:T(8,128)(2,1)S(1)}, bf16[11,32,16,128]{3,2,1,0:T(8,128)(2,1)S(1)}, u32[]{:S(2)}, u32[]{:S(2)}) collective-permute-start(bf16[11,32,16,128]{3,2,1,0:T(8,128)(2,1)S(1)} %constant_dynamic-update-slice_fusion), channel_id=1, source_target_pairs={{0,1},{1,0},{2,3},{3,2},{4,5},{5,4},{6,7},{7,6},{8,9},{9,8},{10,11... | collective-permute-start | bytes 4325384 | tf_op jit(solution)/shard_map/ppermute | solution.py:21
  26.0 9.2 %collective-permute-start.11 = (bf16[3,32,16,128]{3,2,1,0:T(8,128)(2,1)S(1)}, bf16[3,32,16,128]{3,2,1,0:T(8,128)(2,1)S(1)}, u32[]{:S(2)}, u32[]{:S(2)}) collective-permute-start(bf16[3,32,16,128]{3,2,1,0:T(8,128)(2,1)S(1)} %pad_maximum_fusion), channel_id=1, source_target_pairs={{0,4},{1,3},{2,6},{3,1},{4,0},{5,7},{6,2},{7,5},{8,12},{9,11},{10,... | collective-permute-start | bytes 1179656 | tf_op jit(solution)/shard_map/ppermute | solution.py:30
  26.4 7.7 %collective-permute-start.10 = (bf16[1,32,16,128]{3,2,1,0:T(8,128)(2,1)S(1)}, bf16[1,32,16,128]{3,2,1,0:T(8,128)(2,1)S(1)}, u32[]{:S(2)}, u32[]{:S(2)}) collective-permute-start(bf16[1,32,16,128]{3,2,1,0:T(8,128)(2,1)S(1)} %collective-permute-done.5), channel_id=1, source_target_pairs={{0,24},{2,26},{4,28},{6,30},{8,16},{10,18},{12,20},{14,22},{16,8},... | collective-permute-start | bytes 393224 | tf_op jit(solution)/shard_map/ppermute | solution.py:21
  29.7 5.1 %collective-permute-start.9 = (bf16[1,32,16,128]{3,2,1,0:T(8,128)(2,1)S(1)}, bf16[1,32,16,128]{3,2,1,0:T(8,128)(2,1)S(1)}, u32[]{:S(2)}, u32[]{:S(2)}) collective-permute-start(bf16[1,32,16,128]{3,2,1,0:T(8,128)(2,1)S(1)} %collective-permute-done.6), channel_id=1, source_target_pairs={{0,2},{1,5},{2,0},{3,7},{4,6},{5,1},{6,4},{7,3},{8,10},{9,13},{10,... | collective-permute-start | bytes 393224 | tf_op jit(solution)/shard_map/ppermute | solution.py:30
  35.3 2.2 %collective-permute-start.13 = (bf16[5,32,16,128]{3,2,1,0:T(8,128)(2,1)S(1)}, bf16[5,32,16,128]{3,2,1,0:T(8,128)(2,1)S(1)}, u32[]{:S(2)}, u32[]{:S(2)}) collective-permute-start(bf16[5,32,16,128]{3,2,1,0:T(8,128)(2,1)S(1)} %constant_dynamic-update-slice_fusion.9), channel_id=1, source_target_pairs={{0,1},{1,0},{2,3},{3,2},{4,5},{5,4},{6,7},{7,6},{8,9},{9,8},{10,11... | collective-permute-start | bytes 1966088 | tf_op jit(solution)/shard_map/ppermute | solution.py:21
  42.3 1.2 %collective-permute-start.14 = (f32[16,128]{1,0:T(8,128)S(1)}, f32[16,128]{1,0:T(8,128)S(1)}, u32[]{:S(2)}, u32[]{:S(2)}) collective-permute-start(f32[16,128]{1,0:T(8,128)S(1)} %get-tuple-element.52), channel_id=1, source_target_pairs={{0,1},{1,0},{2,3},{3,2},{4,5},{5,4},{6,7},{7,6},{8,9},{9,8},{10,11... | collective-permute-start | bytes 24584 | tf_op jit(solution)/shard_map/ppermute | solution.py:21

commit v17 on v16

--- a/solution.py
+++ b/solution.py
@@ -190,6 +190,12 @@
     return jnp.broadcast_to(x[:, i : i + 1], (x.shape[0], 128))
 
 
+def reciprocal(x):
+    y = pl.reciprocal(x, approx=True)
+    y = y * (2.0 - x * y)
+    return y * (2.0 - x * y)
+
+
 def finish_kernel(total, sums_ref, az_ref, zhm_ref, out_ref, ritz_ref):
     ch, k, r = out_ref.shape
     s = jnp.sum(sums_ref[...], axis=0)
@@ -197,7 +203,7 @@
     cols = [spread(s, 2 * k + i) for i in range(k)]
     x = s
     for i in range(k):
-        scale = 1.0 / cols[i][i : i + 1]
+        scale = reciprocal(cols[i][i : i + 1])
         pivot = x[i : i + 1] * scale
         x = jnp.where(row == i, pivot, x - cols[i] * pivot)
         for j in range(i + 1, k):
@@ -219,7 +225,7 @@
     x = jnp.concatenate([eye.astype(F32), -coef.T, -mix.T, pad], axis=1)
     for i in range(k):
         pivot = cols[i][i : i + 1]
-        scale = 1.0 / pivot
+        scale = reciprocal(pivot)
         below = jnp.where(row > i, cols[i] * scale, 0.0)
         pivot_row = x[i : i + 1]
         x = jnp.where(row == i, pivot_row * (lax.rsqrt(pivot) * (total ** 0.5)), x - below * pivot_row)
@@ -300,6 +306,19 @@
     near0, far_own, diag0 = near_of(own), far_of(own), swap(own, "chan", 3)
     z1 = swap(own, "chan", 4)
     z_even = jnp.concatenate([swap(own, "chan", 4 * z) for z in range(2, nz, 2)])
+    far_own, near0, z1, z_even, diag0 = barrier((far_own, near0, z1, z_even, diag0))
+    some, z_even, diag0 = barrier((jnp.concatenate([z1, z_even]), z_even, diag0))
+    near1, far1 = near_of(some), far_of(some)
+    z_odd = swap(z_even, "chan", 4)
+    inputs = (trial_block, precond_diag, partners, stored_at, ham_blocks)
+    z_odd, far1, near1, diag0, inputs = barrier((z_odd, far1, near1, diag0, inputs))
+    trial_block, precond_diag, partners, stored_at, ham_blocks = inputs
+    early = in_cores(
+        jnp.concatenate([own, z1, z_even, near0, far_own, diag0, near1, z_odd, far1])
+    )
+    near_odd = near_of(z_odd)
+    diag_odd = jnp.concatenate([swap(diag0, "chan", 4 * z) for z in range(3, nz, 2)])
+    far2 = far_of(jnp.concatenate([z_odd, near1]))
     rows, ham, zhm, zl, dc, gram_t = pl.pallas_call(
         functools.partial(prepare_kernel, n_chan, n_rad),
         in_specs=[any_] * 5,
@@ -328,17 +347,6 @@
         in_hbm(stored_at.reshape(-1, 128)),
         in_hbm(ham_blocks),
     )
-    far_own, near0, z1, z_even, diag0, rows = barrier((far_own, near0, z1, z_even, diag0, rows))
-    some, z_even, diag0 = barrier((jnp.concatenate([z1, z_even]), z_even, diag0))
-    near1, far1 = near_of(some), far_of(some)
-    z_odd = swap(z_even, "chan", 4)
-    z_odd, far1, near1, diag0 = barrier((z_odd, far1, near1, diag0))
-    early = in_cores(
-        jnp.concatenate([own, z1, z_even, near0, far_own, diag0, near1, z_odd, far1])
-    )
-    near_odd = near_of(z_odd)
-    diag_odd = jnp.concatenate([swap(diag0, "chan", 4 * z) for z in range(3, nz, 2)])
-    far2 = far_of(jnp.concatenate([z_odd, near1]))
     table = pl.pallas_call(
         assemble_kernel,
         in_specs=[any_] * n_rad,
@@ -348,7 +356,7 @@
         compiler_params=pltpu.CompilerParams(vmem_limit_bytes=VMEM_LIMIT),
         name="assemble",
     )(*[flat(x) for x in early])
-    near_odd, diag_odd, far2, table = barrier((near_odd, diag_odd, far2, table))
+    near_odd, diag_odd, far2, table, rows = barrier((near_odd, diag_odd, far2, table, rows))
     last = [in_vmem(flat(x)) for x in in_cores(jnp.concatenate([near_odd, far2, diag_odd]))]
 
     az, sums, _ = pl.pallas_call(

time: 58.9 us -> 59 us (level)
  transfers between devices with their start and end apart: 15 -> 15, of which waited for: 11 -> 10; matrix products, arithmetic and copies ran while one was open for 0% -> 0% of each run, Pallas kernels for 7% -> 7%
where the time goes in v17:
time: 59 us; the launch traced here: 58.8 us
  starting transfers between devices  16.7 us (28%)
  waiting for transfers between devices  15.4 us (26%)
  Pallas kernels  12.2 us (21%)
  blocking collectives  12.1 us (21%)
  other arithmetic  1.28 us (2%)
  between operations  0.8 us (1%)
    ppermute x9, starting transfers between devices, swap(): return lax.ppermute(x, axis, [(i, i ^ distance) for i in range(n)])  12.6 us
    ppermute x9, waiting for transfers between devices, swap(): return lax.ppermute(x, axis, [(i, i ^ distance) for i in range(n)])  12.6 us
    all_to_all x1, blocking collectives, gather_sums(): lax.all_to_all(every, 'chan', split_axis=0, concat_axis=0, tiled=True)  12.1 us
    pallas_call x1, Pallas kernels, body(): pl.pallas_call(apply_kernel, in_specs=[smem] + [whole] * (6 + n_rad), out...  4.88 us
    ppermute x6, starting transfers between devices, plane_swap(): return lax.ppermute(x, ('chan', 'rad'), pairs)  4.06 us
    pallas_call x1, Pallas kernels, body(): pl.pallas_call(functools.partial(prepare_kernel, n_chan, n_rad), in_specs...  3.66 us
    pallas_call x1, Pallas kernels, body(): pl.pallas_call(functools.partial(finish_kernel, total), out_shape=[jax.Sh...  3.17 us
    ppermute x6, waiting for transfers between devices, plane_swap(): return lax.ppermute(x, ('chan', 'rad'), pairs)  2.77 us
  transfers between devices with their start and end apart: 15, of which 10 were waited for; matrix products, arithmetic and copies ran while one was open for 0% of the time, Pallas kernels for 7%

profile of v17, /device:TPU:0, one launch (start us, length us, event | category | flops | bytes accessed | tf_op | source)
XLA Modules:
  0.0 58.8 jit_solution(16124749440667209425)
XLA Ops:
  0.6 1.1 %convert_element_type.3 = bf16[64,16,64]{2,1,0:T(8,128)(2,1)S(1)} convert(f32[64,16,64]{2,1,0:T(8,128)} %t_hbm) | non-fusion elementwise | flops 65536 | bytes 393216 | tf_op jit(solution)/shard_map/convert_element_type | solution.py:266
  1.7 0.5 collective-permute-start
  2.3 1.0 %collective-permute-done = bf16[32,16,64]{2,1,0:T(8,128)(2,1)S(1)} collective-permute-done((bf16[32,16,64]{2,1,0:T(8,128)(2,1)S(1)}, bf16[32,16,64]{2,1,0:T(8,128)(2,1)S(1)}, u32[]{:S(2)}, u32[]{:S(2)}) %collective-permute-start) | collective-permute-done | bytes 65568 | tf_op jit(solution)/shard_map/ppermute | solution.py:21
  3.3 0.1 constant_dynamic-update-slice_fusion.8
  3.4 3.9 %collective-permute-start.5 = (bf16[1,32,16,128]{3,2,1,0:T(8,128)(2,1)S(1)}, bf16[1,32,16,128]{3,2,1,0:T(8,128)(2,1)S(1)}, u32[]{:S(2)}, u32[]{:S(2)}) collective-permute-start(bf16[1,32,16,128]{3,2,1,0:T(8,128)(2,1)S(1)} %get-tuple-element.67), channel_id=1, source_target_pairs={{0,6},{2,4},{4,2},{6,0},{8,14},{10,12},{12,10},{14,8},{16,22},{18,... | collective-permute-start | bytes 393224 | tf_op jit(solution)/shard_map/ppermute | solution.py:21
  7.3 2.6 %collective-permute-start.4 = (bf16[1,32,16,128]{3,2,1,0:T(8,128)(2,1)S(1)}, bf16[1,32,16,128]{3,2,1,0:T(8,128)(2,1)S(1)}, u32[]{:S(2)}, u32[]{:S(2)}) collective-permute-start(bf16[1,32,16,128]{3,2,1,0:T(8,128)(2,1)S(1)} %get-tuple-element.67), channel_id=1, source_target_pairs={{0,16},{2,18},{4,20},{6,22},{8,24},{10,26},{12,28},{14,30},{16,0},... | collective-permute-start | bytes 393224 | tf_op jit(solution)/shard_map/ppermute | solution.py:21
  9.9 1.6 %collective-permute-start.3 = (bf16[1,32,16,128]{3,2,1,0:T(8,128)(2,1)S(1)}, bf16[1,32,16,128]{3,2,1,0:T(8,128)(2,1)S(1)}, u32[]{:S(2)}, u32[]{:S(2)}) collective-permute-start(bf16[1,32,16,128]{3,2,1,0:T(8,128)(2,1)S(1)} %get-tuple-element.67), channel_id=1, source_target_pairs={{0,8},{2,10},{4,12},{6,14},{8,0},{10,2},{12,4},{14,6},{16,24},{18,... | collective-permute-start | bytes 393224 | tf_op jit(solution)/shard_map/ppermute | solution.py:21
  11.4 0.5 collective-permute-start.2
  12.0 0.5 collective-permute-start.1
  12.5 3.9 %collective-permute-done.4 = bf16[1,32,16,128]{3,2,1,0:T(8,128)(2,1)S(1)} collective-permute-done((bf16[1,32,16,128]{3,2,1,0:T(8,128)(2,1)S(1)}, bf16[1,32,16,128]{3,2,1,0:T(8,128)(2,1)S(1)}, u32[]{:S(2)}, u32[]{:S(2)}) %collective-permute-start.4) | collective-permute-done | bytes 131104 | tf_op jit(solution)/shard_map/ppermute | solution.py:21
  16.3 0.2 collective-permute-done.3
  16.5 0.4 collective-permute-done.1
  17.0 1.6 %collective-permute-start.8 = (bf16[2,32,16,128]{3,2,1,0:T(8,128)(2,1)S(1)}, bf16[2,32,16,128]{3,2,1,0:T(8,128)(2,1)S(1)}, u32[]{:S(2)}, u32[]{:S(2)}) collective-permute-start(bf16[2,32,16,128]{3,2,1,0:T(8,128)(2,1)S(1)} %pad_maximum_fusion.1), channel_id=1, source_target_pairs={{0,2},{1,5},{2,0},{3,7},{4,6},{5,1},{6,4},{7,3},{8,10},{9,13},{10,... | collective-permute-start | bytes 786440 | tf_op jit(solution)/shard_map/ppermute | solution.py:30
  18.5 0.5 collective-permute-start.7
  19.0 0.5 collective-permute-start.6
  19.6 4.4 %collective-permute-done.6 = bf16[1,32,16,128]{3,2,1,0:T(8,128)(2,1)S(1)} collective-permute-done((bf16[1,32,16,128]{3,2,1,0:T(8,128)(2,1)S(1)}, bf16[1,32,16,128]{3,2,1,0:T(8,128)(2,1)S(1)}, u32[]{:S(2)}, u32[]{:S(2)}) %collective-permute-start.6) | collective-permute-done | bytes 131104 | tf_op jit(solution)/shard_map/ppermute | solution.py:21
  24.1 1.6 %collective-permute-done.8 = bf16[2,32,16,128]{3,2,1,0:T(8,128)(2,1)S(1)} collective-permute-done((bf16[2,32,16,128]{3,2,1,0:T(8,128)(2,1)S(1)}, bf16[2,32,16,128]{3,2,1,0:T(8,128)(2,1)S(1)}, u32[]{:S(2)}, u32[]{:S(2)}) %collective-permute-start.8) | collective-permute-done | bytes 262176 | tf_op jit(solution)/shard_map/ppermute | solution.py:30
  25.8 0.1 collective-permute-start.12
  26.0 0.4 collective-permute-start.11
  26.4 3.3 %collective-permute-start.10 = (bf16[1,32,16,128]{3,2,1,0:T(8,128)(2,1)S(1)}, bf16[1,32,16,128]{3,2,1,0:T(8,128)(2,1)S(1)}, u32[]{:S(2)}, u32[]{:S(2)}) collective-permute-start(bf16[1,32,16,128]{3,2,1,0:T(8,128)(2,1)S(1)} %collective-permute-done.5), channel_id=1, source_target_pairs={{0,24},{2,26},{4,28},{6,30},{8,16},{10,18},{12,20},{14,22},{16,8},... | collective-permute-start | bytes 393224 | tf_op jit(solution)/shard_map/ppermute | solution.py:21
  29.7 0.5 collective-permute-start.9
  30.2 3.7 %prepare.1 = (s32[8,64]{1,0:T(8,128)S(1)}, bf16[64,8,64,128]{3,2,1,0:T(8,128)(2,1)S(1)}, bf16[64,4096]{1,0:T(8,128)(2,1)S(1)}, bf16[32,4096]{1,0:T(8,128)(2,1)S(...) custom-call(f32[64,16,64]{2,1,0:T(8,128)} %t_hbm, f32[64,64]{1,0:T(8,128)} %d_hbm, s32[8,64]{1,0:T(8,128)} %bitcast.22, ...), custom_call_target="tpu_custom_call" | custom-call | tf_op jit(solution)/shard_map/prepare/pallas_call | solution.py:322
  33.9 0.5 assemble.1._
  34.4 0.3 collective-permute-done.9
  34.7 0.5 collective-permute-done.11
  35.3 0.1 collective-permute-start.13
  35.4 2.1 %collective-permute-done.13 = bf16[5,32,16,128]{3,2,1,0:T(8,128)(2,1)S(1)} collective-permute-done((bf16[5,32,16,128]{3,2,1,0:T(8,128)(2,1)S(1)}, bf16[5,32,16,128]{3,2,1,0:T(8,128)(2,1)S(1)}, u32[]{:S(2)}, u32[]{:S(2)}) %collective-permute-start.13) | collective-permute-done | bytes 655392 | tf_op jit(solution)/shard_map/ppermute | solution.py:21
  37.5 4.9 %apply.1 = (bf16[32,4096]{1,0:T(8,128)(2,1)S(1)}, f32[16,128]{1,0:T(8,128)S(1)}, bf16[1024,16,128]{2,1,0:T(8,128)(2,1)S(1)}) custom-call(s32[8,64]{1,0:T(8,128)S(1)} %get-tuple-element.52.rows_ref, bf16[64,8,64,128]{3,2,1,0:T(8,128)(2,1)S(1)} %get-tuple-element.53.ham_ref, bf16[1024,16,128]{2,1,0:T(8,128)(2,1)S(1)} %assemble.1._, ...), custom_call_target="tpu_custom_call", output_to_operand_aliasing={{2}: (2, {})} | custom-call | tf_op jit(solution)/shard_map/apply/pallas_call | solution.py:362
  42.3 0.1 collective-permute-start.14
  42.5 1.0 %collective-permute-done.14 = f32[16,128]{1,0:T(8,128)S(1)} collective-permute-done((f32[16,128]{1,0:T(8,128)S(1)}, f32[16,128]{1,0:T(8,128)S(1)}, u32[]{:S(2)}, u32[]{:S(2)}) %collective-permute-start.14) | collective-permute-done | bytes 8224 | tf_op jit(solution)/shard_map/ppermute | solution.py:21
  43.6 12.1 %all_to_all.5.sums_ref = f32[16,16,128]{2,1,0:T(8,128)S(1)} all-to-all(f32[16,16,128]{2,1,0:T(8,128)S(1)} %broadcast_in_dim.7), channel_id=1, replica_groups=mesh['chan'=16,'rad'=2] {'chan'}, dimensions={0} | all-to-all | bytes 262144 | tf_op jit(solution)/shard_map/all_to_all | solution.py:259
  55.6 3.2 %finish.1 = (f32[64,16,64]{2,1,0:T(8,128)}, f32[1,16]{1,0:T(1,128)}) custom-call(f32[16,16,128]{2,1,0:T(8,128)S(1)} %all_to_all.5.sums_ref, bf16[32,4096]{1,0:T(8,128)(2,1)S(1)} %get-tuple-element.63.az_ref, bf16[64,4096]{1,0:T(8,128)(2,1)S(1)} %get-tuple-element.55.zhm_ref), custom_call_target="tpu_custom_call" | custom-call | tf_op jit(solution)/shard_map/finish/pallas_call | solution.py:378
  (22 shorter events, 0.4 us)
Async XLA Ops:
  1.7 1.5 %collective-permute-start = (bf16[32,16,64]{2,1,0:T(8,128)(2,1)S(1)}, bf16[32,16,64]{2,1,0:T(8,128)(2,1)S(1)}, u32[]{:S(2)}, u32[]{:S(2)}) collective-permute-start(bf16[32,16,64]{2,1,0:T(8,128)(2,1)S(1)} %dynamic-slice_bitcast_fusion), channel_id=1, source_target_pairs={{0,1},{1,0},{2,3},{3,2},{4,5},{5,4},{6,7},{7,6},{8,9},{9,8},{10,11... | collective-permute-start | bytes 196616 | tf_op jit(solution)/shard_map/ppermute | solution.py:21
  3.4 9.1 %collective-permute-start.5 = (bf16[1,32,16,128]{3,2,1,0:T(8,128)(2,1)S(1)}, bf16[1,32,16,128]{3,2,1,0:T(8,128)(2,1)S(1)}, u32[]{:S(2)}, u32[]{:S(2)}) collective-permute-start(bf16[1,32,16,128]{3,2,1,0:T(8,128)(2,1)S(1)} %get-tuple-element.67), channel_id=1, source_target_pairs={{0,6},{2,4},{4,2},{6,0},{8,14},{10,12},{12,10},{14,8},{16,22},{18,... | collective-permute-start | bytes 393224 | tf_op jit(solution)/shard_map/ppermute | solution.py:21
  7.3 9.1 %collective-permute-start.4 = (bf16[1,32,16,128]{3,2,1,0:T(8,128)(2,1)S(1)}, bf16[1,32,16,128]{3,2,1,0:T(8,128)(2,1)S(1)}, u32[]{:S(2)}, u32[]{:S(2)}) collective-permute-start(bf16[1,32,16,128]{3,2,1,0:T(8,128)(2,1)S(1)} %get-tuple-element.67), channel_id=1, source_target_pairs={{0,16},{2,18},{4,20},{6,22},{8,24},{10,26},{12,28},{14,30},{16,0},... | collective-permute-start | bytes 393224 | tf_op jit(solution)/shard_map/ppermute | solution.py:21
  9.9 6.7 %collective-permute-start.3 = (bf16[1,32,16,128]{3,2,1,0:T(8,128)(2,1)S(1)}, bf16[1,32,16,128]{3,2,1,0:T(8,128)(2,1)S(1)}, u32[]{:S(2)}, u32[]{:S(2)}) collective-permute-start(bf16[1,32,16,128]{3,2,1,0:T(8,128)(2,1)S(1)} %get-tuple-element.67), channel_id=1, source_target_pairs={{0,8},{2,10},{4,12},{6,14},{8,0},{10,2},{12,4},{14,6},{16,24},{18,... | collective-permute-start | bytes 393224 | tf_op jit(solution)/shard_map/ppermute | solution.py:21
  11.4 5.1 %collective-permute-start.2 = (bf16[1,32,16,128]{3,2,1,0:T(8,128)(2,1)S(1)}, bf16[1,32,16,128]{3,2,1,0:T(8,128)(2,1)S(1)}, u32[]{:S(2)}, u32[]{:S(2)}) collective-permute-start(bf16[1,32,16,128]{3,2,1,0:T(8,128)(2,1)S(1)} %get-tuple-element.67), channel_id=1, source_target_pairs={{0,2},{1,5},{2,0},{3,7},{4,6},{5,1},{6,4},{7,3},{8,10},{9,13},{10,... | collective-permute-start | bytes 393224 | tf_op jit(solution)/shard_map/ppermute | solution.py:30
  12.0 5.0 %collective-permute-start.1 = (bf16[1,32,16,128]{3,2,1,0:T(8,128)(2,1)S(1)}, bf16[1,32,16,128]{3,2,1,0:T(8,128)(2,1)S(1)}, u32[]{:S(2)}, u32[]{:S(2)}) collective-permute-start(bf16[1,32,16,128]{3,2,1,0:T(8,128)(2,1)S(1)} %get-tuple-element.67), channel_id=1, source_target_pairs={{0,4},{1,3},{2,6},{3,1},{4,0},{5,7},{6,2},{7,5},{8,12},{9,11},{10,... | collective-permute-start | bytes 393224 | tf_op jit(solution)/shard_map/ppermute | solution.py:30
  17.0 8.7 %collective-permute-start.8 = (bf16[2,32,16,128]{3,2,1,0:T(8,128)(2,1)S(1)}, bf16[2,32,16,128]{3,2,1,0:T(8,128)(2,1)S(1)}, u32[]{:S(2)}, u32[]{:S(2)}) collective-permute-start(bf16[2,32,16,128]{3,2,1,0:T(8,128)(2,1)S(1)} %pad_maximum_fusion.1), channel_id=1, source_target_pairs={{0,2},{1,5},{2,0},{3,7},{4,6},{5,1},{6,4},{7,3},{8,10},{9,13},{10,... | collective-permute-start | bytes 786440 | tf_op jit(solution)/shard_map/ppermute | solution.py:30
  18.5 7.2 %collective-permute-start.7 = (bf16[2,32,16,128]{3,2,1,0:T(8,128)(2,1)S(1)}, bf16[2,32,16,128]{3,2,1,0:T(8,128)(2,1)S(1)}, u32[]{:S(2)}, u32[]{:S(2)}) collective-permute-start(bf16[2,32,16,128]{3,2,1,0:T(8,128)(2,1)S(1)} %pad_maximum_fusion.1), channel_id=1, source_target_pairs={{0,4},{1,3},{2,6},{3,1},{4,0},{5,7},{6,2},{7,5},{8,12},{9,11},{10,... | collective-permute-start | bytes 786440 | tf_op jit(solution)/shard_map/ppermute | solution.py:30
  19.0 5.0 %collective-permute-start.6 = (bf16[1,32,16,128]{3,2,1,0:T(8,128)(2,1)S(1)}, bf16[1,32,16,128]{3,2,1,0:T(8,128)(2,1)S(1)}, u32[]{:S(2)}, u32[]{:S(2)}) collective-permute-start(bf16[1,32,16,128]{3,2,1,0:T(8,128)(2,1)S(1)} %collective-permute-done.4), channel_id=1, source_target_pairs={{0,8},{2,10},{4,12},{6,14},{8,0},{10,2},{12,4},{14,6},{16,24},{18,... | collective-permute-start | bytes 393224 | tf_op jit(solution)/shard_map/ppermute | solution.py:21
  25.8 8.0 %collective-permute-start.12 = (bf16[11,32,16,128]{3,2,1,0:T(8,128)(2,1)S(1)}, bf16[11,32,16,128]{3,2,1,0:T(8,128)(2,1)S(1)}, u32[]{:S(2)}, u32[]{:S(2)}) collective-permute-start(bf16[11,32,16,128]{3,2,1,0:T(8,128)(2,1)S(1)} %constant_dynamic-update-slice_fusion), channel_id=1, source_target_pairs={{0,1},{1,0},{2,3},{3,2},{4,5},{5,4},{6,7},{7,6},{8,9},{9,8},{10,11... | collective-permute-start | bytes 4325384 | tf_op jit(solution)/shard_map/ppermute | solution.py:21
  26.0 9.2 %collective-permute-start.11 = (bf16[3,32,16,128]{3,2,1,0:T(8,128)(2,1)S(1)}, bf16[3,32,16,128]{3,2,1,0:T(8,128)(2,1)S(1)}, u32[]{:S(2)}, u32[]{:S(2)}) collective-permute-start(bf16[3,32,16,128]{3,2,1,0:T(8,128)(2,1)S(1)} %pad_maximum_fusion), channel_id=1, source_target_pairs={{0,4},{1,3},{2,6},{3,1},{4,0},{5,7},{6,2},{7,5},{8,12},{9,11},{10,... | collective-permute-start | bytes 1179656 | tf_op jit(solution)/shard_map/ppermute | solution.py:30
  26.4 8.0 %collective-permute-start.10 = (bf16[1,32,16,128]{3,2,1,0:T(8,128)(2,1)S(1)}, bf16[1,32,16,128]{3,2,1,0:T(8,128)(2,1)S(1)}, u32[]{:S(2)}, u32[]{:S(2)}) collective-permute-start(bf16[1,32,16,128]{3,2,1,0:T(8,128)(2,1)S(1)} %collective-permute-done.5), channel_id=1, source_target_pairs={{0,24},{2,26},{4,28},{6,30},{8,16},{10,18},{12,20},{14,22},{16,8},... | collective-permute-start | bytes 393224 | tf_op jit(solution)/shard_map/ppermute | solution.py:21
  29.7 5.1 %collective-permute-start.9 = (bf16[1,32,16,128]{3,2,1,0:T(8,128)(2,1)S(1)}, bf16[1,32,16,128]{3,2,1,0:T(8,128)(2,1)S(1)}, u32[]{:S(2)}, u32[]{:S(2)}) collective-permute-start(bf16[1,32,16,128]{3,2,1,0:T(8,128)(2,1)S(1)} %collective-permute-done.6), channel_id=1, source_target_pairs={{0,2},{1,5},{2,0},{3,7},{4,6},{5,1},{6,4},{7,3},{8,10},{9,13},{10,... | collective-permute-start | bytes 393224 | tf_op jit(solution)/shard_map/ppermute | solution.py:30
  35.3 2.2 %collective-permute-start.13 = (bf16[5,32,16,128]{3,2,1,0:T(8,128)(2,1)S(1)}, bf16[5,32,16,128]{3,2,1,0:T(8,128)(2,1)S(1)}, u32[]{:S(2)}, u32[]{:S(2)}) collective-permute-start(bf16[5,32,16,128]{3,2,1,0:T(8,128)(2,1)S(1)} %constant_dynamic-update-slice_fusion.9), channel_id=1, source_target_pairs={{0,1},{1,0},{2,3},{3,2},{4,5},{5,4},{6,7},{7,6},{8,9},{9,8},{10,11... | collective-permute-start | bytes 1966088 | tf_op jit(solution)/shard_map/ppermute | solution.py:21
  42.3 1.2 %collective-permute-start.14 = (f32[16,128]{1,0:T(8,128)S(1)}, f32[16,128]{1,0:T(8,128)S(1)}, u32[]{:S(2)}, u32[]{:S(2)}) collective-permute-start(f32[16,128]{1,0:T(8,128)S(1)} %get-tuple-element.62), channel_id=1, source_target_pairs={{0,1},{1,0},{2,3},{3,2},{4,5},{5,4},{6,7},{7,6},{8,9},{9,8},{10,11... | collective-permute-start | bytes 24584 | tf_op jit(solution)/shard_map/ppermute | solution.py:21

commit v18 on v14

--- a/solution.py
+++ b/solution.py
@@ -30,17 +30,6 @@
     return lax.ppermute(x, ("chan", "rad"), pairs)
 
 
-def early_pieces(nz):
-    some, odd = [1] + list(range(2, nz, 2)), list(range(3, nz, 2))
-    order = [(0, 0)] + [(z, 0) for z in some] + [(0, 1), (0, 2), (0, 3)] + [(z, 1) for z in some]
-    return order + [(z, 0) for z in odd] + [(z, 3) for z in odd] + [(z, 2) for z in some]
-
-
-def late_pieces(nz):
-    even, odd = list(range(2, nz, 2)), list(range(3, nz, 2))
-    return [(z, 1) for z in odd] + [(z, 2) for z in odd] + [(z, 3) for z in even] + [(1, 3)]
-
-
 def table_piece(z, part, nz):
     some, odd = nz // 2, nz // 2 - 1
     is_odd = (z & 1 == 1) & (z > 1)
@@ -51,10 +40,21 @@
         return jnp.where(z == 0, own, jnp.where(is_odd, of_odd + i, of_some + i))
 
     here = pick(0, 1, 2 * some + 4)
-    near = pick(some + 1, some + 4, base + odd + some)
-    far = pick(some + 2, base + odd, base + 2 * odd + some)
-    both = jnp.where(z == 1, 4 * nz - 1, pick(some + 3, base + 3 * odd + some - 1, base))
+    near = pick(some + 1, some + 4, base + some)
+    far = pick(some + 2, base, base + some + odd)
+    both = pick(some + 3, base + some + 2 * odd, base + 2 * some + 2 * odd)
     return jnp.where(part == 0, here, jnp.where(part == 1, near, jnp.where(part == 2, far, both)))
+
+
+def early_pieces(nz):
+    some, odd = [1] + list(range(2, nz, 2)), list(range(3, nz, 2))
+    order = [(0, 0)] + [(z, 0) for z in some] + [(0, 1), (0, 2), (0, 3)] + [(z, 1) for z in some]
+    return order + [(z, 0) for z in odd] + [(z, 2) for z in some]
+
+
+def late_pieces(nz):
+    some, odd = [1] + list(range(2, nz, 2)), list(range(3, nz, 2))
+    return [(z, 1) for z in odd] + [(z, 2) for z in odd] + [(z, 3) for z in some + odd]
 
 
 def merge(refs, table_ref, order, start, share):
@@ -77,7 +77,7 @@
                 table_ref[((start + i) * n_rad + g) * share + n] = row
         return carry
 
-    lax.fori_loop(0, share, rows, 0)
+    lax.fori_loop(0, share, rows, 0, unroll=min(8, share))
 
 
 def in_vmem(x):
@@ -147,7 +147,7 @@
         for c in range(place.shape[0]):
             found = found + jnp.where(wanted == 128 * c, place[c : c + 1], 0.0)
         columns.append(jnp.sum(found, axis=1, keepdims=True))
-    rows_ref[...] = jnp.concatenate(columns, axis=1).astype(jnp.int32)
+    rows_ref[...] = jnp.concatenate(columns, axis=1).T.astype(jnp.int32)
     copies[4].wait()
 
 
@@ -156,18 +156,18 @@
 
 
 def apply_kernel(nz, share, rows_ref, ham_ref, _, zhm_ref, zl_ref, dc_ref, gt_ref, *rest):
-    last, (az_ref, sums_ref, table_ref) = rest[:-3], rest[-3:]
+    last, (az_ref, sums_ref, table_ref, a0_ref) = rest[:-4], rest[-4:]
     merge(last, table_ref, late_pieces(nz), len(early_pieces(nz)), share)
     ch, ncoup, r, splines = ham_ref.shape
     k = zl_ref.shape[0] // 2
     group = 256 // r
 
-    def work(g, gram):
+    def work(g, carry):
         left, right = [], []
         for i in range(group):
             p = g * group + i
             left.append(
-                jnp.concatenate([table_ref[rows_ref[p, j]] for j in range(ncoup)], axis=1)
+                jnp.concatenate([table_ref[rows_ref[j, p]] for j in range(ncoup)], axis=1)
             )
             right.append(jnp.concatenate([ham_ref[p, j] for j in range(ncoup)], axis=1))
         product = lax.dot_general(
@@ -177,16 +177,24 @@
             preferred_element_type=F32,
         )
         own = [product[i * k : (i + 1) * k, i * r : (i + 1) * r] for i in range(group)]
-        at = pl.ds(pl.multiple_of(g * 256, 256), 256)
-        a0 = jnp.concatenate(own, axis=1) * SCALE
+        a0_ref[:, pl.ds(pl.multiple_of(g * 256, 256), 256)] = jnp.concatenate(own, axis=1) * SCALE
+        return carry
+
+    lax.fori_loop(0, ch // group, work, 0, unroll=min(4, ch // group))
+
+    lanes = ch * r
+    block = min(lanes, 1024)
+
+    def gram_block(i, gram):
+        at = pl.ds(pl.multiple_of(i * block, block), block)
+        a0 = a0_ref[:, at]
         a1_terms = split3(a0 / dc_ref[:, at])
         az_ref[:, at] = jnp.concatenate(a1_terms[:2], axis=0)
         right = jnp.concatenate(a1_terms + split3(a0), axis=0)
         left = jnp.concatenate([zhm_ref[:, at], zl_ref[:, at], right[: 3 * k]], axis=0)
         return gram + lax.dot_general(left, right, NT, preferred_element_type=F32)
 
-    groups = ch // group
-    gram = lax.fori_loop(0, groups, work, jnp.zeros((9 * k, 6 * k), F32), unroll=min(4, groups))
+    gram = lax.fori_loop(0, lanes // block, gram_block, jnp.zeros((9 * k, 6 * k), F32))
     ta1 = block_sum(gram[: 6 * k, : 3 * k], 2 * k, k)
     ta0 = block_sum(gram[: 6 * k, 3 * k :], 2 * k, k)
     aa = block_sum(gram[6 * k :, : 3 * k], k, k)
@@ -296,7 +304,7 @@
         in_specs=[any_] * 5,
         out_specs=[whole] * 6,
         out_shape=[
-            jax.ShapeDtypeStruct((ch, ncoup), jnp.int32),
+            jax.ShapeDtypeStruct((ncoup, ch), jnp.int32),
             pltpu.VMEM(ham_blocks.shape, BF16),
             pltpu.VMEM((4 * k, lanes), BF16),
             pltpu.VMEM((2 * k, lanes), BF16),
@@ -323,15 +331,13 @@
     some, z_even, diag0 = barrier((jnp.concatenate([z1, z_even]), z_even, diag0))
     near1, far1 = near_of(some), far_of(some)
     z_odd = swap(z_even, "chan", 4)
+    z_odd, far1, near1, diag0 = barrier((z_odd, far1, near1, diag0))
+    early = in_cores(
+        jnp.concatenate([own, z1, z_even, near0, far_own, diag0, near1, z_odd, far1])
+    )
+    near_odd = near_of(z_odd)
     diag_odd = jnp.concatenate([swap(diag0, "chan", 4 * z) for z in range(3, nz, 2)])
-    diag_odd, z_odd, far1, near1, diag0 = barrier(
-        (diag_odd, z_odd, far1, near1, diag0)
-    )
-    early = in_cores(
-        jnp.concatenate([own, z1, z_even, near0, far_own, diag0, near1, z_odd, diag_odd, far1])
-    )
-    near_odd, diag1 = near_of(z_odd), swap(diag0, "chan", 4)
-    far2 = far_of(jnp.concatenate([z_odd, near1[1:]]))
+    far2 = far_of(jnp.concatenate([z_odd, near1]))
     table = pl.pallas_call(
         functools.partial(assemble_kernel, nz, share),
         in_specs=[whole] * n_rad,
@@ -340,8 +346,8 @@
         compiler_params=pltpu.CompilerParams(vmem_limit_bytes=VMEM_LIMIT),
         name="assemble",
     )(*[in_vmem(flat(x)) for x in early])
-    diag1, near_odd, far2, table, rows = barrier((diag1, near_odd, far2, table, rows))
-    last = [in_vmem(flat(x)) for x in in_cores(jnp.concatenate([near_odd, far2, diag1]))]
+    near_odd, diag_odd, far2, table = barrier((near_odd, diag_odd, far2, table))
+    last = [in_vmem(flat(x)) for x in in_cores(jnp.concatenate([near_odd, far2, diag_odd]))]
 
     az, sums, _ = pl.pallas_call(
         functools.partial(apply_kernel, nz, share),
@@ -353,6 +359,7 @@
             pltpu.VMEM(table.shape, BF16),
         ],
         input_output_aliases={2: 2},
+        scratch_shapes=[pltpu.VMEM((k, lanes), F32)],
         compiler_params=pltpu.CompilerParams(vmem_limit_bytes=VMEM_LIMIT),
         name="apply",
     )(rows, in_vmem(ham), in_vmem(table), in_vmem(zhm), in_vmem(zl), in_vmem(dc), gram_t, *last)

time: 62.3 us -> 57.6 us (0.925)
  Pallas kernels: 19.3 us -> 13.2 us
  waiting for transfers between devices: 9.78 us -> 12.6 us
  starting transfers between devices: 17.8 us -> 16.9 us
    pallas_call x1, Pallas kernels: 9.49 us -> 5.41 us  [body(): pl.pallas_call(functools.partial(apply_kernel, nz, share), in_specs=[smem...]
    pallas_call x1, Pallas kernels: 3.11 us -> 1.05 us  [body(): pl.pallas_call(functools.partial(assemble_kernel, nz, share), in_specs=[w...]
    ppermute x9 -> x8, waiting for transfers between devices: 8.39 us -> 10.2 us  [swap(): return lax.ppermute(x, axis, [(i, i ^ distance) for i in range(n)])]
    ppermute x6, starting transfers between devices: 6.01 us -> 4.64 us  [plane_swap(): return lax.ppermute(x, ('chan', 'rad'), pairs)]
    ppermute x6, waiting for transfers between devices: 1.38 us -> 2.35 us  [plane_swap(): return lax.ppermute(x, ('chan', 'rad'), pairs)]
    ppermute x9 -> x8, starting transfers between devices: 11.8 us -> 12.3 us  [swap(): return lax.ppermute(x, axis, [(i, i ^ distance) for i in range(n)])]
  transfers between devices with their start and end apart: 15 -> 14, of which waited for: 7 -> 10; matrix products, arithmetic and copies ran while one was open for 0% -> 0% of each run, Pallas kernels for 11% -> 8%
where the time goes in v18:
time: 57.6 us; the launch traced here: 57.4 us
  starting transfers between devices  16.9 us (29%)
  Pallas kernels  13.2 us (23%)
  waiting for transfers between devices  12.6 us (22%)
  blocking collectives  12.4 us (22%)
  other arithmetic  1.26 us (2%)
  between operations  0.78 us (1%)
    all_to_all x1, blocking collectives, gather_sums(): lax.all_to_all(every, 'chan', split_axis=0, concat_axis=0, tiled=True)  12.4 us
    ppermute x8, starting transfers between devices, swap(): return lax.ppermute(x, axis, [(i, i ^ distance) for i in range(n)])  12.3 us
    ppermute x8, waiting for transfers between devices, swap(): return lax.ppermute(x, axis, [(i, i ^ distance) for i in range(n)])  10.2 us
    pallas_call x1, Pallas kernels, body(): pl.pallas_call(functools.partial(apply_kernel, nz, share), in_specs=[smem...  5.41 us
    ppermute x6, starting transfers between devices, plane_swap(): return lax.ppermute(x, ('chan', 'rad'), pairs)  4.64 us
    pallas_call x1, Pallas kernels, body(): pl.pallas_call(functools.partial(prepare_kernel, n_chan, n_rad), in_specs...  3.66 us
    pallas_call x1, Pallas kernels, body(): pl.pallas_call(functools.partial(finish_kernel, total), out_shape=[jax.Sh...  3.06 us
    ppermute x6, waiting for transfers between devices, plane_swap(): return lax.ppermute(x, ('chan', 'rad'), pairs)  2.35 us
  transfers between devices with their start and end apart: 14, of which 10 were waited for; matrix products, arithmetic and copies ran while one was open for 0% of the time, Pallas kernels for 8%

profile of v18, /device:TPU:0, one launch (start us, length us, event | category | flops | bytes accessed | tf_op | source)
XLA Modules:
  0.0 57.4 jit_solution(10973947247614563726)
XLA Ops:
  0.6 1.1 %convert_element_type.3 = bf16[64,16,64]{2,1,0:T(8,128)(2,1)S(1)} convert(f32[64,16,64]{2,1,0:T(8,128)} %t_hbm.1) | non-fusion elementwise | flops 65536 | bytes 393216 | tf_op jit(solution)/shard_map/convert_element_type | solution.py:298
  1.7 0.1 constant_dynamic-update-slice_fusion.8
  1.9 4.0 %collective-permute-start.4 = (bf16[1,32,16,128]{3,2,1,0:T(8,128)(2,1)S(1)}, bf16[1,32,16,128]{3,2,1,0:T(8,128)(2,1)S(1)}, u32[]{:S(2)}, u32[]{:S(2)}) collective-permute-start(bf16[1,32,16,128]{3,2,1,0:T(8,128)(2,1)S(1)} %get-tuple-element.57), channel_id=1, source_target_pairs={{0,6},{2,4},{4,2},{6,0},{8,14},{10,12},{12,10},{14,8},{16,22},{18,... | collective-permute-start | bytes 393224 | tf_op jit(solution)/shard_map/ppermute | solution.py:21
  5.8 2.6 %collective-permute-start.3 = (bf16[1,32,16,128]{3,2,1,0:T(8,128)(2,1)S(1)}, bf16[1,32,16,128]{3,2,1,0:T(8,128)(2,1)S(1)}, u32[]{:S(2)}, u32[]{:S(2)}) collective-permute-start(bf16[1,32,16,128]{3,2,1,0:T(8,128)(2,1)S(1)} %get-tuple-element.57), channel_id=1, source_target_pairs={{0,16},{2,18},{4,20},{6,22},{8,24},{10,26},{12,28},{14,30},{16,0},... | collective-permute-start | bytes 393224 | tf_op jit(solution)/shard_map/ppermute | solution.py:21
  8.4 1.6 %collective-permute-start.2 = (bf16[1,32,16,128]{3,2,1,0:T(8,128)(2,1)S(1)}, bf16[1,32,16,128]{3,2,1,0:T(8,128)(2,1)S(1)}, u32[]{:S(2)}, u32[]{:S(2)}) collective-permute-start(bf16[1,32,16,128]{3,2,1,0:T(8,128)(2,1)S(1)} %get-tuple-element.57), channel_id=1, source_target_pairs={{0,8},{2,10},{4,12},{6,14},{8,0},{10,2},{12,4},{14,6},{16,24},{18,... | collective-permute-start | bytes 393224 | tf_op jit(solution)/shard_map/ppermute | solution.py:21
  10.0 0.5 collective-permute-start.1
  10.5 0.5 collective-permute-start
  11.0 3.7 %prepare.1 = (s32[8,64]{1,0:T(8,128)S(1)}, bf16[64,8,64,128]{3,2,1,0:T(8,128)(2,1)S(1)}, bf16[64,4096]{1,0:T(8,128)(2,1)S(1)}, bf16[32,4096]{1,0:T(8,128)(2,1)S(...) custom-call(f32[64,16,64]{2,1,0:T(8,128)} %t_hbm.1, f32[64,64]{1,0:T(8,128)} %d_hbm.1, s32[8,64]{1,0:T(8,128)} %bitcast.14, ...), custom_call_target="tpu_custom_call" | custom-call | tf_op jit(solution)/shard_map/prepare/pallas_call | solution.py:302
  14.7 0.1 collective-permute-done.2
  14.8 0.2 collective-permute-done.1
  14.9 0.5 collective-permute-done
  15.5 1.6 %collective-permute-start.7 = (bf16[2,32,16,128]{3,2,1,0:T(8,128)(2,1)S(1)}, bf16[2,32,16,128]{3,2,1,0:T(8,128)(2,1)S(1)}, u32[]{:S(2)}, u32[]{:S(2)}) collective-permute-start(bf16[2,32,16,128]{3,2,1,0:T(8,128)(2,1)S(1)} %pad_maximum_fusion.1), channel_id=1, source_target_pairs={{0,2},{1,5},{2,0},{3,7},{4,6},{5,1},{6,4},{7,3},{8,10},{9,13},{10,... | collective-permute-start | bytes 786440 | tf_op jit(solution)/shard_map/ppermute | solution.py:30
  17.1 0.8 %collective-permute-start.6 = (bf16[2,32,16,128]{3,2,1,0:T(8,128)(2,1)S(1)}, bf16[2,32,16,128]{3,2,1,0:T(8,128)(2,1)S(1)}, u32[]{:S(2)}, u32[]{:S(2)}) collective-permute-start(bf16[2,32,16,128]{3,2,1,0:T(8,128)(2,1)S(1)} %pad_maximum_fusion.1), channel_id=1, source_target_pairs={{0,4},{1,3},{2,6},{3,1},{4,0},{5,7},{6,2},{7,5},{8,12},{9,11},{10,... | collective-permute-start | bytes 786440 | tf_op jit(solution)/shard_map/ppermute | solution.py:30
  17.9 0.5 collective-permute-start.5
  18.5 4.4 %collective-permute-done.5 = bf16[1,32,16,128]{3,2,1,0:T(8,128)(2,1)S(1)} collective-permute-done((bf16[1,32,16,128]{3,2,1,0:T(8,128)(2,1)S(1)}, bf16[1,32,16,128]{3,2,1,0:T(8,128)(2,1)S(1)}, u32[]{:S(2)}, u32[]{:S(2)}) %collective-permute-start.5) | collective-permute-done | bytes 131104 | tf_op jit(solution)/shard_map/ppermute | solution.py:21
  22.9 0.7 %collective-permute-done.7 = bf16[2,32,16,128]{3,2,1,0:T(8,128)(2,1)S(1)} collective-permute-done((bf16[2,32,16,128]{3,2,1,0:T(8,128)(2,1)S(1)}, bf16[2,32,16,128]{3,2,1,0:T(8,128)(2,1)S(1)}, u32[]{:S(2)}, u32[]{:S(2)}) %collective-permute-start.7) | collective-permute-done | bytes 262176 | tf_op jit(solution)/shard_map/ppermute | solution.py:30
  23.7 0.1 collective-permute-start.11
  23.8 0.7 %collective-permute-start.10 = (bf16[3,32,16,128]{3,2,1,0:T(8,128)(2,1)S(1)}, bf16[3,32,16,128]{3,2,1,0:T(8,128)(2,1)S(1)}, u32[]{:S(2)}, u32[]{:S(2)}) collective-permute-start(bf16[3,32,16,128]{3,2,1,0:T(8,128)(2,1)S(1)} %pad_maximum_fusion), channel_id=1, source_target_pairs={{0,4},{1,3},{2,6},{3,1},{4,0},{5,7},{6,2},{7,5},{8,12},{9,11},{10,... | collective-permute-start | bytes 1179656 | tf_op jit(solution)/shard_map/ppermute | solution.py:30
  24.6 3.3 %collective-permute-start.9 = (bf16[1,32,16,128]{3,2,1,0:T(8,128)(2,1)S(1)}, bf16[1,32,16,128]{3,2,1,0:T(8,128)(2,1)S(1)}, u32[]{:S(2)}, u32[]{:S(2)}) collective-permute-start(bf16[1,32,16,128]{3,2,1,0:T(8,128)(2,1)S(1)} %collective-permute-done.4), channel_id=1, source_target_pairs={{0,24},{2,26},{4,28},{6,30},{8,16},{10,18},{12,20},{14,22},{16,8},... | collective-permute-start | bytes 393224 | tf_op jit(solution)/shard_map/ppermute | solution.py:21
  27.9 0.5 collective-permute-start.8
  28.4 1.1 %assemble.1._ = bf16[1024,16,128]{2,1,0:T(8,128)(2,1)S(1)} custom-call(bf16[352,16,128]{2,1,0:T(8,128)(2,1)S(1)} %bitcast.10, bf16[352,16,128]{2,1,0:T(8,128)(2,1)S(1)} %bitcast.11), custom_call_target="tpu_custom_call" | custom-call | tf_op jit(solution)/shard_map/assemble/pallas_call | solution.py:341
  29.5 2.6 %collective-permute-done.9 = bf16[1,32,16,128]{3,2,1,0:T(8,128)(2,1)S(1)} collective-permute-done((bf16[1,32,16,128]{3,2,1,0:T(8,128)(2,1)S(1)}, bf16[1,32,16,128]{3,2,1,0:T(8,128)(2,1)S(1)}, u32[]{:S(2)}, u32[]{:S(2)}) %collective-permute-start.9) | collective-permute-done | bytes 131104 | tf_op jit(solution)/shard_map/ppermute | solution.py:21
  32.1 0.8 %collective-permute-done.8 = bf16[1,32,16,128]{3,2,1,0:T(8,128)(2,1)S(1)} collective-permute-done((bf16[1,32,16,128]{3,2,1,0:T(8,128)(2,1)S(1)}, bf16[1,32,16,128]{3,2,1,0:T(8,128)(2,1)S(1)}, u32[]{:S(2)}, u32[]{:S(2)}) %collective-permute-start.8) | collective-permute-done | bytes 131104 | tf_op jit(solution)/shard_map/ppermute | solution.py:30
  32.9 0.2 collective-permute-done.10
  33.1 0.1 constant_dynamic-update-slice_fusion.10
  33.2 0.1 collective-permute-start.12
  33.3 2.1 %collective-permute-done.12 = bf16[5,32,16,128]{3,2,1,0:T(8,128)(2,1)S(1)} collective-permute-done((bf16[5,32,16,128]{3,2,1,0:T(8,128)(2,1)S(1)}, bf16[5,32,16,128]{3,2,1,0:T(8,128)(2,1)S(1)}, u32[]{:S(2)}, u32[]{:S(2)}) %collective-permute-start.12) | collective-permute-done | bytes 655392 | tf_op jit(solution)/shard_map/ppermute | solution.py:21
  35.3 5.4 %apply.1 = (bf16[32,4096]{1,0:T(8,128)(2,1)S(1)}, f32[16,128]{1,0:T(8,128)S(1)}, bf16[1024,16,128]{2,1,0:T(8,128)(2,1)S(1)}) custom-call(s32[8,64]{1,0:T(8,128)S(1)} %get-tuple-element.30.rows_ref, bf16[64,8,64,128]{3,2,1,0:T(8,128)(2,1)S(1)} %get-tuple-element.31.ham_ref, bf16[1024,16,128]{2,1,0:T(8,128)(2,1)S(1)} %assemble.1._, ...), custom_call_target="tpu_custom_call", output_to_operand_aliasing={{2}: (2, {})} | custom-call | tf_op jit(solution)/shard_map/apply/pallas_call | solution.py:352
  40.8 0.1 collective-permute-start.13
  40.9 1.0 %collective-permute-done.13 = f32[16,128]{1,0:T(8,128)S(1)} collective-permute-done((f32[16,128]{1,0:T(8,128)S(1)}, f32[16,128]{1,0:T(8,128)S(1)}, u32[]{:S(2)}, u32[]{:S(2)}) %collective-permute-start.13) | collective-permute-done | bytes 8224 | tf_op jit(solution)/shard_map/ppermute | solution.py:21
  42.0 12.4 %all_to_all.5.sums_ref = f32[16,16,128]{2,1,0:T(8,128)S(1)} all-to-all(f32[16,16,128]{2,1,0:T(8,128)S(1)} %broadcast_in_dim.7), channel_id=1, replica_groups=mesh['chan'=16,'rad'=2] {'chan'}, dimensions={0} | all-to-all | bytes 262144 | tf_op jit(solution)/shard_map/all_to_all | solution.py:270
  54.4 3.1 %finish.1 = (f32[64,16,64]{2,1,0:T(8,128)}, f32[1,16]{1,0:T(1,128)}) custom-call(f32[16,16,128]{2,1,0:T(8,128)S(1)} %all_to_all.5.sums_ref, bf16[32,4096]{1,0:T(8,128)(2,1)S(1)} %get-tuple-element.53.az_ref, bf16[64,4096]{1,0:T(8,128)(2,1)S(1)} %get-tuple-element.45.zhm_ref), custom_call_target="tpu_custom_call" | custom-call | tf_op jit(solution)/shard_map/finish/pallas_call | solution.py:368
  (19 shorter events, 0.3 us)
Async XLA Ops:
  1.9 12.8 %collective-permute-start.4 = (bf16[1,32,16,128]{3,2,1,0:T(8,128)(2,1)S(1)}, bf16[1,32,16,128]{3,2,1,0:T(8,128)(2,1)S(1)}, u32[]{:S(2)}, u32[]{:S(2)}) collective-permute-start(bf16[1,32,16,128]{3,2,1,0:T(8,128)(2,1)S(1)} %get-tuple-element.57), channel_id=1, source_target_pairs={{0,6},{2,4},{4,2},{6,0},{8,14},{10,12},{12,10},{14,8},{16,22},{18,... | collective-permute-start | bytes 393224 | tf_op jit(solution)/shard_map/ppermute | solution.py:21
  5.8 8.9 %collective-permute-start.3 = (bf16[1,32,16,128]{3,2,1,0:T(8,128)(2,1)S(1)}, bf16[1,32,16,128]{3,2,1,0:T(8,128)(2,1)S(1)}, u32[]{:S(2)}, u32[]{:S(2)}) collective-permute-start(bf16[1,32,16,128]{3,2,1,0:T(8,128)(2,1)S(1)} %get-tuple-element.57), channel_id=1, source_target_pairs={{0,16},{2,18},{4,20},{6,22},{8,24},{10,26},{12,28},{14,30},{16,0},... | collective-permute-start | bytes 393224 | tf_op jit(solution)/shard_map/ppermute | solution.py:21
  8.4 6.4 %collective-permute-start.2 = (bf16[1,32,16,128]{3,2,1,0:T(8,128)(2,1)S(1)}, bf16[1,32,16,128]{3,2,1,0:T(8,128)(2,1)S(1)}, u32[]{:S(2)}, u32[]{:S(2)}) collective-permute-start(bf16[1,32,16,128]{3,2,1,0:T(8,128)(2,1)S(1)} %get-tuple-element.57), channel_id=1, source_target_pairs={{0,8},{2,10},{4,12},{6,14},{8,0},{10,2},{12,4},{14,6},{16,24},{18,... | collective-permute-start | bytes 393224 | tf_op jit(solution)/shard_map/ppermute | solution.py:21
  10.0 5.0 %collective-permute-start.1 = (bf16[1,32,16,128]{3,2,1,0:T(8,128)(2,1)S(1)}, bf16[1,32,16,128]{3,2,1,0:T(8,128)(2,1)S(1)}, u32[]{:S(2)}, u32[]{:S(2)}) collective-permute-start(bf16[1,32,16,128]{3,2,1,0:T(8,128)(2,1)S(1)} %get-tuple-element.57), channel_id=1, source_target_pairs={{0,2},{1,5},{2,0},{3,7},{4,6},{5,1},{6,4},{7,3},{8,10},{9,13},{10,... | collective-permute-start | bytes 393224 | tf_op jit(solution)/shard_map/ppermute | solution.py:30
  10.5 5.0 %collective-permute-start = (bf16[1,32,16,128]{3,2,1,0:T(8,128)(2,1)S(1)}, bf16[1,32,16,128]{3,2,1,0:T(8,128)(2,1)S(1)}, u32[]{:S(2)}, u32[]{:S(2)}) collective-permute-start(bf16[1,32,16,128]{3,2,1,0:T(8,128)(2,1)S(1)} %get-tuple-element.57), channel_id=1, source_target_pairs={{0,4},{1,3},{2,6},{3,1},{4,0},{5,7},{6,2},{7,5},{8,12},{9,11},{10,... | collective-permute-start | bytes 393224 | tf_op jit(solution)/shard_map/ppermute | solution.py:30
  15.5 8.0 %collective-permute-start.7 = (bf16[2,32,16,128]{3,2,1,0:T(8,128)(2,1)S(1)}, bf16[2,32,16,128]{3,2,1,0:T(8,128)(2,1)S(1)}, u32[]{:S(2)}, u32[]{:S(2)}) collective-permute-start(bf16[2,32,16,128]{3,2,1,0:T(8,128)(2,1)S(1)} %pad_maximum_fusion.1), channel_id=1, source_target_pairs={{0,2},{1,5},{2,0},{3,7},{4,6},{5,1},{6,4},{7,3},{8,10},{9,13},{10,... | collective-permute-start | bytes 786440 | tf_op jit(solution)/shard_map/ppermute | solution.py:30
  17.1 6.5 %collective-permute-start.6 = (bf16[2,32,16,128]{3,2,1,0:T(8,128)(2,1)S(1)}, bf16[2,32,16,128]{3,2,1,0:T(8,128)(2,1)S(1)}, u32[]{:S(2)}, u32[]{:S(2)}) collective-permute-start(bf16[2,32,16,128]{3,2,1,0:T(8,128)(2,1)S(1)} %pad_maximum_fusion.1), channel_id=1, source_target_pairs={{0,4},{1,3},{2,6},{3,1},{4,0},{5,7},{6,2},{7,5},{8,12},{9,11},{10,... | collective-permute-start | bytes 786440 | tf_op jit(solution)/shard_map/ppermute | solution.py:30
  17.9 5.0 %collective-permute-start.5 = (bf16[1,32,16,128]{3,2,1,0:T(8,128)(2,1)S(1)}, bf16[1,32,16,128]{3,2,1,0:T(8,128)(2,1)S(1)}, u32[]{:S(2)}, u32[]{:S(2)}) collective-permute-start(bf16[1,32,16,128]{3,2,1,0:T(8,128)(2,1)S(1)} %collective-permute-done.3), channel_id=1, source_target_pairs={{0,8},{2,10},{4,12},{6,14},{8,0},{10,2},{12,4},{14,6},{16,24},{18,... | collective-permute-start | bytes 393224 | tf_op jit(solution)/shard_map/ppermute | solution.py:21
  23.7 4.7 %collective-permute-start.11 = (bf16[11,32,16,128]{3,2,1,0:T(8,128)(2,1)S(1)}, bf16[11,32,16,128]{3,2,1,0:T(8,128)(2,1)S(1)}, u32[]{:S(2)}, u32[]{:S(2)}) collective-permute-start(bf16[11,32,16,128]{3,2,1,0:T(8,128)(2,1)S(1)} %constant_dynamic-update-slice_fusion), channel_id=1, source_target_pairs={{0,1},{1,0},{2,3},{3,2},{4,5},{5,4},{6,7},{7,6},{8,9},{9,8},{10,11... | collective-permute-start | bytes 4325384 | tf_op jit(solution)/shard_map/ppermute | solution.py:21
  23.8 9.2 %collective-permute-start.10 = (bf16[3,32,16,128]{3,2,1,0:T(8,128)(2,1)S(1)}, bf16[3,32,16,128]{3,2,1,0:T(8,128)(2,1)S(1)}, u32[]{:S(2)}, u32[]{:S(2)}) collective-permute-start(bf16[3,32,16,128]{3,2,1,0:T(8,128)(2,1)S(1)} %pad_maximum_fusion), channel_id=1, source_target_pairs={{0,4},{1,3},{2,6},{3,1},{4,0},{5,7},{6,2},{7,5},{8,12},{9,11},{10,... | collective-permute-start | bytes 1179656 | tf_op jit(solution)/shard_map/ppermute | solution.py:30
  24.6 7.5 %collective-permute-start.9 = (bf16[1,32,16,128]{3,2,1,0:T(8,128)(2,1)S(1)}, bf16[1,32,16,128]{3,2,1,0:T(8,128)(2,1)S(1)}, u32[]{:S(2)}, u32[]{:S(2)}) collective-permute-start(bf16[1,32,16,128]{3,2,1,0:T(8,128)(2,1)S(1)} %collective-permute-done.4), channel_id=1, source_target_pairs={{0,24},{2,26},{4,28},{6,30},{8,16},{10,18},{12,20},{14,22},{16,8},... | collective-permute-start | bytes 393224 | tf_op jit(solution)/shard_map/ppermute | solution.py:21
  27.9 5.0 %collective-permute-start.8 = (bf16[1,32,16,128]{3,2,1,0:T(8,128)(2,1)S(1)}, bf16[1,32,16,128]{3,2,1,0:T(8,128)(2,1)S(1)}, u32[]{:S(2)}, u32[]{:S(2)}) collective-permute-start(bf16[1,32,16,128]{3,2,1,0:T(8,128)(2,1)S(1)} %collective-permute-done.5), channel_id=1, source_target_pairs={{0,2},{1,5},{2,0},{3,7},{4,6},{5,1},{6,4},{7,3},{8,10},{9,13},{10,... | collective-permute-start | bytes 393224 | tf_op jit(solution)/shard_map/ppermute | solution.py:30
  33.2 2.2 %collective-permute-start.12 = (bf16[5,32,16,128]{3,2,1,0:T(8,128)(2,1)S(1)}, bf16[5,32,16,128]{3,2,1,0:T(8,128)(2,1)S(1)}, u32[]{:S(2)}, u32[]{:S(2)}) collective-permute-start(bf16[5,32,16,128]{3,2,1,0:T(8,128)(2,1)S(1)} %constant_dynamic-update-slice_fusion.9), channel_id=1, source_target_pairs={{0,1},{1,0},{2,3},{3,2},{4,5},{5,4},{6,7},{7,6},{8,9},{9,8},{10,11... | collective-permute-start | bytes 1966088 | tf_op jit(solution)/shard_map/ppermute | solution.py:21
  40.8 1.2 %collective-permute-start.13 = (f32[16,128]{1,0:T(8,128)S(1)}, f32[16,128]{1,0:T(8,128)S(1)}, u32[]{:S(2)}, u32[]{:S(2)}) collective-permute-start(f32[16,128]{1,0:T(8,128)S(1)} %get-tuple-element.52), channel_id=1, source_target_pairs={{0,1},{1,0},{2,3},{3,2},{4,5},{5,4},{6,7},{7,6},{8,9},{9,8},{10,11... | collective-permute-start | bytes 24584 | tf_op jit(solution)/shard_map/ppermute | solution.py:21

commit v19 on v18

--- a/solution.py
+++ b/solution.py
@@ -34,22 +34,23 @@
     some, odd = nz // 2, nz // 2 - 1
     is_odd = (z & 1 == 1) & (z > 1)
     i = jnp.where(is_odd, (z - 3) >> 1, jnp.where(z == 1, 0, z >> 1))
-    base = 2 * some + odd + 4
+    base = 2 * some + odd + 3
+    late = base + some + 1
 
     def pick(own, of_some, of_odd):
         return jnp.where(z == 0, own, jnp.where(is_odd, of_odd + i, of_some + i))
 
-    here = pick(0, 1, 2 * some + 4)
-    near = pick(some + 1, some + 4, base + some)
-    far = pick(some + 2, base, base + some + odd)
-    both = pick(some + 3, base + some + 2 * odd, base + 2 * some + 2 * odd)
+    here = pick(0, 1, 2 * some + 3)
+    near = pick(some + 1, some + 3, late)
+    far = pick(some + 2, base, late + odd)
+    both = pick(late - 1, late + 2 * odd, late + 2 * odd + some)
     return jnp.where(part == 0, here, jnp.where(part == 1, near, jnp.where(part == 2, far, both)))
 
 
 def early_pieces(nz):
     some, odd = [1] + list(range(2, nz, 2)), list(range(3, nz, 2))
-    order = [(0, 0)] + [(z, 0) for z in some] + [(0, 1), (0, 2), (0, 3)] + [(z, 1) for z in some]
-    return order + [(z, 0) for z in odd] + [(z, 2) for z in some]
+    order = [(0, 0)] + [(z, 0) for z in some] + [(0, 1), (0, 2)] + [(z, 1) for z in some]
+    return order + [(z, 0) for z in odd] + [(z, 2) for z in some] + [(0, 3)]
 
 
 def late_pieces(nz):
@@ -257,7 +258,7 @@
             out_ref[b * (block // r) + i] = new[:, i * r : (i + 1) * r]
         return carry
 
-    lax.fori_loop(0, ch * r // block, result, 0)
+    lax.fori_loop(0, ch * r // block, result, 0, unroll=True)
 
 
 def gather_sums(x):
@@ -296,7 +297,7 @@
         return [x] + [swap(x, "rad", c) for c in range(1, n_rad)]
 
     own = jnp.concatenate(jnp.split(trial_block.astype(BF16), n_rad), axis=2)[None]
-    near0, far_own, diag0 = near_of(own), far_of(own), swap(own, "chan", 3)
+    near0, far_own = near_of(own), far_of(own)
     z1 = swap(own, "chan", 4)
     z_even = jnp.concatenate([swap(own, "chan", 4 * z) for z in range(2, nz, 2)])
     rows, ham, zhm, zl, dc, gram_t = pl.pallas_call(
@@ -327,13 +328,15 @@
         in_hbm(stored_at.reshape(-1, 128)),
         in_hbm(ham_blocks),
     )
-    far_own, near0, z1, z_even, diag0, rows = barrier((far_own, near0, z1, z_even, diag0, rows))
-    some, z_even, diag0 = barrier((jnp.concatenate([z1, z_even]), z_even, diag0))
-    near1, far1 = near_of(some), far_of(some)
+    far_own, near0, z1, z_even, rows = barrier((far_own, near0, z1, z_even, rows))
+    some = jnp.concatenate([z1, z_even])
+    some, more, z_even = barrier((some, jnp.concatenate([some, near0]), z_even))
+    near1, far1 = near_of(some), far_of(more)
     z_odd = swap(z_even, "chan", 4)
-    z_odd, far1, near1, diag0 = barrier((z_odd, far1, near1, diag0))
+    z_odd, far1, near1 = barrier((z_odd, far1, near1))
+    diag0 = far1[-1:]
     early = in_cores(
-        jnp.concatenate([own, z1, z_even, near0, far_own, diag0, near1, z_odd, far1])
+        jnp.concatenate([own, z1, z_even, near0, far_own, near1, z_odd, far1])
     )
     near_odd = near_of(z_odd)
     diag_odd = jnp.concatenate([swap(diag0, "chan", 4 * z) for z in range(3, nz, 2)])

time: 57.6 us -> 58 us (level)
  waiting for transfers between devices: 12.6 us -> 13.6 us
  Pallas kernels: 13.2 us -> 12.6 us
    ppermute x8 -> x7, starting transfers between devices: 12.3 us -> 9.31 us  [swap(): return lax.ppermute(x, axis, [(i, i ^ distance) for i in range(n)])]
    ppermute x6, starting transfers between devices: 4.64 us -> 7.32 us  [plane_swap(): return lax.ppermute(x, ('chan', 'rad'), pairs)]
    ppermute x6, waiting for transfers between devices: 2.35 us -> 4.75 us  [plane_swap(): return lax.ppermute(x, ('chan', 'rad'), pairs)]
    ppermute x8 -> x7, waiting for transfers between devices: 10.2 us -> 8.89 us  [swap(): return lax.ppermute(x, axis, [(i, i ^ distance) for i in range(n)])]
    pallas_call x1, Pallas kernels: 3.06 us -> 2.47 us  [body(): pl.pallas_call(functools.partial(finish_kernel, total), out_shape=[jax.Sh...]
  transfers between devices with their start and end apart: 14 -> 13, of which waited for: 10 -> 8; matrix products, arithmetic and copies ran while one was open for 0% -> 0% of each run, Pallas kernels for 8% -> 8%
where the time goes in v19:
time: 58 us; the launch traced here: 57.7 us
  starting transfers between devices  16.6 us (29%)
  waiting for transfers between devices  13.6 us (23%)
  Pallas kernels  12.6 us (22%)
  blocking collectives  12.5 us (22%)
  other arithmetic  1.31 us (2%)
  between operations  0.8 us (1%)
    all_to_all x1, blocking collectives, gather_sums(): lax.all_to_all(every, 'chan', split_axis=0, concat_axis=0, tiled=True)  12.5 us
    ppermute x7, starting transfers between devices, swap(): return lax.ppermute(x, axis, [(i, i ^ distance) for i in range(n)])  9.31 us
    ppermute x7, waiting for transfers between devices, swap(): return lax.ppermute(x, axis, [(i, i ^ distance) for i in range(n)])  8.89 us
    ppermute x6, starting transfers between devices, plane_swap(): return lax.ppermute(x, ('chan', 'rad'), pairs)  7.32 us
    pallas_call x1, Pallas kernels, body(): pl.pallas_call(functools.partial(apply_kernel, nz, share), in_specs=[smem...  5.41 us
    ppermute x6, waiting for transfers between devices, plane_swap(): return lax.ppermute(x, ('chan', 'rad'), pairs)  4.75 us
    pallas_call x1, Pallas kernels, body(): pl.pallas_call(functools.partial(prepare_kernel, n_chan, n_rad), in_specs...  3.66 us
    pallas_call x1, Pallas kernels, body(): pl.pallas_call(functools.partial(finish_kernel, total), out_shape=[jax.Sh...  2.47 us
  transfers between devices with their start and end apart: 13, of which 8 were waited for; matrix products, arithmetic and copies ran while one was open for 0% of the time, Pallas kernels for 8%

profile of v19, /device:TPU:0, one launch (start us, length us, event | category | flops | bytes accessed | tf_op | source)
XLA Modules:
  0.0 57.7 jit_solution(13707230084780990213)
XLA Ops:
  0.6 1.1 %convert_element_type.3 = bf16[64,16,64]{2,1,0:T(8,128)(2,1)S(1)} convert(f32[64,16,64]{2,1,0:T(8,128)} %t_hbm.1) | non-fusion elementwise | flops 65536 | bytes 393216 | tf_op jit(solution)/shard_map/convert_element_type | solution.py:299
  1.7 0.1 constant_dynamic-update-slice_fusion.7
  1.9 4.1 %collective-permute-start.3 = (bf16[1,32,16,128]{3,2,1,0:T(8,128)(2,1)S(1)}, bf16[1,32,16,128]{3,2,1,0:T(8,128)(2,1)S(1)}, u32[]{:S(2)}, u32[]{:S(2)}) collective-permute-start(bf16[1,32,16,128]{3,2,1,0:T(8,128)(2,1)S(1)} %get-tuple-element.53), channel_id=1, source_target_pairs={{0,16},{2,18},{4,20},{6,22},{8,24},{10,26},{12,28},{14,30},{16,0},... | collective-permute-start | bytes 393224 | tf_op jit(solution)/shard_map/ppermute | solution.py:21
  6.0 1.6 %collective-permute-start.2 = (bf16[1,32,16,128]{3,2,1,0:T(8,128)(2,1)S(1)}, bf16[1,32,16,128]{3,2,1,0:T(8,128)(2,1)S(1)}, u32[]{:S(2)}, u32[]{:S(2)}) collective-permute-start(bf16[1,32,16,128]{3,2,1,0:T(8,128)(2,1)S(1)} %get-tuple-element.53), channel_id=1, source_target_pairs={{0,8},{2,10},{4,12},{6,14},{8,0},{10,2},{12,4},{14,6},{16,24},{18,... | collective-permute-start | bytes 393224 | tf_op jit(solution)/shard_map/ppermute | solution.py:21
  7.5 1.5 %collective-permute-start.1 = (bf16[1,32,16,128]{3,2,1,0:T(8,128)(2,1)S(1)}, bf16[1,32,16,128]{3,2,1,0:T(8,128)(2,1)S(1)}, u32[]{:S(2)}, u32[]{:S(2)}) collective-permute-start(bf16[1,32,16,128]{3,2,1,0:T(8,128)(2,1)S(1)} %get-tuple-element.53), channel_id=1, source_target_pairs={{0,2},{1,5},{2,0},{3,7},{4,6},{5,1},{6,4},{7,3},{8,10},{9,13},{10,... | collective-permute-start | bytes 393224 | tf_op jit(solution)/shard_map/ppermute | solution.py:30
  9.0 1.5 %collective-permute-start = (bf16[1,32,16,128]{3,2,1,0:T(8,128)(2,1)S(1)}, bf16[1,32,16,128]{3,2,1,0:T(8,128)(2,1)S(1)}, u32[]{:S(2)}, u32[]{:S(2)}) collective-permute-start(bf16[1,32,16,128]{3,2,1,0:T(8,128)(2,1)S(1)} %get-tuple-element.53), channel_id=1, source_target_pairs={{0,4},{1,3},{2,6},{3,1},{4,0},{5,7},{6,2},{7,5},{8,12},{9,11},{10,... | collective-permute-start | bytes 393224 | tf_op jit(solution)/shard_map/ppermute | solution.py:30
  10.5 3.7 %prepare.1 = (s32[8,64]{1,0:T(8,128)S(1)}, bf16[64,8,64,128]{3,2,1,0:T(8,128)(2,1)S(1)}, bf16[64,4096]{1,0:T(8,128)(2,1)S(1)}, bf16[32,4096]{1,0:T(8,128)(2,1)S(...) custom-call(f32[64,16,64]{2,1,0:T(8,128)} %t_hbm.1, f32[64,64]{1,0:T(8,128)} %d_hbm.1, s32[8,64]{1,0:T(8,128)} %bitcast.14, ...), custom_call_target="tpu_custom_call" | custom-call | tf_op jit(solution)/shard_map/prepare/pallas_call | solution.py:303
  14.2 0.0 collective-permute-done.3
  14.2 0.0 collective-permute-done.2
  14.3 1.3 %collective-permute-start.5 = (bf16[3,32,16,128]{3,2,1,0:T(8,128)(2,1)S(1)}, bf16[3,32,16,128]{3,2,1,0:T(8,128)(2,1)S(1)}, u32[]{:S(2)}, u32[]{:S(2)}) collective-permute-start(bf16[3,32,16,128]{3,2,1,0:T(8,128)(2,1)S(1)} %pad_maximum_fusion), channel_id=1, source_target_pairs={{0,4},{1,3},{2,6},{3,1},{4,0},{5,7},{6,2},{7,5},{8,12},{9,11},{10,... | collective-permute-start | bytes 1179656 | tf_op jit(solution)/shard_map/ppermute | solution.py:30
  15.7 0.5 collective-permute-start.4
  16.2 1.1 %collective-permute-start.6 = (bf16[2,32,16,128]{3,2,1,0:T(8,128)(2,1)S(1)}, bf16[2,32,16,128]{3,2,1,0:T(8,128)(2,1)S(1)}, u32[]{:S(2)}, u32[]{:S(2)}) collective-permute-start(bf16[2,32,16,128]{3,2,1,0:T(8,128)(2,1)S(1)} %pad_maximum_fusion.2), channel_id=1, source_target_pairs={{0,2},{1,5},{2,0},{3,7},{4,6},{5,1},{6,4},{7,3},{8,10},{9,13},{10,... | collective-permute-start | bytes 786440 | tf_op jit(solution)/shard_map/ppermute | solution.py:30
  17.3 3.4 %collective-permute-done.4 = bf16[1,32,16,128]{3,2,1,0:T(8,128)(2,1)S(1)} collective-permute-done((bf16[1,32,16,128]{3,2,1,0:T(8,128)(2,1)S(1)}, bf16[1,32,16,128]{3,2,1,0:T(8,128)(2,1)S(1)}, u32[]{:S(2)}, u32[]{:S(2)}) %collective-permute-start.4) | collective-permute-done | bytes 131104 | tf_op jit(solution)/shard_map/ppermute | solution.py:21
  20.7 2.2 %collective-permute-done.6 = bf16[2,32,16,128]{3,2,1,0:T(8,128)(2,1)S(1)} collective-permute-done((bf16[2,32,16,128]{3,2,1,0:T(8,128)(2,1)S(1)}, bf16[2,32,16,128]{3,2,1,0:T(8,128)(2,1)S(1)}, u32[]{:S(2)}, u32[]{:S(2)}) %collective-permute-start.6) | collective-permute-done | bytes 262176 | tf_op jit(solution)/shard_map/ppermute | solution.py:30
  23.0 1.5 %collective-permute-done.5 = bf16[3,32,16,128]{3,2,1,0:T(8,128)(2,1)S(1)} collective-permute-done((bf16[3,32,16,128]{3,2,1,0:T(8,128)(2,1)S(1)}, bf16[3,32,16,128]{3,2,1,0:T(8,128)(2,1)S(1)}, u32[]{:S(2)}, u32[]{:S(2)}) %collective-permute-start.5) | collective-permute-done | bytes 393248 | tf_op jit(solution)/shard_map/ppermute | solution.py:30
  24.5 0.1 constant_dynamic-update-slice_fusion
  24.5 0.1 collective-permute-start.10
  24.7 1.0 %collective-permute-start.9 = (bf16[3,32,16,128]{3,2,1,0:T(8,128)(2,1)S(1)}, bf16[3,32,16,128]{3,2,1,0:T(8,128)(2,1)S(1)}, u32[]{:S(2)}, u32[]{:S(2)}) collective-permute-start(bf16[3,32,16,128]{3,2,1,0:T(8,128)(2,1)S(1)} %pad_maximum_fusion.1), channel_id=1, source_target_pairs={{0,4},{1,3},{2,6},{3,1},{4,0},{5,7},{6,2},{7,5},{8,12},{9,11},{10,... | collective-permute-start | bytes 1179656 | tf_op jit(solution)/shard_map/ppermute | solution.py:30
  25.7 2.8 %collective-permute-start.8 = (bf16[1,32,16,128]{3,2,1,0:T(8,128)(2,1)S(1)}, bf16[1,32,16,128]{3,2,1,0:T(8,128)(2,1)S(1)}, u32[]{:S(2)}, u32[]{:S(2)}) collective-permute-start(bf16[1,32,16,128]{3,2,1,0:T(8,128)(2,1)S(1)} %slice.3), channel_id=1, source_target_pairs={{0,24},{2,26},{4,28},{6,30},{8,16},{10,18},{12,20},{14,22},{16,8},... | collective-permute-start | bytes 393224 | tf_op jit(solution)/shard_map/ppermute | solution.py:21
  28.5 1.0 %collective-permute-start.7 = (bf16[1,32,16,128]{3,2,1,0:T(8,128)(2,1)S(1)}, bf16[1,32,16,128]{3,2,1,0:T(8,128)(2,1)S(1)}, u32[]{:S(2)}, u32[]{:S(2)}) collective-permute-start(bf16[1,32,16,128]{3,2,1,0:T(8,128)(2,1)S(1)} %collective-permute-done.4), channel_id=1, source_target_pairs={{0,2},{1,5},{2,0},{3,7},{4,6},{5,1},{6,4},{7,3},{8,10},{9,13},{10,... | collective-permute-start | bytes 393224 | tf_op jit(solution)/shard_map/ppermute | solution.py:30
  29.4 1.1 %assemble.1._ = bf16[1024,16,128]{2,1,0:T(8,128)(2,1)S(1)} custom-call(bf16[352,16,128]{2,1,0:T(8,128)(2,1)S(1)} %bitcast.10, bf16[352,16,128]{2,1,0:T(8,128)(2,1)S(1)} %bitcast.11), custom_call_target="tpu_custom_call" | custom-call | tf_op jit(solution)/shard_map/assemble/pallas_call | solution.py:344
  30.5 2.4 %collective-permute-done.8 = bf16[1,32,16,128]{3,2,1,0:T(8,128)(2,1)S(1)} collective-permute-done((bf16[1,32,16,128]{3,2,1,0:T(8,128)(2,1)S(1)}, bf16[1,32,16,128]{3,2,1,0:T(8,128)(2,1)S(1)}, u32[]{:S(2)}, u32[]{:S(2)}) %collective-permute-start.8) | collective-permute-done | bytes 131104 | tf_op jit(solution)/shard_map/ppermute | solution.py:21
  32.9 0.6 collective-permute-done.7
  33.4 0.5 collective-permute-done.9
  33.9 0.1 constant_dynamic-update-slice_fusion.9
  34.0 0.1 collective-permute-start.11
  34.1 2.1 %collective-permute-done.11 = bf16[5,32,16,128]{3,2,1,0:T(8,128)(2,1)S(1)} collective-permute-done((bf16[5,32,16,128]{3,2,1,0:T(8,128)(2,1)S(1)}, bf16[5,32,16,128]{3,2,1,0:T(8,128)(2,1)S(1)}, u32[]{:S(2)}, u32[]{:S(2)}) %collective-permute-start.11) | collective-permute-done | bytes 655392 | tf_op jit(solution)/shard_map/ppermute | solution.py:21
  36.2 5.4 %apply.1 = (bf16[32,4096]{1,0:T(8,128)(2,1)S(1)}, f32[16,128]{1,0:T(8,128)S(1)}, bf16[1024,16,128]{2,1,0:T(8,128)(2,1)S(1)}) custom-call(s32[8,64]{1,0:T(8,128)S(1)} %get-tuple-element.28.rows_ref, bf16[64,8,64,128]{3,2,1,0:T(8,128)(2,1)S(1)} %get-tuple-element.29.ham_ref, bf16[1024,16,128]{2,1,0:T(8,128)(2,1)S(1)} %assemble.1._, ...), custom_call_target="tpu_custom_call", output_to_operand_aliasing={{2}: (2, {})} | custom-call | tf_op jit(solution)/shard_map/apply/pallas_call | solution.py:355
  41.6 0.2 collective-permute-start.12
  41.8 1.0 %collective-permute-done.12 = f32[16,128]{1,0:T(8,128)S(1)} collective-permute-done((f32[16,128]{1,0:T(8,128)S(1)}, f32[16,128]{1,0:T(8,128)S(1)}, u32[]{:S(2)}, u32[]{:S(2)}) %collective-permute-start.12) | collective-permute-done | bytes 8224 | tf_op jit(solution)/shard_map/ppermute | solution.py:21
  42.8 12.5 %all_to_all.5.sums_ref = f32[16,16,128]{2,1,0:T(8,128)S(1)} all-to-all(f32[16,16,128]{2,1,0:T(8,128)S(1)} %broadcast_in_dim.7), channel_id=1, replica_groups=mesh['chan'=16,'rad'=2] {'chan'}, dimensions={0} | all-to-all | bytes 262144 | tf_op jit(solution)/shard_map/all_to_all | solution.py:271
  55.3 2.5 %finish.1 = (f32[64,16,64]{2,1,0:T(8,128)}, f32[1,16]{1,0:T(1,128)}) custom-call(f32[16,16,128]{2,1,0:T(8,128)S(1)} %all_to_all.5.sums_ref, bf16[32,4096]{1,0:T(8,128)(2,1)S(1)} %get-tuple-element.49.az_ref, bf16[64,4096]{1,0:T(8,128)(2,1)S(1)} %get-tuple-element.41.zhm_ref), custom_call_target="tpu_custom_call" | custom-call | tf_op jit(solution)/shard_map/finish/pallas_call | solution.py:371
  (18 shorter events, 0.3 us)
Async XLA Ops:
  1.9 12.4 %collective-permute-start.3 = (bf16[1,32,16,128]{3,2,1,0:T(8,128)(2,1)S(1)}, bf16[1,32,16,128]{3,2,1,0:T(8,128)(2,1)S(1)}, u32[]{:S(2)}, u32[]{:S(2)}) collective-permute-start(bf16[1,32,16,128]{3,2,1,0:T(8,128)(2,1)S(1)} %get-tuple-element.53), channel_id=1, source_target_pairs={{0,16},{2,18},{4,20},{6,22},{8,24},{10,26},{12,28},{14,30},{16,0},... | collective-permute-start | bytes 393224 | tf_op jit(solution)/shard_map/ppermute | solution.py:21
  6.0 8.3 %collective-permute-start.2 = (bf16[1,32,16,128]{3,2,1,0:T(8,128)(2,1)S(1)}, bf16[1,32,16,128]{3,2,1,0:T(8,128)(2,1)S(1)}, u32[]{:S(2)}, u32[]{:S(2)}) collective-permute-start(bf16[1,32,16,128]{3,2,1,0:T(8,128)(2,1)S(1)} %get-tuple-element.53), channel_id=1, source_target_pairs={{0,8},{2,10},{4,12},{6,14},{8,0},{10,2},{12,4},{14,6},{16,24},{18,... | collective-permute-start | bytes 393224 | tf_op jit(solution)/shard_map/ppermute | solution.py:21
  7.5 6.7 %collective-permute-start.1 = (bf16[1,32,16,128]{3,2,1,0:T(8,128)(2,1)S(1)}, bf16[1,32,16,128]{3,2,1,0:T(8,128)(2,1)S(1)}, u32[]{:S(2)}, u32[]{:S(2)}) collective-permute-start(bf16[1,32,16,128]{3,2,1,0:T(8,128)(2,1)S(1)} %get-tuple-element.53), channel_id=1, source_target_pairs={{0,2},{1,5},{2,0},{3,7},{4,6},{5,1},{6,4},{7,3},{8,10},{9,13},{10,... | collective-permute-start | bytes 393224 | tf_op jit(solution)/shard_map/ppermute | solution.py:30
  9.0 5.2 %collective-permute-start = (bf16[1,32,16,128]{3,2,1,0:T(8,128)(2,1)S(1)}, bf16[1,32,16,128]{3,2,1,0:T(8,128)(2,1)S(1)}, u32[]{:S(2)}, u32[]{:S(2)}) collective-permute-start(bf16[1,32,16,128]{3,2,1,0:T(8,128)(2,1)S(1)} %get-tuple-element.53), channel_id=1, source_target_pairs={{0,4},{1,3},{2,6},{3,1},{4,0},{5,7},{6,2},{7,5},{8,12},{9,11},{10,... | collective-permute-start | bytes 393224 | tf_op jit(solution)/shard_map/ppermute | solution.py:30
  14.3 10.1 %collective-permute-start.5 = (bf16[3,32,16,128]{3,2,1,0:T(8,128)(2,1)S(1)}, bf16[3,32,16,128]{3,2,1,0:T(8,128)(2,1)S(1)}, u32[]{:S(2)}, u32[]{:S(2)}) collective-permute-start(bf16[3,32,16,128]{3,2,1,0:T(8,128)(2,1)S(1)} %pad_maximum_fusion), channel_id=1, source_target_pairs={{0,4},{1,3},{2,6},{3,1},{4,0},{5,7},{6,2},{7,5},{8,12},{9,11},{10,... | collective-permute-start | bytes 1179656 | tf_op jit(solution)/shard_map/ppermute | solution.py:30
  15.7 5.0 %collective-permute-start.4 = (bf16[1,32,16,128]{3,2,1,0:T(8,128)(2,1)S(1)}, bf16[1,32,16,128]{3,2,1,0:T(8,128)(2,1)S(1)}, u32[]{:S(2)}, u32[]{:S(2)}) collective-permute-start(bf16[1,32,16,128]{3,2,1,0:T(8,128)(2,1)S(1)} %collective-permute-done.3), channel_id=1, source_target_pairs={{0,8},{2,10},{4,12},{6,14},{8,0},{10,2},{12,4},{14,6},{16,24},{18,... | collective-permute-start | bytes 393224 | tf_op jit(solution)/shard_map/ppermute | solution.py:21
  16.2 6.8 %collective-permute-start.6 = (bf16[2,32,16,128]{3,2,1,0:T(8,128)(2,1)S(1)}, bf16[2,32,16,128]{3,2,1,0:T(8,128)(2,1)S(1)}, u32[]{:S(2)}, u32[]{:S(2)}) collective-permute-start(bf16[2,32,16,128]{3,2,1,0:T(8,128)(2,1)S(1)} %pad_maximum_fusion.2), channel_id=1, source_target_pairs={{0,2},{1,5},{2,0},{3,7},{4,6},{5,1},{6,4},{7,3},{8,10},{9,13},{10,... | collective-permute-start | bytes 786440 | tf_op jit(solution)/shard_map/ppermute | solution.py:30
  24.5 4.9 %collective-permute-start.10 = (bf16[11,32,16,128]{3,2,1,0:T(8,128)(2,1)S(1)}, bf16[11,32,16,128]{3,2,1,0:T(8,128)(2,1)S(1)}, u32[]{:S(2)}, u32[]{:S(2)}) collective-permute-start(bf16[11,32,16,128]{3,2,1,0:T(8,128)(2,1)S(1)} %constant_dynamic-update-slice_fusion), channel_id=1, source_target_pairs={{0,1},{1,0},{2,3},{3,2},{4,5},{5,4},{6,7},{7,6},{8,9},{9,8},{10,11... | collective-permute-start | bytes 4325384 | tf_op jit(solution)/shard_map/ppermute | solution.py:21
  24.7 9.2 %collective-permute-start.9 = (bf16[3,32,16,128]{3,2,1,0:T(8,128)(2,1)S(1)}, bf16[3,32,16,128]{3,2,1,0:T(8,128)(2,1)S(1)}, u32[]{:S(2)}, u32[]{:S(2)}) collective-permute-start(bf16[3,32,16,128]{3,2,1,0:T(8,128)(2,1)S(1)} %pad_maximum_fusion.1), channel_id=1, source_target_pairs={{0,4},{1,3},{2,6},{3,1},{4,0},{5,7},{6,2},{7,5},{8,12},{9,11},{10,... | collective-permute-start | bytes 1179656 | tf_op jit(solution)/shard_map/ppermute | solution.py:30
  25.7 7.2 %collective-permute-start.8 = (bf16[1,32,16,128]{3,2,1,0:T(8,128)(2,1)S(1)}, bf16[1,32,16,128]{3,2,1,0:T(8,128)(2,1)S(1)}, u32[]{:S(2)}, u32[]{:S(2)}) collective-permute-start(bf16[1,32,16,128]{3,2,1,0:T(8,128)(2,1)S(1)} %slice.3), channel_id=1, source_target_pairs={{0,24},{2,26},{4,28},{6,30},{8,16},{10,18},{12,20},{14,22},{16,8},... | collective-permute-start | bytes 393224 | tf_op jit(solution)/shard_map/ppermute | solution.py:21
  28.5 5.0 %collective-permute-start.7 = (bf16[1,32,16,128]{3,2,1,0:T(8,128)(2,1)S(1)}, bf16[1,32,16,128]{3,2,1,0:T(8,128)(2,1)S(1)}, u32[]{:S(2)}, u32[]{:S(2)}) collective-permute-start(bf16[1,32,16,128]{3,2,1,0:T(8,128)(2,1)S(1)} %collective-permute-done.4), channel_id=1, source_target_pairs={{0,2},{1,5},{2,0},{3,7},{4,6},{5,1},{6,4},{7,3},{8,10},{9,13},{10,... | collective-permute-start | bytes 393224 | tf_op jit(solution)/shard_map/ppermute | solution.py:30
  34.0 2.2 %collective-permute-start.11 = (bf16[5,32,16,128]{3,2,1,0:T(8,128)(2,1)S(1)}, bf16[5,32,16,128]{3,2,1,0:T(8,128)(2,1)S(1)}, u32[]{:S(2)}, u32[]{:S(2)}) collective-permute-start(bf16[5,32,16,128]{3,2,1,0:T(8,128)(2,1)S(1)} %constant_dynamic-update-slice_fusion.8), channel_id=1, source_target_pairs={{0,1},{1,0},{2,3},{3,2},{4,5},{5,4},{6,7},{7,6},{8,9},{9,8},{10,11... | collective-permute-start | bytes 1966088 | tf_op jit(solution)/shard_map/ppermute | solution.py:21
  41.6 1.2 %collective-permute-start.12 = (f32[16,128]{1,0:T(8,128)S(1)}, f32[16,128]{1,0:T(8,128)S(1)}, u32[]{:S(2)}, u32[]{:S(2)}) collective-permute-start(f32[16,128]{1,0:T(8,128)S(1)} %get-tuple-element.48), channel_id=1, source_target_pairs={{0,1},{1,0},{2,3},{3,2},{4,5},{5,4},{6,7},{7,6},{8,9},{9,8},{10,11... | collective-permute-start | bytes 24584 | tf_op jit(solution)/shard_map/ppermute | solution.py:21

commit v20 on v18

--- a/solution.py
+++ b/solution.py
@@ -194,7 +194,9 @@
         left = jnp.concatenate([zhm_ref[:, at], zl_ref[:, at], right[: 3 * k]], axis=0)
         return gram + lax.dot_general(left, right, NT, preferred_element_type=F32)
 
-    gram = lax.fori_loop(0, lanes // block, gram_block, jnp.zeros((9 * k, 6 * k), F32))
+    gram = lax.fori_loop(
+        0, lanes // block, gram_block, jnp.zeros((9 * k, 6 * k), F32), unroll=True
+    )
     ta1 = block_sum(gram[: 6 * k, : 3 * k], 2 * k, k)
     ta0 = block_sum(gram[: 6 * k, 3 * k :], 2 * k, k)
     aa = block_sum(gram[6 * k :, : 3 * k], k, k)
@@ -257,7 +259,7 @@
             out_ref[b * (block // r) + i] = new[:, i * r : (i + 1) * r]
         return carry
 
-    lax.fori_loop(0, ch * r // block, result, 0)
+    lax.fori_loop(0, ch * r // block, result, 0, unroll=True)
 
 
 def gather_sums(x):

time: 57.6 us -> 56.6 us (0.983)
  Pallas kernels: 13.2 us -> 12.1 us
    pallas_call x1, Pallas kernels: 3.06 us -> 2.47 us  [body(): pl.pallas_call(functools.partial(finish_kernel, total), out_shape=[jax.Sh...]
where the time goes in v20:
time: 56.6 us; the launch traced here: 56.4 us
  starting transfers between devices  16.9 us (30%)
  waiting for transfers between devices  12.6 us (22%)
  blocking collectives  12.4 us (22%)
  Pallas kernels  12.1 us (21%)
  other arithmetic  1.26 us (2%)
  between operations  0.78 us (1%)
    all_to_all x1, blocking collectives, gather_sums(): lax.all_to_all(every, 'chan', split_axis=0, concat_axis=0, tiled=True)  12.4 us
    ppermute x8, starting transfers between devices, swap(): return lax.ppermute(x, axis, [(i, i ^ distance) for i in range(n)])  12.3 us
    ppermute x8, waiting for transfers between devices, swap(): return lax.ppermute(x, axis, [(i, i ^ distance) for i in range(n)])  10.2 us
    pallas_call x1, Pallas kernels, body(): pl.pallas_call(functools.partial(apply_kernel, nz, share), in_specs=[smem...  4.96 us
    ppermute x6, starting transfers between devices, plane_swap(): return lax.ppermute(x, ('chan', 'rad'), pairs)  4.64 us
    pallas_call x1, Pallas kernels, body(): pl.pallas_call(functools.partial(prepare_kernel, n_chan, n_rad), in_specs...  3.66 us
    pallas_call x1, Pallas kernels, body(): pl.pallas_call(functools.partial(finish_kernel, total), out_shape=[jax.Sh...  2.47 us
    ppermute x6, waiting for transfers between devices, plane_swap(): return lax.ppermute(x, ('chan', 'rad'), pairs)  2.35 us
  transfers between devices with their start and end apart: 14, of which 10 were waited for; matrix products, arithmetic and copies ran while one was open for 0% of the time, Pallas kernels for 8%

profile of v20, /device:TPU:0, one launch (start us, length us, event | category | flops | bytes accessed | tf_op | source)
XLA Modules:
  0.0 56.4 jit_solution(4852466116463898246)
XLA Ops:
  0.6 1.1 %convert_element_type.3 = bf16[64,16,64]{2,1,0:T(8,128)(2,1)S(1)} convert(f32[64,16,64]{2,1,0:T(8,128)} %t_hbm.1) | non-fusion elementwise | flops 65536 | bytes 393216 | tf_op jit(solution)/shard_map/convert_element_type | solution.py:300
  1.7 0.1 constant_dynamic-update-slice_fusion.8
  1.9 4.0 %collective-permute-start.4 = (bf16[1,32,16,128]{3,2,1,0:T(8,128)(2,1)S(1)}, bf16[1,32,16,128]{3,2,1,0:T(8,128)(2,1)S(1)}, u32[]{:S(2)}, u32[]{:S(2)}) collective-permute-start(bf16[1,32,16,128]{3,2,1,0:T(8,128)(2,1)S(1)} %get-tuple-element.57), channel_id=1, source_target_pairs={{0,6},{2,4},{4,2},{6,0},{8,14},{10,12},{12,10},{14,8},{16,22},{18,... | collective-permute-start | bytes 393224 | tf_op jit(solution)/shard_map/ppermute | solution.py:21
  5.8 2.6 %collective-permute-start.3 = (bf16[1,32,16,128]{3,2,1,0:T(8,128)(2,1)S(1)}, bf16[1,32,16,128]{3,2,1,0:T(8,128)(2,1)S(1)}, u32[]{:S(2)}, u32[]{:S(2)}) collective-permute-start(bf16[1,32,16,128]{3,2,1,0:T(8,128)(2,1)S(1)} %get-tuple-element.57), channel_id=1, source_target_pairs={{0,16},{2,18},{4,20},{6,22},{8,24},{10,26},{12,28},{14,30},{16,0},... | collective-permute-start | bytes 393224 | tf_op jit(solution)/shard_map/ppermute | solution.py:21
  8.4 1.6 %collective-permute-start.2 = (bf16[1,32,16,128]{3,2,1,0:T(8,128)(2,1)S(1)}, bf16[1,32,16,128]{3,2,1,0:T(8,128)(2,1)S(1)}, u32[]{:S(2)}, u32[]{:S(2)}) collective-permute-start(bf16[1,32,16,128]{3,2,1,0:T(8,128)(2,1)S(1)} %get-tuple-element.57), channel_id=1, source_target_pairs={{0,8},{2,10},{4,12},{6,14},{8,0},{10,2},{12,4},{14,6},{16,24},{18,... | collective-permute-start | bytes 393224 | tf_op jit(solution)/shard_map/ppermute | solution.py:21
  10.0 0.5 collective-permute-start.1
  10.5 0.5 collective-permute-start
  11.0 3.7 %prepare.1 = (s32[8,64]{1,0:T(8,128)S(1)}, bf16[64,8,64,128]{3,2,1,0:T(8,128)(2,1)S(1)}, bf16[64,4096]{1,0:T(8,128)(2,1)S(1)}, bf16[32,4096]{1,0:T(8,128)(2,1)S(...) custom-call(f32[64,16,64]{2,1,0:T(8,128)} %t_hbm.1, f32[64,64]{1,0:T(8,128)} %d_hbm.1, s32[8,64]{1,0:T(8,128)} %bitcast.14, ...), custom_call_target="tpu_custom_call" | custom-call | tf_op jit(solution)/shard_map/prepare/pallas_call | solution.py:304
  14.7 0.1 collective-permute-done.2
  14.8 0.2 collective-permute-done.1
  14.9 0.5 collective-permute-done
  15.5 1.6 %collective-permute-start.7 = (bf16[2,32,16,128]{3,2,1,0:T(8,128)(2,1)S(1)}, bf16[2,32,16,128]{3,2,1,0:T(8,128)(2,1)S(1)}, u32[]{:S(2)}, u32[]{:S(2)}) collective-permute-start(bf16[2,32,16,128]{3,2,1,0:T(8,128)(2,1)S(1)} %pad_maximum_fusion.1), channel_id=1, source_target_pairs={{0,2},{1,5},{2,0},{3,7},{4,6},{5,1},{6,4},{7,3},{8,10},{9,13},{10,... | collective-permute-start | bytes 786440 | tf_op jit(solution)/shard_map/ppermute | solution.py:30
  17.1 0.8 %collective-permute-start.6 = (bf16[2,32,16,128]{3,2,1,0:T(8,128)(2,1)S(1)}, bf16[2,32,16,128]{3,2,1,0:T(8,128)(2,1)S(1)}, u32[]{:S(2)}, u32[]{:S(2)}) collective-permute-start(bf16[2,32,16,128]{3,2,1,0:T(8,128)(2,1)S(1)} %pad_maximum_fusion.1), channel_id=1, source_target_pairs={{0,4},{1,3},{2,6},{3,1},{4,0},{5,7},{6,2},{7,5},{8,12},{9,11},{10,... | collective-permute-start | bytes 786440 | tf_op jit(solution)/shard_map/ppermute | solution.py:30
  17.9 0.5 collective-permute-start.5
  18.5 4.4 %collective-permute-done.5 = bf16[1,32,16,128]{3,2,1,0:T(8,128)(2,1)S(1)} collective-permute-done((bf16[1,32,16,128]{3,2,1,0:T(8,128)(2,1)S(1)}, bf16[1,32,16,128]{3,2,1,0:T(8,128)(2,1)S(1)}, u32[]{:S(2)}, u32[]{:S(2)}) %collective-permute-start.5) | collective-permute-done | bytes 131104 | tf_op jit(solution)/shard_map/ppermute | solution.py:21
  22.9 0.7 %collective-permute-done.7 = bf16[2,32,16,128]{3,2,1,0:T(8,128)(2,1)S(1)} collective-permute-done((bf16[2,32,16,128]{3,2,1,0:T(8,128)(2,1)S(1)}, bf16[2,32,16,128]{3,2,1,0:T(8,128)(2,1)S(1)}, u32[]{:S(2)}, u32[]{:S(2)}) %collective-permute-start.7) | collective-permute-done | bytes 262176 | tf_op jit(solution)/shard_map/ppermute | solution.py:30
  23.7 0.1 collective-permute-start.11
  23.8 0.7 %collective-permute-start.10 = (bf16[3,32,16,128]{3,2,1,0:T(8,128)(2,1)S(1)}, bf16[3,32,16,128]{3,2,1,0:T(8,128)(2,1)S(1)}, u32[]{:S(2)}, u32[]{:S(2)}) collective-permute-start(bf16[3,32,16,128]{3,2,1,0:T(8,128)(2,1)S(1)} %pad_maximum_fusion), channel_id=1, source_target_pairs={{0,4},{1,3},{2,6},{3,1},{4,0},{5,7},{6,2},{7,5},{8,12},{9,11},{10,... | collective-permute-start | bytes 1179656 | tf_op jit(solution)/shard_map/ppermute | solution.py:30
  24.6 3.3 %collective-permute-start.9 = (bf16[1,32,16,128]{3,2,1,0:T(8,128)(2,1)S(1)}, bf16[1,32,16,128]{3,2,1,0:T(8,128)(2,1)S(1)}, u32[]{:S(2)}, u32[]{:S(2)}) collective-permute-start(bf16[1,32,16,128]{3,2,1,0:T(8,128)(2,1)S(1)} %collective-permute-done.4), channel_id=1, source_target_pairs={{0,24},{2,26},{4,28},{6,30},{8,16},{10,18},{12,20},{14,22},{16,8},... | collective-permute-start | bytes 393224 | tf_op jit(solution)/shard_map/ppermute | solution.py:21
  27.9 0.5 collective-permute-start.8
  28.4 1.1 %assemble.1._ = bf16[1024,16,128]{2,1,0:T(8,128)(2,1)S(1)} custom-call(bf16[352,16,128]{2,1,0:T(8,128)(2,1)S(1)} %bitcast.10, bf16[352,16,128]{2,1,0:T(8,128)(2,1)S(1)} %bitcast.11), custom_call_target="tpu_custom_call" | custom-call | tf_op jit(solution)/shard_map/assemble/pallas_call | solution.py:343
  29.5 2.6 %collective-permute-done.9 = bf16[1,32,16,128]{3,2,1,0:T(8,128)(2,1)S(1)} collective-permute-done((bf16[1,32,16,128]{3,2,1,0:T(8,128)(2,1)S(1)}, bf16[1,32,16,128]{3,2,1,0:T(8,128)(2,1)S(1)}, u32[]{:S(2)}, u32[]{:S(2)}) %collective-permute-start.9) | collective-permute-done | bytes 131104 | tf_op jit(solution)/shard_map/ppermute | solution.py:21
  32.1 0.8 %collective-permute-done.8 = bf16[1,32,16,128]{3,2,1,0:T(8,128)(2,1)S(1)} collective-permute-done((bf16[1,32,16,128]{3,2,1,0:T(8,128)(2,1)S(1)}, bf16[1,32,16,128]{3,2,1,0:T(8,128)(2,1)S(1)}, u32[]{:S(2)}, u32[]{:S(2)}) %collective-permute-start.8) | collective-permute-done | bytes 131104 | tf_op jit(solution)/shard_map/ppermute | solution.py:30
  32.9 0.2 collective-permute-done.10
  33.1 0.1 constant_dynamic-update-slice_fusion.10
  33.2 0.1 collective-permute-start.12
  33.3 2.1 %collective-permute-done.12 = bf16[5,32,16,128]{3,2,1,0:T(8,128)(2,1)S(1)} collective-permute-done((bf16[5,32,16,128]{3,2,1,0:T(8,128)(2,1)S(1)}, bf16[5,32,16,128]{3,2,1,0:T(8,128)(2,1)S(1)}, u32[]{:S(2)}, u32[]{:S(2)}) %collective-permute-start.12) | collective-permute-done | bytes 655392 | tf_op jit(solution)/shard_map/ppermute | solution.py:21
  35.3 5.0 %apply.1 = (bf16[32,4096]{1,0:T(8,128)(2,1)S(1)}, f32[16,128]{1,0:T(8,128)S(1)}, bf16[1024,16,128]{2,1,0:T(8,128)(2,1)S(1)}) custom-call(s32[8,64]{1,0:T(8,128)S(1)} %get-tuple-element.30.rows_ref, bf16[64,8,64,128]{3,2,1,0:T(8,128)(2,1)S(1)} %get-tuple-element.31.ham_ref, bf16[1024,16,128]{2,1,0:T(8,128)(2,1)S(1)} %assemble.1._, ...), custom_call_target="tpu_custom_call", output_to_operand_aliasing={{2}: (2, {})} | custom-call | tf_op jit(solution)/shard_map/apply/pallas_call | solution.py:354
  40.3 0.2 collective-permute-start.13
  40.5 1.0 %collective-permute-done.13 = f32[16,128]{1,0:T(8,128)S(1)} collective-permute-done((f32[16,128]{1,0:T(8,128)S(1)}, f32[16,128]{1,0:T(8,128)S(1)}, u32[]{:S(2)}, u32[]{:S(2)}) %collective-permute-start.13) | collective-permute-done | bytes 8224 | tf_op jit(solution)/shard_map/ppermute | solution.py:21
  41.5 12.4 %all_to_all.5.sums_ref = f32[16,16,128]{2,1,0:T(8,128)S(1)} all-to-all(f32[16,16,128]{2,1,0:T(8,128)S(1)} %broadcast_in_dim.7), channel_id=1, replica_groups=mesh['chan'=16,'rad'=2] {'chan'}, dimensions={0} | all-to-all | bytes 262144 | tf_op jit(solution)/shard_map/all_to_all | solution.py:272
  53.9 2.5 %finish.1 = (f32[64,16,64]{2,1,0:T(8,128)}, f32[1,16]{1,0:T(1,128)}) custom-call(f32[16,16,128]{2,1,0:T(8,128)S(1)} %all_to_all.5.sums_ref, bf16[32,4096]{1,0:T(8,128)(2,1)S(1)} %get-tuple-element.53.az_ref, bf16[64,4096]{1,0:T(8,128)(2,1)S(1)} %get-tuple-element.45.zhm_ref), custom_call_target="tpu_custom_call" | custom-call | tf_op jit(solution)/shard_map/finish/pallas_call | solution.py:370
  (19 shorter events, 0.3 us)
Async XLA Ops:
  1.9 12.8 %collective-permute-start.4 = (bf16[1,32,16,128]{3,2,1,0:T(8,128)(2,1)S(1)}, bf16[1,32,16,128]{3,2,1,0:T(8,128)(2,1)S(1)}, u32[]{:S(2)}, u32[]{:S(2)}) collective-permute-start(bf16[1,32,16,128]{3,2,1,0:T(8,128)(2,1)S(1)} %get-tuple-element.57), channel_id=1, source_target_pairs={{0,6},{2,4},{4,2},{6,0},{8,14},{10,12},{12,10},{14,8},{16,22},{18,... | collective-permute-start | bytes 393224 | tf_op jit(solution)/shard_map/ppermute | solution.py:21
  5.8 8.9 %collective-permute-start.3 = (bf16[1,32,16,128]{3,2,1,0:T(8,128)(2,1)S(1)}, bf16[1,32,16,128]{3,2,1,0:T(8,128)(2,1)S(1)}, u32[]{:S(2)}, u32[]{:S(2)}) collective-permute-start(bf16[1,32,16,128]{3,2,1,0:T(8,128)(2,1)S(1)} %get-tuple-element.57), channel_id=1, source_target_pairs={{0,16},{2,18},{4,20},{6,22},{8,24},{10,26},{12,28},{14,30},{16,0},... | collective-permute-start | bytes 393224 | tf_op jit(solution)/shard_map/ppermute | solution.py:21
  8.4 6.4 %collective-permute-start.2 = (bf16[1,32,16,128]{3,2,1,0:T(8,128)(2,1)S(1)}, bf16[1,32,16,128]{3,2,1,0:T(8,128)(2,1)S(1)}, u32[]{:S(2)}, u32[]{:S(2)}) collective-permute-start(bf16[1,32,16,128]{3,2,1,0:T(8,128)(2,1)S(1)} %get-tuple-element.57), channel_id=1, source_target_pairs={{0,8},{2,10},{4,12},{6,14},{8,0},{10,2},{12,4},{14,6},{16,24},{18,... | collective-permute-start | bytes 393224 | tf_op jit(solution)/shard_map/ppermute | solution.py:21
  10.0 5.0 %collective-permute-start.1 = (bf16[1,32,16,128]{3,2,1,0:T(8,128)(2,1)S(1)}, bf16[1,32,16,128]{3,2,1,0:T(8,128)(2,1)S(1)}, u32[]{:S(2)}, u32[]{:S(2)}) collective-permute-start(bf16[1,32,16,128]{3,2,1,0:T(8,128)(2,1)S(1)} %get-tuple-element.57), channel_id=1, source_target_pairs={{0,2},{1,5},{2,0},{3,7},{4,6},{5,1},{6,4},{7,3},{8,10},{9,13},{10,... | collective-permute-start | bytes 393224 | tf_op jit(solution)/shard_map/ppermute | solution.py:30
  10.5 5.0 %collective-permute-start = (bf16[1,32,16,128]{3,2,1,0:T(8,128)(2,1)S(1)}, bf16[1,32,16,128]{3,2,1,0:T(8,128)(2,1)S(1)}, u32[]{:S(2)}, u32[]{:S(2)}) collective-permute-start(bf16[1,32,16,128]{3,2,1,0:T(8,128)(2,1)S(1)} %get-tuple-element.57), channel_id=1, source_target_pairs={{0,4},{1,3},{2,6},{3,1},{4,0},{5,7},{6,2},{7,5},{8,12},{9,11},{10,... | collective-permute-start | bytes 393224 | tf_op jit(solution)/shard_map/ppermute | solution.py:30
  15.5 8.0 %collective-permute-start.7 = (bf16[2,32,16,128]{3,2,1,0:T(8,128)(2,1)S(1)}, bf16[2,32,16,128]{3,2,1,0:T(8,128)(2,1)S(1)}, u32[]{:S(2)}, u32[]{:S(2)}) collective-permute-start(bf16[2,32,16,128]{3,2,1,0:T(8,128)(2,1)S(1)} %pad_maximum_fusion.1), channel_id=1, source_target_pairs={{0,2},{1,5},{2,0},{3,7},{4,6},{5,1},{6,4},{7,3},{8,10},{9,13},{10,... | collective-permute-start | bytes 786440 | tf_op jit(solution)/shard_map/ppermute | solution.py:30
  17.1 6.5 %collective-permute-start.6 = (bf16[2,32,16,128]{3,2,1,0:T(8,128)(2,1)S(1)}, bf16[2,32,16,128]{3,2,1,0:T(8,128)(2,1)S(1)}, u32[]{:S(2)}, u32[]{:S(2)}) collective-permute-start(bf16[2,32,16,128]{3,2,1,0:T(8,128)(2,1)S(1)} %pad_maximum_fusion.1), channel_id=1, source_target_pairs={{0,4},{1,3},{2,6},{3,1},{4,0},{5,7},{6,2},{7,5},{8,12},{9,11},{10,... | collective-permute-start | bytes 786440 | tf_op jit(solution)/shard_map/ppermute | solution.py:30
  17.9 5.0 %collective-permute-start.5 = (bf16[1,32,16,128]{3,2,1,0:T(8,128)(2,1)S(1)}, bf16[1,32,16,128]{3,2,1,0:T(8,128)(2,1)S(1)}, u32[]{:S(2)}, u32[]{:S(2)}) collective-permute-start(bf16[1,32,16,128]{3,2,1,0:T(8,128)(2,1)S(1)} %collective-permute-done.3), channel_id=1, source_target_pairs={{0,8},{2,10},{4,12},{6,14},{8,0},{10,2},{12,4},{14,6},{16,24},{18,... | collective-permute-start | bytes 393224 | tf_op jit(solution)/shard_map/ppermute | solution.py:21
  23.7 4.7 %collective-permute-start.11 = (bf16[11,32,16,128]{3,2,1,0:T(8,128)(2,1)S(1)}, bf16[11,32,16,128]{3,2,1,0:T(8,128)(2,1)S(1)}, u32[]{:S(2)}, u32[]{:S(2)}) collective-permute-start(bf16[11,32,16,128]{3,2,1,0:T(8,128)(2,1)S(1)} %constant_dynamic-update-slice_fusion), channel_id=1, source_target_pairs={{0,1},{1,0},{2,3},{3,2},{4,5},{5,4},{6,7},{7,6},{8,9},{9,8},{10,11... | collective-permute-start | bytes 4325384 | tf_op jit(solution)/shard_map/ppermute | solution.py:21
  23.8 9.2 %collective-permute-start.10 = (bf16[3,32,16,128]{3,2,1,0:T(8,128)(2,1)S(1)}, bf16[3,32,16,128]{3,2,1,0:T(8,128)(2,1)S(1)}, u32[]{:S(2)}, u32[]{:S(2)}) collective-permute-start(bf16[3,32,16,128]{3,2,1,0:T(8,128)(2,1)S(1)} %pad_maximum_fusion), channel_id=1, source_target_pairs={{0,4},{1,3},{2,6},{3,1},{4,0},{5,7},{6,2},{7,5},{8,12},{9,11},{10,... | collective-permute-start | bytes 1179656 | tf_op jit(solution)/shard_map/ppermute | solution.py:30
  24.6 7.5 %collective-permute-start.9 = (bf16[1,32,16,128]{3,2,1,0:T(8,128)(2,1)S(1)}, bf16[1,32,16,128]{3,2,1,0:T(8,128)(2,1)S(1)}, u32[]{:S(2)}, u32[]{:S(2)}) collective-permute-start(bf16[1,32,16,128]{3,2,1,0:T(8,128)(2,1)S(1)} %collective-permute-done.4), channel_id=1, source_target_pairs={{0,24},{2,26},{4,28},{6,30},{8,16},{10,18},{12,20},{14,22},{16,8},... | collective-permute-start | bytes 393224 | tf_op jit(solution)/shard_map/ppermute | solution.py:21
  27.9 5.0 %collective-permute-start.8 = (bf16[1,32,16,128]{3,2,1,0:T(8,128)(2,1)S(1)}, bf16[1,32,16,128]{3,2,1,0:T(8,128)(2,1)S(1)}, u32[]{:S(2)}, u32[]{:S(2)}) collective-permute-start(bf16[1,32,16,128]{3,2,1,0:T(8,128)(2,1)S(1)} %collective-permute-done.5), channel_id=1, source_target_pairs={{0,2},{1,5},{2,0},{3,7},{4,6},{5,1},{6,4},{7,3},{8,10},{9,13},{10,... | collective-permute-start | bytes 393224 | tf_op jit(solution)/shard_map/ppermute | solution.py:30
  33.2 2.2 %collective-permute-start.12 = (bf16[5,32,16,128]{3,2,1,0:T(8,128)(2,1)S(1)}, bf16[5,32,16,128]{3,2,1,0:T(8,128)(2,1)S(1)}, u32[]{:S(2)}, u32[]{:S(2)}) collective-permute-start(bf16[5,32,16,128]{3,2,1,0:T(8,128)(2,1)S(1)} %constant_dynamic-update-slice_fusion.9), channel_id=1, source_target_pairs={{0,1},{1,0},{2,3},{3,2},{4,5},{5,4},{6,7},{7,6},{8,9},{9,8},{10,11... | collective-permute-start | bytes 1966088 | tf_op jit(solution)/shard_map/ppermute | solution.py:21
  40.3 1.2 %collective-permute-start.13 = (f32[16,128]{1,0:T(8,128)S(1)}, f32[16,128]{1,0:T(8,128)S(1)}, u32[]{:S(2)}, u32[]{:S(2)}) collective-permute-start(f32[16,128]{1,0:T(8,128)S(1)} %get-tuple-element.52), channel_id=1, source_target_pairs={{0,1},{1,0},{2,3},{3,2},{4,5},{5,4},{6,7},{7,6},{8,9},{9,8},{10,11... | collective-permute-start | bytes 24584 | tf_op jit(solution)/shard_map/ppermute | solution.py:21

commit v21 on v20

--- a/solution.py
+++ b/solution.py
@@ -57,7 +57,7 @@
     return [(z, 1) for z in odd] + [(z, 2) for z in odd] + [(z, 3) for z in some + odd]
 
 
-def merge(refs, table_ref, order, start, share):
+def merge(refs, table_ref, order, start, share, unroll):
     n_rad = len(refs)
     r = 128 // n_rad
     me = lax.axis_index("rad")
@@ -77,7 +77,7 @@
                 table_ref[((start + i) * n_rad + g) * share + n] = row
         return carry
 
-    lax.fori_loop(0, share, rows, 0, unroll=min(8, share))
+    lax.fori_loop(0, share, rows, 0, unroll=min(unroll, share))
 
 
 def in_vmem(x):
@@ -152,12 +152,12 @@
 
 
 def assemble_kernel(nz, share, *refs):
-    merge(refs[:-1], refs[-1], early_pieces(nz), 0, share)
+    merge(refs[:-1], refs[-1], early_pieces(nz), 0, share, 8)
 
 
 def apply_kernel(nz, share, rows_ref, ham_ref, _, zhm_ref, zl_ref, dc_ref, gt_ref, *rest):
     last, (az_ref, sums_ref, table_ref, a0_ref) = rest[:-4], rest[-4:]
-    merge(last, table_ref, late_pieces(nz), len(early_pieces(nz)), share)
+    merge(last, table_ref, late_pieces(nz), len(early_pieces(nz)), share, 32)
     ch, ncoup, r, splines = ham_ref.shape
     k = zl_ref.shape[0] // 2
     group = 256 // r
@@ -180,7 +180,7 @@
         a0_ref[:, pl.ds(pl.multiple_of(g * 256, 256), 256)] = jnp.concatenate(own, axis=1) * SCALE
         return carry
 
-    lax.fori_loop(0, ch // group, work, 0, unroll=min(4, ch // group))
+    lax.fori_loop(0, ch // group, work, 0, unroll=min(8, ch // group))
 
     lanes = ch * r
     block = min(lanes, 1024)

time: 56.6 us -> 56.1 us (level)
  no operation moved by 1% of the time
where the time goes in v21:
time: 56.1 us; the launch traced here: 55.9 us
  starting transfers between devices  16.9 us (30%)
  waiting for transfers between devices  12.6 us (22%)
  blocking collectives  12.4 us (22%)
  Pallas kernels  11.6 us (21%)
  other arithmetic  1.26 us (2%)
  between operations  0.78 us (1%)
    all_to_all x1, blocking collectives, gather_sums(): lax.all_to_all(every, 'chan', split_axis=0, concat_axis=0, tiled=True)  12.4 us
    ppermute x8, starting transfers between devices, swap(): return lax.ppermute(x, axis, [(i, i ^ distance) for i in range(n)])  12.3 us
    ppermute x8, waiting for transfers between devices, swap(): return lax.ppermute(x, axis, [(i, i ^ distance) for i in range(n)])  10.2 us
    ppermute x6, starting transfers between devices, plane_swap(): return lax.ppermute(x, ('chan', 'rad'), pairs)  4.64 us
    pallas_call x1, Pallas kernels, body(): pl.pallas_call(functools.partial(apply_kernel, nz, share), in_specs=[smem...  4.47 us
    pallas_call x1, Pallas kernels, body(): pl.pallas_call(functools.partial(prepare_kernel, n_chan, n_rad), in_specs...  3.66 us
    pallas_call x1, Pallas kernels, body(): pl.pallas_call(functools.partial(finish_kernel, total), out_shape=[jax.Sh...  2.47 us
    ppermute x6, waiting for transfers between devices, plane_swap(): return lax.ppermute(x, ('chan', 'rad'), pairs)  2.35 us
  transfers between devices with their start and end apart: 14, of which 10 were waited for; matrix products, arithmetic and copies ran while one was open for 0% of the time, Pallas kernels for 8%

profile of v21, /device:TPU:0, one launch (start us, length us, event | category | flops | bytes accessed | tf_op | source)
XLA Modules:
  0.0 55.9 jit_solution(7411812945065660723)
XLA Ops:
  0.6 1.1 %convert_element_type.3 = bf16[64,16,64]{2,1,0:T(8,128)(2,1)S(1)} convert(f32[64,16,64]{2,1,0:T(8,128)} %t_hbm.1) | non-fusion elementwise | flops 65536 | bytes 393216 | tf_op jit(solution)/shard_map/convert_element_type | solution.py:300
  1.7 0.1 constant_dynamic-update-slice_fusion.8
  1.9 4.0 %collective-permute-start.4 = (bf16[1,32,16,128]{3,2,1,0:T(8,128)(2,1)S(1)}, bf16[1,32,16,128]{3,2,1,0:T(8,128)(2,1)S(1)}, u32[]{:S(2)}, u32[]{:S(2)}) collective-permute-start(bf16[1,32,16,128]{3,2,1,0:T(8,128)(2,1)S(1)} %get-tuple-element.57), channel_id=1, source_target_pairs={{0,6},{2,4},{4,2},{6,0},{8,14},{10,12},{12,10},{14,8},{16,22},{18,... | collective-permute-start | bytes 393224 | tf_op jit(solution)/shard_map/ppermute | solution.py:21
  5.8 2.6 %collective-permute-start.3 = (bf16[1,32,16,128]{3,2,1,0:T(8,128)(2,1)S(1)}, bf16[1,32,16,128]{3,2,1,0:T(8,128)(2,1)S(1)}, u32[]{:S(2)}, u32[]{:S(2)}) collective-permute-start(bf16[1,32,16,128]{3,2,1,0:T(8,128)(2,1)S(1)} %get-tuple-element.57), channel_id=1, source_target_pairs={{0,16},{2,18},{4,20},{6,22},{8,24},{10,26},{12,28},{14,30},{16,0},... | collective-permute-start | bytes 393224 | tf_op jit(solution)/shard_map/ppermute | solution.py:21
  8.4 1.6 %collective-permute-start.2 = (bf16[1,32,16,128]{3,2,1,0:T(8,128)(2,1)S(1)}, bf16[1,32,16,128]{3,2,1,0:T(8,128)(2,1)S(1)}, u32[]{:S(2)}, u32[]{:S(2)}) collective-permute-start(bf16[1,32,16,128]{3,2,1,0:T(8,128)(2,1)S(1)} %get-tuple-element.57), channel_id=1, source_target_pairs={{0,8},{2,10},{4,12},{6,14},{8,0},{10,2},{12,4},{14,6},{16,24},{18,... | collective-permute-start | bytes 393224 | tf_op jit(solution)/shard_map/ppermute | solution.py:21
  10.0 0.5 collective-permute-start.1
  10.5 0.5 collective-permute-start
  11.0 3.7 %prepare.1 = (s32[8,64]{1,0:T(8,128)S(1)}, bf16[64,8,64,128]{3,2,1,0:T(8,128)(2,1)S(1)}, bf16[64,4096]{1,0:T(8,128)(2,1)S(1)}, bf16[32,4096]{1,0:T(8,128)(2,1)S(...) custom-call(f32[64,16,64]{2,1,0:T(8,128)} %t_hbm.1, f32[64,64]{1,0:T(8,128)} %d_hbm.1, s32[8,64]{1,0:T(8,128)} %bitcast.14, ...), custom_call_target="tpu_custom_call" | custom-call | tf_op jit(solution)/shard_map/prepare/pallas_call | solution.py:304
  14.7 0.1 collective-permute-done.2
  14.8 0.2 collective-permute-done.1
  14.9 0.5 collective-permute-done
  15.5 1.6 %collective-permute-start.7 = (bf16[2,32,16,128]{3,2,1,0:T(8,128)(2,1)S(1)}, bf16[2,32,16,128]{3,2,1,0:T(8,128)(2,1)S(1)}, u32[]{:S(2)}, u32[]{:S(2)}) collective-permute-start(bf16[2,32,16,128]{3,2,1,0:T(8,128)(2,1)S(1)} %pad_maximum_fusion.1), channel_id=1, source_target_pairs={{0,2},{1,5},{2,0},{3,7},{4,6},{5,1},{6,4},{7,3},{8,10},{9,13},{10,... | collective-permute-start | bytes 786440 | tf_op jit(solution)/shard_map/ppermute | solution.py:30
  17.1 0.8 %collective-permute-start.6 = (bf16[2,32,16,128]{3,2,1,0:T(8,128)(2,1)S(1)}, bf16[2,32,16,128]{3,2,1,0:T(8,128)(2,1)S(1)}, u32[]{:S(2)}, u32[]{:S(2)}) collective-permute-start(bf16[2,32,16,128]{3,2,1,0:T(8,128)(2,1)S(1)} %pad_maximum_fusion.1), channel_id=1, source_target_pairs={{0,4},{1,3},{2,6},{3,1},{4,0},{5,7},{6,2},{7,5},{8,12},{9,11},{10,... | collective-permute-start | bytes 786440 | tf_op jit(solution)/shard_map/ppermute | solution.py:30
  17.9 0.5 collective-permute-start.5
  18.5 4.4 %collective-permute-done.5 = bf16[1,32,16,128]{3,2,1,0:T(8,128)(2,1)S(1)} collective-permute-done((bf16[1,32,16,128]{3,2,1,0:T(8,128)(2,1)S(1)}, bf16[1,32,16,128]{3,2,1,0:T(8,128)(2,1)S(1)}, u32[]{:S(2)}, u32[]{:S(2)}) %collective-permute-start.5) | collective-permute-done | bytes 131104 | tf_op jit(solution)/shard_map/ppermute | solution.py:21
  22.9 0.7 %collective-permute-done.7 = bf16[2,32,16,128]{3,2,1,0:T(8,128)(2,1)S(1)} collective-permute-done((bf16[2,32,16,128]{3,2,1,0:T(8,128)(2,1)S(1)}, bf16[2,32,16,128]{3,2,1,0:T(8,128)(2,1)S(1)}, u32[]{:S(2)}, u32[]{:S(2)}) %collective-permute-start.7) | collective-permute-done | bytes 262176 | tf_op jit(solution)/shard_map/ppermute | solution.py:30
  23.7 0.1 collective-permute-start.11
  23.8 0.7 %collective-permute-start.10 = (bf16[3,32,16,128]{3,2,1,0:T(8,128)(2,1)S(1)}, bf16[3,32,16,128]{3,2,1,0:T(8,128)(2,1)S(1)}, u32[]{:S(2)}, u32[]{:S(2)}) collective-permute-start(bf16[3,32,16,128]{3,2,1,0:T(8,128)(2,1)S(1)} %pad_maximum_fusion), channel_id=1, source_target_pairs={{0,4},{1,3},{2,6},{3,1},{4,0},{5,7},{6,2},{7,5},{8,12},{9,11},{10,... | collective-permute-start | bytes 1179656 | tf_op jit(solution)/shard_map/ppermute | solution.py:30
  24.6 3.3 %collective-permute-start.9 = (bf16[1,32,16,128]{3,2,1,0:T(8,128)(2,1)S(1)}, bf16[1,32,16,128]{3,2,1,0:T(8,128)(2,1)S(1)}, u32[]{:S(2)}, u32[]{:S(2)}) collective-permute-start(bf16[1,32,16,128]{3,2,1,0:T(8,128)(2,1)S(1)} %collective-permute-done.4), channel_id=1, source_target_pairs={{0,24},{2,26},{4,28},{6,30},{8,16},{10,18},{12,20},{14,22},{16,8},... | collective-permute-start | bytes 393224 | tf_op jit(solution)/shard_map/ppermute | solution.py:21
  27.9 0.5 collective-permute-start.8
  28.4 1.1 %assemble.1._ = bf16[1024,16,128]{2,1,0:T(8,128)(2,1)S(1)} custom-call(bf16[352,16,128]{2,1,0:T(8,128)(2,1)S(1)} %bitcast.10, bf16[352,16,128]{2,1,0:T(8,128)(2,1)S(1)} %bitcast.11), custom_call_target="tpu_custom_call" | custom-call | tf_op jit(solution)/shard_map/assemble/pallas_call | solution.py:343
  29.5 2.6 %collective-permute-done.9 = bf16[1,32,16,128]{3,2,1,0:T(8,128)(2,1)S(1)} collective-permute-done((bf16[1,32,16,128]{3,2,1,0:T(8,128)(2,1)S(1)}, bf16[1,32,16,128]{3,2,1,0:T(8,128)(2,1)S(1)}, u32[]{:S(2)}, u32[]{:S(2)}) %collective-permute-start.9) | collective-permute-done | bytes 131104 | tf_op jit(solution)/shard_map/ppermute | solution.py:21
  32.1 0.8 %collective-permute-done.8 = bf16[1,32,16,128]{3,2,1,0:T(8,128)(2,1)S(1)} collective-permute-done((bf16[1,32,16,128]{3,2,1,0:T(8,128)(2,1)S(1)}, bf16[1,32,16,128]{3,2,1,0:T(8,128)(2,1)S(1)}, u32[]{:S(2)}, u32[]{:S(2)}) %collective-permute-start.8) | collective-permute-done | bytes 131104 | tf_op jit(solution)/shard_map/ppermute | solution.py:30
  32.9 0.2 collective-permute-done.10
  33.1 0.1 constant_dynamic-update-slice_fusion.10
  33.2 0.1 collective-permute-start.12
  33.3 2.1 %collective-permute-done.12 = bf16[5,32,16,128]{3,2,1,0:T(8,128)(2,1)S(1)} collective-permute-done((bf16[5,32,16,128]{3,2,1,0:T(8,128)(2,1)S(1)}, bf16[5,32,16,128]{3,2,1,0:T(8,128)(2,1)S(1)}, u32[]{:S(2)}, u32[]{:S(2)}) %collective-permute-start.12) | collective-permute-done | bytes 655392 | tf_op jit(solution)/shard_map/ppermute | solution.py:21
  35.3 4.5 %apply.1 = (bf16[32,4096]{1,0:T(8,128)(2,1)S(1)}, f32[16,128]{1,0:T(8,128)S(1)}, bf16[1024,16,128]{2,1,0:T(8,128)(2,1)S(1)}) custom-call(s32[8,64]{1,0:T(8,128)S(1)} %get-tuple-element.30.rows_ref, bf16[64,8,64,128]{3,2,1,0:T(8,128)(2,1)S(1)} %get-tuple-element.31.ham_ref, bf16[1024,16,128]{2,1,0:T(8,128)(2,1)S(1)} %assemble.1._, ...), custom_call_target="tpu_custom_call", output_to_operand_aliasing={{2}: (2, {})} | custom-call | tf_op jit(solution)/shard_map/apply/pallas_call | solution.py:354
  39.8 0.2 collective-permute-start.13
  40.0 1.0 %collective-permute-done.13 = f32[16,128]{1,0:T(8,128)S(1)} collective-permute-done((f32[16,128]{1,0:T(8,128)S(1)}, f32[16,128]{1,0:T(8,128)S(1)}, u32[]{:S(2)}, u32[]{:S(2)}) %collective-permute-start.13) | collective-permute-done | bytes 8224 | tf_op jit(solution)/shard_map/ppermute | solution.py:21
  41.0 12.4 %all_to_all.5.sums_ref = f32[16,16,128]{2,1,0:T(8,128)S(1)} all-to-all(f32[16,16,128]{2,1,0:T(8,128)S(1)} %broadcast_in_dim.7), channel_id=1, replica_groups=mesh['chan'=16,'rad'=2] {'chan'}, dimensions={0} | all-to-all | bytes 262144 | tf_op jit(solution)/shard_map/all_to_all | solution.py:272
  53.4 2.5 %finish.1 = (f32[64,16,64]{2,1,0:T(8,128)}, f32[1,16]{1,0:T(1,128)}) custom-call(f32[16,16,128]{2,1,0:T(8,128)S(1)} %all_to_all.5.sums_ref, bf16[32,4096]{1,0:T(8,128)(2,1)S(1)} %get-tuple-element.53.az_ref, bf16[64,4096]{1,0:T(8,128)(2,1)S(1)} %get-tuple-element.45.zhm_ref), custom_call_target="tpu_custom_call" | custom-call | tf_op jit(solution)/shard_map/finish/pallas_call | solution.py:370
  (19 shorter events, 0.3 us)
Async XLA Ops:
  1.9 12.8 %collective-permute-start.4 = (bf16[1,32,16,128]{3,2,1,0:T(8,128)(2,1)S(1)}, bf16[1,32,16,128]{3,2,1,0:T(8,128)(2,1)S(1)}, u32[]{:S(2)}, u32[]{:S(2)}) collective-permute-start(bf16[1,32,16,128]{3,2,1,0:T(8,128)(2,1)S(1)} %get-tuple-element.57), channel_id=1, source_target_pairs={{0,6},{2,4},{4,2},{6,0},{8,14},{10,12},{12,10},{14,8},{16,22},{18,... | collective-permute-start | bytes 393224 | tf_op jit(solution)/shard_map/ppermute | solution.py:21
  5.8 8.9 %collective-permute-start.3 = (bf16[1,32,16,128]{3,2,1,0:T(8,128)(2,1)S(1)}, bf16[1,32,16,128]{3,2,1,0:T(8,128)(2,1)S(1)}, u32[]{:S(2)}, u32[]{:S(2)}) collective-permute-start(bf16[1,32,16,128]{3,2,1,0:T(8,128)(2,1)S(1)} %get-tuple-element.57), channel_id=1, source_target_pairs={{0,16},{2,18},{4,20},{6,22},{8,24},{10,26},{12,28},{14,30},{16,0},... | collective-permute-start | bytes 393224 | tf_op jit(solution)/shard_map/ppermute | solution.py:21
  8.4 6.4 %collective-permute-start.2 = (bf16[1,32,16,128]{3,2,1,0:T(8,128)(2,1)S(1)}, bf16[1,32,16,128]{3,2,1,0:T(8,128)(2,1)S(1)}, u32[]{:S(2)}, u32[]{:S(2)}) collective-permute-start(bf16[1,32,16,128]{3,2,1,0:T(8,128)(2,1)S(1)} %get-tuple-element.57), channel_id=1, source_target_pairs={{0,8},{2,10},{4,12},{6,14},{8,0},{10,2},{12,4},{14,6},{16,24},{18,... | collective-permute-start | bytes 393224 | tf_op jit(solution)/shard_map/ppermute | solution.py:21
  10.0 5.0 %collective-permute-start.1 = (bf16[1,32,16,128]{3,2,1,0:T(8,128)(2,1)S(1)}, bf16[1,32,16,128]{3,2,1,0:T(8,128)(2,1)S(1)}, u32[]{:S(2)}, u32[]{:S(2)}) collective-permute-start(bf16[1,32,16,128]{3,2,1,0:T(8,128)(2,1)S(1)} %get-tuple-element.57), channel_id=1, source_target_pairs={{0,2},{1,5},{2,0},{3,7},{4,6},{5,1},{6,4},{7,3},{8,10},{9,13},{10,... | collective-permute-start | bytes 393224 | tf_op jit(solution)/shard_map/ppermute | solution.py:30
  10.5 5.0 %collective-permute-start = (bf16[1,32,16,128]{3,2,1,0:T(8,128)(2,1)S(1)}, bf16[1,32,16,128]{3,2,1,0:T(8,128)(2,1)S(1)}, u32[]{:S(2)}, u32[]{:S(2)}) collective-permute-start(bf16[1,32,16,128]{3,2,1,0:T(8,128)(2,1)S(1)} %get-tuple-element.57), channel_id=1, source_target_pairs={{0,4},{1,3},{2,6},{3,1},{4,0},{5,7},{6,2},{7,5},{8,12},{9,11},{10,... | collective-permute-start | bytes 393224 | tf_op jit(solution)/shard_map/ppermute | solution.py:30
  15.5 8.0 %collective-permute-start.7 = (bf16[2,32,16,128]{3,2,1,0:T(8,128)(2,1)S(1)}, bf16[2,32,16,128]{3,2,1,0:T(8,128)(2,1)S(1)}, u32[]{:S(2)}, u32[]{:S(2)}) collective-permute-start(bf16[2,32,16,128]{3,2,1,0:T(8,128)(2,1)S(1)} %pad_maximum_fusion.1), channel_id=1, source_target_pairs={{0,2},{1,5},{2,0},{3,7},{4,6},{5,1},{6,4},{7,3},{8,10},{9,13},{10,... | collective-permute-start | bytes 786440 | tf_op jit(solution)/shard_map/ppermute | solution.py:30
  17.1 6.5 %collective-permute-start.6 = (bf16[2,32,16,128]{3,2,1,0:T(8,128)(2,1)S(1)}, bf16[2,32,16,128]{3,2,1,0:T(8,128)(2,1)S(1)}, u32[]{:S(2)}, u32[]{:S(2)}) collective-permute-start(bf16[2,32,16,128]{3,2,1,0:T(8,128)(2,1)S(1)} %pad_maximum_fusion.1), channel_id=1, source_target_pairs={{0,4},{1,3},{2,6},{3,1},{4,0},{5,7},{6,2},{7,5},{8,12},{9,11},{10,... | collective-permute-start | bytes 786440 | tf_op jit(solution)/shard_map/ppermute | solution.py:30
  17.9 5.0 %collective-permute-start.5 = (bf16[1,32,16,128]{3,2,1,0:T(8,128)(2,1)S(1)}, bf16[1,32,16,128]{3,2,1,0:T(8,128)(2,1)S(1)}, u32[]{:S(2)}, u32[]{:S(2)}) collective-permute-start(bf16[1,32,16,128]{3,2,1,0:T(8,128)(2,1)S(1)} %collective-permute-done.3), channel_id=1, source_target_pairs={{0,8},{2,10},{4,12},{6,14},{8,0},{10,2},{12,4},{14,6},{16,24},{18,... | collective-permute-start | bytes 393224 | tf_op jit(solution)/shard_map/ppermute | solution.py:21
  23.7 4.7 %collective-permute-start.11 = (bf16[11,32,16,128]{3,2,1,0:T(8,128)(2,1)S(1)}, bf16[11,32,16,128]{3,2,1,0:T(8,128)(2,1)S(1)}, u32[]{:S(2)}, u32[]{:S(2)}) collective-permute-start(bf16[11,32,16,128]{3,2,1,0:T(8,128)(2,1)S(1)} %constant_dynamic-update-slice_fusion), channel_id=1, source_target_pairs={{0,1},{1,0},{2,3},{3,2},{4,5},{5,4},{6,7},{7,6},{8,9},{9,8},{10,11... | collective-permute-start | bytes 4325384 | tf_op jit(solution)/shard_map/ppermute | solution.py:21
  23.8 9.2 %collective-permute-start.10 = (bf16[3,32,16,128]{3,2,1,0:T(8,128)(2,1)S(1)}, bf16[3,32,16,128]{3,2,1,0:T(8,128)(2,1)S(1)}, u32[]{:S(2)}, u32[]{:S(2)}) collective-permute-start(bf16[3,32,16,128]{3,2,1,0:T(8,128)(2,1)S(1)} %pad_maximum_fusion), channel_id=1, source_target_pairs={{0,4},{1,3},{2,6},{3,1},{4,0},{5,7},{6,2},{7,5},{8,12},{9,11},{10,... | collective-permute-start | bytes 1179656 | tf_op jit(solution)/shard_map/ppermute | solution.py:30
  24.6 7.5 %collective-permute-start.9 = (bf16[1,32,16,128]{3,2,1,0:T(8,128)(2,1)S(1)}, bf16[1,32,16,128]{3,2,1,0:T(8,128)(2,1)S(1)}, u32[]{:S(2)}, u32[]{:S(2)}) collective-permute-start(bf16[1,32,16,128]{3,2,1,0:T(8,128)(2,1)S(1)} %collective-permute-done.4), channel_id=1, source_target_pairs={{0,24},{2,26},{4,28},{6,30},{8,16},{10,18},{12,20},{14,22},{16,8},... | collective-permute-start | bytes 393224 | tf_op jit(solution)/shard_map/ppermute | solution.py:21
  27.9 5.0 %collective-permute-start.8 = (bf16[1,32,16,128]{3,2,1,0:T(8,128)(2,1)S(1)}, bf16[1,32,16,128]{3,2,1,0:T(8,128)(2,1)S(1)}, u32[]{:S(2)}, u32[]{:S(2)}) collective-permute-start(bf16[1,32,16,128]{3,2,1,0:T(8,128)(2,1)S(1)} %collective-permute-done.5), channel_id=1, source_target_pairs={{0,2},{1,5},{2,0},{3,7},{4,6},{5,1},{6,4},{7,3},{8,10},{9,13},{10,... | collective-permute-start | bytes 393224 | tf_op jit(solution)/shard_map/ppermute | solution.py:30
  33.2 2.2 %collective-permute-start.12 = (bf16[5,32,16,128]{3,2,1,0:T(8,128)(2,1)S(1)}, bf16[5,32,16,128]{3,2,1,0:T(8,128)(2,1)S(1)}, u32[]{:S(2)}, u32[]{:S(2)}) collective-permute-start(bf16[5,32,16,128]{3,2,1,0:T(8,128)(2,1)S(1)} %constant_dynamic-update-slice_fusion.9), channel_id=1, source_target_pairs={{0,1},{1,0},{2,3},{3,2},{4,5},{5,4},{6,7},{7,6},{8,9},{9,8},{10,11... | collective-permute-start | bytes 1966088 | tf_op jit(solution)/shard_map/ppermute | solution.py:21
  39.8 1.2 %collective-permute-start.13 = (f32[16,128]{1,0:T(8,128)S(1)}, f32[16,128]{1,0:T(8,128)S(1)}, u32[]{:S(2)}, u32[]{:S(2)}) collective-permute-start(f32[16,128]{1,0:T(8,128)S(1)} %get-tuple-element.52), channel_id=1, source_target_pairs={{0,1},{1,0},{2,3},{3,2},{4,5},{5,4},{6,7},{7,6},{8,9},{9,8},{10,11... | collective-permute-start | bytes 24584 | tf_op jit(solution)/shard_map/ppermute | solution.py:21

commit v22 on v21

--- a/solution.py
+++ b/solution.py
@@ -180,7 +180,7 @@
         a0_ref[:, pl.ds(pl.multiple_of(g * 256, 256), 256)] = jnp.concatenate(own, axis=1) * SCALE
         return carry
 
-    lax.fori_loop(0, ch // group, work, 0, unroll=min(8, ch // group))
+    lax.fori_loop(0, ch // group, work, 0, unroll=True)
 
     lanes = ch * r
     block = min(lanes, 1024)
@@ -230,8 +230,14 @@
     known = jnp.concatenate([x[:, :k], s1, s2], axis=0)
     known = known - dot32(jnp.concatenate([x[:, k : 2 * k], b1, b2], axis=0), coef)
     mix, corr, weighted = known[:k], known[k : 2 * k], known[2 * k :]
-    gram = aa - dot32(
-        jnp.concatenate([s2, coef, corr], axis=0), jnp.concatenate([coef, weighted, mix], axis=0), TN
+    left = split3(jnp.concatenate([s2, coef, corr], axis=0))
+    right = split3(jnp.concatenate([coef, weighted, mix], axis=0))
+    pairs = ((0, 0), (0, 1), (1, 0), (1, 1), (0, 2), (2, 0))
+    gram = aa - lax.dot_general(
+        jnp.concatenate([left[i] for i, _ in pairs], axis=0),
+        jnp.concatenate([right[j] for _, j in pairs], axis=0),
+        TN,
+        preferred_element_type=F32,
     )
     cols = [spread(gram, i) for i in range(k)]
     pad = jnp.zeros((k, 128 - 3 * k), F32)

time: 56.1 us -> 55.8 us (level)
  no operation moved by 1% of the time
where the time goes in v22:
time: 55.8 us; the launch traced here: 55.5 us
  starting transfers between devices  16.9 us (30%)
  waiting for transfers between devices  12.6 us (23%)
  blocking collectives  12.4 us (22%)
  Pallas kernels  11.3 us (20%)
  other arithmetic  1.26 us (2%)
  between operations  0.78 us (1%)
    all_to_all x1, blocking collectives, gather_sums(): lax.all_to_all(every, 'chan', split_axis=0, concat_axis=0, tiled=True)  12.4 us
    ppermute x8, starting transfers between devices, swap(): return lax.ppermute(x, axis, [(i, i ^ distance) for i in range(n)])  12.3 us
    ppermute x8, waiting for transfers between devices, swap(): return lax.ppermute(x, axis, [(i, i ^ distance) for i in range(n)])  10.2 us
    ppermute x6, starting transfers between devices, plane_swap(): return lax.ppermute(x, ('chan', 'rad'), pairs)  4.64 us
    pallas_call x1, Pallas kernels, body(): pl.pallas_call(functools.partial(apply_kernel, nz, share), in_specs=[smem...  4.21 us
    pallas_call x1, Pallas kernels, body(): pl.pallas_call(functools.partial(prepare_kernel, n_chan, n_rad), in_specs...  3.66 us
    pallas_call x1, Pallas kernels, body(): pl.pallas_call(functools.partial(finish_kernel, total), out_shape=[jax.Sh...  2.39 us
    ppermute x6, waiting for transfers between devices, plane_swap(): return lax.ppermute(x, ('chan', 'rad'), pairs)  2.35 us
  transfers between devices with their start and end apart: 14, of which 10 were waited for; matrix products, arithmetic and copies ran while one was open for 0% of the time, Pallas kernels for 8%

profile of v22, /device:TPU:0, one launch (start us, length us, event | category | flops | bytes accessed | tf_op | source)
XLA Modules:
  0.0 55.5 jit_solution(675862359898427021)
XLA Ops:
  0.6 1.1 %convert_element_type.3 = bf16[64,16,64]{2,1,0:T(8,128)(2,1)S(1)} convert(f32[64,16,64]{2,1,0:T(8,128)} %t_hbm.1) | non-fusion elementwise | flops 65536 | bytes 393216 | tf_op jit(solution)/shard_map/convert_element_type | solution.py:306
  1.7 0.1 constant_dynamic-update-slice_fusion.8
  1.9 4.0 %collective-permute-start.4 = (bf16[1,32,16,128]{3,2,1,0:T(8,128)(2,1)S(1)}, bf16[1,32,16,128]{3,2,1,0:T(8,128)(2,1)S(1)}, u32[]{:S(2)}, u32[]{:S(2)}) collective-permute-start(bf16[1,32,16,128]{3,2,1,0:T(8,128)(2,1)S(1)} %get-tuple-element.57), channel_id=1, source_target_pairs={{0,6},{2,4},{4,2},{6,0},{8,14},{10,12},{12,10},{14,8},{16,22},{18,... | collective-permute-start | bytes 393224 | tf_op jit(solution)/shard_map/ppermute | solution.py:21
  5.8 2.6 %collective-permute-start.3 = (bf16[1,32,16,128]{3,2,1,0:T(8,128)(2,1)S(1)}, bf16[1,32,16,128]{3,2,1,0:T(8,128)(2,1)S(1)}, u32[]{:S(2)}, u32[]{:S(2)}) collective-permute-start(bf16[1,32,16,128]{3,2,1,0:T(8,128)(2,1)S(1)} %get-tuple-element.57), channel_id=1, source_target_pairs={{0,16},{2,18},{4,20},{6,22},{8,24},{10,26},{12,28},{14,30},{16,0},... | collective-permute-start | bytes 393224 | tf_op jit(solution)/shard_map/ppermute | solution.py:21
  8.4 1.6 %collective-permute-start.2 = (bf16[1,32,16,128]{3,2,1,0:T(8,128)(2,1)S(1)}, bf16[1,32,16,128]{3,2,1,0:T(8,128)(2,1)S(1)}, u32[]{:S(2)}, u32[]{:S(2)}) collective-permute-start(bf16[1,32,16,128]{3,2,1,0:T(8,128)(2,1)S(1)} %get-tuple-element.57), channel_id=1, source_target_pairs={{0,8},{2,10},{4,12},{6,14},{8,0},{10,2},{12,4},{14,6},{16,24},{18,... | collective-permute-start | bytes 393224 | tf_op jit(solution)/shard_map/ppermute | solution.py:21
  10.0 0.5 collective-permute-start.1
  10.5 0.5 collective-permute-start
  11.0 3.7 %prepare.1 = (s32[8,64]{1,0:T(8,128)S(1)}, bf16[64,8,64,128]{3,2,1,0:T(8,128)(2,1)S(1)}, bf16[64,4096]{1,0:T(8,128)(2,1)S(1)}, bf16[32,4096]{1,0:T(8,128)(2,1)S(...) custom-call(f32[64,16,64]{2,1,0:T(8,128)} %t_hbm.1, f32[64,64]{1,0:T(8,128)} %d_hbm.1, s32[8,64]{1,0:T(8,128)} %bitcast.14, ...), custom_call_target="tpu_custom_call" | custom-call | tf_op jit(solution)/shard_map/prepare/pallas_call | solution.py:310
  14.7 0.1 collective-permute-done.2
  14.8 0.2 collective-permute-done.1
  14.9 0.5 collective-permute-done
  15.5 1.6 %collective-permute-start.7 = (bf16[2,32,16,128]{3,2,1,0:T(8,128)(2,1)S(1)}, bf16[2,32,16,128]{3,2,1,0:T(8,128)(2,1)S(1)}, u32[]{:S(2)}, u32[]{:S(2)}) collective-permute-start(bf16[2,32,16,128]{3,2,1,0:T(8,128)(2,1)S(1)} %pad_maximum_fusion.1), channel_id=1, source_target_pairs={{0,2},{1,5},{2,0},{3,7},{4,6},{5,1},{6,4},{7,3},{8,10},{9,13},{10,... | collective-permute-start | bytes 786440 | tf_op jit(solution)/shard_map/ppermute | solution.py:30
  17.1 0.8 %collective-permute-start.6 = (bf16[2,32,16,128]{3,2,1,0:T(8,128)(2,1)S(1)}, bf16[2,32,16,128]{3,2,1,0:T(8,128)(2,1)S(1)}, u32[]{:S(2)}, u32[]{:S(2)}) collective-permute-start(bf16[2,32,16,128]{3,2,1,0:T(8,128)(2,1)S(1)} %pad_maximum_fusion.1), channel_id=1, source_target_pairs={{0,4},{1,3},{2,6},{3,1},{4,0},{5,7},{6,2},{7,5},{8,12},{9,11},{10,... | collective-permute-start | bytes 786440 | tf_op jit(solution)/shard_map/ppermute | solution.py:30
  17.9 0.5 collective-permute-start.5
  18.5 4.4 %collective-permute-done.5 = bf16[1,32,16,128]{3,2,1,0:T(8,128)(2,1)S(1)} collective-permute-done((bf16[1,32,16,128]{3,2,1,0:T(8,128)(2,1)S(1)}, bf16[1,32,16,128]{3,2,1,0:T(8,128)(2,1)S(1)}, u32[]{:S(2)}, u32[]{:S(2)}) %collective-permute-start.5) | collective-permute-done | bytes 131104 | tf_op jit(solution)/shard_map/ppermute | solution.py:21
  22.9 0.7 %collective-permute-done.7 = bf16[2,32,16,128]{3,2,1,0:T(8,128)(2,1)S(1)} collective-permute-done((bf16[2,32,16,128]{3,2,1,0:T(8,128)(2,1)S(1)}, bf16[2,32,16,128]{3,2,1,0:T(8,128)(2,1)S(1)}, u32[]{:S(2)}, u32[]{:S(2)}) %collective-permute-start.7) | collective-permute-done | bytes 262176 | tf_op jit(solution)/shard_map/ppermute | solution.py:30
  23.7 0.1 collective-permute-start.11
  23.8 0.7 %collective-permute-start.10 = (bf16[3,32,16,128]{3,2,1,0:T(8,128)(2,1)S(1)}, bf16[3,32,16,128]{3,2,1,0:T(8,128)(2,1)S(1)}, u32[]{:S(2)}, u32[]{:S(2)}) collective-permute-start(bf16[3,32,16,128]{3,2,1,0:T(8,128)(2,1)S(1)} %pad_maximum_fusion), channel_id=1, source_target_pairs={{0,4},{1,3},{2,6},{3,1},{4,0},{5,7},{6,2},{7,5},{8,12},{9,11},{10,... | collective-permute-start | bytes 1179656 | tf_op jit(solution)/shard_map/ppermute | solution.py:30
  24.6 3.3 %collective-permute-start.9 = (bf16[1,32,16,128]{3,2,1,0:T(8,128)(2,1)S(1)}, bf16[1,32,16,128]{3,2,1,0:T(8,128)(2,1)S(1)}, u32[]{:S(2)}, u32[]{:S(2)}) collective-permute-start(bf16[1,32,16,128]{3,2,1,0:T(8,128)(2,1)S(1)} %collective-permute-done.4), channel_id=1, source_target_pairs={{0,24},{2,26},{4,28},{6,30},{8,16},{10,18},{12,20},{14,22},{16,8},... | collective-permute-start | bytes 393224 | tf_op jit(solution)/shard_map/ppermute | solution.py:21
  27.9 0.5 collective-permute-start.8
  28.4 1.1 %assemble.1._ = bf16[1024,16,128]{2,1,0:T(8,128)(2,1)S(1)} custom-call(bf16[352,16,128]{2,1,0:T(8,128)(2,1)S(1)} %bitcast.10, bf16[352,16,128]{2,1,0:T(8,128)(2,1)S(1)} %bitcast.11), custom_call_target="tpu_custom_call" | custom-call | tf_op jit(solution)/shard_map/assemble/pallas_call | solution.py:349
  29.5 2.6 %collective-permute-done.9 = bf16[1,32,16,128]{3,2,1,0:T(8,128)(2,1)S(1)} collective-permute-done((bf16[1,32,16,128]{3,2,1,0:T(8,128)(2,1)S(1)}, bf16[1,32,16,128]{3,2,1,0:T(8,128)(2,1)S(1)}, u32[]{:S(2)}, u32[]{:S(2)}) %collective-permute-start.9) | collective-permute-done | bytes 131104 | tf_op jit(solution)/shard_map/ppermute | solution.py:21
  32.1 0.8 %collective-permute-done.8 = bf16[1,32,16,128]{3,2,1,0:T(8,128)(2,1)S(1)} collective-permute-done((bf16[1,32,16,128]{3,2,1,0:T(8,128)(2,1)S(1)}, bf16[1,32,16,128]{3,2,1,0:T(8,128)(2,1)S(1)}, u32[]{:S(2)}, u32[]{:S(2)}) %collective-permute-start.8) | collective-permute-done | bytes 131104 | tf_op jit(solution)/shard_map/ppermute | solution.py:30
  32.9 0.2 collective-permute-done.10
  33.1 0.1 constant_dynamic-update-slice_fusion.10
  33.2 0.1 collective-permute-start.12
  33.3 2.1 %collective-permute-done.12 = bf16[5,32,16,128]{3,2,1,0:T(8,128)(2,1)S(1)} collective-permute-done((bf16[5,32,16,128]{3,2,1,0:T(8,128)(2,1)S(1)}, bf16[5,32,16,128]{3,2,1,0:T(8,128)(2,1)S(1)}, u32[]{:S(2)}, u32[]{:S(2)}) %collective-permute-start.12) | collective-permute-done | bytes 655392 | tf_op jit(solution)/shard_map/ppermute | solution.py:21
  35.3 4.2 %apply.1 = (bf16[32,4096]{1,0:T(8,128)(2,1)S(1)}, f32[16,128]{1,0:T(8,128)S(1)}, bf16[1024,16,128]{2,1,0:T(8,128)(2,1)S(1)}) custom-call(s32[8,64]{1,0:T(8,128)S(1)} %get-tuple-element.30.rows_ref, bf16[64,8,64,128]{3,2,1,0:T(8,128)(2,1)S(1)} %get-tuple-element.31.ham_ref, bf16[1024,16,128]{2,1,0:T(8,128)(2,1)S(1)} %assemble.1._, ...), custom_call_target="tpu_custom_call", output_to_operand_aliasing={{2}: (2, {})} | custom-call | tf_op jit(solution)/shard_map/apply/pallas_call | solution.py:360
  39.6 0.2 collective-permute-start.13
  39.7 1.0 %collective-permute-done.13 = f32[16,128]{1,0:T(8,128)S(1)} collective-permute-done((f32[16,128]{1,0:T(8,128)S(1)}, f32[16,128]{1,0:T(8,128)S(1)}, u32[]{:S(2)}, u32[]{:S(2)}) %collective-permute-start.13) | collective-permute-done | bytes 8224 | tf_op jit(solution)/shard_map/ppermute | solution.py:21
  40.8 12.4 %all_to_all.5.sums_ref = f32[16,16,128]{2,1,0:T(8,128)S(1)} all-to-all(f32[16,16,128]{2,1,0:T(8,128)S(1)} %broadcast_in_dim.7), channel_id=1, replica_groups=mesh['chan'=16,'rad'=2] {'chan'}, dimensions={0} | all-to-all | bytes 262144 | tf_op jit(solution)/shard_map/all_to_all | solution.py:278
  53.2 2.4 %finish.1 = (f32[64,16,64]{2,1,0:T(8,128)}, f32[1,16]{1,0:T(1,128)}) custom-call(f32[16,16,128]{2,1,0:T(8,128)S(1)} %all_to_all.5.sums_ref, bf16[32,4096]{1,0:T(8,128)(2,1)S(1)} %get-tuple-element.53.az_ref, bf16[64,4096]{1,0:T(8,128)(2,1)S(1)} %get-tuple-element.45.zhm_ref), custom_call_target="tpu_custom_call" | custom-call | tf_op jit(solution)/shard_map/finish/pallas_call | solution.py:376
  (19 shorter events, 0.3 us)
Async XLA Ops:
  1.9 12.8 %collective-permute-start.4 = (bf16[1,32,16,128]{3,2,1,0:T(8,128)(2,1)S(1)}, bf16[1,32,16,128]{3,2,1,0:T(8,128)(2,1)S(1)}, u32[]{:S(2)}, u32[]{:S(2)}) collective-permute-start(bf16[1,32,16,128]{3,2,1,0:T(8,128)(2,1)S(1)} %get-tuple-element.57), channel_id=1, source_target_pairs={{0,6},{2,4},{4,2},{6,0},{8,14},{10,12},{12,10},{14,8},{16,22},{18,... | collective-permute-start | bytes 393224 | tf_op jit(solution)/shard_map/ppermute | solution.py:21
  5.8 8.9 %collective-permute-start.3 = (bf16[1,32,16,128]{3,2,1,0:T(8,128)(2,1)S(1)}, bf16[1,32,16,128]{3,2,1,0:T(8,128)(2,1)S(1)}, u32[]{:S(2)}, u32[]{:S(2)}) collective-permute-start(bf16[1,32,16,128]{3,2,1,0:T(8,128)(2,1)S(1)} %get-tuple-element.57), channel_id=1, source_target_pairs={{0,16},{2,18},{4,20},{6,22},{8,24},{10,26},{12,28},{14,30},{16,0},... | collective-permute-start | bytes 393224 | tf_op jit(solution)/shard_map/ppermute | solution.py:21
  8.4 6.4 %collective-permute-start.2 = (bf16[1,32,16,128]{3,2,1,0:T(8,128)(2,1)S(1)}, bf16[1,32,16,128]{3,2,1,0:T(8,128)(2,1)S(1)}, u32[]{:S(2)}, u32[]{:S(2)}) collective-permute-start(bf16[1,32,16,128]{3,2,1,0:T(8,128)(2,1)S(1)} %get-tuple-element.57), channel_id=1, source_target_pairs={{0,8},{2,10},{4,12},{6,14},{8,0},{10,2},{12,4},{14,6},{16,24},{18,... | collective-permute-start | bytes 393224 | tf_op jit(solution)/shard_map/ppermute | solution.py:21
  10.0 5.0 %collective-permute-start.1 = (bf16[1,32,16,128]{3,2,1,0:T(8,128)(2,1)S(1)}, bf16[1,32,16,128]{3,2,1,0:T(8,128)(2,1)S(1)}, u32[]{:S(2)}, u32[]{:S(2)}) collective-permute-start(bf16[1,32,16,128]{3,2,1,0:T(8,128)(2,1)S(1)} %get-tuple-element.57), channel_id=1, source_target_pairs={{0,2},{1,5},{2,0},{3,7},{4,6},{5,1},{6,4},{7,3},{8,10},{9,13},{10,... | collective-permute-start | bytes 393224 | tf_op jit(solution)/shard_map/ppermute | solution.py:30
  10.5 5.0 %collective-permute-start = (bf16[1,32,16,128]{3,2,1,0:T(8,128)(2,1)S(1)}, bf16[1,32,16,128]{3,2,1,0:T(8,128)(2,1)S(1)}, u32[]{:S(2)}, u32[]{:S(2)}) collective-permute-start(bf16[1,32,16,128]{3,2,1,0:T(8,128)(2,1)S(1)} %get-tuple-element.57), channel_id=1, source_target_pairs={{0,4},{1,3},{2,6},{3,1},{4,0},{5,7},{6,2},{7,5},{8,12},{9,11},{10,... | collective-permute-start | bytes 393224 | tf_op jit(solution)/shard_map/ppermute | solution.py:30
  15.5 8.0 %collective-permute-start.7 = (bf16[2,32,16,128]{3,2,1,0:T(8,128)(2,1)S(1)}, bf16[2,32,16,128]{3,2,1,0:T(8,128)(2,1)S(1)}, u32[]{:S(2)}, u32[]{:S(2)}) collective-permute-start(bf16[2,32,16,128]{3,2,1,0:T(8,128)(2,1)S(1)} %pad_maximum_fusion.1), channel_id=1, source_target_pairs={{0,2},{1,5},{2,0},{3,7},{4,6},{5,1},{6,4},{7,3},{8,10},{9,13},{10,... | collective-permute-start | bytes 786440 | tf_op jit(solution)/shard_map/ppermute | solution.py:30
  17.1 6.5 %collective-permute-start.6 = (bf16[2,32,16,128]{3,2,1,0:T(8,128)(2,1)S(1)}, bf16[2,32,16,128]{3,2,1,0:T(8,128)(2,1)S(1)}, u32[]{:S(2)}, u32[]{:S(2)}) collective-permute-start(bf16[2,32,16,128]{3,2,1,0:T(8,128)(2,1)S(1)} %pad_maximum_fusion.1), channel_id=1, source_target_pairs={{0,4},{1,3},{2,6},{3,1},{4,0},{5,7},{6,2},{7,5},{8,12},{9,11},{10,... | collective-permute-start | bytes 786440 | tf_op jit(solution)/shard_map/ppermute | solution.py:30
  17.9 5.0 %collective-permute-start.5 = (bf16[1,32,16,128]{3,2,1,0:T(8,128)(2,1)S(1)}, bf16[1,32,16,128]{3,2,1,0:T(8,128)(2,1)S(1)}, u32[]{:S(2)}, u32[]{:S(2)}) collective-permute-start(bf16[1,32,16,128]{3,2,1,0:T(8,128)(2,1)S(1)} %collective-permute-done.3), channel_id=1, source_target_pairs={{0,8},{2,10},{4,12},{6,14},{8,0},{10,2},{12,4},{14,6},{16,24},{18,... | collective-permute-start | bytes 393224 | tf_op jit(solution)/shard_map/ppermute | solution.py:21
  23.7 4.7 %collective-permute-start.11 = (bf16[11,32,16,128]{3,2,1,0:T(8,128)(2,1)S(1)}, bf16[11,32,16,128]{3,2,1,0:T(8,128)(2,1)S(1)}, u32[]{:S(2)}, u32[]{:S(2)}) collective-permute-start(bf16[11,32,16,128]{3,2,1,0:T(8,128)(2,1)S(1)} %constant_dynamic-update-slice_fusion), channel_id=1, source_target_pairs={{0,1},{1,0},{2,3},{3,2},{4,5},{5,4},{6,7},{7,6},{8,9},{9,8},{10,11... | collective-permute-start | bytes 4325384 | tf_op jit(solution)/shard_map/ppermute | solution.py:21
  23.8 9.2 %collective-permute-start.10 = (bf16[3,32,16,128]{3,2,1,0:T(8,128)(2,1)S(1)}, bf16[3,32,16,128]{3,2,1,0:T(8,128)(2,1)S(1)}, u32[]{:S(2)}, u32[]{:S(2)}) collective-permute-start(bf16[3,32,16,128]{3,2,1,0:T(8,128)(2,1)S(1)} %pad_maximum_fusion), channel_id=1, source_target_pairs={{0,4},{1,3},{2,6},{3,1},{4,0},{5,7},{6,2},{7,5},{8,12},{9,11},{10,... | collective-permute-start | bytes 1179656 | tf_op jit(solution)/shard_map/ppermute | solution.py:30
  24.6 7.5 %collective-permute-start.9 = (bf16[1,32,16,128]{3,2,1,0:T(8,128)(2,1)S(1)}, bf16[1,32,16,128]{3,2,1,0:T(8,128)(2,1)S(1)}, u32[]{:S(2)}, u32[]{:S(2)}) collective-permute-start(bf16[1,32,16,128]{3,2,1,0:T(8,128)(2,1)S(1)} %collective-permute-done.4), channel_id=1, source_target_pairs={{0,24},{2,26},{4,28},{6,30},{8,16},{10,18},{12,20},{14,22},{16,8},... | collective-permute-start | bytes 393224 | tf_op jit(solution)/shard_map/ppermute | solution.py:21
  27.9 5.0 %collective-permute-start.8 = (bf16[1,32,16,128]{3,2,1,0:T(8,128)(2,1)S(1)}, bf16[1,32,16,128]{3,2,1,0:T(8,128)(2,1)S(1)}, u32[]{:S(2)}, u32[]{:S(2)}) collective-permute-start(bf16[1,32,16,128]{3,2,1,0:T(8,128)(2,1)S(1)} %collective-permute-done.5), channel_id=1, source_target_pairs={{0,2},{1,5},{2,0},{3,7},{4,6},{5,1},{6,4},{7,3},{8,10},{9,13},{10,... | collective-permute-start | bytes 393224 | tf_op jit(solution)/shard_map/ppermute | solution.py:30
  33.2 2.2 %collective-permute-start.12 = (bf16[5,32,16,128]{3,2,1,0:T(8,128)(2,1)S(1)}, bf16[5,32,16,128]{3,2,1,0:T(8,128)(2,1)S(1)}, u32[]{:S(2)}, u32[]{:S(2)}) collective-permute-start(bf16[5,32,16,128]{3,2,1,0:T(8,128)(2,1)S(1)} %constant_dynamic-update-slice_fusion.9), channel_id=1, source_target_pairs={{0,1},{1,0},{2,3},{3,2},{4,5},{5,4},{6,7},{7,6},{8,9},{9,8},{10,11... | collective-permute-start | bytes 1966088 | tf_op jit(solution)/shard_map/ppermute | solution.py:21
  39.6 1.2 %collective-permute-start.13 = (f32[16,128]{1,0:T(8,128)S(1)}, f32[16,128]{1,0:T(8,128)S(1)}, u32[]{:S(2)}, u32[]{:S(2)}) collective-permute-start(f32[16,128]{1,0:T(8,128)S(1)} %get-tuple-element.52), channel_id=1, source_target_pairs={{0,1},{1,0},{2,3},{3,2},{4,5},{5,4},{6,7},{7,6},{8,9},{9,8},{10,11... | collective-permute-start | bytes 24584 | tf_op jit(solution)/shard_map/ppermute | solution.py:21

commit v23 on v22

--- a/solution.py
+++ b/solution.py
@@ -335,7 +335,7 @@
         in_hbm(stored_at.reshape(-1, 128)),
         in_hbm(ham_blocks),
     )
-    far_own, near0, z1, z_even, diag0, rows = barrier((far_own, near0, z1, z_even, diag0, rows))
+    far_own, near0, z1, diag0, z_even, rows = barrier((far_own, near0, z1, diag0, z_even, rows))
     some, z_even, diag0 = barrier((jnp.concatenate([z1, z_even]), z_even, diag0))
     near1, far1 = near_of(some), far_of(some)
     z_odd = swap(z_even, "chan", 4)

time: 55.8 us -> 55.1 us (0.987)
  blocking collectives: 12.4 us -> 11.7 us
    ppermute x8, starting transfers between devices: 12.3 us -> 11 us  [swap(): return lax.ppermute(x, axis, [(i, i ^ distance) for i in range(n)])]
    ppermute x6, starting transfers between devices: 4.64 us -> 5.71 us  [plane_swap(): return lax.ppermute(x, ('chan', 'rad'), pairs)]
    all_to_all x1, blocking collectives: 12.4 us -> 11.7 us  [gather_sums(): lax.all_to_all(every, 'chan', split_axis=0, concat_axis=0, tiled=True)]
  transfers between devices with their start and end apart: 14 -> 14, of which waited for: 10 -> 9; matrix products, arithmetic and copies ran while one was open for 0% -> 0% of each run, Pallas kernels for 8% -> 9%
where the time goes in v23:
time: 55.1 us; the launch traced here: 54.9 us
  starting transfers between devices  16.7 us (30%)
  waiting for transfers between devices  12.8 us (23%)
  blocking collectives  11.7 us (21%)
  Pallas kernels  11.3 us (21%)
  other arithmetic  1.26 us (2%)
  between operations  0.79 us (1%)
    all_to_all x1, blocking collectives, gather_sums(): lax.all_to_all(every, 'chan', split_axis=0, concat_axis=0, tiled=True)  11.7 us
    ppermute x8, starting transfers between devices, swap(): return lax.ppermute(x, axis, [(i, i ^ distance) for i in range(n)])  11 us
    ppermute x8, waiting for transfers between devices, swap(): return lax.ppermute(x, axis, [(i, i ^ distance) for i in range(n)])  10.6 us
    ppermute x6, starting transfers between devices, plane_swap(): return lax.ppermute(x, ('chan', 'rad'), pairs)  5.71 us
    pallas_call x1, Pallas kernels, body(): pl.pallas_call(functools.partial(apply_kernel, nz, share), in_specs=[smem...  4.21 us
    pallas_call x1, Pallas kernels, body(): pl.pallas_call(functools.partial(prepare_kernel, n_chan, n_rad), in_specs...  3.66 us
    pallas_call x1, Pallas kernels, body(): pl.pallas_call(functools.partial(finish_kernel, total), out_shape=[jax.Sh...  2.39 us
    ppermute x6, waiting for transfers between devices, plane_swap(): return lax.ppermute(x, ('chan', 'rad'), pairs)  2.19 us
  transfers between devices with their start and end apart: 14, of which 9 were waited for; matrix products, arithmetic and copies ran while one was open for 0% of the time, Pallas kernels for 9%

profile of v23, /device:TPU:0, one launch (start us, length us, event | category | flops | bytes accessed | tf_op | source)
XLA Modules:
  0.0 54.9 jit_solution(2586738481365959273)
XLA Ops:
  0.6 1.1 %convert_element_type.3 = bf16[64,16,64]{2,1,0:T(8,128)(2,1)S(1)} convert(f32[64,16,64]{2,1,0:T(8,128)} %t_hbm.1) | non-fusion elementwise | flops 65536 | bytes 393216 | tf_op jit(solution)/shard_map/convert_element_type | solution.py:306
  1.7 0.1 constant_dynamic-update-slice_fusion.8
  1.9 4.1 %collective-permute-start.4 = (bf16[1,32,16,128]{3,2,1,0:T(8,128)(2,1)S(1)}, bf16[1,32,16,128]{3,2,1,0:T(8,128)(2,1)S(1)}, u32[]{:S(2)}, u32[]{:S(2)}) collective-permute-start(bf16[1,32,16,128]{3,2,1,0:T(8,128)(2,1)S(1)} %get-tuple-element.57), channel_id=1, source_target_pairs={{0,16},{2,18},{4,20},{6,22},{8,24},{10,26},{12,28},{14,30},{16,0},... | collective-permute-start | bytes 393224 | tf_op jit(solution)/shard_map/ppermute | solution.py:21
  6.0 2.4 %collective-permute-start.3 = (bf16[1,32,16,128]{3,2,1,0:T(8,128)(2,1)S(1)}, bf16[1,32,16,128]{3,2,1,0:T(8,128)(2,1)S(1)}, u32[]{:S(2)}, u32[]{:S(2)}) collective-permute-start(bf16[1,32,16,128]{3,2,1,0:T(8,128)(2,1)S(1)} %get-tuple-element.57), channel_id=1, source_target_pairs={{0,6},{2,4},{4,2},{6,0},{8,14},{10,12},{12,10},{14,8},{16,22},{18,... | collective-permute-start | bytes 393224 | tf_op jit(solution)/shard_map/ppermute | solution.py:21
  8.4 1.6 %collective-permute-start.2 = (bf16[1,32,16,128]{3,2,1,0:T(8,128)(2,1)S(1)}, bf16[1,32,16,128]{3,2,1,0:T(8,128)(2,1)S(1)}, u32[]{:S(2)}, u32[]{:S(2)}) collective-permute-start(bf16[1,32,16,128]{3,2,1,0:T(8,128)(2,1)S(1)} %get-tuple-element.57), channel_id=1, source_target_pairs={{0,8},{2,10},{4,12},{6,14},{8,0},{10,2},{12,4},{14,6},{16,24},{18,... | collective-permute-start | bytes 393224 | tf_op jit(solution)/shard_map/ppermute | solution.py:21
  10.0 0.5 collective-permute-start.1
  10.5 0.5 collective-permute-start
  11.0 3.7 %prepare.1 = (s32[8,64]{1,0:T(8,128)S(1)}, bf16[64,8,64,128]{3,2,1,0:T(8,128)(2,1)S(1)}, bf16[64,4096]{1,0:T(8,128)(2,1)S(1)}, bf16[32,4096]{1,0:T(8,128)(2,1)S(...) custom-call(f32[64,16,64]{2,1,0:T(8,128)} %t_hbm.1, f32[64,64]{1,0:T(8,128)} %d_hbm.1, s32[8,64]{1,0:T(8,128)} %bitcast.14, ...), custom_call_target="tpu_custom_call" | custom-call | tf_op jit(solution)/shard_map/prepare/pallas_call | solution.py:310
  14.7 0.0 collective-permute-done.3
  14.7 0.2 collective-permute-done.1
  14.9 0.5 collective-permute-done
  15.5 1.6 %collective-permute-start.7 = (bf16[2,32,16,128]{3,2,1,0:T(8,128)(2,1)S(1)}, bf16[2,32,16,128]{3,2,1,0:T(8,128)(2,1)S(1)}, u32[]{:S(2)}, u32[]{:S(2)}) collective-permute-start(bf16[2,32,16,128]{3,2,1,0:T(8,128)(2,1)S(1)} %pad_maximum_fusion.1), channel_id=1, source_target_pairs={{0,2},{1,5},{2,0},{3,7},{4,6},{5,1},{6,4},{7,3},{8,10},{9,13},{10,... | collective-permute-start | bytes 786440 | tf_op jit(solution)/shard_map/ppermute | solution.py:30
  17.1 0.8 %collective-permute-start.6 = (bf16[2,32,16,128]{3,2,1,0:T(8,128)(2,1)S(1)}, bf16[2,32,16,128]{3,2,1,0:T(8,128)(2,1)S(1)}, u32[]{:S(2)}, u32[]{:S(2)}) collective-permute-start(bf16[2,32,16,128]{3,2,1,0:T(8,128)(2,1)S(1)} %pad_maximum_fusion.1), channel_id=1, source_target_pairs={{0,4},{1,3},{2,6},{3,1},{4,0},{5,7},{6,2},{7,5},{8,12},{9,11},{10,... | collective-permute-start | bytes 786440 | tf_op jit(solution)/shard_map/ppermute | solution.py:30
  17.9 1.0 %collective-permute-start.5 = (bf16[1,32,16,128]{3,2,1,0:T(8,128)(2,1)S(1)}, bf16[1,32,16,128]{3,2,1,0:T(8,128)(2,1)S(1)}, u32[]{:S(2)}, u32[]{:S(2)}) collective-permute-start(bf16[1,32,16,128]{3,2,1,0:T(8,128)(2,1)S(1)} %collective-permute-done.4), channel_id=1, source_target_pairs={{0,8},{2,10},{4,12},{6,14},{8,0},{10,2},{12,4},{14,6},{16,24},{18,... | collective-permute-start | bytes 393224 | tf_op jit(solution)/shard_map/ppermute | solution.py:21
  18.9 4.0 %collective-permute-done.5 = bf16[1,32,16,128]{3,2,1,0:T(8,128)(2,1)S(1)} collective-permute-done((bf16[1,32,16,128]{3,2,1,0:T(8,128)(2,1)S(1)}, bf16[1,32,16,128]{3,2,1,0:T(8,128)(2,1)S(1)}, u32[]{:S(2)}, u32[]{:S(2)}) %collective-permute-start.5) | collective-permute-done | bytes 131104 | tf_op jit(solution)/shard_map/ppermute | solution.py:21
  22.9 0.7 %collective-permute-done.7 = bf16[2,32,16,128]{3,2,1,0:T(8,128)(2,1)S(1)} collective-permute-done((bf16[2,32,16,128]{3,2,1,0:T(8,128)(2,1)S(1)}, bf16[2,32,16,128]{3,2,1,0:T(8,128)(2,1)S(1)}, u32[]{:S(2)}, u32[]{:S(2)}) %collective-permute-start.7) | collective-permute-done | bytes 262176 | tf_op jit(solution)/shard_map/ppermute | solution.py:30
  23.7 0.1 collective-permute-start.11
  23.8 0.8 %collective-permute-start.10 = (bf16[3,32,16,128]{3,2,1,0:T(8,128)(2,1)S(1)}, bf16[3,32,16,128]{3,2,1,0:T(8,128)(2,1)S(1)}, u32[]{:S(2)}, u32[]{:S(2)}) collective-permute-start(bf16[3,32,16,128]{3,2,1,0:T(8,128)(2,1)S(1)} %pad_maximum_fusion), channel_id=1, source_target_pairs={{0,4},{1,3},{2,6},{3,1},{4,0},{5,7},{6,2},{7,5},{8,12},{9,11},{10,... | collective-permute-start | bytes 1179656 | tf_op jit(solution)/shard_map/ppermute | solution.py:30
  24.7 1.6 %collective-permute-start.9 = (bf16[1,32,16,128]{3,2,1,0:T(8,128)(2,1)S(1)}, bf16[1,32,16,128]{3,2,1,0:T(8,128)(2,1)S(1)}, u32[]{:S(2)}, u32[]{:S(2)}) collective-permute-start(bf16[1,32,16,128]{3,2,1,0:T(8,128)(2,1)S(1)} %collective-permute-done.3), channel_id=1, source_target_pairs={{0,24},{2,26},{4,28},{6,30},{8,16},{10,18},{12,20},{14,22},{16,8},... | collective-permute-start | bytes 393224 | tf_op jit(solution)/shard_map/ppermute | solution.py:21
  26.3 1.5 %collective-permute-start.8 = (bf16[1,32,16,128]{3,2,1,0:T(8,128)(2,1)S(1)}, bf16[1,32,16,128]{3,2,1,0:T(8,128)(2,1)S(1)}, u32[]{:S(2)}, u32[]{:S(2)}) collective-permute-start(bf16[1,32,16,128]{3,2,1,0:T(8,128)(2,1)S(1)} %collective-permute-done.5), channel_id=1, source_target_pairs={{0,2},{1,5},{2,0},{3,7},{4,6},{5,1},{6,4},{7,3},{8,10},{9,13},{10,... | collective-permute-start | bytes 393224 | tf_op jit(solution)/shard_map/ppermute | solution.py:30
  27.8 1.1 %assemble.1._ = bf16[1024,16,128]{2,1,0:T(8,128)(2,1)S(1)} custom-call(bf16[352,16,128]{2,1,0:T(8,128)(2,1)S(1)} %bitcast.10, bf16[352,16,128]{2,1,0:T(8,128)(2,1)S(1)} %bitcast.11), custom_call_target="tpu_custom_call" | custom-call | tf_op jit(solution)/shard_map/assemble/pallas_call | solution.py:349
  28.8 3.5 %collective-permute-done.9 = bf16[1,32,16,128]{3,2,1,0:T(8,128)(2,1)S(1)} collective-permute-done((bf16[1,32,16,128]{3,2,1,0:T(8,128)(2,1)S(1)}, bf16[1,32,16,128]{3,2,1,0:T(8,128)(2,1)S(1)}, u32[]{:S(2)}, u32[]{:S(2)}) %collective-permute-start.9) | collective-permute-done | bytes 131104 | tf_op jit(solution)/shard_map/ppermute | solution.py:21
  32.3 0.3 collective-permute-done.8
  32.6 0.5 collective-permute-done.10
  33.1 0.1 constant_dynamic-update-slice_fusion.10
  33.2 0.1 collective-permute-start.12
  33.3 2.1 %collective-permute-done.12 = bf16[5,32,16,128]{3,2,1,0:T(8,128)(2,1)S(1)} collective-permute-done((bf16[5,32,16,128]{3,2,1,0:T(8,128)(2,1)S(1)}, bf16[5,32,16,128]{3,2,1,0:T(8,128)(2,1)S(1)}, u32[]{:S(2)}, u32[]{:S(2)}) %collective-permute-start.12) | collective-permute-done | bytes 655392 | tf_op jit(solution)/shard_map/ppermute | solution.py:21
  35.3 4.2 %apply.1 = (bf16[32,4096]{1,0:T(8,128)(2,1)S(1)}, f32[16,128]{1,0:T(8,128)S(1)}, bf16[1024,16,128]{2,1,0:T(8,128)(2,1)S(1)}) custom-call(s32[8,64]{1,0:T(8,128)S(1)} %get-tuple-element.30.rows_ref, bf16[64,8,64,128]{3,2,1,0:T(8,128)(2,1)S(1)} %get-tuple-element.31.ham_ref, bf16[1024,16,128]{2,1,0:T(8,128)(2,1)S(1)} %assemble.1._, ...), custom_call_target="tpu_custom_call", output_to_operand_aliasing={{2}: (2, {})} | custom-call | tf_op jit(solution)/shard_map/apply/pallas_call | solution.py:360
  39.5 0.2 collective-permute-start.13
  39.7 1.0 %collective-permute-done.13 = f32[16,128]{1,0:T(8,128)S(1)} collective-permute-done((f32[16,128]{1,0:T(8,128)S(1)}, f32[16,128]{1,0:T(8,128)S(1)}, u32[]{:S(2)}, u32[]{:S(2)}) %collective-permute-start.13) | collective-permute-done | bytes 8224 | tf_op jit(solution)/shard_map/ppermute | solution.py:21
  40.8 11.7 %all_to_all.5.sums_ref = f32[16,16,128]{2,1,0:T(8,128)S(1)} all-to-all(f32[16,16,128]{2,1,0:T(8,128)S(1)} %broadcast_in_dim.7), channel_id=1, replica_groups=mesh['chan'=16,'rad'=2] {'chan'}, dimensions={0} | all-to-all | bytes 262144 | tf_op jit(solution)/shard_map/all_to_all | solution.py:278
  52.5 2.4 %finish.1 = (f32[64,16,64]{2,1,0:T(8,128)}, f32[1,16]{1,0:T(1,128)}) custom-call(f32[16,16,128]{2,1,0:T(8,128)S(1)} %all_to_all.5.sums_ref, bf16[32,4096]{1,0:T(8,128)(2,1)S(1)} %get-tuple-element.53.az_ref, bf16[64,4096]{1,0:T(8,128)(2,1)S(1)} %get-tuple-element.45.zhm_ref), custom_call_target="tpu_custom_call" | custom-call | tf_op jit(solution)/shard_map/finish/pallas_call | solution.py:376
  (19 shorter events, 0.3 us)
Async XLA Ops:
  1.9 12.8 %collective-permute-start.4 = (bf16[1,32,16,128]{3,2,1,0:T(8,128)(2,1)S(1)}, bf16[1,32,16,128]{3,2,1,0:T(8,128)(2,1)S(1)}, u32[]{:S(2)}, u32[]{:S(2)}) collective-permute-start(bf16[1,32,16,128]{3,2,1,0:T(8,128)(2,1)S(1)} %get-tuple-element.57), channel_id=1, source_target_pairs={{0,16},{2,18},{4,20},{6,22},{8,24},{10,26},{12,28},{14,30},{16,0},... | collective-permute-start | bytes 393224 | tf_op jit(solution)/shard_map/ppermute | solution.py:21
  6.0 8.7 %collective-permute-start.3 = (bf16[1,32,16,128]{3,2,1,0:T(8,128)(2,1)S(1)}, bf16[1,32,16,128]{3,2,1,0:T(8,128)(2,1)S(1)}, u32[]{:S(2)}, u32[]{:S(2)}) collective-permute-start(bf16[1,32,16,128]{3,2,1,0:T(8,128)(2,1)S(1)} %get-tuple-element.57), channel_id=1, source_target_pairs={{0,6},{2,4},{4,2},{6,0},{8,14},{10,12},{12,10},{14,8},{16,22},{18,... | collective-permute-start | bytes 393224 | tf_op jit(solution)/shard_map/ppermute | solution.py:21
  8.4 6.3 %collective-permute-start.2 = (bf16[1,32,16,128]{3,2,1,0:T(8,128)(2,1)S(1)}, bf16[1,32,16,128]{3,2,1,0:T(8,128)(2,1)S(1)}, u32[]{:S(2)}, u32[]{:S(2)}) collective-permute-start(bf16[1,32,16,128]{3,2,1,0:T(8,128)(2,1)S(1)} %get-tuple-element.57), channel_id=1, source_target_pairs={{0,8},{2,10},{4,12},{6,14},{8,0},{10,2},{12,4},{14,6},{16,24},{18,... | collective-permute-start | bytes 393224 | tf_op jit(solution)/shard_map/ppermute | solution.py:21
  10.0 5.0 %collective-permute-start.1 = (bf16[1,32,16,128]{3,2,1,0:T(8,128)(2,1)S(1)}, bf16[1,32,16,128]{3,2,1,0:T(8,128)(2,1)S(1)}, u32[]{:S(2)}, u32[]{:S(2)}) collective-permute-start(bf16[1,32,16,128]{3,2,1,0:T(8,128)(2,1)S(1)} %get-tuple-element.57), channel_id=1, source_target_pairs={{0,2},{1,5},{2,0},{3,7},{4,6},{5,1},{6,4},{7,3},{8,10},{9,13},{10,... | collective-permute-start | bytes 393224 | tf_op jit(solution)/shard_map/ppermute | solution.py:30
  10.5 5.0 %collective-permute-start = (bf16[1,32,16,128]{3,2,1,0:T(8,128)(2,1)S(1)}, bf16[1,32,16,128]{3,2,1,0:T(8,128)(2,1)S(1)}, u32[]{:S(2)}, u32[]{:S(2)}) collective-permute-start(bf16[1,32,16,128]{3,2,1,0:T(8,128)(2,1)S(1)} %get-tuple-element.57), channel_id=1, source_target_pairs={{0,4},{1,3},{2,6},{3,1},{4,0},{5,7},{6,2},{7,5},{8,12},{9,11},{10,... | collective-permute-start | bytes 393224 | tf_op jit(solution)/shard_map/ppermute | solution.py:30
  15.5 8.0 %collective-permute-start.7 = (bf16[2,32,16,128]{3,2,1,0:T(8,128)(2,1)S(1)}, bf16[2,32,16,128]{3,2,1,0:T(8,128)(2,1)S(1)}, u32[]{:S(2)}, u32[]{:S(2)}) collective-permute-start(bf16[2,32,16,128]{3,2,1,0:T(8,128)(2,1)S(1)} %pad_maximum_fusion.1), channel_id=1, source_target_pairs={{0,2},{1,5},{2,0},{3,7},{4,6},{5,1},{6,4},{7,3},{8,10},{9,13},{10,... | collective-permute-start | bytes 786440 | tf_op jit(solution)/shard_map/ppermute | solution.py:30
  17.1 6.5 %collective-permute-start.6 = (bf16[2,32,16,128]{3,2,1,0:T(8,128)(2,1)S(1)}, bf16[2,32,16,128]{3,2,1,0:T(8,128)(2,1)S(1)}, u32[]{:S(2)}, u32[]{:S(2)}) collective-permute-start(bf16[2,32,16,128]{3,2,1,0:T(8,128)(2,1)S(1)} %pad_maximum_fusion.1), channel_id=1, source_target_pairs={{0,4},{1,3},{2,6},{3,1},{4,0},{5,7},{6,2},{7,5},{8,12},{9,11},{10,... | collective-permute-start | bytes 786440 | tf_op jit(solution)/shard_map/ppermute | solution.py:30
  17.9 5.0 %collective-permute-start.5 = (bf16[1,32,16,128]{3,2,1,0:T(8,128)(2,1)S(1)}, bf16[1,32,16,128]{3,2,1,0:T(8,128)(2,1)S(1)}, u32[]{:S(2)}, u32[]{:S(2)}) collective-permute-start(bf16[1,32,16,128]{3,2,1,0:T(8,128)(2,1)S(1)} %collective-permute-done.4), channel_id=1, source_target_pairs={{0,8},{2,10},{4,12},{6,14},{8,0},{10,2},{12,4},{14,6},{16,24},{18,... | collective-permute-start | bytes 393224 | tf_op jit(solution)/shard_map/ppermute | solution.py:21
  23.7 4.1 %collective-permute-start.11 = (bf16[11,32,16,128]{3,2,1,0:T(8,128)(2,1)S(1)}, bf16[11,32,16,128]{3,2,1,0:T(8,128)(2,1)S(1)}, u32[]{:S(2)}, u32[]{:S(2)}) collective-permute-start(bf16[11,32,16,128]{3,2,1,0:T(8,128)(2,1)S(1)} %constant_dynamic-update-slice_fusion), channel_id=1, source_target_pairs={{0,1},{1,0},{2,3},{3,2},{4,5},{5,4},{6,7},{7,6},{8,9},{9,8},{10,11... | collective-permute-start | bytes 4325384 | tf_op jit(solution)/shard_map/ppermute | solution.py:21
  23.8 9.2 %collective-permute-start.10 = (bf16[3,32,16,128]{3,2,1,0:T(8,128)(2,1)S(1)}, bf16[3,32,16,128]{3,2,1,0:T(8,128)(2,1)S(1)}, u32[]{:S(2)}, u32[]{:S(2)}) collective-permute-start(bf16[3,32,16,128]{3,2,1,0:T(8,128)(2,1)S(1)} %pad_maximum_fusion), channel_id=1, source_target_pairs={{0,4},{1,3},{2,6},{3,1},{4,0},{5,7},{6,2},{7,5},{8,12},{9,11},{10,... | collective-permute-start | bytes 1179656 | tf_op jit(solution)/shard_map/ppermute | solution.py:30
  24.7 7.6 %collective-permute-start.9 = (bf16[1,32,16,128]{3,2,1,0:T(8,128)(2,1)S(1)}, bf16[1,32,16,128]{3,2,1,0:T(8,128)(2,1)S(1)}, u32[]{:S(2)}, u32[]{:S(2)}) collective-permute-start(bf16[1,32,16,128]{3,2,1,0:T(8,128)(2,1)S(1)} %collective-permute-done.3), channel_id=1, source_target_pairs={{0,24},{2,26},{4,28},{6,30},{8,16},{10,18},{12,20},{14,22},{16,8},... | collective-permute-start | bytes 393224 | tf_op jit(solution)/shard_map/ppermute | solution.py:21
  26.3 6.3 %collective-permute-start.8 = (bf16[1,32,16,128]{3,2,1,0:T(8,128)(2,1)S(1)}, bf16[1,32,16,128]{3,2,1,0:T(8,128)(2,1)S(1)}, u32[]{:S(2)}, u32[]{:S(2)}) collective-permute-start(bf16[1,32,16,128]{3,2,1,0:T(8,128)(2,1)S(1)} %collective-permute-done.5), channel_id=1, source_target_pairs={{0,2},{1,5},{2,0},{3,7},{4,6},{5,1},{6,4},{7,3},{8,10},{9,13},{10,... | collective-permute-start | bytes 393224 | tf_op jit(solution)/shard_map/ppermute | solution.py:30
  33.2 2.2 %collective-permute-start.12 = (bf16[5,32,16,128]{3,2,1,0:T(8,128)(2,1)S(1)}, bf16[5,32,16,128]{3,2,1,0:T(8,128)(2,1)S(1)}, u32[]{:S(2)}, u32[]{:S(2)}) collective-permute-start(bf16[5,32,16,128]{3,2,1,0:T(8,128)(2,1)S(1)} %constant_dynamic-update-slice_fusion.9), channel_id=1, source_target_pairs={{0,1},{1,0},{2,3},{3,2},{4,5},{5,4},{6,7},{7,6},{8,9},{9,8},{10,11... | collective-permute-start | bytes 1966088 | tf_op jit(solution)/shard_map/ppermute | solution.py:21
  39.5 1.2 %collective-permute-start.13 = (f32[16,128]{1,0:T(8,128)S(1)}, f32[16,128]{1,0:T(8,128)S(1)}, u32[]{:S(2)}, u32[]{:S(2)}) collective-permute-start(f32[16,128]{1,0:T(8,128)S(1)} %get-tuple-element.52), channel_id=1, source_target_pairs={{0,1},{1,0},{2,3},{3,2},{4,5},{5,4},{6,7},{7,6},{8,9},{9,8},{10,11... | collective-permute-start | bytes 24584 | tf_op jit(solution)/shard_map/ppermute | solution.py:21
